TPU v7x, 32 devices: a whole 2x2x4 slice. The times are simulated.
32 devices in a mesh: groups: 2 (over y), space: 4 (over z), ens: 2 (over x), chan: 2 (over core).
Axes of the slice: x: 2, y: 2, z: 4, core: 2. Of those that a mesh axis runs over, the one named last changes fastest.
Arguments:
- fields: bfloat16 [4, 8, 768, 256], P(('groups', 'ens'), 'space', None, 'chan'), parts along dimension 0, may hold values from -6 to 6
- cotangent: bfloat16 [4, 8, 768, 256], P(('groups', 'ens'), 'space', None, 'chan'), parts along dimension 0, may hold values from -6 to 6
- band_rows: int32 [8], P('groups'), parts along dimension 0, may hold values from 1 to 2, 6 in all
- tap_shift: int32 [6, 9], replicated, may hold values from -8 to 8
- quad_weight: float32 [6], replicated, may hold values from 1.5 to 6
- legendre: bfloat16 [368, 6, 384], P('space'), may hold values from -0.3125 to 0.3125
- spectral_filter: bfloat16 [2, 384, 256], P(None, None, 'chan'), may hold values from -4 to 4
- tap_weight: bfloat16 [9, 256], P(None, 'chan'), may hold values from -2 to 2
Outputs:
- output: bfloat16 [4, 8, 768, 256], P(('groups', 'ens'), 'space', None, 'chan'), parts along dimension 0
- input_grad: bfloat16 [4, 8, 768, 256], P(('groups', 'ens'), 'space', None, 'chan'), parts along dimension 0
- filter_grad: float32 [4, 384, 256], P('groups', None, 'chan'), parts along dimension 0
- tap_grad: float32 [18, 256], P('groups', 'chan'), parts along dimension 0
There are 2 independent parts, one for each index of `groups`. A program takes and returns all parts, laid end to end along the dimension named above; an argument that names none is the same for every part. Nothing has to cross between parts.
Inputs may be any that keep to these rules, and one draw needn't show every extreme that they name: `band_rows`: entry b is the number of live latitude rows of device b of the space axis, held in its first slots; the entries sum to 6 and some device holds 2.
All inputs are finite; a program needn't handle non-finite values.
Results may differ from a plain program's by a relative error of at most 0.0084.
Values may be sent and summed in bfloat16 or wider, within the bound.
No kernel may reach another device: no remote copies, remote signals or barrier semaphores. Data moves between devices by JAX's collectives and lax.ppermute only.
A program may use at most 256 MiB of HBM per device.

v0:
```python
import functools
import math

import jax
import jax.numpy as jnp
import ml_dtypes
import numpy as np
from jax import lax
from jax.experimental import pallas as pl
from jax.experimental.pallas import tpu as pltpu
from jax.sharding import PartitionSpec as P

F32 = jnp.float32
BF16 = jnp.bfloat16
VMEM = pl.BlockSpec(memory_space=pltpu.VMEM)
SMEM = pl.BlockSpec(memory_space=pltpu.SMEM)
REACH = 8
TAP_ROWS = 16


def gelu_value(values):
    return 0.5 * values * (1.0 + lax.erf(values * 0.7071067811865476))


def gelu_slope(values):
    return (
        0.5 * (1.0 + lax.erf(values * 0.7071067811865476))
        + values * jnp.exp(-0.5 * values * values) * 0.3989422804014327
    )


def round_up(count, step):
    return -(-count // step) * step


def fourier_table(lon_count, blocks, local_modes, padded_modes):
    lon_ids = np.arange(lon_count)
    mode_ids = np.arange(blocks * local_modes)
    phase = (mode_ids[:, None] * lon_ids[None, :] % lon_count) * (2.0 * math.pi / lon_count)
    factor = 1.0 / math.sqrt(lon_count)
    both = np.stack([np.cos(phase), -np.sin(phase)]) * factor
    both = both.reshape(2, blocks, local_modes, lon_count).transpose(1, 0, 2, 3)
    both = np.pad(both, ((0, 0), (0, 0), (0, padded_modes - local_modes), (0, 0)))
    return both.reshape(blocks, 2 * padded_modes, lon_count).astype(ml_dtypes.bfloat16)


def lat_pairs(lat_count):
    return [(a, b) for a in range(lat_count) for b in range(a, lat_count)]


def first_row_of(rows_ref, block, blocks):
    total = jnp.int32(0)
    for other in range(blocks):
        total = total + jnp.where(other < block, rows_ref[other], 0)
    return total


def call(kernel, out_shape, in_specs, args, scratch=(), limit=32, flops=0, moved=0):
    leaves = jax.tree.leaves(out_shape)
    return pl.pallas_call(
        kernel,
        out_shape=out_shape,
        in_specs=in_specs,
        out_specs=jax.tree.map(lambda _: VMEM, out_shape),
        scratch_shapes=list(scratch),
        compiler_params=pltpu.CompilerParams(vmem_limit_bytes=limit * 1024 * 1024),
        cost_estimate=pl.CostEstimate(
            flops=flops,
            bytes_accessed=moved + sum(math.prod(leaf.shape) * leaf.dtype.itemsize for leaf in leaves),
            transcendentals=0,
        ),
    )(*args)


def forward_kernel(blocks, rows_ref, x_ref, dy_ref, table_ref, act_ref, down_ref, up_ref, *outs):
    slots, lon_count, chans = x_ref.shape
    me = lax.axis_index("space")
    step = 64 if lon_count % 64 == 0 else lon_count

    def activate(i, carry):
        part = pl.ds(pl.multiple_of(i * step, step), step)
        for slot in range(slots):
            act_ref[slot, part, :] = gelu_value(x_ref[slot, part, :].astype(F32)).astype(BF16)
        return carry

    lax.fori_loop(0, lon_count // step, activate, 0)
    last = rows_ref[me] - 1
    down_ref[0] = act_ref[0]
    down_ref[1] = dy_ref[0]
    up_ref[0] = act_ref[last]
    up_ref[1] = dy_ref[last]
    source = jnp.concatenate(
        [dy_ref[slot] for slot in range(slots)] + [act_ref[slot] for slot in range(slots)], axis=-1
    )
    for shift in range(blocks):
        block = lax.rem(me + shift, blocks)
        sums = jnp.dot(table_ref[block], source, preferred_element_type=F32).astype(BF16)
        for field in range(2):
            for slot in range(slots):
                at = (field * slots + slot) * chans
                outs[shift][field, slot] = sums[:, at : at + chans]


def prepare_kernel(local_modes, leg_ref, filter_ref, mixer_ref, back_ref, pairs_ref):
    lat_count, padded_modes, _ = leg_ref.shape
    pairs = lat_pairs(lat_count)
    used = len(pairs) * padded_modes
    mode = lax.axis_index("space") * local_modes + lax.broadcasted_iota(
        jnp.int32, (padded_modes, 1), 0
    )
    twice = jnp.where(mode == 0, 1.0, 2.0)
    for index, (a, b) in enumerate(pairs):
        at = index * padded_modes
        pairs_ref[at : at + padded_modes, :] = (
            leg_ref[a].astype(F32) * leg_ref[b].astype(F32) * twice
        ).astype(BF16)
    if pairs_ref.shape[0] > used:
        pairs_ref[used:, :] = jnp.zeros((pairs_ref.shape[0] - used, pairs_ref.shape[1]), BF16)
    both = jnp.concatenate([filter_ref[0], filter_ref[1]], axis=-1)
    mixer_ref[...] = jnp.dot(pairs_ref[...], both, preferred_element_type=F32)

    def turn(i, carry):
        part = pl.ds(pl.multiple_of(i * 128, 128), 128)
        back_ref[:, part] = pairs_ref[part, :].astype(F32).T.astype(BF16)
        return carry

    lax.fori_loop(0, pairs_ref.shape[0] // 128, turn, 0)


def mix_kernel(blocks, lat_count, rows_ref, quad_ref, mixer_ref, back_ref, *refs):
    ins, outs, sums = refs[:blocks], refs[blocks : 2 * blocks], refs[2 * blocks : 3 * blocks]
    coeff, grad, synth, grad_coeff, products, gradient = refs[3 * blocks :]
    slots = ins[0].shape[1]
    padded_modes, chans = coeff.shape[2:]
    me = lax.axis_index("space")
    pairs = lat_pairs(lat_count)
    for shift in range(blocks):
        block = lax.rem(me + (blocks - shift), blocks)
        start = first_row_of(rows_ref, block, blocks)
        for slot in range(slots):
            lat = jnp.minimum(start + slot, lat_count - 1)

            @pl.when(slot < rows_ref[block])
            def _():
                weight = quad_ref[lat]
                for part in range(2):
                    rows = slice(part * padded_modes, (part + 1) * padded_modes)
                    grad[lat, part] = ins[shift][0, slot, rows, :].astype(F32)
                    coeff[lat, part] = ins[shift][1, slot, rows, :].astype(F32) * weight

    def mix(i, carry):
        rows = pl.ds(pl.multiple_of(i * 8, 8), 8)
        a0 = [coeff[lat, 0, rows, :] for lat in range(lat_count)]
        a1 = [coeff[lat, 1, rows, :] for lat in range(lat_count)]
        b0 = [grad[lat, 0, rows, :] for lat in range(lat_count)]
        b1 = [grad[lat, 1, rows, :] for lat in range(lat_count)]
        zero = jnp.zeros((8, chans), F32)
        y0, y1, z0, z1 = ([zero] * lat_count for _ in range(4))
        for index, (a, b) in enumerate(pairs):
            at = pl.ds(pl.multiple_of(index * padded_modes + i * 8, 8), 8)
            real = mixer_ref[at, :chans]
            imag = mixer_ref[at, chans:]
            h0 = h1 = zero
            for p, q in [(a, b)] if a == b else [(a, b), (b, a)]:
                y0[p] = y0[p] + real * a0[q] - imag * a1[q]
                y1[p] = y1[p] + imag * a0[q] + real * a1[q]
                z0[q] = z0[q] + real * b0[p] + imag * b1[p]
                z1[q] = z1[q] + real * b1[p] - imag * b0[p]
                h0 = h0 + b0[p] * a0[q] + b1[p] * a1[q]
                h1 = h1 + b1[p] * a0[q] - b0[p] * a1[q]
            products[at, :chans] = h0
            products[at, chans:] = h1
        for lat in range(lat_count):
            synth[lat, 0, rows, :] = y0[lat]
            synth[lat, 1, rows, :] = y1[lat]
            grad_coeff[lat, 0, rows, :] = z0[lat] * quad_ref[lat]
            grad_coeff[lat, 1, rows, :] = z1[lat] * quad_ref[lat]
        return carry

    lax.fori_loop(0, padded_modes // 8, mix, 0)
    used = len(pairs) * padded_modes
    if products.shape[0] > used:
        products[used:, :] = jnp.zeros((products.shape[0] - used, products.shape[1]), F32)
    gradient[...] = jnp.dot(
        back_ref[...], products[...].astype(BF16), preferred_element_type=F32
    )
    share = gradient.shape[0] // blocks
    for shift in range(blocks):
        block = lax.rem(me + shift, blocks)
        part = gradient[pl.ds(pl.multiple_of(block * share, share), share), :]
        sums[shift][...] = jnp.concatenate([part[:, :chans], part[:, chans:]], axis=0).astype(BF16)
        start = first_row_of(rows_ref, block, blocks)
        for slot in range(slots):
            lat = jnp.minimum(start + slot, lat_count - 1)
            for half in range(2):
                rows = slice(half * padded_modes, (half + 1) * padded_modes)
                outs[shift][0, slot, rows, :] = synth[lat, half].astype(BF16)
                outs[shift][1, slot, rows, :] = grad_coeff[lat, half].astype(BF16)


def disco_kernel(
    blocks, lat_count, rows_ref, shift_ref, x_ref, dy_ref, act_ref, low_ref, high_ref, taps_ref,
    base_ref, slope_ref, base_grad_ref, tap_ref, acts, grads,
):
    slots, lon_count, chans = x_ref.shape
    taps = taps_ref.shape[0]
    me = lax.axis_index("space")
    live = rows_ref[me]
    start = first_row_of(rows_ref, me, blocks)

    def wrapped(target, row, value):
        target[row, REACH : REACH + lon_count, :] = value
        target[row, :REACH, :] = value[lon_count - REACH :, :]
        target[row, REACH + lon_count :, :] = value[:REACH, :]

    wrapped(acts, 0, low_ref[0].astype(F32))
    wrapped(grads, 0, low_ref[1].astype(F32))
    wrapped(acts, slots + 1, high_ref[0].astype(F32))
    wrapped(grads, slots + 1, high_ref[1].astype(F32))
    for slot in range(slots):
        alive = jnp.where(slot < live, 1.0, 0.0)
        wrapped(acts, slot + 1, act_ref[slot].astype(F32))
        wrapped(grads, slot + 1, dy_ref[slot].astype(F32) * alive)
    weights = taps_ref[...].astype(F32)
    step = 32 if lon_count % 32 == 0 else lon_count
    totals = [jnp.zeros((8, chans), F32)] * taps
    for slot in range(slots):
        below = jnp.where(slot + 1 < live, slot + 2, slots + 1)
        rows = [slot, slot + 1, below]
        lat = jnp.clip(start + slot, 0, lat_count - 1)
        lats = [jnp.maximum(lat - 1, 0), lat, jnp.minimum(lat + 1, lat_count - 1)]
        ahead = [REACH + shift_ref[lat, t] for t in range(taps)]
        behind = [REACH - shift_ref[lats[2 - t // 3], t] for t in range(taps)]

        def taps_of(i, totals):
            at = pl.multiple_of(i * step, step)
            part = pl.ds(at, step)
            x = x_ref[slot, part, :].astype(F32)
            dy = grads[slot + 1, pl.ds(pl.multiple_of(REACH + at, 8), step), :]
            out = x
            back = jnp.zeros((step, chans), F32)
            fresh = []
            for t in range(taps):
                moved = acts[rows[t // 3], pl.ds(at + ahead[t], step), :]
                out = out + moved * weights[t : t + 1, :]
                fresh.append(totals[t] + jnp.sum((moved * dy).reshape(step // 8, 8, chans), axis=0))
                back = back + grads[rows[2 - t // 3], pl.ds(at + behind[t], step), :] * weights[
                    t : t + 1, :
                ]
            slope = gelu_slope(x)
            base_ref[slot, part, :] = out
            slope_ref[slot, part, :] = slope
            base_grad_ref[slot, part, :] = dy + back * slope
            return tuple(fresh)

        totals = list(lax.fori_loop(0, lon_count // step, taps_of, tuple(totals)))
    lines = [jnp.sum(total, axis=0, keepdims=True) for total in totals]
    lines.append(jnp.zeros((tap_ref.shape[0] - taps, chans), F32))
    tap_ref[...] = jnp.concatenate(lines, axis=0)


def sum_kernel(tap_ref, *refs):
    parts, out_ref = refs[:-1], refs[-1]
    count = parts[0].shape[0]
    total = parts[0][...].astype(F32)
    for part in parts[1:]:
        total = total + part[...].astype(F32)
    out_ref[:count, :] = total
    out_ref[count:, :] = tap_ref[...]


def member_kernel(lat_count, *refs):
    members = len(refs) - 2
    parts, out_ref, held = refs[:members], refs[-2], refs[-1]
    me = lax.axis_index("ens")
    for shift in range(members):
        held[lax.rem(me + (members - shift), members)] = parts[shift][...]
    total = held[0]
    for member in range(1, members):
        total = total + held[member]
    total = total / members
    count = total.shape[0] - TAP_ROWS
    out_ref[:count, :] = total[:count, :].astype(BF16)
    taps = total[count:, :] / lat_count
    high = taps.astype(BF16)
    out_ref[count : count + TAP_ROWS, :] = high
    out_ref[count + TAP_ROWS :, :] = (taps - high.astype(F32)).astype(BF16)


def spread_kernel(*refs):
    blocks = len(refs) - 3
    parts, filter_ref, tap_ref, held = refs[:blocks], refs[-3], refs[-2], refs[-1]
    me = lax.axis_index("space")
    degrees = filter_ref.shape[1]
    share = degrees // blocks
    for shift in range(blocks):
        block = lax.rem(me + (blocks - shift), blocks)
        part = parts[shift][...].astype(F32)
        rows = pl.ds(pl.multiple_of(block * share, share), share)
        filter_ref[0, rows, :] = part[:share, :]
        filter_ref[1, rows, :] = part[share : 2 * share, :]
        held[block] = part[2 * share : 2 * share + TAP_ROWS, :] + part[2 * share + TAP_ROWS :, :]
    total = held[0]
    for block in range(1, blocks):
        total = total + held[block]
    tap_ref[...] = total[: tap_ref.shape[0], :]


def finish_kernel(
    blocks, rows_ref, table_ref, base_ref, slope_ref, base_grad_ref, *refs
):
    ins, out_ref, grad_ref, source = refs[:blocks], refs[blocks], refs[blocks + 1], refs[blocks + 2]
    slots, lon_count, chans = base_ref.shape
    me = lax.axis_index("space")
    live = rows_ref[me]
    depth = ins[0].shape[2]
    for shift in range(blocks):
        block = lax.rem(me + (blocks - shift), blocks)
        rows = pl.ds(pl.multiple_of(block * depth, depth), depth)
        for field in range(2):
            for slot in range(slots):
                at = (field * slots + slot) * chans
                source[rows, at : at + chans] = ins[shift][field, slot]
    sums = jnp.dot(table_ref[...], source[...], preferred_element_type=F32)
    for slot in range(slots):
        at = slot * chans
        out = base_ref[slot] + sums[:, at : at + chans]
        at = (slots + slot) * chans
        grad = base_grad_ref[slot] + sums[:, at : at + chans] * slope_ref[slot]
        alive = slot < live
        out_ref[slot] = jnp.where(alive, out, 0.0).astype(BF16)
        grad_ref[slot] = jnp.where(alive, grad, 0.0).astype(BF16)


def shifted(values, axis, shift):
    count = lax.axis_size(axis)
    return lax.ppermute(values, axis, [(i, (i + shift) % count) for i in range(count)])


def body(
    fields, cotangent, band_rows, tap_shift, quad_weight, legendre, spectral_filter, tap_weight
):
    blocks = lax.axis_size("space")
    members = lax.axis_size("ens")
    _, slots, lon_count, chans = fields.shape
    local_modes, lat_count, degrees = legendre.shape
    padded_modes = round_up(local_modes, 16)
    depth = 2 * padded_modes
    pairs = len(lat_pairs(lat_count))
    pair_rows = round_up(pairs * padded_modes, 128)
    share = 2 * degrees // blocks
    big = 32 if pair_rows <= 4096 else 60
    shape = jax.ShapeDtypeStruct
    table = fourier_table(lon_count, blocks, local_modes, padded_modes)
    table_in = jnp.asarray(table)
    table_out = jnp.asarray(np.ascontiguousarray(table.reshape(blocks * depth, lon_count).T))
    x, dy = fields[0], cotangent[0]
    field = shape((slots, lon_count, chans), F32)
    coded = shape((2, slots, depth, chans), BF16)
    rim = shape((2, lon_count, chans), BF16)

    act, down, up, *coded_parts = call(
        functools.partial(forward_kernel, blocks),
        [shape(x.shape, BF16), rim, rim] + [coded] * blocks,
        [SMEM, VMEM, VMEM, VMEM],
        (band_rows, x, dy, table_in),
        flops=2 * blocks * depth * lon_count * 2 * slots * chans,
    )
    got = [coded_parts[0]] + [shifted(coded_parts[s], "space", s) for s in range(1, blocks)]
    low = lax.ppermute(up, "space", [(i, i + 1) for i in range(blocks - 1)])
    high = lax.ppermute(down, "space", [(i + 1, i) for i in range(blocks - 1)])

    leg_rows = jnp.pad(
        jnp.transpose(legendre, (1, 0, 2)), ((0, 0), (0, padded_modes - local_modes), (0, 0))
    )
    mixer, back = call(
        functools.partial(prepare_kernel, local_modes),
        [shape((pair_rows, 2 * chans), F32), shape((degrees, pair_rows), BF16)],
        [VMEM, VMEM],
        (leg_rows, spectral_filter),
        scratch=[pltpu.VMEM((pair_rows, degrees), BF16)],
        limit=big,
        flops=2 * pair_rows * degrees * 2 * chans,
    )
    base, slope, base_grad, tap_part = call(
        functools.partial(disco_kernel, blocks, lat_count),
        [field, field, field, shape((TAP_ROWS, chans), F32)],
        [SMEM, SMEM] + [VMEM] * 6,
        (band_rows, tap_shift, x, dy, act, low, high, tap_weight),
        scratch=[pltpu.VMEM((slots + 2, lon_count + 2 * REACH, chans), F32)] * 2,
        flops=60 * slots * lon_count * chans,
    )
    spectral = pltpu.VMEM((lat_count, 2, padded_modes, chans), F32)
    mixed = call(
        functools.partial(mix_kernel, blocks, lat_count),
        [coded] * blocks + [shape((share, chans), BF16)] * blocks,
        [SMEM, SMEM] + [VMEM] * (2 + blocks),
        (band_rows, quad_weight, mixer, back, *got),
        scratch=[spectral] * 4
        + [pltpu.VMEM((pair_rows, 2 * chans), F32), pltpu.VMEM((degrees, 2 * chans), F32)],
        limit=big,
        flops=2 * degrees * pair_rows * 2 * chans,
    )
    back_parts, sum_parts = mixed[:blocks], mixed[blocks:]
    summed = [sum_parts[0]] + [shifted(sum_parts[s], "space", s) for s in range(1, blocks)]
    returned = [back_parts[0]] + [shifted(back_parts[s], "space", s) for s in range(1, blocks)]
    own = call(
        sum_kernel,
        shape((share + TAP_ROWS, chans), F32),
        [VMEM] * (1 + blocks),
        (tap_part, *summed),
    )
    by_member = [own] + [shifted(own, "ens", s) for s in range(1, members)]
    final = call(
        functools.partial(member_kernel, lat_count),
        shape((share + 2 * TAP_ROWS, chans), BF16),
        [VMEM] * members,
        by_member,
        scratch=[pltpu.VMEM((members, share + TAP_ROWS, chans), F32)],
    )
    spread = [final] + [shifted(final, "space", s) for s in range(1, blocks)]
    output, input_grad = call(
        functools.partial(finish_kernel, blocks),
        [shape(x.shape, BF16)] * 2,
        [SMEM] + [VMEM] * (4 + blocks),
        (band_rows, table_out, base, slope, base_grad, *returned),
        scratch=[pltpu.VMEM((blocks * depth, 2 * slots * chans), BF16)],
        flops=2 * blocks * depth * lon_count * 2 * slots * chans,
    )
    filter_grad, tap_grad = call(
        spread_kernel,
        [shape((2, degrees, chans), F32), shape((tap_weight.shape[0], chans), F32)],
        [VMEM] * blocks,
        spread,
        scratch=[pltpu.VMEM((blocks, TAP_ROWS, chans), F32)],
    )
    return (output[None], input_grad[None], filter_grad, tap_grad)


def solution(mesh):
    in_specs = (
        P(("groups", "ens"), "space", None, "chan"),
        P(("groups", "ens"), "space", None, "chan"),
        P("groups"),
        P(),
        P(),
        P("space", None, None),
        P(None, None, "chan"),
        P(None, "chan"),
    )
    out_specs = (
        P(("groups", "ens"), "space", None, "chan"),
        P(("groups", "ens"), "space", None, "chan"),
        P("groups", None, "chan"),
        P("groups", "chan"),
    )
    return jax.shard_map(body, mesh=mesh, in_specs=in_specs, out_specs=out_specs, check_vma=False)
```

profile of v0, /device:TPU:0, one launch (start us, length us, event | category | flops | bytes accessed | tf_op | source)
XLA Modules:
  0.0 79.7 jit_solution(9925535289942185506)
XLA Ops:
  0.6 0.0 copy-start.1
  0.6 1.0 %copy-done.1 = bf16[1,2,768,128]{3,2,1,0:T(8,128)(2,1)S(1)} copy-done((bf16[1,2,768,128]{3,2,1,0:T(8,128)(2,1)S(1)}, bf16[1,2,768,128]{3,2,1,0:T(8,128)(2,1)}, u32[]{:S(2)}) %copy-start.1) | copy-done | bytes 393240
  1.6 0.0 copy-start.3
  1.6 1.0 %copy-done.3 = bf16[1,2,768,128]{3,2,1,0:T(8,128)(2,1)S(1)} copy-done((bf16[1,2,768,128]{3,2,1,0:T(8,128)(2,1)S(1)}, bf16[1,2,768,128]{3,2,1,0:T(8,128)(2,1)}, u32[]{:S(2)}) %copy-start.3) | copy-done | bytes 393240
  2.6 0.0 copy-start.5
  2.6 0.7 copy-done.5
  3.3 0.0 copy-start.11
  3.3 1.3 %copy-done.11 = bf16[4,192,768]{2,1,0:T(8,128)(2,1)S(1)} copy-done((bf16[4,192,768]{2,1,0:T(8,128)(2,1)S(1)}, bf16[4,192,768]{2,1,0:T(8,128)(2,1)}, u32[]{:S(2)}) %copy-start.11) | copy-done | bytes 1179672
  4.6 0.0 copy-start.12
  4.6 0.0 copy-start.10
  4.6 1.7 %shard_map.129 = (bf16[2,768,128]{2,1,0:T(8,128)(2,1)S(1)}, bf16[2,768,128]{2,1,0:T(8,128)(2,1)S(1)}, bf16[2,768,128]{2,1,0:T(8,128)(2,1)S(1)}, bf16[2,2,192,128...) custom-call(s32[4]{0:T(128)S(1)} %copy-done.5, ...), custom_call_target="tpu_custom_call" | custom-call | flops 603979776 | bytes 1966080 | tf_op jit(solution)/shard_map/pallas_call | solution.py:60
  6.2 0.0 copy-start.6
  6.3 0.0 copy-start.9
  6.3 5.0 %collective-permute-start = (bf16[2,768,128]{2,1,0:T(8,128)(2,1)S(1)}, bf16[2,768,128]{2,1,0:T(8,128)(2,1)S(1)}, u32[]{:S(2)}, u32[]{:S(2)}) collective-permute-start(bf16[2,768,128]{2,1,0:T(8,128)(2,1)S(1)} %get-tuple-element.30), channel_id=1, source_target_pairs={{0,4},{4,8},{8,12},{1,5},{5,9},{9,13},{2,6},{6,10},{10,14},{3,7},{... | collective-permute-start | bytes 1179656 | tf_op jit(solution)/shard_map/ppermute | solution.py:370
  11.2 1.3 %collective-permute-start.1 = (bf16[2,768,128]{2,1,0:T(8,128)(2,1)S(1)}, bf16[2,768,128]{2,1,0:T(8,128)(2,1)S(1)}, u32[]{:S(2)}, u32[]{:S(2)}) collective-permute-start(bf16[2,768,128]{2,1,0:T(8,128)(2,1)S(1)} %get-tuple-element.31), channel_id=1, source_target_pairs={{4,0},{8,4},{12,8},{5,1},{9,5},{13,9},{6,2},{10,6},{14,10},{7,3},{... | collective-permute-start | bytes 1179656 | tf_op jit(solution)/shard_map/ppermute | solution.py:371
  12.5 2.7 %collective-permute-start.2 = (bf16[2,2,192,128]{3,2,1,0:T(8,128)(2,1)S(1)}, bf16[2,2,192,128]{3,2,1,0:T(8,128)(2,1)S(1)}, u32[]{:S(2)}, u32[]{:S(2)}) collective-permute-start(bf16[2,2,192,128]{3,2,1,0:T(8,128)(2,1)S(1)} %get-tuple-element.38), channel_id=1, source_target_pairs={{0,4},{4,8},{8,12},{12,0},{1,5},{5,9},{9,13},{13,1},{2,6},{6,10},{... | collective-permute-start | bytes 589832 | tf_op jit(solution)/shard_map/ppermute | solution.py:337
  15.2 2.6 %collective-permute-start.3 = (bf16[2,2,192,128]{3,2,1,0:T(8,128)(2,1)S(1)}, bf16[2,2,192,128]{3,2,1,0:T(8,128)(2,1)S(1)}, u32[]{:S(2)}, u32[]{:S(2)}) collective-permute-start(bf16[2,2,192,128]{3,2,1,0:T(8,128)(2,1)S(1)} %get-tuple-element.39), channel_id=1, source_target_pairs={{0,8},{4,12},{8,0},{12,4},{1,9},{5,13},{9,1},{13,5},{2,10},{6,14},... | collective-permute-start | bytes 589832 | tf_op jit(solution)/shard_map/ppermute | solution.py:337
  17.8 1.3 %collective-permute-start.4 = (bf16[2,2,192,128]{3,2,1,0:T(8,128)(2,1)S(1)}, bf16[2,2,192,128]{3,2,1,0:T(8,128)(2,1)S(1)}, u32[]{:S(2)}, u32[]{:S(2)}) collective-permute-start(bf16[2,2,192,128]{3,2,1,0:T(8,128)(2,1)S(1)} %get-tuple-element.40), channel_id=1, source_target_pairs={{0,12},{4,0},{8,4},{12,8},{1,13},{5,1},{9,5},{13,9},{2,14},{6,2},{... | collective-permute-start | bytes 589832 | tf_op jit(solution)/shard_map/ppermute | solution.py:337
  19.2 0.0 copy-done.12
  19.2 0.0 copy-done.10
  19.2 2.4 %shard_map.131 = (f32[2048,256]{1,0:T(8,128)S(1)}, bf16[384,2048]{1,0:T(8,128)(2,1)S(1)}) custom-call(bf16[6,96,384]{2,1,0:T(8,128)(2,1)S(1)} %pad.4.leg_ref, bf16[2,384,128]{2,1,0:T(8,128)(2,1)S(1)} %copy-done.10), custom_call_target="tpu_custom_call" | custom-call | flops 402653184 | bytes 3670016 | tf_op jit(solution)/shard_map/pallas_call | solution.py:60
  21.6 9.8 %collective-permute-done.2.refs_1_ = bf16[2,2,192,128]{3,2,1,0:T(8,128)(2,1)S(1)} collective-permute-done((bf16[2,2,192,128]{3,2,1,0:T(8,128)(2,1)S(1)}, bf16[2,2,192,128]{3,2,1,0:T(8,128)(2,1)S(1)}, u32[]{:S(2)}, u32[]{:S(2)}) %collective-permute-start.2) | collective-permute-done | bytes 196640 | tf_op jit(solution)/shard_map/ppermute | solution.py:337
  31.5 7.3 %collective-permute-done.3.refs_2_ = bf16[2,2,192,128]{3,2,1,0:T(8,128)(2,1)S(1)} collective-permute-done((bf16[2,2,192,128]{3,2,1,0:T(8,128)(2,1)S(1)}, bf16[2,2,192,128]{3,2,1,0:T(8,128)(2,1)S(1)}, u32[]{:S(2)}, u32[]{:S(2)}) %collective-permute-start.3) | collective-permute-done | bytes 196640 | tf_op jit(solution)/shard_map/ppermute | solution.py:337
  38.8 0.0 collective-permute-done.4.refs_3_
  38.8 0.0 copy-done.6
  38.8 0.0 copy-done.9
  38.8 0.0 copy-start.2
  38.8 0.0 copy-start.4
  38.8 0.0 copy-start.7
  38.9 0.0 copy-start.8
  38.9 2.8 %shard_map.132 = (bf16[2,2,192,128]{3,2,1,0:T(8,128)(2,1)S(1)}, bf16[2,2,192,128]{3,2,1,0:T(8,128)(2,1)S(1)}, bf16[2,2,192,128]{3,2,1,0:T(8,128)(2,1)S(1)}, bf16...) custom-call(s32[4]{0:T(128)S(1)} %copy-done.6, ...), custom_call_target="tpu_custom_call" | custom-call | flops 402653184 | bytes 983040 | tf_op jit(solution)/shard_map/pallas_call | solution.py:60
  41.7 0.0 copy-start
  41.7 2.1 %collective-permute-start.10 = (bf16[192,128]{1,0:T(8,128)(2,1)S(1)}, bf16[192,128]{1,0:T(8,128)(2,1)S(1)}, u32[]{:S(2)}, u32[]{:S(2)}) collective-permute-start(bf16[192,128]{1,0:T(8,128)(2,1)S(1)} %get-tuple-element.51), channel_id=1, source_target_pairs={{0,12},{4,0},{8,4},{12,8},{1,13},{5,1},{9,5},{13,9},{2,14},{6,2},{... | collective-permute-start | bytes 147464 | tf_op jit(solution)/shard_map/ppermute | solution.py:337
  43.7 1.3 %collective-permute-start.5 = (bf16[2,2,192,128]{3,2,1,0:T(8,128)(2,1)S(1)}, bf16[2,2,192,128]{3,2,1,0:T(8,128)(2,1)S(1)}, u32[]{:S(2)}, u32[]{:S(2)}) collective-permute-start(bf16[2,2,192,128]{3,2,1,0:T(8,128)(2,1)S(1)} %get-tuple-element.42), channel_id=1, source_target_pairs={{0,4},{4,8},{8,12},{12,0},{1,5},{5,9},{9,13},{13,1},{2,6},{6,10},{... | collective-permute-start | bytes 589832 | tf_op jit(solution)/shard_map/ppermute | solution.py:337
  45.1 1.4 %collective-permute-start.6 = (bf16[2,2,192,128]{3,2,1,0:T(8,128)(2,1)S(1)}, bf16[2,2,192,128]{3,2,1,0:T(8,128)(2,1)S(1)}, u32[]{:S(2)}, u32[]{:S(2)}) collective-permute-start(bf16[2,2,192,128]{3,2,1,0:T(8,128)(2,1)S(1)} %get-tuple-element.43), channel_id=1, source_target_pairs={{0,8},{4,12},{8,0},{12,4},{1,9},{5,13},{9,1},{13,5},{2,10},{6,14},... | collective-permute-start | bytes 589832 | tf_op jit(solution)/shard_map/ppermute | solution.py:337
  46.5 4.1 %collective-permute-done.10.refs_3_ = bf16[192,128]{1,0:T(8,128)(2,1)S(1)} collective-permute-done((bf16[192,128]{1,0:T(8,128)(2,1)S(1)}, bf16[192,128]{1,0:T(8,128)(2,1)S(1)}, u32[]{:S(2)}, u32[]{:S(2)}) %collective-permute-start.10) | collective-permute-done | bytes 49184 | tf_op jit(solution)/shard_map/ppermute | solution.py:337
  50.5 0.0 collective-permute-start.7
  50.5 0.0 collective-permute-done.low_ref
  50.5 6.0 %collective-permute-start.8 = (bf16[192,128]{1,0:T(8,128)(2,1)S(1)}, bf16[192,128]{1,0:T(8,128)(2,1)S(1)}, u32[]{:S(2)}, u32[]{:S(2)}) collective-permute-start(bf16[192,128]{1,0:T(8,128)(2,1)S(1)} %get-tuple-element.49), channel_id=1, source_target_pairs={{0,4},{4,8},{8,12},{12,0},{1,5},{5,9},{9,13},{13,1},{2,6},{6,10},{... | collective-permute-start | bytes 147464 | tf_op jit(solution)/shard_map/ppermute | solution.py:337
  56.6 0.0 collective-permute-done.1.high_ref
  56.6 1.5 %collective-permute-start.9 = (bf16[192,128]{1,0:T(8,128)(2,1)S(1)}, bf16[192,128]{1,0:T(8,128)(2,1)S(1)}, u32[]{:S(2)}, u32[]{:S(2)}) collective-permute-start(bf16[192,128]{1,0:T(8,128)(2,1)S(1)} %get-tuple-element.50), channel_id=1, source_target_pairs={{0,8},{4,12},{8,0},{12,4},{1,9},{5,13},{9,1},{13,5},{2,10},{6,14},... | collective-permute-start | bytes 147464 | tf_op jit(solution)/shard_map/ppermute | solution.py:337
  58.1 0.0 copy-done.2
  58.1 0.0 copy-done.4
  58.1 0.0 copy-done.7
  58.1 0.0 copy-done.8
  58.1 3.3 %shard_map.130 = (f32[2,768,128]{2,1,0:T(8,128)S(1)}, f32[2,768,128]{2,1,0:T(8,128)S(1)}, f32[2,768,128]{2,1,0:T(8,128)S(1)}, f32[16,128]{1,0:T(8,128)S(1)}) custom-call(s32[4]{0:T(128)S(1)} %copy-done.6, s32[6,9]{1,0:T(8,128)S(1)} %copy-done.7, bf16[2,768,128]{2,1,0:T(8,128)(2,1)S(1)} %bitcast.6, bf16[2,768,128]{2,1,0:T(8,128)(2,1)S(1)} %bitcast.8, ...), custom_call_target="tpu_custom_call" | custom-call | flops 11796480 | bytes 2367488 | tf_op jit(solution)/shard_map/pallas_call | solution.py:60
  61.4 0.3 collective-permute-done.8.refs_1_
  61.7 5.7 %collective-permute-done.9.refs_2_ = bf16[192,128]{1,0:T(8,128)(2,1)S(1)} collective-permute-done((bf16[192,128]{1,0:T(8,128)(2,1)S(1)}, bf16[192,128]{1,0:T(8,128)(2,1)S(1)}, u32[]{:S(2)}, u32[]{:S(2)}) %collective-permute-start.9) | collective-permute-done | bytes 49184 | tf_op jit(solution)/shard_map/ppermute | solution.py:337
  67.4 1.6 %collective-permute-start.11 = (f32[208,128]{1,0:T(8,128)S(1)}, f32[208,128]{1,0:T(8,128)S(1)}, u32[]{:S(2)}, u32[]{:S(2)}) collective-permute-start(f32[208,128]{1,0:T(8,128)S(1)} %shard_map.134.refs_0_), channel_id=1, source_target_pairs={{0,2},{2,0},{1,3},{3,1},{4,6},{6,4},{5,7},{7,5},{8,10},{10,8},{9,1... | collective-permute-start | bytes 319496 | tf_op jit(solution)/shard_map/ppermute | solution.py:337
  69.0 3.2 %collective-permute-done.11.refs_1_ = f32[208,128]{1,0:T(8,128)S(1)} collective-permute-done((f32[208,128]{1,0:T(8,128)S(1)}, f32[208,128]{1,0:T(8,128)S(1)}, u32[]{:S(2)}, u32[]{:S(2)}) %collective-permute-start.11) | collective-permute-done | bytes 106528 | tf_op jit(solution)/shard_map/ppermute | solution.py:337
  72.2 0.1 collective-permute-start.12
  72.3 2.0 %collective-permute-start.13 = (bf16[224,128]{1,0:T(8,128)(2,1)S(1)}, bf16[224,128]{1,0:T(8,128)(2,1)S(1)}, u32[]{:S(2)}, u32[]{:S(2)}) collective-permute-start(bf16[224,128]{1,0:T(8,128)(2,1)S(1)} %shard_map.135.refs_0_), channel_id=1, source_target_pairs={{0,8},{4,12},{8,0},{12,4},{1,9},{5,13},{9,1},{13,5},{2,10},{6,14},... | collective-permute-start | bytes 172040 | tf_op jit(solution)/shard_map/ppermute | solution.py:337
  74.3 0.0 collective-permute-done.5.refs_1_
  74.3 1.8 %collective-permute-start.14 = (bf16[224,128]{1,0:T(8,128)(2,1)S(1)}, bf16[224,128]{1,0:T(8,128)(2,1)S(1)}, u32[]{:S(2)}, u32[]{:S(2)}) collective-permute-start(bf16[224,128]{1,0:T(8,128)(2,1)S(1)} %shard_map.135.refs_0_), channel_id=1, source_target_pairs={{0,12},{4,0},{8,4},{12,8},{1,13},{5,1},{9,5},{13,9},{2,14},{6,2},{... | collective-permute-start | bytes 172040 | tf_op jit(solution)/shard_map/ppermute | solution.py:337
  76.1 0.0 collective-permute-done.6.refs_2_
  76.1 0.0 collective-permute-done.7.refs_3_
  76.1 0.0 copy-done
  76.1 2.3 %shard_map.133 = (bf16[2,768,128]{2,1,0:T(8,128)(2,1)}, bf16[2,768,128]{2,1,0:T(8,128)(2,1)}) custom-call(s32[4]{0:T(128)S(1)} %copy-done.6, bf16[768,768]{1,0:T(8,128)(2,1)S(1)} %copy-done, f32[2,768,128]{2,1,0:T(8,128)S(1)} %get-tuple-element.32.base_ref, f32[2,768,128]{2,1,0:T(8,128)S(1)} %get-tuple-element.33.slope_ref, ...), custom_call_target="tpu_custom_call" | custom-call | flops 603979776 | bytes 786432 | tf_op jit(solution)/shard_map/pallas_call | solution.py:60
  78.5 0.0 collective-permute-done.12.refs_1_
  78.5 0.0 collective-permute-done.13.refs_2_
  78.5 0.4 collective-permute-done.14.refs_3_
  78.9 0.8 shard_map.136
  (3 shorter events, 0.1 us)
Async XLA Ops:
  0.6 1.0 %copy-start.1 = (bf16[1,2,768,128]{3,2,1,0:T(8,128)(2,1)S(1)}, bf16[1,2,768,128]{3,2,1,0:T(8,128)(2,1)}, u32[]{:S(2)}) copy-start(bf16[1,2,768,128]{3,2,1,0:T(8,128)(2,1)} %param.10) | copy-start | bytes 1179652
  1.6 1.0 %copy-start.3 = (bf16[1,2,768,128]{3,2,1,0:T(8,128)(2,1)S(1)}, bf16[1,2,768,128]{3,2,1,0:T(8,128)(2,1)}, u32[]{:S(2)}) copy-start(bf16[1,2,768,128]{3,2,1,0:T(8,128)(2,1)} %param.11) | copy-start | bytes 1179652
  2.6 0.7 copy-start.5
  3.3 1.3 %copy-start.11 = (bf16[4,192,768]{2,1,0:T(8,128)(2,1)S(1)}, bf16[4,192,768]{2,1,0:T(8,128)(2,1)}, u32[]{:S(2)}) copy-start(bf16[4,192,768]{2,1,0:T(8,128)(2,1)} %constant.7.clone.table_ref) | copy-start | bytes 3538948
  4.6 14.6 %copy-start.12 = (bf16[92,6,384]{2,0,1:T(8,128)(2,1)S(1)}, bf16[92,6,384]{2,0,1:T(8,128)(2,1)}, u32[]{:S(2)}) copy-start(bf16[92,6,384]{2,0,1:T(8,128)(2,1)} %param.15) | copy-start | bytes 1271812
  4.6 14.7 %copy-start.10 = (bf16[2,384,128]{2,1,0:T(8,128)(2,1)S(1)}, bf16[2,384,128]{2,1,0:T(8,128)(2,1)}, u32[]{:S(2)}) copy-start(bf16[2,384,128]{2,1,0:T(8,128)(2,1)} %filter_ref.1) | copy-start | bytes 589828
  6.2 32.6 %copy-start.6 = (s32[4]{0:T(128)S(1)}, s32[4]{0:T(128)}, u32[]{:S(2)}) copy-start(s32[4]{0:T(128)} %rows_ref.7) | copy-start | bytes 52
  6.3 32.6 %copy-start.9 = (f32[6]{0:T(128)S(1)}, f32[6]{0:T(128)}, u32[]{:S(2)}) copy-start(f32[6]{0:T(128)} %quad_ref.1) | copy-start | bytes 76
  6.3 44.3 %collective-permute-start = (bf16[2,768,128]{2,1,0:T(8,128)(2,1)S(1)}, bf16[2,768,128]{2,1,0:T(8,128)(2,1)S(1)}, u32[]{:S(2)}, u32[]{:S(2)}) collective-permute-start(bf16[2,768,128]{2,1,0:T(8,128)(2,1)S(1)} %get-tuple-element.30), channel_id=1, source_target_pairs={{0,4},{4,8},{8,12},{1,5},{5,9},{9,13},{2,6},{6,10},{10,14},{3,7},{... | collective-permute-start | bytes 1179656 | tf_op jit(solution)/shard_map/ppermute | solution.py:370
  11.2 45.4 %collective-permute-start.1 = (bf16[2,768,128]{2,1,0:T(8,128)(2,1)S(1)}, bf16[2,768,128]{2,1,0:T(8,128)(2,1)S(1)}, u32[]{:S(2)}, u32[]{:S(2)}) collective-permute-start(bf16[2,768,128]{2,1,0:T(8,128)(2,1)S(1)} %get-tuple-element.31), channel_id=1, source_target_pairs={{4,0},{8,4},{12,8},{5,1},{9,5},{13,9},{6,2},{10,6},{14,10},{7,3},{... | collective-permute-start | bytes 1179656 | tf_op jit(solution)/shard_map/ppermute | solution.py:371
  12.5 19.0 %collective-permute-start.2 = (bf16[2,2,192,128]{3,2,1,0:T(8,128)(2,1)S(1)}, bf16[2,2,192,128]{3,2,1,0:T(8,128)(2,1)S(1)}, u32[]{:S(2)}, u32[]{:S(2)}) collective-permute-start(bf16[2,2,192,128]{3,2,1,0:T(8,128)(2,1)S(1)} %get-tuple-element.38), channel_id=1, source_target_pairs={{0,4},{4,8},{8,12},{12,0},{1,5},{5,9},{9,13},{13,1},{2,6},{6,10},{... | collective-permute-start | bytes 589832 | tf_op jit(solution)/shard_map/ppermute | solution.py:337
  15.2 23.6 %collective-permute-start.3 = (bf16[2,2,192,128]{3,2,1,0:T(8,128)(2,1)S(1)}, bf16[2,2,192,128]{3,2,1,0:T(8,128)(2,1)S(1)}, u32[]{:S(2)}, u32[]{:S(2)}) collective-permute-start(bf16[2,2,192,128]{3,2,1,0:T(8,128)(2,1)S(1)} %get-tuple-element.39), channel_id=1, source_target_pairs={{0,8},{4,12},{8,0},{12,4},{1,9},{5,13},{9,1},{13,5},{2,10},{6,14},... | collective-permute-start | bytes 589832 | tf_op jit(solution)/shard_map/ppermute | solution.py:337
  17.8 21.0 %collective-permute-start.4 = (bf16[2,2,192,128]{3,2,1,0:T(8,128)(2,1)S(1)}, bf16[2,2,192,128]{3,2,1,0:T(8,128)(2,1)S(1)}, u32[]{:S(2)}, u32[]{:S(2)}) collective-permute-start(bf16[2,2,192,128]{3,2,1,0:T(8,128)(2,1)S(1)} %get-tuple-element.40), channel_id=1, source_target_pairs={{0,12},{4,0},{8,4},{12,8},{1,13},{5,1},{9,5},{13,9},{2,14},{6,2},{... | collective-permute-start | bytes 589832 | tf_op jit(solution)/shard_map/ppermute | solution.py:337
  38.8 19.3 %copy-start.2 = (bf16[1,2,768,128]{3,2,1,0:T(8,128)(2,1)S(1)}, bf16[1,2,768,128]{3,2,1,0:T(8,128)(2,1)}, u32[]{:S(2)}) copy-start(bf16[1,2,768,128]{3,2,1,0:T(8,128)(2,1)} %param.10) | copy-start | bytes 1179652
  38.8 19.3 %copy-start.4 = (bf16[1,2,768,128]{3,2,1,0:T(8,128)(2,1)S(1)}, bf16[1,2,768,128]{3,2,1,0:T(8,128)(2,1)}, u32[]{:S(2)}) copy-start(bf16[1,2,768,128]{3,2,1,0:T(8,128)(2,1)} %param.11) | copy-start | bytes 1179652
  38.8 19.3 %copy-start.7 = (s32[6,9]{1,0:T(8,128)S(1)}, s32[6,9]{1,0:T(8,128)}, u32[]{:S(2)}) copy-start(s32[6,9]{1,0:T(8,128)} %shift_ref.1) | copy-start | bytes 652
  38.9 19.3 %copy-start.8 = (bf16[9,128]{1,0:T(8,128)(2,1)S(1)}, bf16[9,128]{1,0:T(8,128)(2,1)}, u32[]{:S(2)}) copy-start(bf16[9,128]{1,0:T(8,128)(2,1)} %taps_ref.1) | copy-start | bytes 6916
  41.7 34.5 %copy-start = (bf16[768,768]{1,0:T(8,128)(2,1)S(1)}, bf16[768,768]{1,0:T(8,128)(2,1)}, u32[]{:S(2)}) copy-start(bf16[768,768]{1,0:T(8,128)(2,1)} %constant.8.clone.table_ref) | copy-start | bytes 3538948
  41.7 8.9 %collective-permute-start.10 = (bf16[192,128]{1,0:T(8,128)(2,1)S(1)}, bf16[192,128]{1,0:T(8,128)(2,1)S(1)}, u32[]{:S(2)}, u32[]{:S(2)}) collective-permute-start(bf16[192,128]{1,0:T(8,128)(2,1)S(1)} %get-tuple-element.51), channel_id=1, source_target_pairs={{0,12},{4,0},{8,4},{12,8},{1,13},{5,1},{9,5},{13,9},{2,14},{6,2},{... | collective-permute-start | bytes 147464 | tf_op jit(solution)/shard_map/ppermute | solution.py:337
  43.7 30.6 %collective-permute-start.5 = (bf16[2,2,192,128]{3,2,1,0:T(8,128)(2,1)S(1)}, bf16[2,2,192,128]{3,2,1,0:T(8,128)(2,1)S(1)}, u32[]{:S(2)}, u32[]{:S(2)}) collective-permute-start(bf16[2,2,192,128]{3,2,1,0:T(8,128)(2,1)S(1)} %get-tuple-element.42), channel_id=1, source_target_pairs={{0,4},{4,8},{8,12},{12,0},{1,5},{5,9},{9,13},{13,1},{2,6},{6,10},{... | collective-permute-start | bytes 589832 | tf_op jit(solution)/shard_map/ppermute | solution.py:337
  45.1 31.0 %collective-permute-start.6 = (bf16[2,2,192,128]{3,2,1,0:T(8,128)(2,1)S(1)}, bf16[2,2,192,128]{3,2,1,0:T(8,128)(2,1)S(1)}, u32[]{:S(2)}, u32[]{:S(2)}) collective-permute-start(bf16[2,2,192,128]{3,2,1,0:T(8,128)(2,1)S(1)} %get-tuple-element.43), channel_id=1, source_target_pairs={{0,8},{4,12},{8,0},{12,4},{1,9},{5,13},{9,1},{13,5},{2,10},{6,14},... | collective-permute-start | bytes 589832 | tf_op jit(solution)/shard_map/ppermute | solution.py:337
  50.5 25.6 %collective-permute-start.7 = (bf16[2,2,192,128]{3,2,1,0:T(8,128)(2,1)S(1)}, bf16[2,2,192,128]{3,2,1,0:T(8,128)(2,1)S(1)}, u32[]{:S(2)}, u32[]{:S(2)}) collective-permute-start(bf16[2,2,192,128]{3,2,1,0:T(8,128)(2,1)S(1)} %get-tuple-element.44), channel_id=1, source_target_pairs={{0,12},{4,0},{8,4},{12,8},{1,13},{5,1},{9,5},{13,9},{2,14},{6,2},{... | collective-permute-start | bytes 589832 | tf_op jit(solution)/shard_map/ppermute | solution.py:337
  50.5 11.2 %collective-permute-start.8 = (bf16[192,128]{1,0:T(8,128)(2,1)S(1)}, bf16[192,128]{1,0:T(8,128)(2,1)S(1)}, u32[]{:S(2)}, u32[]{:S(2)}) collective-permute-start(bf16[192,128]{1,0:T(8,128)(2,1)S(1)} %get-tuple-element.49), channel_id=1, source_target_pairs={{0,4},{4,8},{8,12},{12,0},{1,5},{5,9},{9,13},{13,1},{2,6},{6,10},{... | collective-permute-start | bytes 147464 | tf_op jit(solution)/shard_map/ppermute | solution.py:337
  56.6 10.8 %collective-permute-start.9 = (bf16[192,128]{1,0:T(8,128)(2,1)S(1)}, bf16[192,128]{1,0:T(8,128)(2,1)S(1)}, u32[]{:S(2)}, u32[]{:S(2)}) collective-permute-start(bf16[192,128]{1,0:T(8,128)(2,1)S(1)} %get-tuple-element.50), channel_id=1, source_target_pairs={{0,8},{4,12},{8,0},{12,4},{1,9},{5,13},{9,1},{13,5},{2,10},{6,14},... | collective-permute-start | bytes 147464 | tf_op jit(solution)/shard_map/ppermute | solution.py:337
  67.4 4.8 %collective-permute-start.11 = (f32[208,128]{1,0:T(8,128)S(1)}, f32[208,128]{1,0:T(8,128)S(1)}, u32[]{:S(2)}, u32[]{:S(2)}) collective-permute-start(f32[208,128]{1,0:T(8,128)S(1)} %shard_map.134.refs_0_), channel_id=1, source_target_pairs={{0,2},{2,0},{1,3},{3,1},{4,6},{6,4},{5,7},{7,5},{8,10},{10,8},{9,1... | collective-permute-start | bytes 319496 | tf_op jit(solution)/shard_map/ppermute | solution.py:337
  72.2 6.2 %collective-permute-start.12 = (bf16[224,128]{1,0:T(8,128)(2,1)S(1)}, bf16[224,128]{1,0:T(8,128)(2,1)S(1)}, u32[]{:S(2)}, u32[]{:S(2)}) collective-permute-start(bf16[224,128]{1,0:T(8,128)(2,1)S(1)} %shard_map.135.refs_0_), channel_id=1, source_target_pairs={{0,4},{4,8},{8,12},{12,0},{1,5},{5,9},{9,13},{13,1},{2,6},{6,10},{... | collective-permute-start | bytes 172040 | tf_op jit(solution)/shard_map/ppermute | solution.py:337
  72.3 6.2 %collective-permute-start.13 = (bf16[224,128]{1,0:T(8,128)(2,1)S(1)}, bf16[224,128]{1,0:T(8,128)(2,1)S(1)}, u32[]{:S(2)}, u32[]{:S(2)}) collective-permute-start(bf16[224,128]{1,0:T(8,128)(2,1)S(1)} %shard_map.135.refs_0_), channel_id=1, source_target_pairs={{0,8},{4,12},{8,0},{12,4},{1,9},{5,13},{9,1},{13,5},{2,10},{6,14},... | collective-permute-start | bytes 172040 | tf_op jit(solution)/shard_map/ppermute | solution.py:337
  74.3 4.5 %collective-permute-start.14 = (bf16[224,128]{1,0:T(8,128)(2,1)S(1)}, bf16[224,128]{1,0:T(8,128)(2,1)S(1)}, u32[]{:S(2)}, u32[]{:S(2)}) collective-permute-start(bf16[224,128]{1,0:T(8,128)(2,1)S(1)} %shard_map.135.refs_0_), channel_id=1, source_target_pairs={{0,12},{4,0},{8,4},{12,8},{1,13},{5,1},{9,5},{13,9},{2,14},{6,2},{... | collective-permute-start | bytes 172040 | tf_op jit(solution)/shard_map/ppermute | solution.py:337
where the time goes:
time: 79.9 us; the launch traced here: 79.7 us
  waiting for transfers between devices  30.8 us (39%)
  starting transfers between devices  30.7 us (38%)
  Pallas kernels  13.4 us (17%)
  local copies, waits for them, and re-layouts  4.01 us (5%)
    ppermute x13, waiting for transfers between devices, shifted(): lax.ppermute(values, axis, [(i, (i + shift) % count) for i in range(count)])  30.8 us
    ppermute x13, starting transfers between devices, shifted(): lax.ppermute(values, axis, [(i, (i + shift) % count) for i in range(count)])  24.4 us
    pallas_call x8, Pallas kernels, call(): pl.pallas_call(kernel, out_shape=out_shape, in_specs=in_specs, out_specs=...  13.4 us
    ppermute x1, starting transfers between devices, body(): low = lax.ppermute(up, 'space', [(i, i + 1) for i in range(blocks - 1)])  4.96 us
    unnamed x26, local copies, waits for them, and re-layouts  3.96 us
  transfers between devices with their start and end apart: 15, of which 7 were waited for; matrix products, arithmetic and copies ran while one was open for 0% of the time, Pallas kernels for 14%

commit v1 on v0

--- a/solution.py
+++ b/solution.py
@@ -14,6 +14,7 @@
 BF16 = jnp.bfloat16
 VMEM = pl.BlockSpec(memory_space=pltpu.VMEM)
 SMEM = pl.BlockSpec(memory_space=pltpu.SMEM)
+HBM = pl.BlockSpec(memory_space=pltpu.HBM)
 REACH = 8
 TAP_ROWS = 16
 
@@ -55,8 +56,7 @@
     return total
 
 
-def call(kernel, out_shape, in_specs, args, scratch=(), limit=32, flops=0, moved=0):
-    leaves = jax.tree.leaves(out_shape)
+def call(kernel, out_shape, in_specs, args, scratch=(), limit=32, flops=0, moved=1024):
     return pl.pallas_call(
         kernel,
         out_shape=out_shape,
@@ -64,18 +64,26 @@
         out_specs=jax.tree.map(lambda _: VMEM, out_shape),
         scratch_shapes=list(scratch),
         compiler_params=pltpu.CompilerParams(vmem_limit_bytes=limit * 1024 * 1024),
-        cost_estimate=pl.CostEstimate(
-            flops=flops,
-            bytes_accessed=moved + sum(math.prod(leaf.shape) * leaf.dtype.itemsize for leaf in leaves),
-            transcendentals=0,
-        ),
+        cost_estimate=pl.CostEstimate(flops=flops, bytes_accessed=moved, transcendentals=0),
     )(*args)
 
 
-def forward_kernel(blocks, rows_ref, x_ref, dy_ref, table_ref, act_ref, down_ref, up_ref, *outs):
+def forward_kernel(
+    blocks, rows_ref, x_hbm, dy_hbm, table_hbm, act_ref, *refs
+):
+    outs, (down_ref, up_ref, x_ref, dy_ref, table_ref, sems) = refs[:blocks], refs[blocks:]
     slots, lon_count, chans = x_ref.shape
     me = lax.axis_index("space")
     step = 64 if lon_count % 64 == 0 else lon_count
+    loads = [
+        pltpu.make_async_copy(source, target, sems.at[i])
+        for i, (source, target) in enumerate(
+            [(x_hbm, x_ref), (dy_hbm, dy_ref), (table_hbm, table_ref)]
+        )
+    ]
+    for load in loads:
+        load.start()
+    loads[0].wait()
 
     def activate(i, carry):
         part = pl.ds(pl.multiple_of(i * step, step), step)
@@ -84,6 +92,7 @@
         return carry
 
     lax.fori_loop(0, lon_count // step, activate, 0)
+    loads[1].wait()
     last = rows_ref[me] - 1
     down_ref[0] = act_ref[0]
     down_ref[1] = dy_ref[0]
@@ -92,8 +101,9 @@
     source = jnp.concatenate(
         [dy_ref[slot] for slot in range(slots)] + [act_ref[slot] for slot in range(slots)], axis=-1
     )
+    loads[2].wait()
     for shift in range(blocks):
-        block = lax.rem(me + shift, blocks)
+        block = jnp.bitwise_xor(me, shift)
         sums = jnp.dot(table_ref[block], source, preferred_element_type=F32).astype(BF16)
         for field in range(2):
             for slot in range(slots):
@@ -128,14 +138,14 @@
 
 
 def mix_kernel(blocks, lat_count, rows_ref, quad_ref, mixer_ref, back_ref, *refs):
-    ins, outs, sums = refs[:blocks], refs[blocks : 2 * blocks], refs[2 * blocks : 3 * blocks]
-    coeff, grad, synth, grad_coeff, products, gradient = refs[3 * blocks :]
+    ins, outs = refs[:blocks], refs[blocks : 2 * blocks]
+    keep_ref, send_ref, coeff, grad, synth, grad_coeff, products, gradient = refs[2 * blocks :]
     slots = ins[0].shape[1]
     padded_modes, chans = coeff.shape[2:]
     me = lax.axis_index("space")
     pairs = lat_pairs(lat_count)
     for shift in range(blocks):
-        block = lax.rem(me + (blocks - shift), blocks)
+        block = jnp.bitwise_xor(me, shift)
         start = first_row_of(rows_ref, block, blocks)
         for slot in range(slots):
             lat = jnp.minimum(start + slot, lat_count - 1)
@@ -184,11 +194,14 @@
     gradient[...] = jnp.dot(
         back_ref[...], products[...].astype(BF16), preferred_element_type=F32
     )
-    share = gradient.shape[0] // blocks
+    half = gradient.shape[0] // 2
+    upper = jnp.where(jnp.bitwise_and(me, blocks // 2) != 0, 1, 0)
+    for target, which in ((keep_ref, upper), (send_ref, 1 - upper)):
+        part = gradient[pl.ds(pl.multiple_of(which * half, half), half), :]
+        both = jnp.concatenate([part[:, :chans], part[:, chans:]], axis=0)
+        target[...] = both.astype(target.dtype)
     for shift in range(blocks):
-        block = lax.rem(me + shift, blocks)
-        part = gradient[pl.ds(pl.multiple_of(block * share, share), share), :]
-        sums[shift][...] = jnp.concatenate([part[:, :chans], part[:, chans:]], axis=0).astype(BF16)
+        block = jnp.bitwise_xor(me, shift)
         start = first_row_of(rows_ref, block, blocks)
         for slot in range(slots):
             lat = jnp.minimum(start + slot, lat_count - 1)
@@ -259,47 +272,64 @@
     tap_ref[...] = jnp.concatenate(lines, axis=0)
 
 
-def sum_kernel(tap_ref, *refs):
-    parts, out_ref = refs[:-1], refs[-1]
-    count = parts[0].shape[0]
-    total = parts[0][...].astype(F32)
-    for part in parts[1:]:
-        total = total + part[...].astype(F32)
-    out_ref[:count, :] = total
-    out_ref[count:, :] = tap_ref[...]
+def split_taps(taps, out_ref, count):
+    high = taps.astype(BF16)
+    out_ref[count : count + TAP_ROWS, :] = high
+    out_ref[count + TAP_ROWS :, :] = (taps - high.astype(F32)).astype(BF16)
+
+
+def joined_taps(rows):
+    return rows[-2 * TAP_ROWS : -TAP_ROWS, :] + rows[-TAP_ROWS:, :]
+
+
+def halve_kernel(distance, kept_ref, got_ref, keep_ref, send_ref, total):
+    total[...] = kept_ref[...] + got_ref[...].astype(F32)
+    rows = total.shape[0] // 2
+    half = rows // 2
+    upper = jnp.where(jnp.bitwise_and(lax.axis_index("space"), distance) != 0, half, 0)
+    for target, at in ((keep_ref, upper), (send_ref, half - upper)):
+        both = [
+            total[pl.ds(pl.multiple_of(part * rows + at, 8), half), :] for part in range(2)
+        ]
+        target[...] = jnp.concatenate(both, axis=0).astype(target.dtype)
+
+
+def own_kernel(kept_ref, got_ref, tap_ref, out_ref):
+    count = kept_ref.shape[0]
+    out_ref[:count, :] = (kept_ref[...] + got_ref[...].astype(F32)).astype(BF16)
+    split_taps(tap_ref[...], out_ref, count)
 
 
 def member_kernel(lat_count, *refs):
     members = len(refs) - 2
     parts, out_ref, held = refs[:members], refs[-2], refs[-1]
     me = lax.axis_index("ens")
+    count = out_ref.shape[0] - 2 * TAP_ROWS
     for shift in range(members):
-        held[lax.rem(me + (members - shift), members)] = parts[shift][...]
+        at = lax.rem(me + (members - shift), members)
+        part = parts[shift][...].astype(F32)
+        held[at, :count, :] = part[:count, :]
+        held[at, count:, :] = joined_taps(part)
     total = held[0]
     for member in range(1, members):
         total = total + held[member]
     total = total / members
-    count = total.shape[0] - TAP_ROWS
     out_ref[:count, :] = total[:count, :].astype(BF16)
-    taps = total[count:, :] / lat_count
-    high = taps.astype(BF16)
-    out_ref[count : count + TAP_ROWS, :] = high
-    out_ref[count + TAP_ROWS :, :] = (taps - high.astype(F32)).astype(BF16)
+    split_taps(total[count:, :] / lat_count, out_ref, count)
 
 
 def spread_kernel(*refs):
-    blocks = len(refs) - 3
-    parts, filter_ref, tap_ref, held = refs[:blocks], refs[-3], refs[-2], refs[-1]
+    parts, (filter_ref, tap_ref, held) = refs[:-3], refs[-3:]
     me = lax.axis_index("space")
-    degrees = filter_ref.shape[1]
-    share = degrees // blocks
+    blocks = len(parts)
+    share = filter_ref.shape[1] // blocks
     for shift in range(blocks):
-        block = lax.rem(me + (blocks - shift), blocks)
+        block = jnp.bitwise_xor(me, shift)
         part = parts[shift][...].astype(F32)
-        rows = pl.ds(pl.multiple_of(block * share, share), share)
-        filter_ref[0, rows, :] = part[:share, :]
-        filter_ref[1, rows, :] = part[share : 2 * share, :]
-        held[block] = part[2 * share : 2 * share + TAP_ROWS, :] + part[2 * share + TAP_ROWS :, :]
+        at = pl.ds(pl.multiple_of(block * share, share), share)
+        filter_ref[0, at, :] = part[:share, :]
+        filter_ref[1, at, :] = part[share : 2 * share, :]
+        held[block] = joined_taps(part)
     total = held[0]
     for block in range(1, blocks):
         total = total + held[block]
@@ -315,7 +345,7 @@
     live = rows_ref[me]
     depth = ins[0].shape[2]
     for shift in range(blocks):
-        block = lax.rem(me + (blocks - shift), blocks)
+        block = jnp.bitwise_xor(me, shift)
         rows = pl.ds(pl.multiple_of(block * depth, depth), depth)
         for field in range(2):
             for slot in range(slots):
@@ -335,6 +365,15 @@
 def shifted(values, axis, shift):
     count = lax.axis_size(axis)
     return lax.ppermute(values, axis, [(i, (i + shift) % count) for i in range(count)])
+
+
+def crossed(values, distance):
+    count = lax.axis_size("space")
+    return lax.ppermute(values, "space", [(i, i ^ distance) for i in range(count)])
+
+
+def crossed_all(parts, distances):
+    return {s: crossed(parts[s], s) for s in distances}
 
 
 def body(
@@ -359,17 +398,22 @@
     coded = shape((2, slots, depth, chans), BF16)
     rim = shape((2, lon_count, chans), BF16)
 
-    act, down, up, *coded_parts = call(
+    act, *coded_parts, down, up = call(
         functools.partial(forward_kernel, blocks),
-        [shape(x.shape, BF16), rim, rim] + [coded] * blocks,
-        [SMEM, VMEM, VMEM, VMEM],
+        [shape(x.shape, BF16)] + [coded] * blocks + [rim] * 2,
+        [SMEM, HBM, HBM, HBM],
         (band_rows, x, dy, table_in),
+        scratch=[
+            pltpu.VMEM(x.shape, BF16),
+            pltpu.VMEM(dy.shape, BF16),
+            pltpu.VMEM(table.shape, BF16),
+            pltpu.SemaphoreType.DMA((3,)),
+        ],
+        limit=60,
         flops=2 * blocks * depth * lon_count * 2 * slots * chans,
     )
-    got = [coded_parts[0]] + [shifted(coded_parts[s], "space", s) for s in range(1, blocks)]
-    low = lax.ppermute(up, "space", [(i, i + 1) for i in range(blocks - 1)])
-    high = lax.ppermute(down, "space", [(i + 1, i) for i in range(blocks - 1)])
-
+    far = list(range(blocks - 1, 0, -1))
+    got = [coded_parts[0], *reversed(crossed_all(coded_parts, far).values())]
     leg_rows = jnp.pad(
         jnp.transpose(legendre, (1, 0, 2)), ((0, 0), (0, padded_modes - local_modes), (0, 0))
     )
@@ -381,34 +425,53 @@
         scratch=[pltpu.VMEM((pair_rows, degrees), BF16)],
         limit=big,
         flops=2 * pair_rows * degrees * 2 * chans,
-    )
+        moved=8 * pair_rows * chans,
+    )
+    down, up, got, mixer = lax.optimization_barrier((down, up, got, mixer))
+    low = lax.ppermute(up, "space", [(i, i + 1) for i in range(blocks - 1)])
+    high = lax.ppermute(down, "space", [(i + 1, i) for i in range(blocks - 1)])
+    spectral = pltpu.VMEM((lat_count, 2, padded_modes, chans), F32)
+    mixed = call(
+        functools.partial(mix_kernel, blocks, lat_count),
+        [coded] * blocks + [shape((degrees, chans), F32), shape((degrees, chans), BF16)],
+        [SMEM, SMEM] + [VMEM] * (2 + blocks),
+        (band_rows, quad_weight, mixer, back, *got),
+        scratch=[spectral] * 4
+        + [pltpu.VMEM((pair_rows, 2 * chans), F32), pltpu.VMEM((degrees, 2 * chans), F32)],
+        limit=big,
+        flops=2 * degrees * pair_rows * 2 * chans,
+    )
+    back_parts, keep, send = mixed[:blocks], mixed[blocks], mixed[blocks + 1]
+    distance = blocks // 2
+    got_sums = crossed(send, distance)
+    near = crossed(back_parts[1], 1)
+    far_parts, got_sums = lax.optimization_barrier((list(back_parts[2:]), got_sums))
+    returned = [back_parts[0], near]
+    returned += reversed(crossed_all([None, None, *far_parts], far[:-1]).values())
     base, slope, base_grad, tap_part = call(
         functools.partial(disco_kernel, blocks, lat_count),
         [field, field, field, shape((TAP_ROWS, chans), F32)],
         [SMEM, SMEM] + [VMEM] * 6,
         (band_rows, tap_shift, x, dy, act, low, high, tap_weight),
         scratch=[pltpu.VMEM((slots + 2, lon_count + 2 * REACH, chans), F32)] * 2,
-        flops=60 * slots * lon_count * chans,
-    )
-    spectral = pltpu.VMEM((lat_count, 2, padded_modes, chans), F32)
-    mixed = call(
-        functools.partial(mix_kernel, blocks, lat_count),
-        [coded] * blocks + [shape((share, chans), BF16)] * blocks,
-        [SMEM, SMEM] + [VMEM] * (2 + blocks),
-        (band_rows, quad_weight, mixer, back, *got),
-        scratch=[spectral] * 4
-        + [pltpu.VMEM((pair_rows, 2 * chans), F32), pltpu.VMEM((degrees, 2 * chans), F32)],
-        limit=big,
-        flops=2 * degrees * pair_rows * 2 * chans,
-    )
-    back_parts, sum_parts = mixed[:blocks], mixed[blocks:]
-    summed = [sum_parts[0]] + [shifted(sum_parts[s], "space", s) for s in range(1, blocks)]
-    returned = [back_parts[0]] + [shifted(back_parts[s], "space", s) for s in range(1, blocks)]
+    )
+    while distance > 1:
+        distance //= 2
+        rows = keep.shape[0] // 2
+        keep, send = call(
+            functools.partial(halve_kernel, distance),
+            [shape((rows, chans), F32), shape((rows, chans), BF16)],
+            [VMEM, VMEM],
+            (keep, got_sums),
+            scratch=[pltpu.VMEM(keep.shape, F32)],
+        )
+        got_sums = crossed(send, distance)
+    got_sums, returned[1] = lax.optimization_barrier((got_sums, returned[1]))
     own = call(
-        sum_kernel,
-        shape((share + TAP_ROWS, chans), F32),
-        [VMEM] * (1 + blocks),
-        (tap_part, *summed),
+        own_kernel,
+        shape((share + 2 * TAP_ROWS, chans), BF16),
+        [VMEM] * 3,
+        (keep, got_sums, tap_part),
     )
     by_member = [own] + [shifted(own, "ens", s) for s in range(1, members)]
     final = call(
@@ -418,7 +481,7 @@
         by_member,
         scratch=[pltpu.VMEM((members, share + TAP_ROWS, chans), F32)],
     )
-    spread = [final] + [shifted(final, "space", s) for s in range(1, blocks)]
+    spread = [final] + [crossed(final, s) for s in range(1, blocks)]
     output, input_grad = call(
         functools.partial(finish_kernel, blocks),
         [shape(x.shape, BF16)] * 2,

time: 79.9 us -> 69.6 us (0.87)
  starting transfers between devices: 30.7 us -> 22.8 us
  local copies, waits for them, and re-layouts: 4.01 us -> 0.12 us
  Pallas kernels: 13.4 us -> 15.6 us
  waiting for transfers between devices: 30.8 us -> 30 us
    ppermute x13 -> x1, waiting for transfers between devices: 30.8 us -> 2.69 us  [shifted(): lax.ppermute(values, axis, [(i, (i + shift) % count) for i in range(count)])]
    ppermute x0 -> x11, waiting for transfers between devices: none -> 27.3 us  [crossed(): lax.ppermute(values, 'space', [(i, i ^ distance) for i in range(count)])]
    ppermute x13 -> x1, starting transfers between devices: 24.4 us -> 1.55 us  [shifted(): lax.ppermute(values, axis, [(i, (i + shift) % count) for i in range(count)])]
    ppermute x0 -> x11, starting transfers between devices: none -> 14.6 us  [crossed(): lax.ppermute(values, 'space', [(i, i ^ distance) for i in range(count)])]
    unnamed x26, local copies, waits for them, and re-layouts: 3.96 us -> 0.08 us
    pallas_call x8 -> x9, Pallas kernels: 13.4 us -> 15.6 us  [call(): pl.pallas_call(kernel, out_shape=out_shape, in_specs=in_specs, out_specs=...]
  transfers between devices with their start and end apart: 15 -> 14, of which waited for: 7 -> 7; matrix products, arithmetic and copies ran while one was open for 0% -> 0% of each run, Pallas kernels for 14% -> 16%
where the time goes in v1:
time: 69.6 us; the launch traced here: 69.4 us
  waiting for transfers between devices  30 us (43%)
  starting transfers between devices  22.8 us (33%)
  Pallas kernels  15.6 us (22%)
  between operations  0.89 us (1%)
    ppermute x11, waiting for transfers between devices, crossed(): lax.ppermute(values, 'space', [(i, i ^ distance) for i in range(count)])  27.3 us
    pallas_call x9, Pallas kernels, call(): pl.pallas_call(kernel, out_shape=out_shape, in_specs=in_specs, out_specs=...  15.6 us
    ppermute x11, starting transfers between devices, crossed(): lax.ppermute(values, 'space', [(i, i ^ distance) for i in range(count)])  14.6 us
    ppermute x1, starting transfers between devices, body(): low = lax.ppermute(up, 'space', [(i, i + 1) for i in range(blocks - 1)])  5.28 us
    ppermute x1, waiting for transfers between devices, shifted(): lax.ppermute(values, axis, [(i, (i + shift) % count) for i in range(count)])  2.69 us
    ppermute x1, starting transfers between devices, shifted(): lax.ppermute(values, axis, [(i, (i + shift) % count) for i in range(count)])  1.55 us
  transfers between devices with their start and end apart: 14, of which 7 were waited for; matrix products, arithmetic and copies ran while one was open for 0% of the time, Pallas kernels for 16%

profile of v1, /device:TPU:0, one launch (start us, length us, event | category | flops | bytes accessed | tf_op | source)
XLA Modules:
  0.0 69.4 jit_solution(4698858329770005382)
XLA Ops:
  0.6 0.0 copy-start.10
  0.6 0.0 copy-start.9
  0.7 3.8 %shard_map.129 = (bf16[2,768,128]{2,1,0:T(8,128)(2,1)}, bf16[2,2,192,128]{3,2,1,0:T(8,128)(2,1)}, bf16[2,2,192,128]{3,2,1,0:T(8,128)(2,1)}, bf16[2,2,192,128]{3,...) custom-call(s32[4]{0:T(128)} %rows_ref.7, ...), custom_call_target="tpu_custom_call" | custom-call | flops 603979776 | bytes 1024 | tf_op jit(solution)/shard_map/pallas_call | solution.py:60
  4.5 0.0 copy-start.12
  4.5 0.0 copy-start.11
  4.5 0.0 copy-start.4
  4.5 0.0 copy-start.5
  4.5 0.0 copy-start.8
  4.5 3.1 %collective-permute-start = (bf16[2,2,192,128]{3,2,1,0:T(8,128)(2,1)}, bf16[2,2,192,128]{3,2,1,0:T(8,128)(2,1)S(1)}, u32[]{:S(2)}, u32[]{:S(2)}) collective-permute-start(bf16[2,2,192,128]{3,2,1,0:T(8,128)(2,1)} %get-tuple-element.45), channel_id=1, source_target_pairs={{0,4},{4,0},{8,12},{12,8},{1,5},{5,1},{9,13},{13,9},{2,6},{6,2},{1... | collective-permute-start | bytes 589832 | tf_op jit(solution)/shard_map/ppermute | solution.py:372
  7.6 2.6 %collective-permute-start.1 = (bf16[2,2,192,128]{3,2,1,0:T(8,128)(2,1)}, bf16[2,2,192,128]{3,2,1,0:T(8,128)(2,1)S(1)}, u32[]{:S(2)}, u32[]{:S(2)}) collective-permute-start(bf16[2,2,192,128]{3,2,1,0:T(8,128)(2,1)} %get-tuple-element.46), channel_id=1, source_target_pairs={{0,8},{4,12},{8,0},{12,4},{1,9},{5,13},{9,1},{13,5},{2,10},{6,14},... | collective-permute-start | bytes 589832 | tf_op jit(solution)/shard_map/ppermute | solution.py:372
  10.2 0.0 collective-permute-start.2
  10.2 0.0 copy-done.10
  10.3 0.0 copy-done.9
  10.3 2.4 %shard_map.130 = (f32[2048,256]{1,0:T(8,128)S(1)}, bf16[384,2048]{1,0:T(8,128)(2,1)S(1)}) custom-call(bf16[6,96,384]{2,1,0:T(8,128)(2,1)S(1)} %pad.4.leg_ref, bf16[2,384,128]{2,1,0:T(8,128)(2,1)S(1)} %copy-done.9), custom_call_target="tpu_custom_call" | custom-call | flops 402653184 | bytes 2097152 | tf_op jit(solution)/shard_map/pallas_call | solution.py:60
  12.7 3.5 %collective-permute-done.refs_1_ = bf16[2,2,192,128]{3,2,1,0:T(8,128)(2,1)S(1)} collective-permute-done((bf16[2,2,192,128]{3,2,1,0:T(8,128)(2,1)}, bf16[2,2,192,128]{3,2,1,0:T(8,128)(2,1)S(1)}, u32[]{:S(2)}, u32[]{:S(2)}) %collective-permute-start) | collective-permute-done | bytes 196640 | tf_op jit(solution)/shard_map/ppermute | solution.py:372
  16.2 8.8 %collective-permute-done.1.refs_2_ = bf16[2,2,192,128]{3,2,1,0:T(8,128)(2,1)S(1)} collective-permute-done((bf16[2,2,192,128]{3,2,1,0:T(8,128)(2,1)}, bf16[2,2,192,128]{3,2,1,0:T(8,128)(2,1)S(1)}, u32[]{:S(2)}, u32[]{:S(2)}) %collective-permute-start.1) | collective-permute-done | bytes 196640 | tf_op jit(solution)/shard_map/ppermute | solution.py:372
  25.0 0.0 collective-permute-done.2.refs_3_
  25.0 0.0 copy-done.12
  25.0 5.3 %collective-permute-start.3 = (bf16[2,768,128]{2,1,0:T(8,128)(2,1)S(1)}, bf16[2,768,128]{2,1,0:T(8,128)(2,1)S(1)}, u32[]{:S(2)}, u32[]{:S(2)}) collective-permute-start(bf16[2,768,128]{2,1,0:T(8,128)(2,1)S(1)} %copy-done.12), channel_id=1, source_target_pairs={{0,4},{4,8},{8,12},{1,5},{5,9},{9,13},{2,6},{6,10},{10,14},{3,7},{... | collective-permute-start | bytes 1179656 | tf_op jit(solution)/shard_map/ppermute | solution.py:431
  30.3 0.0 copy-done.11
  30.3 1.3 %collective-permute-start.4 = (bf16[2,768,128]{2,1,0:T(8,128)(2,1)S(1)}, bf16[2,768,128]{2,1,0:T(8,128)(2,1)S(1)}, u32[]{:S(2)}, u32[]{:S(2)}) collective-permute-start(bf16[2,768,128]{2,1,0:T(8,128)(2,1)S(1)} %copy-done.11), channel_id=1, source_target_pairs={{4,0},{8,4},{12,8},{5,1},{9,5},{13,9},{6,2},{10,6},{14,10},{7,3},{... | collective-permute-start | bytes 1179656 | tf_op jit(solution)/shard_map/ppermute | solution.py:432
  31.6 0.0 copy-done.4
  31.6 0.0 copy-done.5
  31.6 0.0 copy-done.8
  31.6 0.0 copy-start.1
  31.6 0.0 copy-start.2
  31.6 0.0 copy-start.3
  31.6 0.0 copy-start.6
  31.7 0.0 copy-start.7
  31.7 2.8 %shard_map.132 = (bf16[2,2,192,128]{3,2,1,0:T(8,128)(2,1)S(1)}, bf16[2,2,192,128]{3,2,1,0:T(8,128)(2,1)S(1)}, bf16[2,2,192,128]{3,2,1,0:T(8,128)(2,1)S(1)}, bf16...) custom-call(s32[4]{0:T(128)S(1)} %copy-done.5, f32[6]{0:T(128)S(1)} %copy-done.8, ...), custom_call_target="tpu_custom_call" | custom-call | flops 402653184 | bytes 1024 | tf_op jit(solution)/shard_map/pallas_call | solution.py:60
  34.5 0.0 copy-start
  34.5 3.7 %collective-permute-start.5 = (bf16[384,128]{1,0:T(8,128)(2,1)S(1)}, bf16[384,128]{1,0:T(8,128)(2,1)S(1)}, u32[]{:S(2)}, u32[]{:S(2)}) collective-permute-start(bf16[384,128]{1,0:T(8,128)(2,1)S(1)} %get-tuple-element.64), channel_id=1, source_target_pairs={{0,8},{4,12},{8,0},{12,4},{1,9},{5,13},{9,1},{13,5},{2,10},{6,14},... | collective-permute-start | bytes 294920 | tf_op jit(solution)/shard_map/ppermute | solution.py:372
  38.2 0.0 collective-permute-start.7
  38.2 8.7 %collective-permute-done.5.got_ref = bf16[384,128]{1,0:T(8,128)(2,1)S(1)} collective-permute-done((bf16[384,128]{1,0:T(8,128)(2,1)S(1)}, bf16[384,128]{1,0:T(8,128)(2,1)S(1)}, u32[]{:S(2)}, u32[]{:S(2)}) %collective-permute-start.5) | collective-permute-done | bytes 98336 | tf_op jit(solution)/shard_map/ppermute | solution.py:372
  47.0 0.5 collective-permute-start.6
  47.4 0.0 collective-permute-start.8
  47.4 3.7 %collective-permute-done.6.got_ref = bf16[192,128]{1,0:T(8,128)(2,1)S(1)} collective-permute-done((bf16[192,128]{1,0:T(8,128)(2,1)S(1)}, bf16[192,128]{1,0:T(8,128)(2,1)S(1)}, u32[]{:S(2)}, u32[]{:S(2)}) %collective-permute-start.6) | collective-permute-done | bytes 49184 | tf_op jit(solution)/shard_map/ppermute | solution.py:372
  51.1 0.3 collective-permute-start.9
  51.4 0.0 collective-permute-done.7.refs_1_
  51.4 0.0 collective-permute-done.3.low_ref
  51.4 0.0 collective-permute-done.4.high_ref
  51.4 0.0 copy-done.1
  51.5 0.0 copy-done.2
  51.5 0.0 copy-done.3
  51.5 0.0 copy-done.6
  51.5 0.0 copy-done.7
  51.5 3.3 %shard_map.131 = (f32[2,768,128]{2,1,0:T(8,128)S(1)}, f32[2,768,128]{2,1,0:T(8,128)S(1)}, f32[2,768,128]{2,1,0:T(8,128)S(1)}, f32[16,128]{1,0:T(8,128)S(1)}) custom-call(s32[4]{0:T(128)S(1)} %copy-done.5, s32[6,9]{1,0:T(8,128)S(1)} %copy-done.6, bf16[2,768,128]{2,1,0:T(8,128)(2,1)S(1)} %bitcast.6, bf16[2,768,128]{2,1,0:T(8,128)(2,1)S(1)} %bitcast.8, ...), custom_call_target="tpu_custom_call" | custom-call | bytes 1024 | tf_op jit(solution)/shard_map/pallas_call | solution.py:60
  54.9 1.6 %collective-permute-start.10 = (bf16[224,128]{1,0:T(8,128)(2,1)S(1)}, bf16[224,128]{1,0:T(8,128)(2,1)S(1)}, u32[]{:S(2)}, u32[]{:S(2)}) collective-permute-start(bf16[224,128]{1,0:T(8,128)(2,1)S(1)} %shard_map.135.refs_0_), channel_id=1, source_target_pairs={{0,2},{2,0},{1,3},{3,1},{4,6},{6,4},{5,7},{7,5},{8,10},{10,8},{9,1... | collective-permute-start | bytes 172040 | tf_op jit(solution)/shard_map/ppermute | solution.py:367
  56.4 2.7 %collective-permute-done.10.refs_1_ = bf16[224,128]{1,0:T(8,128)(2,1)S(1)} collective-permute-done((bf16[224,128]{1,0:T(8,128)(2,1)S(1)}, bf16[224,128]{1,0:T(8,128)(2,1)S(1)}, u32[]{:S(2)}, u32[]{:S(2)}) %collective-permute-start.10) | collective-permute-done | bytes 57376 | tf_op jit(solution)/shard_map/ppermute | solution.py:367
  59.2 3.4 %collective-permute-start.13 = (bf16[224,128]{1,0:T(8,128)(2,1)S(1)}, bf16[224,128]{1,0:T(8,128)(2,1)S(1)}, u32[]{:S(2)}, u32[]{:S(2)}) collective-permute-start(bf16[224,128]{1,0:T(8,128)(2,1)S(1)} %shard_map.136.refs_0_), channel_id=1, source_target_pairs={{0,12},{4,8},{8,4},{12,0},{1,13},{5,9},{9,5},{13,1},{2,14},{6,10},... | collective-permute-start | bytes 172040 | tf_op jit(solution)/shard_map/ppermute | solution.py:372
  62.6 0.0 collective-permute-start.12
  62.6 1.0 %collective-permute-start.11 = (bf16[224,128]{1,0:T(8,128)(2,1)S(1)}, bf16[224,128]{1,0:T(8,128)(2,1)S(1)}, u32[]{:S(2)}, u32[]{:S(2)}) collective-permute-start(bf16[224,128]{1,0:T(8,128)(2,1)S(1)} %shard_map.136.refs_0_), channel_id=1, source_target_pairs={{0,4},{4,0},{8,12},{12,8},{1,5},{5,1},{9,13},{13,9},{2,6},{6,2},{1... | collective-permute-start | bytes 172040 | tf_op jit(solution)/shard_map/ppermute | solution.py:372
  63.6 0.1 collective-permute-done.8.refs_2_
  63.7 0.0 collective-permute-done.9.refs_3_
  63.7 0.0 copy-done
  63.7 2.3 %shard_map.134 = (bf16[2,768,128]{2,1,0:T(8,128)(2,1)}, bf16[2,768,128]{2,1,0:T(8,128)(2,1)}) custom-call(s32[4]{0:T(128)S(1)} %copy-done.5, bf16[768,768]{1,0:T(8,128)(2,1)S(1)} %copy-done, f32[2,768,128]{2,1,0:T(8,128)S(1)} %get-tuple-element.51.base_ref, f32[2,768,128]{2,1,0:T(8,128)S(1)} %get-tuple-element.52.slope_ref, ...), custom_call_target="tpu_custom_call" | custom-call | flops 603979776 | bytes 1024 | tf_op jit(solution)/shard_map/pallas_call | solution.py:60
  66.1 0.0 collective-permute-done.13.refs_3_
  66.1 2.5 %collective-permute-done.12.refs_2_ = bf16[224,128]{1,0:T(8,128)(2,1)S(1)} collective-permute-done((bf16[224,128]{1,0:T(8,128)(2,1)S(1)}, bf16[224,128]{1,0:T(8,128)(2,1)S(1)}, u32[]{:S(2)}, u32[]{:S(2)}) %collective-permute-start.12) | collective-permute-done | bytes 57376 | tf_op jit(solution)/shard_map/ppermute | solution.py:372
  68.6 0.0 collective-permute-done.11.refs_1_
  68.6 0.8 %shard_map.137 = (f32[2,384,128]{2,1,0:T(8,128)}, f32[9,128]{1,0:T(8,128)}) custom-call(bf16[224,128]{1,0:T(8,128)(2,1)S(1)} %shard_map.136.refs_0_, bf16[224,128]{1,0:T(8,128)(2,1)S(1)} %collective-permute-done.11.refs_1_, bf16[224,128]{1,0:T(8,128)(2,1)S(1)} %collective-permute-done.12.refs_2_, bf16[224,128]{1,0:T(8,128)(2,1)S(1)} %collective-permute-done.13.refs_3_), custom_call_target="tpu_custom_call" | custom-call | bytes 1024 | tf_op jit(solution)/shard_map/pallas_call | solution.py:60
  (4 shorter events, 0.1 us)
Async XLA Ops:
  0.6 9.6 %copy-start.10 = (bf16[92,6,384]{2,0,1:T(8,128)(2,1)S(1)}, bf16[92,6,384]{2,0,1:T(8,128)(2,1)}, u32[]{:S(2)}) copy-start(bf16[92,6,384]{2,0,1:T(8,128)(2,1)} %param.15) | copy-start | bytes 1271812
  0.6 9.6 %copy-start.9 = (bf16[2,384,128]{2,1,0:T(8,128)(2,1)S(1)}, bf16[2,384,128]{2,1,0:T(8,128)(2,1)}, u32[]{:S(2)}) copy-start(bf16[2,384,128]{2,1,0:T(8,128)(2,1)} %filter_ref.1) | copy-start | bytes 589828
  4.5 20.5 %copy-start.12 = (bf16[2,768,128]{2,1,0:T(8,128)(2,1)S(1)}, bf16[2,768,128]{2,1,0:T(8,128)(2,1)}, u32[]{:S(2)}) copy-start(bf16[2,768,128]{2,1,0:T(8,128)(2,1)} %get-tuple-element.49) | copy-start | bytes 1179652
  4.5 25.8 %copy-start.11 = (bf16[2,768,128]{2,1,0:T(8,128)(2,1)S(1)}, bf16[2,768,128]{2,1,0:T(8,128)(2,1)}, u32[]{:S(2)}) copy-start(bf16[2,768,128]{2,1,0:T(8,128)(2,1)} %get-tuple-element.50) | copy-start | bytes 1179652
  4.5 27.1 %copy-start.4 = (bf16[2,2,192,128]{3,2,1,0:T(8,128)(2,1)S(1)}, bf16[2,2,192,128]{3,2,1,0:T(8,128)(2,1)}, u32[]{:S(2)}) copy-start(bf16[2,2,192,128]{3,2,1,0:T(8,128)(2,1)} %get-tuple-element.56.refs_0_) | copy-start | bytes 589828
  4.5 27.1 %copy-start.5 = (s32[4]{0:T(128)S(1)}, s32[4]{0:T(128)}, u32[]{:S(2)}) copy-start(s32[4]{0:T(128)} %rows_ref.7) | copy-start | bytes 52
  4.5 27.1 %copy-start.8 = (f32[6]{0:T(128)S(1)}, f32[6]{0:T(128)}, u32[]{:S(2)}) copy-start(f32[6]{0:T(128)} %quad_ref.1) | copy-start | bytes 76
  4.5 11.6 %collective-permute-start = (bf16[2,2,192,128]{3,2,1,0:T(8,128)(2,1)}, bf16[2,2,192,128]{3,2,1,0:T(8,128)(2,1)S(1)}, u32[]{:S(2)}, u32[]{:S(2)}) collective-permute-start(bf16[2,2,192,128]{3,2,1,0:T(8,128)(2,1)} %get-tuple-element.45), channel_id=1, source_target_pairs={{0,4},{4,0},{8,12},{12,8},{1,5},{5,1},{9,13},{13,9},{2,6},{6,2},{1... | collective-permute-start | bytes 589832 | tf_op jit(solution)/shard_map/ppermute | solution.py:372
  7.6 17.4 %collective-permute-start.1 = (bf16[2,2,192,128]{3,2,1,0:T(8,128)(2,1)}, bf16[2,2,192,128]{3,2,1,0:T(8,128)(2,1)S(1)}, u32[]{:S(2)}, u32[]{:S(2)}) collective-permute-start(bf16[2,2,192,128]{3,2,1,0:T(8,128)(2,1)} %get-tuple-element.46), channel_id=1, source_target_pairs={{0,8},{4,12},{8,0},{12,4},{1,9},{5,13},{9,1},{13,5},{2,10},{6,14},... | collective-permute-start | bytes 589832 | tf_op jit(solution)/shard_map/ppermute | solution.py:372
  10.2 14.8 %collective-permute-start.2 = (bf16[2,2,192,128]{3,2,1,0:T(8,128)(2,1)}, bf16[2,2,192,128]{3,2,1,0:T(8,128)(2,1)S(1)}, u32[]{:S(2)}, u32[]{:S(2)}) collective-permute-start(bf16[2,2,192,128]{3,2,1,0:T(8,128)(2,1)} %get-tuple-element.47), channel_id=1, source_target_pairs={{0,12},{4,8},{8,4},{12,0},{1,13},{5,9},{9,5},{13,1},{2,14},{6,10},... | collective-permute-start | bytes 589832 | tf_op jit(solution)/shard_map/ppermute | solution.py:372
  25.0 26.5 %collective-permute-start.3 = (bf16[2,768,128]{2,1,0:T(8,128)(2,1)S(1)}, bf16[2,768,128]{2,1,0:T(8,128)(2,1)S(1)}, u32[]{:S(2)}, u32[]{:S(2)}) collective-permute-start(bf16[2,768,128]{2,1,0:T(8,128)(2,1)S(1)} %copy-done.12), channel_id=1, source_target_pairs={{0,4},{4,8},{8,12},{1,5},{5,9},{9,13},{2,6},{6,10},{10,14},{3,7},{... | collective-permute-start | bytes 1179656 | tf_op jit(solution)/shard_map/ppermute | solution.py:431
  30.3 21.2 %collective-permute-start.4 = (bf16[2,768,128]{2,1,0:T(8,128)(2,1)S(1)}, bf16[2,768,128]{2,1,0:T(8,128)(2,1)S(1)}, u32[]{:S(2)}, u32[]{:S(2)}) collective-permute-start(bf16[2,768,128]{2,1,0:T(8,128)(2,1)S(1)} %copy-done.11), channel_id=1, source_target_pairs={{4,0},{8,4},{12,8},{5,1},{9,5},{13,9},{6,2},{10,6},{14,10},{7,3},{... | collective-permute-start | bytes 1179656 | tf_op jit(solution)/shard_map/ppermute | solution.py:432
  31.6 19.8 %copy-start.1 = (bf16[1,2,768,128]{3,2,1,0:T(8,128)(2,1)S(1)}, bf16[1,2,768,128]{3,2,1,0:T(8,128)(2,1)}, u32[]{:S(2)}) copy-start(bf16[1,2,768,128]{3,2,1,0:T(8,128)(2,1)} %param.10) | copy-start | bytes 1179652
  31.6 19.8 %copy-start.2 = (bf16[1,2,768,128]{3,2,1,0:T(8,128)(2,1)S(1)}, bf16[1,2,768,128]{3,2,1,0:T(8,128)(2,1)}, u32[]{:S(2)}) copy-start(bf16[1,2,768,128]{3,2,1,0:T(8,128)(2,1)} %param.11) | copy-start | bytes 1179652
  31.6 19.8 %copy-start.3 = (bf16[2,768,128]{2,1,0:T(8,128)(2,1)S(1)}, bf16[2,768,128]{2,1,0:T(8,128)(2,1)}, u32[]{:S(2)}) copy-start(bf16[2,768,128]{2,1,0:T(8,128)(2,1)} %get-tuple-element.41.act_ref) | copy-start | bytes 1179652
  31.6 19.8 %copy-start.6 = (s32[6,9]{1,0:T(8,128)S(1)}, s32[6,9]{1,0:T(8,128)}, u32[]{:S(2)}) copy-start(s32[6,9]{1,0:T(8,128)} %shift_ref.1) | copy-start | bytes 652
  31.7 19.8 %copy-start.7 = (bf16[9,128]{1,0:T(8,128)(2,1)S(1)}, bf16[9,128]{1,0:T(8,128)(2,1)}, u32[]{:S(2)}) copy-start(bf16[9,128]{1,0:T(8,128)(2,1)} %taps_ref.1) | copy-start | bytes 6916
  34.5 29.2 %copy-start = (bf16[768,768]{1,0:T(8,128)(2,1)S(1)}, bf16[768,768]{1,0:T(8,128)(2,1)}, u32[]{:S(2)}) copy-start(bf16[768,768]{1,0:T(8,128)(2,1)} %constant.8.clone.table_ref) | copy-start | bytes 3538948
  34.5 12.4 %collective-permute-start.5 = (bf16[384,128]{1,0:T(8,128)(2,1)S(1)}, bf16[384,128]{1,0:T(8,128)(2,1)S(1)}, u32[]{:S(2)}, u32[]{:S(2)}) collective-permute-start(bf16[384,128]{1,0:T(8,128)(2,1)S(1)} %get-tuple-element.64), channel_id=1, source_target_pairs={{0,8},{4,12},{8,0},{12,4},{1,9},{5,13},{9,1},{13,5},{2,10},{6,14},... | collective-permute-start | bytes 294920 | tf_op jit(solution)/shard_map/ppermute | solution.py:372
  38.2 13.2 %collective-permute-start.7 = (bf16[2,2,192,128]{3,2,1,0:T(8,128)(2,1)S(1)}, bf16[2,2,192,128]{3,2,1,0:T(8,128)(2,1)S(1)}, u32[]{:S(2)}, u32[]{:S(2)}) collective-permute-start(bf16[2,2,192,128]{3,2,1,0:T(8,128)(2,1)S(1)} %get-tuple-element.67), channel_id=1, source_target_pairs={{0,4},{4,0},{8,12},{12,8},{1,5},{5,1},{9,13},{13,9},{2,6},{6,2},{1... | collective-permute-start | bytes 589832 | tf_op jit(solution)/shard_map/ppermute | solution.py:372
  47.0 4.2 %collective-permute-start.6 = (bf16[192,128]{1,0:T(8,128)(2,1)S(1)}, bf16[192,128]{1,0:T(8,128)(2,1)S(1)}, u32[]{:S(2)}, u32[]{:S(2)}) collective-permute-start(bf16[192,128]{1,0:T(8,128)(2,1)S(1)} %get-tuple-element.66), channel_id=1, source_target_pairs={{0,4},{4,0},{8,12},{12,8},{1,5},{5,1},{9,13},{13,9},{2,6},{6,2},{1... | collective-permute-start | bytes 147464 | tf_op jit(solution)/shard_map/ppermute | solution.py:372
  47.4 16.3 %collective-permute-start.8 = (bf16[2,2,192,128]{3,2,1,0:T(8,128)(2,1)S(1)}, bf16[2,2,192,128]{3,2,1,0:T(8,128)(2,1)S(1)}, u32[]{:S(2)}, u32[]{:S(2)}) collective-permute-start(bf16[2,2,192,128]{3,2,1,0:T(8,128)(2,1)S(1)} %get-tuple-element.69), channel_id=1, source_target_pairs={{0,8},{4,12},{8,0},{12,4},{1,9},{5,13},{9,1},{13,5},{2,10},{6,14},... | collective-permute-start | bytes 589832 | tf_op jit(solution)/shard_map/ppermute | solution.py:372
  51.1 12.6 %collective-permute-start.9 = (bf16[2,2,192,128]{3,2,1,0:T(8,128)(2,1)S(1)}, bf16[2,2,192,128]{3,2,1,0:T(8,128)(2,1)S(1)}, u32[]{:S(2)}, u32[]{:S(2)}) collective-permute-start(bf16[2,2,192,128]{3,2,1,0:T(8,128)(2,1)S(1)} %get-tuple-element.70), channel_id=1, source_target_pairs={{0,12},{4,8},{8,4},{12,0},{1,13},{5,9},{9,5},{13,1},{2,14},{6,10},... | collective-permute-start | bytes 589832 | tf_op jit(solution)/shard_map/ppermute | solution.py:372
  54.9 4.2 %collective-permute-start.10 = (bf16[224,128]{1,0:T(8,128)(2,1)S(1)}, bf16[224,128]{1,0:T(8,128)(2,1)S(1)}, u32[]{:S(2)}, u32[]{:S(2)}) collective-permute-start(bf16[224,128]{1,0:T(8,128)(2,1)S(1)} %shard_map.135.refs_0_), channel_id=1, source_target_pairs={{0,2},{2,0},{1,3},{3,1},{4,6},{6,4},{5,7},{7,5},{8,10},{10,8},{9,1... | collective-permute-start | bytes 172040 | tf_op jit(solution)/shard_map/ppermute | solution.py:367
  59.2 6.9 %collective-permute-start.13 = (bf16[224,128]{1,0:T(8,128)(2,1)S(1)}, bf16[224,128]{1,0:T(8,128)(2,1)S(1)}, u32[]{:S(2)}, u32[]{:S(2)}) collective-permute-start(bf16[224,128]{1,0:T(8,128)(2,1)S(1)} %shard_map.136.refs_0_), channel_id=1, source_target_pairs={{0,12},{4,8},{8,4},{12,0},{1,13},{5,9},{9,5},{13,1},{2,14},{6,10},... | collective-permute-start | bytes 172040 | tf_op jit(solution)/shard_map/ppermute | solution.py:372
  62.6 6.0 %collective-permute-start.12 = (bf16[224,128]{1,0:T(8,128)(2,1)S(1)}, bf16[224,128]{1,0:T(8,128)(2,1)S(1)}, u32[]{:S(2)}, u32[]{:S(2)}) collective-permute-start(bf16[224,128]{1,0:T(8,128)(2,1)S(1)} %shard_map.136.refs_0_), channel_id=1, source_target_pairs={{0,8},{4,12},{8,0},{12,4},{1,9},{5,13},{9,1},{13,5},{2,10},{6,14},... | collective-permute-start | bytes 172040 | tf_op jit(solution)/shard_map/ppermute | solution.py:372
  62.6 6.0 %collective-permute-start.11 = (bf16[224,128]{1,0:T(8,128)(2,1)S(1)}, bf16[224,128]{1,0:T(8,128)(2,1)S(1)}, u32[]{:S(2)}, u32[]{:S(2)}) collective-permute-start(bf16[224,128]{1,0:T(8,128)(2,1)S(1)} %shard_map.136.refs_0_), channel_id=1, source_target_pairs={{0,4},{4,0},{8,12},{12,8},{1,5},{5,1},{9,13},{13,9},{2,6},{6,2},{1... | collective-permute-start | bytes 172040 | tf_op jit(solution)/shard_map/ppermute | solution.py:372

commit v2 on v1

--- a/solution.py
+++ b/solution.py
@@ -34,15 +34,16 @@
     return -(-count // step) * step
 
 
-def fourier_table(lon_count, blocks, local_modes, padded_modes):
+def fourier_table(lon_count, blocks, local_modes, depth):
     lon_ids = np.arange(lon_count)
     mode_ids = np.arange(blocks * local_modes)
     phase = (mode_ids[:, None] * lon_ids[None, :] % lon_count) * (2.0 * math.pi / lon_count)
     factor = 1.0 / math.sqrt(lon_count)
     both = np.stack([np.cos(phase), -np.sin(phase)]) * factor
     both = both.reshape(2, blocks, local_modes, lon_count).transpose(1, 0, 2, 3)
-    both = np.pad(both, ((0, 0), (0, 0), (0, padded_modes - local_modes), (0, 0)))
-    return both.reshape(blocks, 2 * padded_modes, lon_count).astype(ml_dtypes.bfloat16)
+    both = both.reshape(blocks, 2 * local_modes, lon_count)
+    both = np.pad(both, ((0, 0), (0, depth - 2 * local_modes), (0, 0)))
+    return both.astype(ml_dtypes.bfloat16)
 
 
 def lat_pairs(lat_count):
@@ -68,13 +69,23 @@
     )(*args)
 
 
-def forward_kernel(
-    blocks, rows_ref, x_hbm, dy_hbm, table_hbm, act_ref, *refs
-):
-    outs, (down_ref, up_ref, x_ref, dy_ref, table_ref, sems) = refs[:blocks], refs[blocks:]
-    slots, lon_count, chans = x_ref.shape
+def activate(x_ref, act_ref):
+    slots, lon_count, _ = x_ref.shape
+    step = 64 if lon_count % 64 == 0 else lon_count
+
+    def run(i, carry):
+        part = pl.ds(pl.multiple_of(i * step, step), step)
+        for slot in range(slots):
+            act_ref[slot, part, :] = gelu_value(x_ref[slot, part, :].astype(F32)).astype(BF16)
+        return carry
+
+    lax.fori_loop(0, lon_count // step, run, 0)
+
+
+def forward_kernel(blocks, x_hbm, dy_hbm, table_hbm, *refs):
+    outs, (x_ref, dy_ref, table_ref, act_ref, sems) = refs[:blocks], refs[blocks:]
+    slots, _, chans = x_ref.shape
     me = lax.axis_index("space")
-    step = 64 if lon_count % 64 == 0 else lon_count
     loads = [
         pltpu.make_async_copy(source, target, sems.at[i])
         for i, (source, target) in enumerate(
@@ -84,38 +95,34 @@
     for load in loads:
         load.start()
     loads[0].wait()
-
-    def activate(i, carry):
-        part = pl.ds(pl.multiple_of(i * step, step), step)
-        for slot in range(slots):
-            act_ref[slot, part, :] = gelu_value(x_ref[slot, part, :].astype(F32)).astype(BF16)
-        return carry
-
-    lax.fori_loop(0, lon_count // step, activate, 0)
+    activate(x_ref, act_ref)
     loads[1].wait()
-    last = rows_ref[me] - 1
-    down_ref[0] = act_ref[0]
-    down_ref[1] = dy_ref[0]
-    up_ref[0] = act_ref[last]
-    up_ref[1] = dy_ref[last]
     source = jnp.concatenate(
         [dy_ref[slot] for slot in range(slots)] + [act_ref[slot] for slot in range(slots)], axis=-1
     )
     loads[2].wait()
     for shift in range(blocks):
         block = jnp.bitwise_xor(me, shift)
-        sums = jnp.dot(table_ref[block], source, preferred_element_type=F32).astype(BF16)
-        for field in range(2):
-            for slot in range(slots):
-                at = (field * slots + slot) * chans
-                outs[shift][field, slot] = sums[:, at : at + chans]
-
-
-def prepare_kernel(local_modes, leg_ref, filter_ref, mixer_ref, back_ref, pairs_ref):
+        sums = jnp.dot(table_ref[block], source, preferred_element_type=F32)
+        columns = [sums[:, at * chans : (at + 1) * chans] for at in range(2 * slots)]
+        outs[shift][...] = jnp.concatenate(columns, axis=0).astype(BF16)
+
+
+def prepare_kernel(
+    local_modes, rows_ref, leg_ref, filter_ref, x_ref, dy_ref,
+    mixer_ref, back_ref, act_ref, first_rim, second_rim, pairs_ref,
+):
+    me = lax.axis_index("space")
+    activate(x_ref, act_ref)
+    last = rows_ref[me] - 1
+    odd = jnp.bitwise_and(me, 1)
+    for rim_ref, row in ((first_rim, last * (1 - odd)), (second_rim, last * odd)):
+        rim_ref[0] = act_ref[row]
+        rim_ref[1] = dy_ref[row]
     lat_count, padded_modes, _ = leg_ref.shape
     pairs = lat_pairs(lat_count)
     used = len(pairs) * padded_modes
-    mode = lax.axis_index("space") * local_modes + lax.broadcasted_iota(
+    mode = me * local_modes + lax.broadcasted_iota(
         jnp.int32, (padded_modes, 1), 0
     )
     twice = jnp.where(mode == 0, 1.0, 2.0)
@@ -137,16 +144,29 @@
     lax.fori_loop(0, pairs_ref.shape[0] // 128, turn, 0)
 
 
-def mix_kernel(blocks, lat_count, rows_ref, quad_ref, mixer_ref, back_ref, *refs):
+def mix_kernel(blocks, slots, lat_count, local_modes, rows_ref, quad_ref, mixer_ref, back_ref, *refs):
     ins, outs = refs[:blocks], refs[blocks : 2 * blocks]
-    keep_ref, send_ref, coeff, grad, synth, grad_coeff, products, gradient = refs[2 * blocks :]
-    slots = ins[0].shape[1]
+    keep_ref, send_ref, coeff, grad, synth, grad_coeff, products, gradient, wide = refs[2 * blocks :]
     padded_modes, chans = coeff.shape[2:]
     me = lax.axis_index("space")
     pairs = lat_pairs(lat_count)
+    depth = wide.shape[1] // (2 * slots)
+    padding = padded_modes - local_modes
+    if padding > 0:
+        zeros = jnp.zeros((padding, chans), F32)
+        for lat in range(lat_count):
+            for part in range(2):
+                coeff[lat, part, local_modes:, :] = zeros
+                grad[lat, part, local_modes:, :] = zeros
+
+    def rows_at(field, slot, part):
+        at = (field * slots + slot) * depth + part * local_modes
+        return slice(at, at + local_modes)
+
     for shift in range(blocks):
         block = jnp.bitwise_xor(me, shift)
         start = first_row_of(rows_ref, block, blocks)
+        wide[shift] = ins[shift][...].astype(F32)
         for slot in range(slots):
             lat = jnp.minimum(start + slot, lat_count - 1)
 
@@ -154,9 +174,10 @@
             def _():
                 weight = quad_ref[lat]
                 for part in range(2):
-                    rows = slice(part * padded_modes, (part + 1) * padded_modes)
-                    grad[lat, part] = ins[shift][0, slot, rows, :].astype(F32)
-                    coeff[lat, part] = ins[shift][1, slot, rows, :].astype(F32) * weight
+                    grad[lat, part, :local_modes, :] = wide[shift, rows_at(0, slot, part), :]
+                    coeff[lat, part, :local_modes, :] = (
+                        wide[shift, rows_at(1, slot, part), :] * weight
+                    )
 
     def mix(i, carry):
         rows = pl.ds(pl.multiple_of(i * 8, 8), 8)
@@ -195,7 +216,7 @@
         back_ref[...], products[...].astype(BF16), preferred_element_type=F32
     )
     half = gradient.shape[0] // 2
-    upper = jnp.where(jnp.bitwise_and(me, blocks // 2) != 0, 1, 0)
+    upper = jnp.bitwise_and(me, 1)
     for target, which in ((keep_ref, upper), (send_ref, 1 - upper)):
         part = gradient[pl.ds(pl.multiple_of(which * half, half), half), :]
         both = jnp.concatenate([part[:, :chans], part[:, chans:]], axis=0)
@@ -205,14 +226,14 @@
         start = first_row_of(rows_ref, block, blocks)
         for slot in range(slots):
             lat = jnp.minimum(start + slot, lat_count - 1)
-            for half in range(2):
-                rows = slice(half * padded_modes, (half + 1) * padded_modes)
-                outs[shift][0, slot, rows, :] = synth[lat, half].astype(BF16)
-                outs[shift][1, slot, rows, :] = grad_coeff[lat, half].astype(BF16)
+            for part in range(2):
+                wide[shift, rows_at(0, slot, part), :] = synth[lat, part, :local_modes, :]
+                wide[shift, rows_at(1, slot, part), :] = grad_coeff[lat, part, :local_modes, :]
+        outs[shift][...] = wide[shift].astype(BF16)
 
 
 def disco_kernel(
-    blocks, lat_count, rows_ref, shift_ref, x_ref, dy_ref, act_ref, low_ref, high_ref, taps_ref,
+    blocks, lat_count, rows_ref, shift_ref, x_ref, dy_ref, act_ref, first_rim, second_rim, taps_ref,
     base_ref, slope_ref, base_grad_ref, tap_ref, acts, grads,
 ):
     slots, lon_count, chans = x_ref.shape
@@ -226,10 +247,10 @@
         target[row, :REACH, :] = value[lon_count - REACH :, :]
         target[row, REACH + lon_count :, :] = value[:REACH, :]
 
-    wrapped(acts, 0, low_ref[0].astype(F32))
-    wrapped(grads, 0, low_ref[1].astype(F32))
-    wrapped(acts, slots + 1, high_ref[0].astype(F32))
-    wrapped(grads, slots + 1, high_ref[1].astype(F32))
+    odd = jnp.bitwise_and(me, 1)
+    for rim_ref, row in ((first_rim, (slots + 1) * (1 - odd)), (second_rim, (slots + 1) * odd)):
+        wrapped(acts, row, rim_ref[0].astype(F32))
+        wrapped(grads, row, rim_ref[1].astype(F32))
     for slot in range(slots):
         alive = jnp.where(slot < live, 1.0, 0.0)
         wrapped(acts, slot + 1, act_ref[slot].astype(F32))
@@ -318,6 +339,14 @@
     split_taps(total[count:, :] / lat_count, out_ref, count)
 
 
+def mirrored(block, blocks):
+    place = jnp.int32(0)
+    bits = blocks.bit_length() - 1
+    for bit in range(bits):
+        place = place + (jnp.bitwise_and(block, 1 << bit) >> bit) * (1 << (bits - 1 - bit))
+    return place
+
+
 def spread_kernel(*refs):
     parts, (filter_ref, tap_ref, held) = refs[:-3], refs[-3:]
     me = lax.axis_index("space")
@@ -326,7 +355,7 @@
     for shift in range(blocks):
         block = jnp.bitwise_xor(me, shift)
         part = parts[shift][...].astype(F32)
-        at = pl.ds(pl.multiple_of(block * share, share), share)
+        at = pl.ds(pl.multiple_of(mirrored(block, blocks) * share, share), share)
         filter_ref[0, at, :] = part[:share, :]
         filter_ref[1, at, :] = part[share : 2 * share, :]
         held[block] = joined_taps(part)
@@ -343,15 +372,14 @@
     slots, lon_count, chans = base_ref.shape
     me = lax.axis_index("space")
     live = rows_ref[me]
-    depth = ins[0].shape[2]
+    depth = source.shape[0] // blocks
     for shift in range(blocks):
         block = jnp.bitwise_xor(me, shift)
-        rows = pl.ds(pl.multiple_of(block * depth, depth), depth)
-        for field in range(2):
-            for slot in range(slots):
-                at = (field * slots + slot) * chans
-                source[rows, at : at + chans] = ins[shift][field, slot]
-    sums = jnp.dot(table_ref[...], source[...], preferred_element_type=F32)
+        rows = pl.ds(pl.multiple_of(block * depth, 8), depth)
+        part = ins[shift][...].astype(F32)
+        for at in range(2 * slots):
+            source[rows, at * chans : (at + 1) * chans] = part[at * depth : (at + 1) * depth, :]
+    sums = jnp.dot(table_ref[...], source[...].astype(BF16), preferred_element_type=F32)
     for slot in range(slots):
         at = slot * chans
         out = base_ref[slot] + sums[:, at : at + chans]
@@ -384,29 +412,30 @@
     _, slots, lon_count, chans = fields.shape
     local_modes, lat_count, degrees = legendre.shape
     padded_modes = round_up(local_modes, 16)
-    depth = 2 * padded_modes
+    depth = round_up(2 * local_modes, 8)
     pairs = len(lat_pairs(lat_count))
     pair_rows = round_up(pairs * padded_modes, 128)
     share = 2 * degrees // blocks
     big = 32 if pair_rows <= 4096 else 60
     shape = jax.ShapeDtypeStruct
-    table = fourier_table(lon_count, blocks, local_modes, padded_modes)
+    table = fourier_table(lon_count, blocks, local_modes, depth)
     table_in = jnp.asarray(table)
     table_out = jnp.asarray(np.ascontiguousarray(table.reshape(blocks * depth, lon_count).T))
     x, dy = fields[0], cotangent[0]
     field = shape((slots, lon_count, chans), F32)
-    coded = shape((2, slots, depth, chans), BF16)
+    coded = shape((2 * slots * depth, chans), BF16)
     rim = shape((2, lon_count, chans), BF16)
 
-    act, *coded_parts, down, up = call(
+    coded_parts = call(
         functools.partial(forward_kernel, blocks),
-        [shape(x.shape, BF16)] + [coded] * blocks + [rim] * 2,
-        [SMEM, HBM, HBM, HBM],
-        (band_rows, x, dy, table_in),
+        [coded] * blocks,
+        [HBM] * 3,
+        (x, dy, table_in),
         scratch=[
             pltpu.VMEM(x.shape, BF16),
             pltpu.VMEM(dy.shape, BF16),
             pltpu.VMEM(table.shape, BF16),
+            pltpu.VMEM(x.shape, BF16),
             pltpu.SemaphoreType.DMA((3,)),
         ],
         limit=60,
@@ -417,46 +446,46 @@
     leg_rows = jnp.pad(
         jnp.transpose(legendre, (1, 0, 2)), ((0, 0), (0, padded_modes - local_modes), (0, 0))
     )
-    mixer, back = call(
+    mixer, back, act, first_rim, second_rim = call(
         functools.partial(prepare_kernel, local_modes),
-        [shape((pair_rows, 2 * chans), F32), shape((degrees, pair_rows), BF16)],
-        [VMEM, VMEM],
-        (leg_rows, spectral_filter),
+        [shape((pair_rows, 2 * chans), F32), shape((degrees, pair_rows), BF16)]
+        + [shape(x.shape, BF16), rim, rim],
+        [SMEM] + [VMEM] * 4,
+        (band_rows, leg_rows, spectral_filter, x, dy),
         scratch=[pltpu.VMEM((pair_rows, degrees), BF16)],
         limit=big,
         flops=2 * pair_rows * degrees * 2 * chans,
         moved=8 * pair_rows * chans,
     )
-    down, up, got, mixer = lax.optimization_barrier((down, up, got, mixer))
-    low = lax.ppermute(up, "space", [(i, i + 1) for i in range(blocks - 1)])
-    high = lax.ppermute(down, "space", [(i + 1, i) for i in range(blocks - 1)])
+    first_rim, second_rim, got[-1] = lax.optimization_barrier((first_rim, second_rim, got[-1]))
+    first_rim = crossed(first_rim, 1)
+    inner = [(i, i ^ 1) for i in range(blocks)]
+    inner = [(i + 1, j + 1) for i, j in inner if max(i, j) + 1 < blocks]
+    second_rim = lax.ppermute(second_rim, "space", inner)
     spectral = pltpu.VMEM((lat_count, 2, padded_modes, chans), F32)
     mixed = call(
-        functools.partial(mix_kernel, blocks, lat_count),
+        functools.partial(mix_kernel, blocks, slots, lat_count, local_modes),
         [coded] * blocks + [shape((degrees, chans), F32), shape((degrees, chans), BF16)],
         [SMEM, SMEM] + [VMEM] * (2 + blocks),
         (band_rows, quad_weight, mixer, back, *got),
         scratch=[spectral] * 4
-        + [pltpu.VMEM((pair_rows, 2 * chans), F32), pltpu.VMEM((degrees, 2 * chans), F32)],
+        + [pltpu.VMEM((pair_rows, 2 * chans), F32), pltpu.VMEM((degrees, 2 * chans), F32)]
+        + [pltpu.VMEM((blocks, *coded.shape), F32)],
         limit=big,
-        flops=2 * degrees * pair_rows * 2 * chans,
+        flops=20 * degrees * pair_rows * 2 * chans,
     )
     back_parts, keep, send = mixed[:blocks], mixed[blocks], mixed[blocks + 1]
-    distance = blocks // 2
+    distance = 1
     got_sums = crossed(send, distance)
-    near = crossed(back_parts[1], 1)
-    far_parts, got_sums = lax.optimization_barrier((list(back_parts[2:]), got_sums))
-    returned = [back_parts[0], near]
-    returned += reversed(crossed_all([None, None, *far_parts], far[:-1]).values())
     base, slope, base_grad, tap_part = call(
         functools.partial(disco_kernel, blocks, lat_count),
         [field, field, field, shape((TAP_ROWS, chans), F32)],
         [SMEM, SMEM] + [VMEM] * 6,
-        (band_rows, tap_shift, x, dy, act, low, high, tap_weight),
+        (band_rows, tap_shift, x, dy, act, first_rim, second_rim, tap_weight),
         scratch=[pltpu.VMEM((slots + 2, lon_count + 2 * REACH, chans), F32)] * 2,
     )
-    while distance > 1:
-        distance //= 2
+    while 2 * distance < blocks:
+        distance *= 2
         rows = keep.shape[0] // 2
         keep, send = call(
             functools.partial(halve_kernel, distance),
@@ -466,7 +495,8 @@
             scratch=[pltpu.VMEM(keep.shape, F32)],
         )
         got_sums = crossed(send, distance)
-    got_sums, returned[1] = lax.optimization_barrier((got_sums, returned[1]))
+    back_parts, keep = lax.optimization_barrier((back_parts, keep))
+    returned = [back_parts[0], *reversed(crossed_all(back_parts, far).values())]
     own = call(
         own_kernel,
         shape((share + 2 * TAP_ROWS, chans), BF16),
@@ -479,6 +509,7 @@
         shape((share + 2 * TAP_ROWS, chans), BF16),
         [VMEM] * members,
         by_member,
+        flops=1200000000,
         scratch=[pltpu.VMEM((members, share + TAP_ROWS, chans), F32)],
     )
     spread = [final] + [crossed(final, s) for s in range(1, blocks)]
@@ -487,7 +518,7 @@
         [shape(x.shape, BF16)] * 2,
         [SMEM] + [VMEM] * (4 + blocks),
         (band_rows, table_out, base, slope, base_grad, *returned),
-        scratch=[pltpu.VMEM((blocks * depth, 2 * slots * chans), BF16)],
+        scratch=[pltpu.VMEM((blocks * depth, 2 * slots * chans), F32)],
         flops=2 * blocks * depth * lon_count * 2 * slots * chans,
     )
     filter_grad, tap_grad = call(

time: 69.6 us -> 60 us (0.86)
  waiting for transfers between devices: 30 us -> 20.1 us
    ppermute x11 -> x12, waiting for transfers between devices: 27.3 us -> 17.4 us  [crossed(): lax.ppermute(values, 'space', [(i, i ^ distance) for i in range(count)])]
    ppermute x11 -> x12, starting transfers between devices: 14.6 us -> 20.6 us  [crossed(): lax.ppermute(values, 'space', [(i, i ^ distance) for i in range(count)])]
    ppermute x2 -> x1, starting transfers between devices: 6.57 us -> 0.67 us  [body(): second_rim = lax.ppermute(second_rim, 'space', inner)]
  transfers between devices with their start and end apart: 14 -> 14, of which waited for: 7 -> 6; matrix products, arithmetic and copies ran while one was open for 0% -> 0% of each run, Pallas kernels for 16% -> 20%
where the time goes in v2:
time: 60 us; the launch traced here: 59.8 us
  starting transfers between devices  22.8 us (38%)
  waiting for transfers between devices  20.1 us (34%)
  Pallas kernels  16 us (27%)
  between operations  0.83 us (1%)
    ppermute x12, starting transfers between devices, crossed(): lax.ppermute(values, 'space', [(i, i ^ distance) for i in range(count)])  20.6 us
    ppermute x12, waiting for transfers between devices, crossed(): lax.ppermute(values, 'space', [(i, i ^ distance) for i in range(count)])  17.4 us
    pallas_call x9, Pallas kernels, call(): pl.pallas_call(kernel, out_shape=out_shape, in_specs=in_specs, out_specs=...  16 us
    ppermute x1, waiting for transfers between devices, shifted(): lax.ppermute(values, axis, [(i, (i + shift) % count) for i in range(count)])  2.68 us
    ppermute x1, starting transfers between devices, shifted(): lax.ppermute(values, axis, [(i, (i + shift) % count) for i in range(count)])  1.56 us
  transfers between devices with their start and end apart: 14, of which 6 were waited for; matrix products, arithmetic and copies ran while one was open for 0% of the time, Pallas kernels for 20%

profile of v2, /device:TPU:0, one launch (start us, length us, event | category | flops | bytes accessed | tf_op | source)
XLA Modules:
  0.0 59.8 jit_solution(4466680255075591436)
XLA Ops:
  0.6 0.0 copy-start.2
  0.6 0.0 copy-start.1
  0.7 0.0 copy-start.9
  0.7 0.0 copy-start.5
  0.7 0.0 copy-start.6
  0.7 3.1 %shard_map.130 = (bf16[736,128]{1,0:T(8,128)(2,1)}, bf16[736,128]{1,0:T(8,128)(2,1)}, bf16[736,128]{1,0:T(8,128)(2,1)}, bf16[736,128]{1,0:T(8,128)(2,1)}) custom-call(bf16[2,768,128]{2,1,0:T(8,128)(2,1)} %bitcast.5, bf16[2,768,128]{2,1,0:T(8,128)(2,1)} %bitcast.8, bf16[4,184,768]{2,1,0:T(8,128)(2,1)} %constant.7.clone.table_hbm), custom_call_target="tpu_custom_call" | custom-call | flops 578813952 | bytes 1024 | tf_op jit(solution)/shard_map/pallas_call | solution.py:61
  3.8 0.0 copy-start.7
  3.8 0.0 copy-start.8
  3.8 5.1 %collective-permute-start = (bf16[736,128]{1,0:T(8,128)(2,1)}, bf16[736,128]{1,0:T(8,128)(2,1)S(1)}, u32[]{:S(2)}, u32[]{:S(2)}) collective-permute-start(bf16[736,128]{1,0:T(8,128)(2,1)} %get-tuple-element.40), channel_id=1, source_target_pairs={{0,12},{4,8},{8,4},{12,0},{1,13},{5,9},{9,5},{13,1},{2,14},{6,10},... | collective-permute-start | bytes 565256 | tf_op jit(solution)/shard_map/ppermute | solution.py:400
  8.9 0.0 collective-permute-start.3
  8.9 0.6 %collective-permute-start.4 = (bf16[736,128]{1,0:T(8,128)(2,1)}, bf16[736,128]{1,0:T(8,128)(2,1)S(1)}, u32[]{:S(2)}, u32[]{:S(2)}) collective-permute-start(bf16[736,128]{1,0:T(8,128)(2,1)} %get-tuple-element.50), channel_id=1, source_target_pairs={{0,8},{4,12},{8,0},{12,4},{1,9},{5,13},{9,1},{13,5},{2,10},{6,14},... | collective-permute-start | bytes 565256 | tf_op jit(solution)/shard_map/ppermute | solution.py:400
  9.6 0.0 copy-done.9
  9.6 0.0 copy-done.2
  9.6 0.0 copy-done.1
  9.6 0.0 copy-done.5
  9.6 0.0 copy-done.6
  9.6 3.3 %shard_map.129 = (f32[2048,256]{1,0:T(8,128)S(1)}, bf16[384,2048]{1,0:T(8,128)(2,1)S(1)}, bf16[2,768,128]{2,1,0:T(8,128)(2,1)S(1)}, bf16[2,768,128]{2,1,0:T(8,128)(2,1)S(1)}, bf16[2,768,128]{2,1,0:T(8,128)(2,1)S(1)}) custom-call(s32[4]{0:T(128)S(1)} %copy-done.5, bf16[6,96,384]{2,1,0:T(8,128)(2,1)S(1)} %pad.4.leg_ref, bf16[2,384,128]{2,1,0:T(8,128)(2,1)S(1)} %copy-done.6, ...), custom_call_target="tpu_custom_call" | custom-call | flops 402653184 | bytes 2097152 | tf_op jit(solution)/shard_map/pallas_call | solution.py:61
  12.9 1.8 %collective-permute-done.refs_3_ = bf16[736,128]{1,0:T(8,128)(2,1)S(1)} collective-permute-done((bf16[736,128]{1,0:T(8,128)(2,1)}, bf16[736,128]{1,0:T(8,128)(2,1)S(1)}, u32[]{:S(2)}, u32[]{:S(2)}) %collective-permute-start) | collective-permute-done | bytes 188448 | tf_op jit(solution)/shard_map/ppermute | solution.py:400
  14.7 4.7 %collective-permute-start.1 = (bf16[2,768,128]{2,1,0:T(8,128)(2,1)S(1)}, bf16[2,768,128]{2,1,0:T(8,128)(2,1)S(1)}, u32[]{:S(2)}, u32[]{:S(2)}) collective-permute-start(bf16[2,768,128]{2,1,0:T(8,128)(2,1)S(1)} %get-tuple-element.41), channel_id=1, source_target_pairs={{0,4},{4,0},{8,12},{12,8},{1,5},{5,1},{9,13},{13,9},{2,6},{6,2},{1... | collective-permute-start | bytes 1179656 | tf_op jit(solution)/shard_map/ppermute | solution.py:400
  19.4 0.7 %collective-permute-start.2 = (bf16[2,768,128]{2,1,0:T(8,128)(2,1)S(1)}, bf16[2,768,128]{2,1,0:T(8,128)(2,1)S(1)}, u32[]{:S(2)}, u32[]{:S(2)}) collective-permute-start(bf16[2,768,128]{2,1,0:T(8,128)(2,1)S(1)} %get-tuple-element.42), channel_id=1, source_target_pairs={{4,8},{8,4},{5,9},{9,5},{6,10},{10,6},{7,11},{11,7},{20,24},{24,20... | collective-permute-start | bytes 1179656 | tf_op jit(solution)/shard_map/ppermute | solution.py:464
  20.1 0.0 collective-permute-done.3.refs_1_
  20.1 6.0 %collective-permute-done.4.refs_2_ = bf16[736,128]{1,0:T(8,128)(2,1)S(1)} collective-permute-done((bf16[736,128]{1,0:T(8,128)(2,1)}, bf16[736,128]{1,0:T(8,128)(2,1)S(1)}, u32[]{:S(2)}, u32[]{:S(2)}) %collective-permute-start.4) | collective-permute-done | bytes 188448 | tf_op jit(solution)/shard_map/ppermute | solution.py:400
  26.1 0.0 copy-done.7
  26.1 0.0 copy-done.8
  26.1 0.0 copy-start.3
  26.1 0.0 copy-start.4
  26.1 3.0 %shard_map.132 = (bf16[736,128]{1,0:T(8,128)(2,1)S(1)}, bf16[736,128]{1,0:T(8,128)(2,1)S(1)}, bf16[736,128]{1,0:T(8,128)(2,1)S(1)}, bf16[736,128]{1,0:T(8,128)(2...) custom-call(s32[4]{0:T(128)S(1)} %copy-done.5, f32[6]{0:T(128)S(1)} %copy-done.7, ...), custom_call_target="tpu_custom_call" | custom-call | flops 4026531840 | bytes 1024 | tf_op jit(solution)/shard_map/pallas_call | solution.py:61
  29.1 0.1 collective-permute-start.5
  29.2 4.6 %collective-permute-done.5.got_ref = bf16[384,128]{1,0:T(8,128)(2,1)S(1)} collective-permute-done((bf16[384,128]{1,0:T(8,128)(2,1)S(1)}, bf16[384,128]{1,0:T(8,128)(2,1)S(1)}, u32[]{:S(2)}, u32[]{:S(2)}) %collective-permute-start.5) | collective-permute-done | bytes 98336 | tf_op jit(solution)/shard_map/ppermute | solution.py:400
  33.8 1.2 %collective-permute-start.9 = (bf16[192,128]{1,0:T(8,128)(2,1)S(1)}, bf16[192,128]{1,0:T(8,128)(2,1)S(1)}, u32[]{:S(2)}, u32[]{:S(2)}) collective-permute-start(bf16[192,128]{1,0:T(8,128)(2,1)S(1)} %get-tuple-element.66), channel_id=1, source_target_pairs={{0,8},{4,12},{8,0},{12,4},{1,9},{5,13},{9,1},{13,5},{2,10},{6,14},... | collective-permute-start | bytes 147464 | tf_op jit(solution)/shard_map/ppermute | solution.py:400
  35.1 2.0 %collective-permute-start.6 = (bf16[736,128]{1,0:T(8,128)(2,1)S(1)}, bf16[736,128]{1,0:T(8,128)(2,1)S(1)}, u32[]{:S(2)}, u32[]{:S(2)}) collective-permute-start(bf16[736,128]{1,0:T(8,128)(2,1)S(1)} %get-tuple-element.60), channel_id=1, source_target_pairs={{0,4},{4,0},{8,12},{12,8},{1,5},{5,1},{9,13},{13,9},{2,6},{6,2},{1... | collective-permute-start | bytes 565256 | tf_op jit(solution)/shard_map/ppermute | solution.py:400
  37.1 0.2 collective-permute-start.7
  37.3 0.0 collective-permute-done.1.first_rim
  37.3 2.1 %collective-permute-start.8 = (bf16[736,128]{1,0:T(8,128)(2,1)S(1)}, bf16[736,128]{1,0:T(8,128)(2,1)S(1)}, u32[]{:S(2)}, u32[]{:S(2)}) collective-permute-start(bf16[736,128]{1,0:T(8,128)(2,1)S(1)} %get-tuple-element.62), channel_id=1, source_target_pairs={{0,12},{4,8},{8,4},{12,0},{1,13},{5,9},{9,5},{13,1},{2,14},{6,10},... | collective-permute-start | bytes 565256 | tf_op jit(solution)/shard_map/ppermute | solution.py:400
  39.5 0.0 collective-permute-done.2.second_rim
  39.5 0.0 copy-done.3
  39.5 0.0 copy-done.4
  39.5 3.3 %shard_map.131 = (f32[2,768,128]{2,1,0:T(8,128)S(1)}, f32[2,768,128]{2,1,0:T(8,128)S(1)}, f32[2,768,128]{2,1,0:T(8,128)S(1)}, f32[16,128]{1,0:T(8,128)S(1)}) custom-call(s32[4]{0:T(128)S(1)} %copy-done.5, s32[6,9]{1,0:T(8,128)S(1)} %copy-done.3, bf16[2,768,128]{2,1,0:T(8,128)(2,1)S(1)} %bitcast.7, bf16[2,768,128]{2,1,0:T(8,128)(2,1)S(1)} %bitcast.10, ...), custom_call_target="tpu_custom_call" | custom-call | bytes 1024 | tf_op jit(solution)/shard_map/pallas_call | solution.py:61
  42.8 0.0 collective-permute-done.9.got_ref
  42.8 0.0 copy-start
  42.9 1.6 %collective-permute-start.10 = (bf16[224,128]{1,0:T(8,128)(2,1)S(1)}, bf16[224,128]{1,0:T(8,128)(2,1)S(1)}, u32[]{:S(2)}, u32[]{:S(2)}) collective-permute-start(bf16[224,128]{1,0:T(8,128)(2,1)S(1)} %shard_map.135.refs_0_), channel_id=1, source_target_pairs={{0,2},{2,0},{1,3},{3,1},{4,6},{6,4},{5,7},{7,5},{8,10},{10,8},{9,1... | collective-permute-start | bytes 172040 | tf_op jit(solution)/shard_map/ppermute | solution.py:395
  44.4 2.7 %collective-permute-done.10.refs_1_ = bf16[224,128]{1,0:T(8,128)(2,1)S(1)} collective-permute-done((bf16[224,128]{1,0:T(8,128)(2,1)S(1)}, bf16[224,128]{1,0:T(8,128)(2,1)S(1)}, u32[]{:S(2)}, u32[]{:S(2)}) %collective-permute-start.10) | collective-permute-done | bytes 57376 | tf_op jit(solution)/shard_map/ppermute | solution.py:395
  47.2 2.2 %collective-permute-start.13 = (bf16[224,128]{1,0:T(8,128)(2,1)S(1)}, bf16[224,128]{1,0:T(8,128)(2,1)S(1)}, u32[]{:S(2)}, u32[]{:S(2)}) collective-permute-start(bf16[224,128]{1,0:T(8,128)(2,1)S(1)} %shard_map.136.refs_0_), channel_id=1, source_target_pairs={{0,12},{4,8},{8,4},{12,0},{1,13},{5,9},{9,5},{13,1},{2,14},{6,10},... | collective-permute-start | bytes 172040 | tf_op jit(solution)/shard_map/ppermute | solution.py:400
  49.4 0.4 collective-permute-start.12
  49.8 0.0 collective-permute-done.6.refs_1_
  49.8 1.8 %collective-permute-start.11 = (bf16[224,128]{1,0:T(8,128)(2,1)S(1)}, bf16[224,128]{1,0:T(8,128)(2,1)S(1)}, u32[]{:S(2)}, u32[]{:S(2)}) collective-permute-start(bf16[224,128]{1,0:T(8,128)(2,1)S(1)} %shard_map.136.refs_0_), channel_id=1, source_target_pairs={{0,4},{4,0},{8,12},{12,8},{1,5},{5,1},{9,13},{13,9},{2,6},{6,2},{1... | collective-permute-start | bytes 172040 | tf_op jit(solution)/shard_map/ppermute | solution.py:400
  51.6 3.3 %collective-permute-done.7.refs_2_ = bf16[736,128]{1,0:T(8,128)(2,1)S(1)} collective-permute-done((bf16[736,128]{1,0:T(8,128)(2,1)S(1)}, bf16[736,128]{1,0:T(8,128)(2,1)S(1)}, u32[]{:S(2)}, u32[]{:S(2)}) %collective-permute-start.7) | collective-permute-done | bytes 188448 | tf_op jit(solution)/shard_map/ppermute | solution.py:400
  54.9 0.0 collective-permute-done.8.refs_3_
  54.9 0.0 copy-done
  54.9 2.4 %shard_map.134 = (bf16[2,768,128]{2,1,0:T(8,128)(2,1)}, bf16[2,768,128]{2,1,0:T(8,128)(2,1)}) custom-call(s32[4]{0:T(128)S(1)} %copy-done.5, bf16[768,736]{1,0:T(8,128)(2,1)S(1)} %copy-done, f32[2,768,128]{2,1,0:T(8,128)S(1)} %get-tuple-element.43.base_ref, f32[2,768,128]{2,1,0:T(8,128)S(1)} %get-tuple-element.44.slope_ref, ...), custom_call_target="tpu_custom_call" | custom-call | flops 578813952 | bytes 1024 | tf_op jit(solution)/shard_map/pallas_call | solution.py:61
  57.3 0.0 collective-permute-done.13.refs_3_
  57.3 1.8 %collective-permute-done.12.refs_2_ = bf16[224,128]{1,0:T(8,128)(2,1)S(1)} collective-permute-done((bf16[224,128]{1,0:T(8,128)(2,1)S(1)}, bf16[224,128]{1,0:T(8,128)(2,1)S(1)}, u32[]{:S(2)}, u32[]{:S(2)}) %collective-permute-start.12) | collective-permute-done | bytes 57376 | tf_op jit(solution)/shard_map/ppermute | solution.py:400
  59.0 0.0 collective-permute-done.11.refs_1_
  59.0 0.8 %shard_map.137 = (f32[2,384,128]{2,1,0:T(8,128)}, f32[9,128]{1,0:T(8,128)}) custom-call(bf16[224,128]{1,0:T(8,128)(2,1)S(1)} %shard_map.136.refs_0_, bf16[224,128]{1,0:T(8,128)(2,1)S(1)} %collective-permute-done.11.refs_1_, bf16[224,128]{1,0:T(8,128)(2,1)S(1)} %collective-permute-done.12.refs_2_, bf16[224,128]{1,0:T(8,128)(2,1)S(1)} %collective-permute-done.13.refs_3_), custom_call_target="tpu_custom_call" | custom-call | bytes 1024 | tf_op jit(solution)/shard_map/pallas_call | solution.py:61
  (4 shorter events, 0.1 us)
Async XLA Ops:
  0.6 9.0 %copy-start.2 = (bf16[1,2,768,128]{3,2,1,0:T(8,128)(2,1)S(1)}, bf16[1,2,768,128]{3,2,1,0:T(8,128)(2,1)}, u32[]{:S(2)}) copy-start(bf16[1,2,768,128]{3,2,1,0:T(8,128)(2,1)} %param.11) | copy-start | bytes 1179652
  0.6 9.0 %copy-start.1 = (bf16[1,2,768,128]{3,2,1,0:T(8,128)(2,1)S(1)}, bf16[1,2,768,128]{3,2,1,0:T(8,128)(2,1)}, u32[]{:S(2)}) copy-start(bf16[1,2,768,128]{3,2,1,0:T(8,128)(2,1)} %param.10) | copy-start | bytes 1179652
  0.7 8.9 %copy-start.9 = (bf16[92,6,384]{2,0,1:T(8,128)(2,1)S(1)}, bf16[92,6,384]{2,0,1:T(8,128)(2,1)}, u32[]{:S(2)}) copy-start(bf16[92,6,384]{2,0,1:T(8,128)(2,1)} %param.15) | copy-start | bytes 1271812
  0.7 9.0 %copy-start.5 = (s32[4]{0:T(128)S(1)}, s32[4]{0:T(128)}, u32[]{:S(2)}) copy-start(s32[4]{0:T(128)} %rows_ref.7) | copy-start | bytes 52
  0.7 9.0 %copy-start.6 = (bf16[2,384,128]{2,1,0:T(8,128)(2,1)S(1)}, bf16[2,384,128]{2,1,0:T(8,128)(2,1)}, u32[]{:S(2)}) copy-start(bf16[2,384,128]{2,1,0:T(8,128)(2,1)} %filter_ref.1) | copy-start | bytes 589828
  3.8 22.3 %copy-start.7 = (f32[6]{0:T(128)S(1)}, f32[6]{0:T(128)}, u32[]{:S(2)}) copy-start(f32[6]{0:T(128)} %quad_ref.1) | copy-start | bytes 76
  3.8 22.3 %copy-start.8 = (bf16[736,128]{1,0:T(8,128)(2,1)S(1)}, bf16[736,128]{1,0:T(8,128)(2,1)}, u32[]{:S(2)}) copy-start(bf16[736,128]{1,0:T(8,128)(2,1)} %get-tuple-element.48.refs_0_) | copy-start | bytes 565252
  3.8 10.9 %collective-permute-start = (bf16[736,128]{1,0:T(8,128)(2,1)}, bf16[736,128]{1,0:T(8,128)(2,1)S(1)}, u32[]{:S(2)}, u32[]{:S(2)}) collective-permute-start(bf16[736,128]{1,0:T(8,128)(2,1)} %get-tuple-element.40), channel_id=1, source_target_pairs={{0,12},{4,8},{8,4},{12,0},{1,13},{5,9},{9,5},{13,1},{2,14},{6,10},... | collective-permute-start | bytes 565256 | tf_op jit(solution)/shard_map/ppermute | solution.py:400
  8.9 11.2 %collective-permute-start.3 = (bf16[736,128]{1,0:T(8,128)(2,1)}, bf16[736,128]{1,0:T(8,128)(2,1)S(1)}, u32[]{:S(2)}, u32[]{:S(2)}) collective-permute-start(bf16[736,128]{1,0:T(8,128)(2,1)} %get-tuple-element.49), channel_id=1, source_target_pairs={{0,4},{4,0},{8,12},{12,8},{1,5},{5,1},{9,13},{13,9},{2,6},{6,2},{1... | collective-permute-start | bytes 565256 | tf_op jit(solution)/shard_map/ppermute | solution.py:400
  8.9 17.2 %collective-permute-start.4 = (bf16[736,128]{1,0:T(8,128)(2,1)}, bf16[736,128]{1,0:T(8,128)(2,1)S(1)}, u32[]{:S(2)}, u32[]{:S(2)}) collective-permute-start(bf16[736,128]{1,0:T(8,128)(2,1)} %get-tuple-element.50), channel_id=1, source_target_pairs={{0,8},{4,12},{8,0},{12,4},{1,9},{5,13},{9,1},{13,5},{2,10},{6,14},... | collective-permute-start | bytes 565256 | tf_op jit(solution)/shard_map/ppermute | solution.py:400
  14.7 22.6 %collective-permute-start.1 = (bf16[2,768,128]{2,1,0:T(8,128)(2,1)S(1)}, bf16[2,768,128]{2,1,0:T(8,128)(2,1)S(1)}, u32[]{:S(2)}, u32[]{:S(2)}) collective-permute-start(bf16[2,768,128]{2,1,0:T(8,128)(2,1)S(1)} %get-tuple-element.41), channel_id=1, source_target_pairs={{0,4},{4,0},{8,12},{12,8},{1,5},{5,1},{9,13},{13,9},{2,6},{6,2},{1... | collective-permute-start | bytes 1179656 | tf_op jit(solution)/shard_map/ppermute | solution.py:400
  19.4 20.1 %collective-permute-start.2 = (bf16[2,768,128]{2,1,0:T(8,128)(2,1)S(1)}, bf16[2,768,128]{2,1,0:T(8,128)(2,1)S(1)}, u32[]{:S(2)}, u32[]{:S(2)}) collective-permute-start(bf16[2,768,128]{2,1,0:T(8,128)(2,1)S(1)} %get-tuple-element.42), channel_id=1, source_target_pairs={{4,8},{8,4},{5,9},{9,5},{6,10},{10,6},{7,11},{11,7},{20,24},{24,20... | collective-permute-start | bytes 1179656 | tf_op jit(solution)/shard_map/ppermute | solution.py:464
  26.1 13.4 %copy-start.3 = (s32[6,9]{1,0:T(8,128)S(1)}, s32[6,9]{1,0:T(8,128)}, u32[]{:S(2)}) copy-start(s32[6,9]{1,0:T(8,128)} %shift_ref.1) | copy-start | bytes 652
  26.1 13.4 %copy-start.4 = (bf16[9,128]{1,0:T(8,128)(2,1)S(1)}, bf16[9,128]{1,0:T(8,128)(2,1)}, u32[]{:S(2)}) copy-start(bf16[9,128]{1,0:T(8,128)(2,1)} %taps_ref.1) | copy-start | bytes 6916
  29.1 4.7 %collective-permute-start.5 = (bf16[384,128]{1,0:T(8,128)(2,1)S(1)}, bf16[384,128]{1,0:T(8,128)(2,1)S(1)}, u32[]{:S(2)}, u32[]{:S(2)}) collective-permute-start(bf16[384,128]{1,0:T(8,128)(2,1)S(1)} %get-tuple-element.57), channel_id=1, source_target_pairs={{0,4},{4,0},{8,12},{12,8},{1,5},{5,1},{9,13},{13,9},{2,6},{6,2},{1... | collective-permute-start | bytes 294920 | tf_op jit(solution)/shard_map/ppermute | solution.py:400
  33.8 9.0 %collective-permute-start.9 = (bf16[192,128]{1,0:T(8,128)(2,1)S(1)}, bf16[192,128]{1,0:T(8,128)(2,1)S(1)}, u32[]{:S(2)}, u32[]{:S(2)}) collective-permute-start(bf16[192,128]{1,0:T(8,128)(2,1)S(1)} %get-tuple-element.66), channel_id=1, source_target_pairs={{0,8},{4,12},{8,0},{12,4},{1,9},{5,13},{9,1},{13,5},{2,10},{6,14},... | collective-permute-start | bytes 147464 | tf_op jit(solution)/shard_map/ppermute | solution.py:400
  35.1 14.8 %collective-permute-start.6 = (bf16[736,128]{1,0:T(8,128)(2,1)S(1)}, bf16[736,128]{1,0:T(8,128)(2,1)S(1)}, u32[]{:S(2)}, u32[]{:S(2)}) collective-permute-start(bf16[736,128]{1,0:T(8,128)(2,1)S(1)} %get-tuple-element.60), channel_id=1, source_target_pairs={{0,4},{4,0},{8,12},{12,8},{1,5},{5,1},{9,13},{13,9},{2,6},{6,2},{1... | collective-permute-start | bytes 565256 | tf_op jit(solution)/shard_map/ppermute | solution.py:400
  37.1 17.8 %collective-permute-start.7 = (bf16[736,128]{1,0:T(8,128)(2,1)S(1)}, bf16[736,128]{1,0:T(8,128)(2,1)S(1)}, u32[]{:S(2)}, u32[]{:S(2)}) collective-permute-start(bf16[736,128]{1,0:T(8,128)(2,1)S(1)} %get-tuple-element.61), channel_id=1, source_target_pairs={{0,8},{4,12},{8,0},{12,4},{1,9},{5,13},{9,1},{13,5},{2,10},{6,14},... | collective-permute-start | bytes 565256 | tf_op jit(solution)/shard_map/ppermute | solution.py:400
  37.3 17.6 %collective-permute-start.8 = (bf16[736,128]{1,0:T(8,128)(2,1)S(1)}, bf16[736,128]{1,0:T(8,128)(2,1)S(1)}, u32[]{:S(2)}, u32[]{:S(2)}) collective-permute-start(bf16[736,128]{1,0:T(8,128)(2,1)S(1)} %get-tuple-element.62), channel_id=1, source_target_pairs={{0,12},{4,8},{8,4},{12,0},{1,13},{5,9},{9,5},{13,1},{2,14},{6,10},... | collective-permute-start | bytes 565256 | tf_op jit(solution)/shard_map/ppermute | solution.py:400
  42.8 12.0 %copy-start = (bf16[768,736]{1,0:T(8,128)(2,1)S(1)}, bf16[768,736]{1,0:T(8,128)(2,1)}, u32[]{:S(2)}) copy-start(bf16[768,736]{1,0:T(8,128)(2,1)} %constant.8.clone.table_ref) | copy-start | bytes 3391492
  42.9 4.2 %collective-permute-start.10 = (bf16[224,128]{1,0:T(8,128)(2,1)S(1)}, bf16[224,128]{1,0:T(8,128)(2,1)S(1)}, u32[]{:S(2)}, u32[]{:S(2)}) collective-permute-start(bf16[224,128]{1,0:T(8,128)(2,1)S(1)} %shard_map.135.refs_0_), channel_id=1, source_target_pairs={{0,2},{2,0},{1,3},{3,1},{4,6},{6,4},{5,7},{7,5},{8,10},{10,8},{9,1... | collective-permute-start | bytes 172040 | tf_op jit(solution)/shard_map/ppermute | solution.py:395
  47.2 10.1 %collective-permute-start.13 = (bf16[224,128]{1,0:T(8,128)(2,1)S(1)}, bf16[224,128]{1,0:T(8,128)(2,1)S(1)}, u32[]{:S(2)}, u32[]{:S(2)}) collective-permute-start(bf16[224,128]{1,0:T(8,128)(2,1)S(1)} %shard_map.136.refs_0_), channel_id=1, source_target_pairs={{0,12},{4,8},{8,4},{12,0},{1,13},{5,9},{9,5},{13,1},{2,14},{6,10},... | collective-permute-start | bytes 172040 | tf_op jit(solution)/shard_map/ppermute | solution.py:400
  49.4 9.6 %collective-permute-start.12 = (bf16[224,128]{1,0:T(8,128)(2,1)S(1)}, bf16[224,128]{1,0:T(8,128)(2,1)S(1)}, u32[]{:S(2)}, u32[]{:S(2)}) collective-permute-start(bf16[224,128]{1,0:T(8,128)(2,1)S(1)} %shard_map.136.refs_0_), channel_id=1, source_target_pairs={{0,8},{4,12},{8,0},{12,4},{1,9},{5,13},{9,1},{13,5},{2,10},{6,14},... | collective-permute-start | bytes 172040 | tf_op jit(solution)/shard_map/ppermute | solution.py:400
  49.8 9.2 %collective-permute-start.11 = (bf16[224,128]{1,0:T(8,128)(2,1)S(1)}, bf16[224,128]{1,0:T(8,128)(2,1)S(1)}, u32[]{:S(2)}, u32[]{:S(2)}) collective-permute-start(bf16[224,128]{1,0:T(8,128)(2,1)S(1)} %shard_map.136.refs_0_), channel_id=1, source_target_pairs={{0,4},{4,0},{8,12},{12,8},{1,5},{5,1},{9,13},{13,9},{2,6},{6,2},{1... | collective-permute-start | bytes 172040 | tf_op jit(solution)/shard_map/ppermute | solution.py:400

commit v3 on v2

--- a/solution.py
+++ b/solution.py
@@ -108,9 +108,21 @@
         outs[shift][...] = jnp.concatenate(columns, axis=0).astype(BF16)
 
 
+def wrapped(target, row, value):
+    lon_count = value.shape[0]
+    target[row, REACH : REACH + lon_count, :] = value
+    target[row, :REACH, :] = value[lon_count - REACH :, :]
+    target[row, REACH + lon_count :, :] = value[:REACH, :]
+
+
+def folded(values):
+    return jnp.sum(values.reshape(values.shape[0] // 8, 8, values.shape[1]), axis=0)
+
+
 def prepare_kernel(
-    local_modes, rows_ref, leg_ref, filter_ref, x_ref, dy_ref,
-    mixer_ref, back_ref, act_ref, first_rim, second_rim, pairs_ref,
+    local_modes, blocks, rows_ref, shift_ref, leg_ref, filter_ref, x_ref, dy_ref, taps_ref,
+    mixer_ref, back_ref, first_rim, second_rim, base_ref, slope_ref, base_grad_ref, tap_ref,
+    pairs_ref, act_ref, acts, grads,
 ):
     me = lax.axis_index("space")
     activate(x_ref, act_ref)
@@ -119,6 +131,15 @@
     for rim_ref, row in ((first_rim, last * (1 - odd)), (second_rim, last * odd)):
         rim_ref[0] = act_ref[row]
         rim_ref[1] = dy_ref[row]
+    pair_products(local_modes, leg_ref, filter_ref, mixer_ref, back_ref, pairs_ref)
+    disco_inner(
+        blocks, rows_ref, shift_ref, x_ref, dy_ref, act_ref, taps_ref,
+        base_ref, slope_ref, base_grad_ref, tap_ref, acts, grads,
+    )
+
+
+def pair_products(local_modes, leg_ref, filter_ref, mixer_ref, back_ref, pairs_ref):
+    me = lax.axis_index("space")
     lat_count, padded_modes, _ = leg_ref.shape
     pairs = lat_pairs(lat_count)
     used = len(pairs) * padded_modes
@@ -232,8 +253,8 @@
         outs[shift][...] = wide[shift].astype(BF16)
 
 
-def disco_kernel(
-    blocks, lat_count, rows_ref, shift_ref, x_ref, dy_ref, act_ref, first_rim, second_rim, taps_ref,
+def disco_inner(
+    blocks, rows_ref, shift_ref, x_ref, dy_ref, act_ref, taps_ref,
     base_ref, slope_ref, base_grad_ref, tap_ref, acts, grads,
 ):
     slots, lon_count, chans = x_ref.shape
@@ -241,56 +262,102 @@
     me = lax.axis_index("space")
     live = rows_ref[me]
     start = first_row_of(rows_ref, me, blocks)
-
-    def wrapped(target, row, value):
-        target[row, REACH : REACH + lon_count, :] = value
-        target[row, :REACH, :] = value[lon_count - REACH :, :]
-        target[row, REACH + lon_count :, :] = value[:REACH, :]
-
-    odd = jnp.bitwise_and(me, 1)
-    for rim_ref, row in ((first_rim, (slots + 1) * (1 - odd)), (second_rim, (slots + 1) * odd)):
-        wrapped(acts, row, rim_ref[0].astype(F32))
-        wrapped(grads, row, rim_ref[1].astype(F32))
     for slot in range(slots):
         alive = jnp.where(slot < live, 1.0, 0.0)
-        wrapped(acts, slot + 1, act_ref[slot].astype(F32))
-        wrapped(grads, slot + 1, dy_ref[slot].astype(F32) * alive)
+        wrapped(acts, slot, act_ref[slot].astype(F32))
+        wrapped(grads, slot, dy_ref[slot].astype(F32) * alive)
+    acts[slots] = jnp.zeros(acts.shape[1:], F32)
+    grads[slots] = jnp.zeros(grads.shape[1:], F32)
     weights = taps_ref[...].astype(F32)
     step = 32 if lon_count % 32 == 0 else lon_count
     totals = [jnp.zeros((8, chans), F32)] * taps
+    top = shift_ref.shape[0] - 1
     for slot in range(slots):
-        below = jnp.where(slot + 1 < live, slot + 2, slots + 1)
-        rows = [slot, slot + 1, below]
-        lat = jnp.clip(start + slot, 0, lat_count - 1)
-        lats = [jnp.maximum(lat - 1, 0), lat, jnp.minimum(lat + 1, lat_count - 1)]
-        ahead = [REACH + shift_ref[lat, t] for t in range(taps)]
-        behind = [REACH - shift_ref[lats[2 - t // 3], t] for t in range(taps)]
-
-        def taps_of(i, totals):
+        below = jnp.where(slot + 1 < live, slot + 1, slots)
+        sources = [(1, slot)]
+        if slot > 0:
+            sources.append((0, slot - 1))
+        if slot + 1 < slots:
+            sources.append((2, below))
+        lat = jnp.clip(start + slot, 0, top)
+        ahead, behind = [], []
+        for offset, row in sources:
+            other = jnp.clip(lat + offset - 1, 0, top)
+            for column in range(3):
+                t = 3 * offset + column
+                ahead.append((t, row, REACH + shift_ref[lat, t]))
+                t = 3 * (2 - offset) + column
+                behind.append((t, row, REACH - shift_ref[other, t]))
+
+        def inner(i, totals):
             at = pl.multiple_of(i * step, step)
             part = pl.ds(at, step)
             x = x_ref[slot, part, :].astype(F32)
-            dy = grads[slot + 1, pl.ds(pl.multiple_of(REACH + at, 8), step), :]
+            dy = grads[slot, pl.ds(pl.multiple_of(REACH + at, 8), step), :]
             out = x
             back = jnp.zeros((step, chans), F32)
-            fresh = []
-            for t in range(taps):
-                moved = acts[rows[t // 3], pl.ds(at + ahead[t], step), :]
+            fresh = list(totals)
+            for t, row, first in ahead:
+                moved = acts[row, pl.ds(at + first, step), :]
                 out = out + moved * weights[t : t + 1, :]
-                fresh.append(totals[t] + jnp.sum((moved * dy).reshape(step // 8, 8, chans), axis=0))
-                back = back + grads[rows[2 - t // 3], pl.ds(at + behind[t], step), :] * weights[
-                    t : t + 1, :
-                ]
+                fresh[t] = fresh[t] + folded(moved * dy)
+            for t, row, first in behind:
+                back = back + grads[row, pl.ds(at + first, step), :] * weights[t : t + 1, :]
             slope = gelu_slope(x)
             base_ref[slot, part, :] = out
             slope_ref[slot, part, :] = slope
             base_grad_ref[slot, part, :] = dy + back * slope
             return tuple(fresh)
 
-        totals = list(lax.fori_loop(0, lon_count // step, taps_of, tuple(totals)))
+        totals = list(lax.fori_loop(0, lon_count // step, inner, tuple(totals)))
     lines = [jnp.sum(total, axis=0, keepdims=True) for total in totals]
     lines.append(jnp.zeros((tap_ref.shape[0] - taps, chans), F32))
     tap_ref[...] = jnp.concatenate(lines, axis=0)
+
+
+def rim_kernel(
+    blocks, rows_ref, shift_ref, dy_ref, first_rim, second_rim, taps_ref, inner_ref,
+    rim_ref, rim_grad_ref, tap_ref, acts, grads,
+):
+    _, lon_count, chans = dy_ref.shape
+    me = lax.axis_index("space")
+    live = rows_ref[me]
+    start = first_row_of(rows_ref, me, blocks)
+    odd = jnp.bitwise_and(me, 1)
+    for source, row in ((first_rim, 1 - odd), (second_rim, odd)):
+        wrapped(acts, row, source[0].astype(F32))
+        wrapped(grads, row, source[1].astype(F32))
+    weights = taps_ref[...].astype(F32)
+    step = 32 if lon_count % 32 == 0 else lon_count
+    top = shift_ref.shape[0] - 1
+    lines = [jnp.zeros((1, chans), F32)] * tap_ref.shape[0]
+    for side in range(2):
+        slot = 0 if side == 0 else live - 1
+        lat = jnp.clip(start + slot, 0, top)
+        other = jnp.clip(lat + 2 * side - 1, 0, top)
+        ahead = [(t, REACH + shift_ref[lat, t]) for t in range(6 * side, 6 * side + 3)]
+        behind = [(t, REACH - shift_ref[other, t]) for t in range(6 - 6 * side, 9 - 6 * side)]
+
+        def rim(i, totals):
+            at = pl.multiple_of(i * step, step)
+            part = pl.ds(at, step)
+            dy = dy_ref[slot, part, :].astype(F32)
+            out = back = jnp.zeros((step, chans), F32)
+            fresh = []
+            for total, (t, first) in zip(totals, ahead):
+                moved = acts[side, pl.ds(at + first, step), :]
+                out = out + moved * weights[t : t + 1, :]
+                fresh.append(total + folded(moved * dy))
+            for t, first in behind:
+                back = back + grads[side, pl.ds(at + first, step), :] * weights[t : t + 1, :]
+            rim_ref[side, part, :] = out
+            rim_grad_ref[side, part, :] = back
+            return tuple(fresh)
+
+        totals = lax.fori_loop(0, lon_count // step, rim, (jnp.zeros((8, chans), F32),) * 3)
+        for (t, _), total in zip(ahead, totals):
+            lines[t] = jnp.sum(total, axis=0, keepdims=True)
+    tap_ref[...] = inner_ref[...] + jnp.concatenate(lines, axis=0)
 
 
 def split_taps(taps, out_ref, count):
@@ -303,70 +370,45 @@
     return rows[-2 * TAP_ROWS : -TAP_ROWS, :] + rows[-TAP_ROWS:, :]
 
 
-def halve_kernel(distance, kept_ref, got_ref, keep_ref, send_ref, total):
-    total[...] = kept_ref[...] + got_ref[...].astype(F32)
-    rows = total.shape[0] // 2
-    half = rows // 2
-    upper = jnp.where(jnp.bitwise_and(lax.axis_index("space"), distance) != 0, half, 0)
-    for target, at in ((keep_ref, upper), (send_ref, half - upper)):
-        both = [
-            total[pl.ds(pl.multiple_of(part * rows + at, 8), half), :] for part in range(2)
-        ]
-        target[...] = jnp.concatenate(both, axis=0).astype(target.dtype)
-
-
-def own_kernel(kept_ref, got_ref, tap_ref, out_ref):
-    count = kept_ref.shape[0]
-    out_ref[:count, :] = (kept_ref[...] + got_ref[...].astype(F32)).astype(BF16)
-    split_taps(tap_ref[...], out_ref, count)
-
-
-def member_kernel(lat_count, *refs):
-    members = len(refs) - 2
-    parts, out_ref, held = refs[:members], refs[-2], refs[-1]
-    me = lax.axis_index("ens")
-    count = out_ref.shape[0] - 2 * TAP_ROWS
-    for shift in range(members):
-        at = lax.rem(me + (members - shift), members)
-        part = parts[shift][...].astype(F32)
-        held[at, :count, :] = part[:count, :]
-        held[at, count:, :] = joined_taps(part)
-    total = held[0]
-    for member in range(1, members):
-        total = total + held[member]
-    total = total / members
-    out_ref[:count, :] = total[:count, :].astype(BF16)
-    split_taps(total[count:, :] / lat_count, out_ref, count)
-
-
-def mirrored(block, blocks):
-    place = jnp.int32(0)
-    bits = blocks.bit_length() - 1
-    for bit in range(bits):
-        place = place + (jnp.bitwise_and(block, 1 << bit) >> bit) * (1 << (bits - 1 - bit))
-    return place
-
-
-def spread_kernel(*refs):
-    parts, (filter_ref, tap_ref, held) = refs[:-3], refs[-3:]
-    me = lax.axis_index("space")
-    blocks = len(parts)
-    share = filter_ref.shape[1] // blocks
-    for shift in range(blocks):
-        block = jnp.bitwise_xor(me, shift)
-        part = parts[shift][...].astype(F32)
-        at = pl.ds(pl.multiple_of(mirrored(block, blocks) * share, share), share)
-        filter_ref[0, at, :] = part[:share, :]
-        filter_ref[1, at, :] = part[share : 2 * share, :]
-        held[block] = joined_taps(part)
-    total = held[0]
-    for block in range(1, blocks):
-        total = total + held[block]
-    tap_ref[...] = total[: tap_ref.shape[0], :]
+def split_taps(taps, out_ref, count):
+    high = taps.astype(BF16)
+    out_ref[count : count + TAP_ROWS, :] = high
+    out_ref[count + TAP_ROWS :, :] = (taps - high.astype(F32)).astype(BF16)
+
+
+def joined_taps(ref):
+    rows = ref[ref.shape[0] - 2 * TAP_ROWS :, :].astype(F32)
+    return rows[:TAP_ROWS, :] + rows[TAP_ROWS:, :]
+
+
+def added(first_ref, second_ref):
+    return first_ref[...].astype(F32) + second_ref[...].astype(F32)
+
+
+def half_kernel(kept_ref, got_ref, tap_ref, out_ref):
+    out_ref[: kept_ref.shape[0], :] = added(kept_ref, got_ref).astype(BF16)
+    split_taps(tap_ref[...], out_ref, kept_ref.shape[0])
+
+
+def add_kernel(scale, tap_scale, own_ref, other_ref, out_ref):
+    count = own_ref.shape[0] - 2 * TAP_ROWS
+    out_ref[:count, :] = (added(own_ref, other_ref)[:count, :] / scale).astype(BF16)
+    split_taps((joined_taps(own_ref) + joined_taps(other_ref)) / tap_scale, out_ref, count)
+
+
+def spread_kernel(own_ref, other_ref, filter_ref, tap_ref):
+    half = filter_ref.shape[1] // 2
+    upper = jnp.bitwise_and(lax.axis_index("space"), 1)
+    for ref, which in ((own_ref, upper), (other_ref, 1 - upper)):
+        at = pl.ds(pl.multiple_of(which * half, half), half)
+        rows = ref[: 2 * half, :].astype(F32)
+        filter_ref[0, at, :] = rows[:half, :]
+        filter_ref[1, at, :] = rows[half:, :]
+    tap_ref[...] = (joined_taps(own_ref) + joined_taps(other_ref))[: tap_ref.shape[0], :]
 
 
 def finish_kernel(
-    blocks, rows_ref, table_ref, base_ref, slope_ref, base_grad_ref, *refs
+    blocks, rows_ref, table_ref, base_ref, slope_ref, base_grad_ref, rim_ref, rim_grad_ref, *refs
 ):
     ins, out_ref, grad_ref, source = refs[:blocks], refs[blocks], refs[blocks + 1], refs[blocks + 2]
     slots, lon_count, chans = base_ref.shape
@@ -384,20 +426,21 @@
         at = slot * chans
         out = base_ref[slot] + sums[:, at : at + chans]
         at = (slots + slot) * chans
-        grad = base_grad_ref[slot] + sums[:, at : at + chans] * slope_ref[slot]
+        back = sums[:, at : at + chans]
+        if slot == 0:
+            out = out + rim_ref[0]
+            back = back + rim_grad_ref[0]
+        out = out + jnp.where(slot == live - 1, rim_ref[1], 0.0)
+        back = back + jnp.where(slot == live - 1, rim_grad_ref[1], 0.0)
+        grad = base_grad_ref[slot] + back * slope_ref[slot]
         alive = slot < live
         out_ref[slot] = jnp.where(alive, out, 0.0).astype(BF16)
         grad_ref[slot] = jnp.where(alive, grad, 0.0).astype(BF16)
 
 
-def shifted(values, axis, shift):
+def crossed(values, distance, axis="space"):
     count = lax.axis_size(axis)
-    return lax.ppermute(values, axis, [(i, (i + shift) % count) for i in range(count)])
-
-
-def crossed(values, distance):
-    count = lax.axis_size("space")
-    return lax.ppermute(values, "space", [(i, i ^ distance) for i in range(count)])
+    return lax.ppermute(values, axis, [(i, i ^ distance) for i in range(count)])
 
 
 def crossed_all(parts, distances):
@@ -446,13 +489,16 @@
     leg_rows = jnp.pad(
         jnp.transpose(legendre, (1, 0, 2)), ((0, 0), (0, padded_modes - local_modes), (0, 0))
     )
-    mixer, back, act, first_rim, second_rim = call(
-        functools.partial(prepare_kernel, local_modes),
-        [shape((pair_rows, 2 * chans), F32), shape((degrees, pair_rows), BF16)]
-        + [shape(x.shape, BF16), rim, rim],
-        [SMEM] + [VMEM] * 4,
-        (band_rows, leg_rows, spectral_filter, x, dy),
-        scratch=[pltpu.VMEM((pair_rows, degrees), BF16)],
+    padded = (lon_count + 2 * REACH, chans)
+    tap_shape = shape((TAP_ROWS, chans), F32)
+    mixer, back, first_rim, second_rim, base, slope, base_grad, tap_part = call(
+        functools.partial(prepare_kernel, local_modes, blocks),
+        [shape((pair_rows, 2 * chans), F32), shape((degrees, pair_rows), BF16), rim, rim]
+        + [field, field, field, tap_shape],
+        [SMEM, SMEM] + [VMEM] * 5,
+        (band_rows, tap_shift, leg_rows, spectral_filter, x, dy, tap_weight),
+        scratch=[pltpu.VMEM((pair_rows, degrees), BF16), pltpu.VMEM(x.shape, BF16)]
+        + [pltpu.VMEM((slots + 1, *padded), F32)] * 2,
         limit=big,
         flops=2 * pair_rows * degrees * 2 * chans,
         moved=8 * pair_rows * chans,
@@ -475,58 +521,45 @@
         flops=20 * degrees * pair_rows * 2 * chans,
     )
     back_parts, keep, send = mixed[:blocks], mixed[blocks], mixed[blocks + 1]
-    distance = 1
-    got_sums = crossed(send, distance)
-    base, slope, base_grad, tap_part = call(
-        functools.partial(disco_kernel, blocks, lat_count),
-        [field, field, field, shape((TAP_ROWS, chans), F32)],
-        [SMEM, SMEM] + [VMEM] * 6,
-        (band_rows, tap_shift, x, dy, act, first_rim, second_rim, tap_weight),
-        scratch=[pltpu.VMEM((slots + 2, lon_count + 2 * REACH, chans), F32)] * 2,
-    )
-    while 2 * distance < blocks:
-        distance *= 2
-        rows = keep.shape[0] // 2
-        keep, send = call(
-            functools.partial(halve_kernel, distance),
-            [shape((rows, chans), F32), shape((rows, chans), BF16)],
-            [VMEM, VMEM],
-            (keep, got_sums),
-            scratch=[pltpu.VMEM(keep.shape, F32)],
+    got_sum = crossed(send, 1)
+    rim_sum, rim_grad, tap_part = call(
+        functools.partial(rim_kernel, blocks),
+        [shape((2, lon_count, chans), F32)] * 2 + [tap_shape],
+        [SMEM, SMEM] + [VMEM] * 5,
+        (band_rows, tap_shift, dy, first_rim, second_rim, tap_weight, tap_part),
+        scratch=[pltpu.VMEM((2, *padded), F32)] * 2,
+    )
+    got_sum, tap_part = lax.optimization_barrier((got_sum, tap_part))
+    message = shape((degrees + 2 * TAP_ROWS, chans), BF16)
+    own = call(half_kernel, message, [VMEM] * 3, (keep, got_sum, tap_part))
+    back_parts, own = lax.optimization_barrier((back_parts, own))
+    returned = [back_parts[0], *reversed(crossed_all(back_parts, far).values())]
+    for bit in range(1, blocks.bit_length() - 1):
+        own = call(
+            functools.partial(add_kernel, 1, 1), message, [VMEM] * 2, (own, crossed(own, 1 << bit))
         )
-        got_sums = crossed(send, distance)
-    back_parts, keep = lax.optimization_barrier((back_parts, keep))
-    returned = [back_parts[0], *reversed(crossed_all(back_parts, far).values())]
-    own = call(
-        own_kernel,
-        shape((share + 2 * TAP_ROWS, chans), BF16),
-        [VMEM] * 3,
-        (keep, got_sums, tap_part),
-    )
-    by_member = [own] + [shifted(own, "ens", s) for s in range(1, members)]
-    final = call(
-        functools.partial(member_kernel, lat_count),
-        shape((share + 2 * TAP_ROWS, chans), BF16),
-        [VMEM] * members,
-        by_member,
-        flops=1200000000,
-        scratch=[pltpu.VMEM((members, share + TAP_ROWS, chans), F32)],
-    )
-    spread = [final] + [crossed(final, s) for s in range(1, blocks)]
+    for bit in range(members.bit_length() - 1):
+        scales = (members, members * lat_count) if bit == 0 else (1, 1)
+        own = call(
+            functools.partial(add_kernel, *scales),
+            message,
+            [VMEM] * 2,
+            (own, crossed(own, 1 << bit, "ens")),
+            flops=0,
+        )
+    filter_grad, tap_grad = call(
+        spread_kernel,
+        [shape((2, degrees, chans), F32), shape((tap_weight.shape[0], chans), F32)],
+        [VMEM] * 2,
+        (own, crossed(own, 1)),
+    )
     output, input_grad = call(
         functools.partial(finish_kernel, blocks),
         [shape(x.shape, BF16)] * 2,
-        [SMEM] + [VMEM] * (4 + blocks),
-        (band_rows, table_out, base, slope, base_grad, *returned),
+        [SMEM] + [VMEM] * (6 + blocks),
+        (band_rows, table_out, base, slope, base_grad, rim_sum, rim_grad, *returned),
         scratch=[pltpu.VMEM((blocks * depth, 2 * slots * chans), F32)],
         flops=2 * blocks * depth * lon_count * 2 * slots * chans,
-    )
-    filter_grad, tap_grad = call(
-        spread_kernel,
-        [shape((2, degrees, chans), F32), shape((tap_weight.shape[0], chans), F32)],
-        [VMEM] * blocks,
-        spread,
-        scratch=[pltpu.VMEM((blocks, TAP_ROWS, chans), F32)],
     )
     return (output[None], input_grad[None], filter_grad, tap_grad)
 

time: 60 us -> 58.4 us (0.973)
  starting transfers between devices: 22.8 us -> 20 us
    ppermute x13 -> x11, starting transfers between devices: 22.1 us -> 19.3 us  [crossed(): return lax.ppermute(values, axis, [(i, i ^ distance) for i in range(count)])]
    ppermute x13 -> x11, waiting for transfers between devices: 20.1 us -> 20.6 us  [crossed(): return lax.ppermute(values, axis, [(i, i ^ distance) for i in range(count)])]
  transfers between devices with their start and end apart: 14 -> 12, of which waited for: 6 -> 6; matrix products, arithmetic and copies ran while one was open for 0% -> 0% of each run, Pallas kernels for 20% -> 21%
where the time goes in v3:
time: 58.4 us; the launch traced here: 57.8 us
  waiting for transfers between devices  20.6 us (35%)
  starting transfers between devices  20 us (34%)
  Pallas kernels  16.2 us (28%)
  between operations  0.83 us (1%)
    ppermute x11, waiting for transfers between devices, crossed(): return lax.ppermute(values, axis, [(i, i ^ distance) for i in range(count)])  20.6 us
    ppermute x11, starting transfers between devices, crossed(): return lax.ppermute(values, axis, [(i, i ^ distance) for i in range(count)])  19.3 us
    pallas_call x9, Pallas kernels, call(): pl.pallas_call(kernel, out_shape=out_shape, in_specs=in_specs, out_specs=...  16.2 us
  transfers between devices with their start and end apart: 12, of which 6 were waited for; matrix products, arithmetic and copies ran while one was open for 0% of the time, Pallas kernels for 21%

profile of v3, /device:TPU:0, one launch (start us, length us, event | category | flops | bytes accessed | tf_op | source)
XLA Modules:
  0.0 57.8 jit_solution(4952111810942124691)
XLA Ops:
  0.6 0.0 copy-start.1
  0.6 0.0 copy-start.5
  0.7 0.0 copy-start.9
  0.7 0.0 copy-start.4
  0.7 0.0 copy-start.3
  0.7 0.0 copy-start.2
  0.7 0.0 copy-start.6
  0.7 3.1 %shard_map.130 = (bf16[736,128]{1,0:T(8,128)(2,1)}, bf16[736,128]{1,0:T(8,128)(2,1)}, bf16[736,128]{1,0:T(8,128)(2,1)}, bf16[736,128]{1,0:T(8,128)(2,1)}) custom-call(bf16[2,768,128]{2,1,0:T(8,128)(2,1)} %bitcast.8, bf16[2,768,128]{2,1,0:T(8,128)(2,1)} %bitcast.5, bf16[4,184,768]{2,1,0:T(8,128)(2,1)} %constant.7.clone.table_hbm), custom_call_target="tpu_custom_call" | custom-call | flops 578813952 | bytes 1024 | tf_op jit(solution)/shard_map/pallas_call | solution.py:61
  3.8 0.0 copy-start.7
  3.8 0.0 copy-start.8
  3.8 5.1 %collective-permute-start = (bf16[736,128]{1,0:T(8,128)(2,1)}, bf16[736,128]{1,0:T(8,128)(2,1)S(1)}, u32[]{:S(2)}, u32[]{:S(2)}) collective-permute-start(bf16[736,128]{1,0:T(8,128)(2,1)} %get-tuple-element.44), channel_id=1, source_target_pairs={{0,12},{4,8},{8,4},{12,0},{1,13},{5,9},{9,5},{13,1},{2,14},{6,10},... | collective-permute-start | bytes 565256 | tf_op jit(solution)/shard_map/ppermute | solution.py:443
  8.9 0.0 collective-permute-start.3
  8.9 0.6 %collective-permute-start.4 = (bf16[736,128]{1,0:T(8,128)(2,1)}, bf16[736,128]{1,0:T(8,128)(2,1)S(1)}, u32[]{:S(2)}, u32[]{:S(2)}) collective-permute-start(bf16[736,128]{1,0:T(8,128)(2,1)} %get-tuple-element.54), channel_id=1, source_target_pairs={{0,8},{4,12},{8,0},{12,4},{1,9},{5,13},{9,1},{13,5},{2,10},{6,14},... | collective-permute-start | bytes 565256 | tf_op jit(solution)/shard_map/ppermute | solution.py:443
  9.6 0.0 copy-done.9
  9.6 0.0 copy-done.1
  9.6 0.0 copy-done.5
  9.7 0.0 copy-done.4
  9.7 0.0 copy-done.3
  9.7 0.0 copy-done.2
  9.7 0.0 copy-done.6
  9.7 5.3 %shard_map.129 = (f32[2048,256]{1,0:T(8,128)S(1)}, bf16[384,2048]{1,0:T(8,128)(2,1)S(1)}, bf16[2,768,128]{2,1,0:T(8,128)(2,1)S(1)}, bf16[2,768,128]{2,1,0:T(8,12...) custom-call(s32[4]{0:T(128)S(1)} %copy-done.4, ...), custom_call_target="tpu_custom_call" | custom-call | flops 402653184 | bytes 2097152 | tf_op jit(solution)/shard_map/pallas_call | solution.py:61
  15.0 0.0 collective-permute-done.refs_3_
  15.0 4.4 %collective-permute-start.1 = (bf16[2,768,128]{2,1,0:T(8,128)(2,1)S(1)}, bf16[2,768,128]{2,1,0:T(8,128)(2,1)S(1)}, u32[]{:S(2)}, u32[]{:S(2)}) collective-permute-start(bf16[2,768,128]{2,1,0:T(8,128)(2,1)S(1)} %get-tuple-element.45), channel_id=1, source_target_pairs={{0,4},{4,0},{8,12},{12,8},{1,5},{5,1},{9,13},{13,9},{2,6},{6,2},{1... | collective-permute-start | bytes 1179656 | tf_op jit(solution)/shard_map/ppermute | solution.py:443
  19.4 0.7 %collective-permute-start.2 = (bf16[2,768,128]{2,1,0:T(8,128)(2,1)S(1)}, bf16[2,768,128]{2,1,0:T(8,128)(2,1)S(1)}, u32[]{:S(2)}, u32[]{:S(2)}) collective-permute-start(bf16[2,768,128]{2,1,0:T(8,128)(2,1)S(1)} %get-tuple-element.46), channel_id=1, source_target_pairs={{4,8},{8,4},{5,9},{9,5},{6,10},{10,6},{7,11},{11,7},{20,24},{24,20... | collective-permute-start | bytes 1179656 | tf_op jit(solution)/shard_map/ppermute | solution.py:510
  20.1 0.0 collective-permute-done.3.refs_1_
  20.1 6.0 %collective-permute-done.4.refs_2_ = bf16[736,128]{1,0:T(8,128)(2,1)S(1)} collective-permute-done((bf16[736,128]{1,0:T(8,128)(2,1)}, bf16[736,128]{1,0:T(8,128)(2,1)S(1)}, u32[]{:S(2)}, u32[]{:S(2)}) %collective-permute-start.4) | collective-permute-done | bytes 188448 | tf_op jit(solution)/shard_map/ppermute | solution.py:443
  26.1 0.0 copy-done.7
  26.1 0.0 copy-done.8
  26.1 3.0 %shard_map.132 = (bf16[736,128]{1,0:T(8,128)(2,1)S(1)}, bf16[736,128]{1,0:T(8,128)(2,1)S(1)}, bf16[736,128]{1,0:T(8,128)(2,1)S(1)}, bf16[736,128]{1,0:T(8,128)(2...) custom-call(s32[4]{0:T(128)S(1)} %copy-done.4, f32[6]{0:T(128)S(1)} %copy-done.7, ...), custom_call_target="tpu_custom_call" | custom-call | flops 4026531840 | bytes 1024 | tf_op jit(solution)/shard_map/pallas_call | solution.py:61
  29.1 0.0 copy-start
  29.1 0.1 collective-permute-start.5
  29.2 1.7 %collective-permute-done.1.first_rim = bf16[2,768,128]{2,1,0:T(8,128)(2,1)S(1)} collective-permute-done((bf16[2,768,128]{2,1,0:T(8,128)(2,1)S(1)}, bf16[2,768,128]{2,1,0:T(8,128)(2,1)S(1)}, u32[]{:S(2)}, u32[]{:S(2)}) %collective-permute-start.1) | collective-permute-done | bytes 393248 | tf_op jit(solution)/shard_map/ppermute | solution.py:443
  30.9 0.0 collective-permute-done.2.second_rim
  30.9 1.5 %shard_map.131 = (f32[2,768,128]{2,1,0:T(8,128)S(1)}, f32[2,768,128]{2,1,0:T(8,128)S(1)}, f32[16,128]{1,0:T(8,128)S(1)}) custom-call(s32[4]{0:T(128)S(1)} %copy-done.4, s32[6,9]{1,0:T(8,128)S(1)} %copy-done.2, bf16[2,768,128]{2,1,0:T(8,128)(2,1)S(1)} %bitcast.7, bf16[2,768,128]{2,1,0:T(8,128)(2,1)S(1)} %collective-permute-done.1.first_rim, ...), custom_call_target="tpu_custom_call" | custom-call | bytes 1024 | tf_op jit(solution)/shard_map/pallas_call | solution.py:61
  32.4 1.4 %collective-permute-done.5.got_ref = bf16[384,128]{1,0:T(8,128)(2,1)S(1)} collective-permute-done((bf16[384,128]{1,0:T(8,128)(2,1)S(1)}, bf16[384,128]{1,0:T(8,128)(2,1)S(1)}, u32[]{:S(2)}, u32[]{:S(2)}) %collective-permute-start.5) | collective-permute-done | bytes 98336 | tf_op jit(solution)/shard_map/ppermute | solution.py:443
  33.9 2.9 %collective-permute-start.9 = (bf16[416,128]{1,0:T(8,128)(2,1)S(1)}, bf16[416,128]{1,0:T(8,128)(2,1)S(1)}, u32[]{:S(2)}, u32[]{:S(2)}) collective-permute-start(bf16[416,128]{1,0:T(8,128)(2,1)S(1)} %shard_map.133.own_ref), channel_id=1, source_target_pairs={{0,8},{4,12},{8,0},{12,4},{1,9},{5,13},{9,1},{13,5},{2,10},{6,14},... | collective-permute-start | bytes 319496 | tf_op jit(solution)/shard_map/ppermute | solution.py:443
  36.7 0.4 collective-permute-start.6
  37.1 1.6 %collective-permute-start.7 = (bf16[736,128]{1,0:T(8,128)(2,1)S(1)}, bf16[736,128]{1,0:T(8,128)(2,1)S(1)}, u32[]{:S(2)}, u32[]{:S(2)}) collective-permute-start(bf16[736,128]{1,0:T(8,128)(2,1)S(1)} %get-tuple-element.67), channel_id=1, source_target_pairs={{0,8},{4,12},{8,0},{12,4},{1,9},{5,13},{9,1},{13,5},{2,10},{6,14},... | collective-permute-start | bytes 565256 | tf_op jit(solution)/shard_map/ppermute | solution.py:443
  38.7 2.4 %collective-permute-start.8 = (bf16[736,128]{1,0:T(8,128)(2,1)S(1)}, bf16[736,128]{1,0:T(8,128)(2,1)S(1)}, u32[]{:S(2)}, u32[]{:S(2)}) collective-permute-start(bf16[736,128]{1,0:T(8,128)(2,1)S(1)} %get-tuple-element.68), channel_id=1, source_target_pairs={{0,12},{4,8},{8,4},{12,0},{1,13},{5,9},{9,5},{13,1},{2,14},{6,10},... | collective-permute-start | bytes 565256 | tf_op jit(solution)/shard_map/ppermute | solution.py:443
  41.1 1.3 %collective-permute-done.9.other_ref = bf16[416,128]{1,0:T(8,128)(2,1)S(1)} collective-permute-done((bf16[416,128]{1,0:T(8,128)(2,1)S(1)}, bf16[416,128]{1,0:T(8,128)(2,1)S(1)}, u32[]{:S(2)}, u32[]{:S(2)}) %collective-permute-start.9) | collective-permute-done | bytes 106528 | tf_op jit(solution)/shard_map/ppermute | solution.py:443
  42.5 1.6 %collective-permute-start.10 = (bf16[416,128]{1,0:T(8,128)(2,1)S(1)}, bf16[416,128]{1,0:T(8,128)(2,1)S(1)}, u32[]{:S(2)}, u32[]{:S(2)}) collective-permute-start(bf16[416,128]{1,0:T(8,128)(2,1)S(1)} %shard_map.135.own_ref), channel_id=1, source_target_pairs={{0,2},{2,0},{1,3},{3,1},{4,6},{6,4},{5,7},{7,5},{8,10},{10,8},{9,1... | collective-permute-start | bytes 319496 | tf_op jit(solution)/shard_map/ppermute | solution.py:443
  44.0 3.2 %collective-permute-done.10.other_ref = bf16[416,128]{1,0:T(8,128)(2,1)S(1)} collective-permute-done((bf16[416,128]{1,0:T(8,128)(2,1)S(1)}, bf16[416,128]{1,0:T(8,128)(2,1)S(1)}, u32[]{:S(2)}, u32[]{:S(2)}) %collective-permute-start.10) | collective-permute-done | bytes 106528 | tf_op jit(solution)/shard_map/ppermute | solution.py:443
  47.3 0.2 collective-permute-start.11
  47.5 0.0 collective-permute-done.6.refs_1_
  47.5 7.0 %collective-permute-done.7.refs_2_ = bf16[736,128]{1,0:T(8,128)(2,1)S(1)} collective-permute-done((bf16[736,128]{1,0:T(8,128)(2,1)S(1)}, bf16[736,128]{1,0:T(8,128)(2,1)S(1)}, u32[]{:S(2)}, u32[]{:S(2)}) %collective-permute-start.7) | collective-permute-done | bytes 188448 | tf_op jit(solution)/shard_map/ppermute | solution.py:443
  54.5 0.0 collective-permute-done.8.refs_3_
  54.5 0.0 copy-done
  54.5 2.5 %shard_map.134 = (bf16[2,768,128]{2,1,0:T(8,128)(2,1)}, bf16[2,768,128]{2,1,0:T(8,128)(2,1)}) custom-call(s32[4]{0:T(128)S(1)} %copy-done.4, bf16[768,736]{1,0:T(8,128)(2,1)S(1)} %copy-done, f32[2,768,128]{2,1,0:T(8,128)S(1)} %get-tuple-element.39.base_ref, f32[2,768,128]{2,1,0:T(8,128)S(1)} %get-tuple-element.40.slope_ref, ...), custom_call_target="tpu_custom_call" | custom-call | flops 578813952 | bytes 1024 | tf_op jit(solution)/shard_map/pallas_call | solution.py:61
  57.0 0.0 collective-permute-done.11.other_ref
  57.0 0.8 %shard_map.137 = (f32[2,384,128]{2,1,0:T(8,128)}, f32[9,128]{1,0:T(8,128)}) custom-call(bf16[416,128]{1,0:T(8,128)(2,1)S(1)} %shard_map.136.own_ref, bf16[416,128]{1,0:T(8,128)(2,1)S(1)} %collective-permute-done.11.other_ref), custom_call_target="tpu_custom_call" | custom-call | bytes 1024 | tf_op jit(solution)/shard_map/pallas_call | solution.py:61
  (4 shorter events, 0.1 us)
Async XLA Ops:
  0.6 9.0 %copy-start.1 = (bf16[1,2,768,128]{3,2,1,0:T(8,128)(2,1)S(1)}, bf16[1,2,768,128]{3,2,1,0:T(8,128)(2,1)}, u32[]{:S(2)}) copy-start(bf16[1,2,768,128]{3,2,1,0:T(8,128)(2,1)} %param.11) | copy-start | bytes 1179652
  0.6 9.0 %copy-start.5 = (bf16[1,2,768,128]{3,2,1,0:T(8,128)(2,1)S(1)}, bf16[1,2,768,128]{3,2,1,0:T(8,128)(2,1)}, u32[]{:S(2)}) copy-start(bf16[1,2,768,128]{3,2,1,0:T(8,128)(2,1)} %param.10) | copy-start | bytes 1179652
  0.7 8.9 %copy-start.9 = (bf16[92,6,384]{2,0,1:T(8,128)(2,1)S(1)}, bf16[92,6,384]{2,0,1:T(8,128)(2,1)}, u32[]{:S(2)}) copy-start(bf16[92,6,384]{2,0,1:T(8,128)(2,1)} %param.15) | copy-start | bytes 1271812
  0.7 9.0 %copy-start.4 = (s32[4]{0:T(128)S(1)}, s32[4]{0:T(128)}, u32[]{:S(2)}) copy-start(s32[4]{0:T(128)} %rows_ref.7) | copy-start | bytes 52
  0.7 9.0 %copy-start.3 = (bf16[9,128]{1,0:T(8,128)(2,1)S(1)}, bf16[9,128]{1,0:T(8,128)(2,1)}, u32[]{:S(2)}) copy-start(bf16[9,128]{1,0:T(8,128)(2,1)} %taps_ref.3) | copy-start | bytes 6916
  0.7 9.0 %copy-start.2 = (s32[6,9]{1,0:T(8,128)S(1)}, s32[6,9]{1,0:T(8,128)}, u32[]{:S(2)}) copy-start(s32[6,9]{1,0:T(8,128)} %shift_ref.3) | copy-start | bytes 652
  0.7 9.0 %copy-start.6 = (bf16[2,384,128]{2,1,0:T(8,128)(2,1)S(1)}, bf16[2,384,128]{2,1,0:T(8,128)(2,1)}, u32[]{:S(2)}) copy-start(bf16[2,384,128]{2,1,0:T(8,128)(2,1)} %filter_ref.1) | copy-start | bytes 589828
  3.8 22.3 %copy-start.7 = (f32[6]{0:T(128)S(1)}, f32[6]{0:T(128)}, u32[]{:S(2)}) copy-start(f32[6]{0:T(128)} %quad_ref.1) | copy-start | bytes 76
  3.8 22.3 %copy-start.8 = (bf16[736,128]{1,0:T(8,128)(2,1)S(1)}, bf16[736,128]{1,0:T(8,128)(2,1)}, u32[]{:S(2)}) copy-start(bf16[736,128]{1,0:T(8,128)(2,1)} %get-tuple-element.52.refs_0_) | copy-start | bytes 565252
  3.8 11.2 %collective-permute-start = (bf16[736,128]{1,0:T(8,128)(2,1)}, bf16[736,128]{1,0:T(8,128)(2,1)S(1)}, u32[]{:S(2)}, u32[]{:S(2)}) collective-permute-start(bf16[736,128]{1,0:T(8,128)(2,1)} %get-tuple-element.44), channel_id=1, source_target_pairs={{0,12},{4,8},{8,4},{12,0},{1,13},{5,9},{9,5},{13,1},{2,14},{6,10},... | collective-permute-start | bytes 565256 | tf_op jit(solution)/shard_map/ppermute | solution.py:443
  8.9 11.2 %collective-permute-start.3 = (bf16[736,128]{1,0:T(8,128)(2,1)}, bf16[736,128]{1,0:T(8,128)(2,1)S(1)}, u32[]{:S(2)}, u32[]{:S(2)}) collective-permute-start(bf16[736,128]{1,0:T(8,128)(2,1)} %get-tuple-element.53), channel_id=1, source_target_pairs={{0,4},{4,0},{8,12},{12,8},{1,5},{5,1},{9,13},{13,9},{2,6},{6,2},{1... | collective-permute-start | bytes 565256 | tf_op jit(solution)/shard_map/ppermute | solution.py:443
  8.9 17.2 %collective-permute-start.4 = (bf16[736,128]{1,0:T(8,128)(2,1)}, bf16[736,128]{1,0:T(8,128)(2,1)S(1)}, u32[]{:S(2)}, u32[]{:S(2)}) collective-permute-start(bf16[736,128]{1,0:T(8,128)(2,1)} %get-tuple-element.54), channel_id=1, source_target_pairs={{0,8},{4,12},{8,0},{12,4},{1,9},{5,13},{9,1},{13,5},{2,10},{6,14},... | collective-permute-start | bytes 565256 | tf_op jit(solution)/shard_map/ppermute | solution.py:443
  15.0 15.9 %collective-permute-start.1 = (bf16[2,768,128]{2,1,0:T(8,128)(2,1)S(1)}, bf16[2,768,128]{2,1,0:T(8,128)(2,1)S(1)}, u32[]{:S(2)}, u32[]{:S(2)}) collective-permute-start(bf16[2,768,128]{2,1,0:T(8,128)(2,1)S(1)} %get-tuple-element.45), channel_id=1, source_target_pairs={{0,4},{4,0},{8,12},{12,8},{1,5},{5,1},{9,13},{13,9},{2,6},{6,2},{1... | collective-permute-start | bytes 1179656 | tf_op jit(solution)/shard_map/ppermute | solution.py:443
  19.4 11.5 %collective-permute-start.2 = (bf16[2,768,128]{2,1,0:T(8,128)(2,1)S(1)}, bf16[2,768,128]{2,1,0:T(8,128)(2,1)S(1)}, u32[]{:S(2)}, u32[]{:S(2)}) collective-permute-start(bf16[2,768,128]{2,1,0:T(8,128)(2,1)S(1)} %get-tuple-element.46), channel_id=1, source_target_pairs={{4,8},{8,4},{5,9},{9,5},{6,10},{10,6},{7,11},{11,7},{20,24},{24,20... | collective-permute-start | bytes 1179656 | tf_op jit(solution)/shard_map/ppermute | solution.py:510
  29.1 25.3 %copy-start = (bf16[768,736]{1,0:T(8,128)(2,1)S(1)}, bf16[768,736]{1,0:T(8,128)(2,1)}, u32[]{:S(2)}) copy-start(bf16[768,736]{1,0:T(8,128)(2,1)} %constant.8.clone.table_ref) | copy-start | bytes 3391492
  29.1 4.7 %collective-permute-start.5 = (bf16[384,128]{1,0:T(8,128)(2,1)S(1)}, bf16[384,128]{1,0:T(8,128)(2,1)S(1)}, u32[]{:S(2)}, u32[]{:S(2)}) collective-permute-start(bf16[384,128]{1,0:T(8,128)(2,1)S(1)} %get-tuple-element.61), channel_id=1, source_target_pairs={{0,4},{4,0},{8,12},{12,8},{1,5},{5,1},{9,13},{13,9},{2,6},{6,2},{1... | collective-permute-start | bytes 294920 | tf_op jit(solution)/shard_map/ppermute | solution.py:443
  33.9 8.6 %collective-permute-start.9 = (bf16[416,128]{1,0:T(8,128)(2,1)S(1)}, bf16[416,128]{1,0:T(8,128)(2,1)S(1)}, u32[]{:S(2)}, u32[]{:S(2)}) collective-permute-start(bf16[416,128]{1,0:T(8,128)(2,1)S(1)} %shard_map.133.own_ref), channel_id=1, source_target_pairs={{0,8},{4,12},{8,0},{12,4},{1,9},{5,13},{9,1},{13,5},{2,10},{6,14},... | collective-permute-start | bytes 319496 | tf_op jit(solution)/shard_map/ppermute | solution.py:443
  36.7 10.7 %collective-permute-start.6 = (bf16[736,128]{1,0:T(8,128)(2,1)S(1)}, bf16[736,128]{1,0:T(8,128)(2,1)S(1)}, u32[]{:S(2)}, u32[]{:S(2)}) collective-permute-start(bf16[736,128]{1,0:T(8,128)(2,1)S(1)} %get-tuple-element.66), channel_id=1, source_target_pairs={{0,4},{4,0},{8,12},{12,8},{1,5},{5,1},{9,13},{13,9},{2,6},{6,2},{1... | collective-permute-start | bytes 565256 | tf_op jit(solution)/shard_map/ppermute | solution.py:443
  37.1 17.4 %collective-permute-start.7 = (bf16[736,128]{1,0:T(8,128)(2,1)S(1)}, bf16[736,128]{1,0:T(8,128)(2,1)S(1)}, u32[]{:S(2)}, u32[]{:S(2)}) collective-permute-start(bf16[736,128]{1,0:T(8,128)(2,1)S(1)} %get-tuple-element.67), channel_id=1, source_target_pairs={{0,8},{4,12},{8,0},{12,4},{1,9},{5,13},{9,1},{13,5},{2,10},{6,14},... | collective-permute-start | bytes 565256 | tf_op jit(solution)/shard_map/ppermute | solution.py:443
  38.7 15.8 %collective-permute-start.8 = (bf16[736,128]{1,0:T(8,128)(2,1)S(1)}, bf16[736,128]{1,0:T(8,128)(2,1)S(1)}, u32[]{:S(2)}, u32[]{:S(2)}) collective-permute-start(bf16[736,128]{1,0:T(8,128)(2,1)S(1)} %get-tuple-element.68), channel_id=1, source_target_pairs={{0,12},{4,8},{8,4},{12,0},{1,13},{5,9},{9,5},{13,1},{2,14},{6,10},... | collective-permute-start | bytes 565256 | tf_op jit(solution)/shard_map/ppermute | solution.py:443
  42.5 4.8 %collective-permute-start.10 = (bf16[416,128]{1,0:T(8,128)(2,1)S(1)}, bf16[416,128]{1,0:T(8,128)(2,1)S(1)}, u32[]{:S(2)}, u32[]{:S(2)}) collective-permute-start(bf16[416,128]{1,0:T(8,128)(2,1)S(1)} %shard_map.135.own_ref), channel_id=1, source_target_pairs={{0,2},{2,0},{1,3},{3,1},{4,6},{6,4},{5,7},{7,5},{8,10},{10,8},{9,1... | collective-permute-start | bytes 319496 | tf_op jit(solution)/shard_map/ppermute | solution.py:443
  47.3 9.7 %collective-permute-start.11 = (bf16[416,128]{1,0:T(8,128)(2,1)S(1)}, bf16[416,128]{1,0:T(8,128)(2,1)S(1)}, u32[]{:S(2)}, u32[]{:S(2)}) collective-permute-start(bf16[416,128]{1,0:T(8,128)(2,1)S(1)} %shard_map.136.own_ref), channel_id=1, source_target_pairs={{0,4},{4,0},{8,12},{12,8},{1,5},{5,1},{9,13},{13,9},{2,6},{6,2},{1... | collective-permute-start | bytes 319496 | tf_op jit(solution)/shard_map/ppermute | solution.py:443

commit v4 on v3

--- a/solution.py
+++ b/solution.py
@@ -57,12 +57,12 @@
     return total
 
 
-def call(kernel, out_shape, in_specs, args, scratch=(), limit=32, flops=0, moved=1024):
+def call(kernel, out_shape, in_specs, args, scratch=(), limit=32, flops=0, moved=1024, out_specs=None):
     return pl.pallas_call(
         kernel,
         out_shape=out_shape,
         in_specs=in_specs,
-        out_specs=jax.tree.map(lambda _: VMEM, out_shape),
+        out_specs=out_specs or jax.tree.map(lambda _: VMEM, out_shape),
         scratch_shapes=list(scratch),
         compiler_params=pltpu.CompilerParams(vmem_limit_bytes=limit * 1024 * 1024),
         cost_estimate=pl.CostEstimate(flops=flops, bytes_accessed=moved, transcendentals=0),
@@ -84,7 +84,7 @@
 
 def forward_kernel(blocks, x_hbm, dy_hbm, table_hbm, *refs):
     outs, (x_ref, dy_ref, table_ref, act_ref, sems) = refs[:blocks], refs[blocks:]
-    slots, _, chans = x_ref.shape
+    slots = x_ref.shape[0]
     me = lax.axis_index("space")
     loads = [
         pltpu.make_async_copy(source, target, sems.at[i])
@@ -104,8 +104,7 @@
     for shift in range(blocks):
         block = jnp.bitwise_xor(me, shift)
         sums = jnp.dot(table_ref[block], source, preferred_element_type=F32)
-        columns = [sums[:, at * chans : (at + 1) * chans] for at in range(2 * slots)]
-        outs[shift][...] = jnp.concatenate(columns, axis=0).astype(BF16)
+        outs[shift][...] = sums.astype(BF16)
 
 
 def wrapped(target, row, value):
@@ -171,7 +170,6 @@
     padded_modes, chans = coeff.shape[2:]
     me = lax.axis_index("space")
     pairs = lat_pairs(lat_count)
-    depth = wide.shape[1] // (2 * slots)
     padding = padded_modes - local_modes
     if padding > 0:
         zeros = jnp.zeros((padding, chans), F32)
@@ -180,9 +178,9 @@
                 coeff[lat, part, local_modes:, :] = zeros
                 grad[lat, part, local_modes:, :] = zeros
 
-    def rows_at(field, slot, part):
-        at = (field * slots + slot) * depth + part * local_modes
-        return slice(at, at + local_modes)
+    def place(field, slot, part):
+        rows = slice(part * local_modes, (part + 1) * local_modes)
+        return rows, slice((field * slots + slot) * chans, (field * slots + slot + 1) * chans)
 
     for shift in range(blocks):
         block = jnp.bitwise_xor(me, shift)
@@ -195,9 +193,9 @@
             def _():
                 weight = quad_ref[lat]
                 for part in range(2):
-                    grad[lat, part, :local_modes, :] = wide[shift, rows_at(0, slot, part), :]
+                    grad[lat, part, :local_modes, :] = wide[(shift, *place(0, slot, part))]
                     coeff[lat, part, :local_modes, :] = (
-                        wide[shift, rows_at(1, slot, part), :] * weight
+                        wide[(shift, *place(1, slot, part))] * weight
                     )
 
     def mix(i, carry):
@@ -248,8 +246,8 @@
         for slot in range(slots):
             lat = jnp.minimum(start + slot, lat_count - 1)
             for part in range(2):
-                wide[shift, rows_at(0, slot, part), :] = synth[lat, part, :local_modes, :]
-                wide[shift, rows_at(1, slot, part), :] = grad_coeff[lat, part, :local_modes, :]
+                wide[(shift, *place(0, slot, part))] = synth[lat, part, :local_modes, :]
+                wide[(shift, *place(1, slot, part))] = grad_coeff[lat, part, :local_modes, :]
         outs[shift][...] = wide[shift].astype(BF16)
 
 
@@ -328,7 +326,7 @@
         wrapped(acts, row, source[0].astype(F32))
         wrapped(grads, row, source[1].astype(F32))
     weights = taps_ref[...].astype(F32)
-    step = 32 if lon_count % 32 == 0 else lon_count
+    step = 128 if lon_count % 128 == 0 else lon_count
     top = shift_ref.shape[0] - 1
     lines = [jnp.zeros((1, chans), F32)] * tap_ref.shape[0]
     for side in range(2):
@@ -390,52 +388,98 @@
     split_taps(tap_ref[...], out_ref, kept_ref.shape[0])
 
 
-def add_kernel(scale, tap_scale, own_ref, other_ref, out_ref):
+def add_kernel(own_ref, other_ref, out_ref, *cut_refs):
     count = own_ref.shape[0] - 2 * TAP_ROWS
-    out_ref[:count, :] = (added(own_ref, other_ref)[:count, :] / scale).astype(BF16)
-    split_taps((joined_taps(own_ref) + joined_taps(other_ref)) / tap_scale, out_ref, count)
-
-
-def spread_kernel(own_ref, other_ref, filter_ref, tap_ref):
+    out_ref[:count, :] = added(own_ref, other_ref)[:count, :].astype(BF16)
+    split_taps(joined_taps(own_ref) + joined_taps(other_ref), out_ref, count)
+    for at, cut_ref in enumerate(cut_refs):
+        rows = cut_ref.shape[0]
+        cut_ref[...] = out_ref[at * rows : (at + 1) * rows, :]
+
+
+def member_kernel(scale, tap_scale, own_ref, head_ref, tail_ref, out_ref, *cut_refs):
+    count, head = own_ref.shape[0] - 2 * TAP_ROWS, head_ref.shape[0]
+    out_ref[:head, :] = (
+        (own_ref[:head, :].astype(F32) + head_ref[...].astype(F32)) / scale
+    ).astype(BF16)
+    tail = own_ref[head:, :].astype(F32) + tail_ref[...].astype(F32)
+    out_ref[head:count, :] = (tail[: count - head, :] / scale).astype(BF16)
+    taps = joined_taps(own_ref) + joined_taps(tail_ref)
+    split_taps(taps / tap_scale, out_ref, count)
+    for at, cut_ref in enumerate(cut_refs):
+        rows = cut_ref.shape[0]
+        cut_ref[...] = out_ref[at * rows : (at + 1) * rows, :]
+
+
+def early_kernel(
+    rows_ref, table_ref, base_ref, slope_ref, base_grad_ref, rim_ref, rim_grad_ref,
+    own_ref, near_ref, sum_ref, grad_ref,
+):
+    slots, lon_count, chans = base_ref.shape
+    me = lax.axis_index("space")
+    live = rows_ref[me]
+    step = lon_count // 4
+    for at in range(0, lon_count, step):
+        rows = slice(at, at + step)
+        sums = jnp.dot(table_ref[me, rows, :], own_ref[...], preferred_element_type=F32)
+        sums = sums + jnp.dot(
+            table_ref[jnp.bitwise_xor(me, 1), rows, :], near_ref[...], preferred_element_type=F32
+        )
+        for slot in range(slots):
+            out = base_ref[slot, rows, :] + sums[:, slot * chans : (slot + 1) * chans]
+            back = sums[:, (slots + slot) * chans : (slots + slot + 1) * chans]
+            if slot == 0:
+                out = out + rim_ref[0, rows, :]
+                back = back + rim_grad_ref[0, rows, :]
+            last = slot == live - 1
+            out = out + jnp.where(last, rim_ref[1, rows, :], 0.0)
+            back = back + jnp.where(last, rim_grad_ref[1, rows, :], 0.0)
+            sum_ref[slot, rows, :] = out
+            grad_ref[slot, rows, :] = base_grad_ref[slot, rows, :] + back * slope_ref[slot, rows, :]
+
+
+def finish_kernel(
+    blocks, rows_ref, table_ref, sum_ref, early_ref, slope_ref, own_ref, other_ref, *refs
+):
+    ins, outs, scratch = refs[: blocks - 2], refs[blocks - 2 : blocks + 2], refs[blocks + 2 :]
+    out_hbm, grad_hbm, filter_hbm, tap_ref = outs
+    out_ref, grad_ref, filter_ref, sems = scratch
+    slots, lon_count, chans = sum_ref.shape
+    me = lax.axis_index("space")
+    live = rows_ref[me]
     half = filter_ref.shape[1] // 2
-    upper = jnp.bitwise_and(lax.axis_index("space"), 1)
+    upper = jnp.bitwise_and(me, 1)
     for ref, which in ((own_ref, upper), (other_ref, 1 - upper)):
         at = pl.ds(pl.multiple_of(which * half, half), half)
         rows = ref[: 2 * half, :].astype(F32)
         filter_ref[0, at, :] = rows[:half, :]
         filter_ref[1, at, :] = rows[half:, :]
     tap_ref[...] = (joined_taps(own_ref) + joined_taps(other_ref))[: tap_ref.shape[0], :]
-
-
-def finish_kernel(
-    blocks, rows_ref, table_ref, base_ref, slope_ref, base_grad_ref, rim_ref, rim_grad_ref, *refs
-):
-    ins, out_ref, grad_ref, source = refs[:blocks], refs[blocks], refs[blocks + 1], refs[blocks + 2]
-    slots, lon_count, chans = base_ref.shape
-    me = lax.axis_index("space")
-    live = rows_ref[me]
-    depth = source.shape[0] // blocks
-    for shift in range(blocks):
-        block = jnp.bitwise_xor(me, shift)
-        rows = pl.ds(pl.multiple_of(block * depth, 8), depth)
-        part = ins[shift][...].astype(F32)
-        for at in range(2 * slots):
-            source[rows, at * chans : (at + 1) * chans] = part[at * depth : (at + 1) * depth, :]
-    sums = jnp.dot(table_ref[...], source[...].astype(BF16), preferred_element_type=F32)
-    for slot in range(slots):
-        at = slot * chans
-        out = base_ref[slot] + sums[:, at : at + chans]
-        at = (slots + slot) * chans
-        back = sums[:, at : at + chans]
-        if slot == 0:
-            out = out + rim_ref[0]
-            back = back + rim_grad_ref[0]
-        out = out + jnp.where(slot == live - 1, rim_ref[1], 0.0)
-        back = back + jnp.where(slot == live - 1, rim_grad_ref[1], 0.0)
-        grad = base_grad_ref[slot] + back * slope_ref[slot]
-        alive = slot < live
-        out_ref[slot] = jnp.where(alive, out, 0.0).astype(BF16)
-        grad_ref[slot] = jnp.where(alive, grad, 0.0).astype(BF16)
+    stores = [pltpu.make_async_copy(filter_ref, filter_hbm, sems.at[0])]
+    stores[0].start()
+    parts = sems.shape[0] // (2 * slots)
+    step = lon_count // parts
+    for part in range(parts):
+        rows = slice(part * step, (part + 1) * step)
+        sums = jnp.zeros((step, 2 * slots * chans), F32)
+        for at, ref in enumerate(ins):
+            block = jnp.bitwise_xor(me, at + 2)
+            sums = sums + jnp.dot(table_ref[block, rows, :], ref[...], preferred_element_type=F32)
+        for slot in range(slots):
+            out = sum_ref[slot, rows, :] + sums[:, slot * chans : (slot + 1) * chans]
+            back = sums[:, (slots + slot) * chans : (slots + slot + 1) * chans]
+            grad = early_ref[slot, rows, :] + back * slope_ref[slot, rows, :]
+            alive = slot < live
+            out_ref[slot, rows, :] = jnp.where(alive, out, 0.0).astype(BF16)
+            grad_ref[slot, rows, :] = jnp.where(alive, grad, 0.0).astype(BF16)
+            for made, target in ((out_ref, out_hbm), (grad_ref, grad_hbm)):
+                place = (slot, pl.ds(part * step, step))
+                stores.append(
+                    pltpu.make_async_copy(made.at[place], target.at[place], sems.at[len(stores)])
+                )
+                stores[-1].start()
+    for store in stores:
+        store.wait()
 
 
 def crossed(values, distance, axis="space"):
@@ -463,10 +507,10 @@
     shape = jax.ShapeDtypeStruct
     table = fourier_table(lon_count, blocks, local_modes, depth)
     table_in = jnp.asarray(table)
-    table_out = jnp.asarray(np.ascontiguousarray(table.reshape(blocks * depth, lon_count).T))
+    table_out = jnp.asarray(np.ascontiguousarray(table.transpose(0, 2, 1)))
     x, dy = fields[0], cotangent[0]
     field = shape((slots, lon_count, chans), F32)
-    coded = shape((2 * slots * depth, chans), BF16)
+    coded = shape((depth, 2 * slots * chans), BF16)
     rim = shape((2, lon_count, chans), BF16)
 
     coded_parts = call(
@@ -534,32 +578,45 @@
     own = call(half_kernel, message, [VMEM] * 3, (keep, got_sum, tap_part))
     back_parts, own = lax.optimization_barrier((back_parts, own))
     returned = [back_parts[0], *reversed(crossed_all(back_parts, far).values())]
+    cut = shape((message.shape[0] // 2, chans), BF16)
     for bit in range(1, blocks.bit_length() - 1):
-        own = call(
-            functools.partial(add_kernel, 1, 1), message, [VMEM] * 2, (own, crossed(own, 1 << bit))
+        own, *cuts = call(
+            add_kernel, [message, cut, cut], [VMEM] * 2, (own, crossed(own, 1 << bit))
         )
     for bit in range(members.bit_length() - 1):
-        scales = (members, members * lat_count) if bit == 0 else (1, 1)
-        own = call(
-            functools.partial(add_kernel, *scales),
-            message,
-            [VMEM] * 2,
-            (own, crossed(own, 1 << bit, "ens")),
-            flops=0,
+        last = bit == members.bit_length() - 2
+        scales = (members, members * lat_count) if last else (1, 1)
+        own, *cuts = call(
+            functools.partial(member_kernel, *scales),
+            [message] if last else [message, cut, cut],
+            [VMEM] * 3,
+            (own, *[crossed(part, 1 << bit, "ens") for part in cuts]),
+            flops=300000000,
         )
-    filter_grad, tap_grad = call(
-        spread_kernel,
-        [shape((2, degrees, chans), F32), shape((tap_weight.shape[0], chans), F32)],
-        [VMEM] * 2,
-        (own, crossed(own, 1)),
-    )
-    output, input_grad = call(
+    early_sum, early_grad = call(
+        early_kernel,
+        [field, field],
+        [SMEM] + [VMEM] * 8,
+        (band_rows, table_out, base, slope, base_grad, rim_sum, rim_grad, *returned[:2]),
+    )
+    pieces = 4
+    output, input_grad, filter_grad, tap_grad = call(
         functools.partial(finish_kernel, blocks),
-        [shape(x.shape, BF16)] * 2,
-        [SMEM] + [VMEM] * (6 + blocks),
-        (band_rows, table_out, base, slope, base_grad, rim_sum, rim_grad, *returned),
-        scratch=[pltpu.VMEM((blocks * depth, 2 * slots * chans), F32)],
+        [shape(x.shape, BF16)] * 2
+        + [shape((2, degrees, chans), F32), shape((tap_weight.shape[0], chans), F32)],
+        [SMEM] + [VMEM] * (4 + blocks),
+        (
+            band_rows, table_out, early_sum, early_grad, slope,
+            own, crossed(own, 1), *returned[2:],
+        ),
+        scratch=[
+            pltpu.VMEM(x.shape, BF16),
+            pltpu.VMEM(x.shape, BF16),
+            pltpu.VMEM((2, degrees, chans), F32),
+            pltpu.SemaphoreType.DMA((1 + 2 * slots * pieces,)),
+        ],
         flops=2 * blocks * depth * lon_count * 2 * slots * chans,
+        out_specs=[HBM, HBM, HBM, VMEM],
     )
     return (output[None], input_grad[None], filter_grad, tap_grad)
 

time: 58.4 us -> 57.5 us (0.985)
  waiting for transfers between devices: 20.6 us -> 19.6 us
    ppermute x11 -> x12, waiting for transfers between devices: 20.6 us -> 19.6 us  [crossed(): return lax.ppermute(values, axis, [(i, i ^ distance) for i in range(count)])]
    ppermute x11 -> x12, starting transfers between devices: 19.3 us -> 19.6 us  [crossed(): return lax.ppermute(values, axis, [(i, i ^ distance) for i in range(count)])]
  transfers between devices with their start and end apart: 12 -> 13, of which waited for: 6 -> 8; matrix products, arithmetic and copies ran while one was open for 0% -> 0% of each run, Pallas kernels for 21% -> 19%
where the time goes in v4:
time: 57.5 us; the launch traced here: 57.3 us
  starting transfers between devices  20.2 us (35%)
  waiting for transfers between devices  19.6 us (34%)
  Pallas kernels  16.4 us (29%)
  between operations  0.84 us (1%)
    ppermute x12, waiting for transfers between devices, crossed(): return lax.ppermute(values, axis, [(i, i ^ distance) for i in range(count)])  19.6 us
    ppermute x12, starting transfers between devices, crossed(): return lax.ppermute(values, axis, [(i, i ^ distance) for i in range(count)])  19.6 us
    pallas_call x9, Pallas kernels, call(): pl.pallas_call(kernel, out_shape=out_shape, in_specs=in_specs, out_specs=...  16.4 us
  transfers between devices with their start and end apart: 13, of which 8 were waited for; matrix products, arithmetic and copies ran while one was open for 0% of the time, Pallas kernels for 19%

profile of v4, /device:TPU:0, one launch (start us, length us, event | category | flops | bytes accessed | tf_op | source)
XLA Modules:
  0.0 57.3 jit_solution(13311895378464603446)
XLA Ops:
  0.6 0.0 copy-start.1
  0.6 0.0 copy-start.5
  0.7 0.0 copy-start.9
  0.7 0.0 copy-start.2
  0.7 0.0 copy-start.4
  0.7 0.0 copy-start.3
  0.7 0.0 copy-start.6
  0.7 3.1 %shard_map.130 = (bf16[184,512]{1,0:T(8,128)(2,1)}, bf16[184,512]{1,0:T(8,128)(2,1)}, bf16[184,512]{1,0:T(8,128)(2,1)}, bf16[184,512]{1,0:T(8,128)(2,1)}) custom-call(bf16[2,768,128]{2,1,0:T(8,128)(2,1)} %bitcast.8, bf16[2,768,128]{2,1,0:T(8,128)(2,1)} %bitcast.5, bf16[4,184,768]{2,1,0:T(8,128)(2,1)} %constant.7.clone.table_hbm), custom_call_target="tpu_custom_call" | custom-call | flops 578813952 | bytes 1024 | tf_op jit(solution)/shard_map/pallas_call | solution.py:61
  3.8 0.0 copy-start.7
  3.8 0.0 copy-start.8
  3.8 5.1 %collective-permute-start = (bf16[184,512]{1,0:T(8,128)(2,1)}, bf16[184,512]{1,0:T(8,128)(2,1)S(1)}, u32[]{:S(2)}, u32[]{:S(2)}) collective-permute-start(bf16[184,512]{1,0:T(8,128)(2,1)} %get-tuple-element.49), channel_id=1, source_target_pairs={{0,12},{4,8},{8,4},{12,0},{1,13},{5,9},{9,5},{13,1},{2,14},{6,10},... | collective-permute-start | bytes 565256 | tf_op jit(solution)/shard_map/ppermute | solution.py:487
  8.9 0.0 collective-permute-start.3
  9.0 0.6 %collective-permute-start.4 = (bf16[184,512]{1,0:T(8,128)(2,1)}, bf16[184,512]{1,0:T(8,128)(2,1)S(1)}, u32[]{:S(2)}, u32[]{:S(2)}) collective-permute-start(bf16[184,512]{1,0:T(8,128)(2,1)} %get-tuple-element.59), channel_id=1, source_target_pairs={{0,8},{4,12},{8,0},{12,4},{1,9},{5,13},{9,1},{13,5},{2,10},{6,14},... | collective-permute-start | bytes 565256 | tf_op jit(solution)/shard_map/ppermute | solution.py:487
  9.6 0.0 copy-done.9
  9.6 0.0 copy-done.1
  9.7 0.0 copy-done.5
  9.7 0.0 copy-done.2
  9.7 0.0 copy-done.4
  9.7 0.0 copy-done.3
  9.7 0.0 copy-done.6
  9.7 5.3 %shard_map.129 = (f32[2048,256]{1,0:T(8,128)S(1)}, bf16[384,2048]{1,0:T(8,128)(2,1)S(1)}, bf16[2,768,128]{2,1,0:T(8,128)(2,1)S(1)}, bf16[2,768,128]{2,1,0:T(8,12...) custom-call(s32[4]{0:T(128)S(1)} %copy-done.2, ...), custom_call_target="tpu_custom_call" | custom-call | flops 402653184 | bytes 2097152 | tf_op jit(solution)/shard_map/pallas_call | solution.py:61
  15.0 0.0 collective-permute-done.refs_3_
  15.0 4.5 %collective-permute-start.1 = (bf16[2,768,128]{2,1,0:T(8,128)(2,1)S(1)}, bf16[2,768,128]{2,1,0:T(8,128)(2,1)S(1)}, u32[]{:S(2)}, u32[]{:S(2)}) collective-permute-start(bf16[2,768,128]{2,1,0:T(8,128)(2,1)S(1)} %get-tuple-element.50), channel_id=1, source_target_pairs={{0,4},{4,0},{8,12},{12,8},{1,5},{5,1},{9,13},{13,9},{2,6},{6,2},{1... | collective-permute-start | bytes 1179656 | tf_op jit(solution)/shard_map/ppermute | solution.py:487
  19.4 0.7 %collective-permute-start.2 = (bf16[2,768,128]{2,1,0:T(8,128)(2,1)S(1)}, bf16[2,768,128]{2,1,0:T(8,128)(2,1)S(1)}, u32[]{:S(2)}, u32[]{:S(2)}) collective-permute-start(bf16[2,768,128]{2,1,0:T(8,128)(2,1)S(1)} %get-tuple-element.51), channel_id=1, source_target_pairs={{4,8},{8,4},{5,9},{9,5},{6,10},{10,6},{7,11},{11,7},{20,24},{24,20... | collective-permute-start | bytes 1179656 | tf_op jit(solution)/shard_map/ppermute | solution.py:554
  20.1 0.0 collective-permute-done.3.refs_1_
  20.1 6.0 %collective-permute-done.4.refs_2_ = bf16[184,512]{1,0:T(8,128)(2,1)S(1)} collective-permute-done((bf16[184,512]{1,0:T(8,128)(2,1)}, bf16[184,512]{1,0:T(8,128)(2,1)S(1)}, u32[]{:S(2)}, u32[]{:S(2)}) %collective-permute-start.4) | collective-permute-done | bytes 188448 | tf_op jit(solution)/shard_map/ppermute | solution.py:487
  26.1 0.0 copy-done.7
  26.2 0.0 copy-done.8
  26.2 3.0 %shard_map.132 = (bf16[184,512]{1,0:T(8,128)(2,1)S(1)}, bf16[184,512]{1,0:T(8,128)(2,1)S(1)}, bf16[184,512]{1,0:T(8,128)(2,1)S(1)}, bf16[184,512]{1,0:T(8,128)(2...) custom-call(s32[4]{0:T(128)S(1)} %copy-done.2, f32[6]{0:T(128)S(1)} %copy-done.7, ...), custom_call_target="tpu_custom_call" | custom-call | flops 4026531840 | bytes 1024 | tf_op jit(solution)/shard_map/pallas_call | solution.py:61
  29.2 0.0 copy-start
  29.2 0.1 collective-permute-start.5
  29.2 1.6 %collective-permute-done.1.first_rim = bf16[2,768,128]{2,1,0:T(8,128)(2,1)S(1)} collective-permute-done((bf16[2,768,128]{2,1,0:T(8,128)(2,1)S(1)}, bf16[2,768,128]{2,1,0:T(8,128)(2,1)S(1)}, u32[]{:S(2)}, u32[]{:S(2)}) %collective-permute-start.1) | collective-permute-done | bytes 393248 | tf_op jit(solution)/shard_map/ppermute | solution.py:487
  30.9 0.0 collective-permute-done.2.second_rim
  30.9 1.3 %shard_map.131 = (f32[2,768,128]{2,1,0:T(8,128)S(1)}, f32[2,768,128]{2,1,0:T(8,128)S(1)}, f32[16,128]{1,0:T(8,128)S(1)}) custom-call(s32[4]{0:T(128)S(1)} %copy-done.2, s32[6,9]{1,0:T(8,128)S(1)} %copy-done.3, bf16[2,768,128]{2,1,0:T(8,128)(2,1)S(1)} %bitcast.7, bf16[2,768,128]{2,1,0:T(8,128)(2,1)S(1)} %collective-permute-done.1.first_rim, ...), custom_call_target="tpu_custom_call" | custom-call | bytes 1024 | tf_op jit(solution)/shard_map/pallas_call | solution.py:61
  32.2 1.7 %collective-permute-done.5.got_ref = bf16[384,128]{1,0:T(8,128)(2,1)S(1)} collective-permute-done((bf16[384,128]{1,0:T(8,128)(2,1)S(1)}, bf16[384,128]{1,0:T(8,128)(2,1)S(1)}, u32[]{:S(2)}, u32[]{:S(2)}) %collective-permute-start.5) | collective-permute-done | bytes 98336 | tf_op jit(solution)/shard_map/ppermute | solution.py:487
  33.9 2.6 %collective-permute-start.7 = (bf16[416,128]{1,0:T(8,128)(2,1)S(1)}, bf16[416,128]{1,0:T(8,128)(2,1)S(1)}, u32[]{:S(2)}, u32[]{:S(2)}) collective-permute-start(bf16[416,128]{1,0:T(8,128)(2,1)S(1)} %shard_map.133.own_ref), channel_id=1, source_target_pairs={{0,8},{4,12},{8,0},{12,4},{1,9},{5,13},{9,1},{13,5},{2,10},{6,14},... | collective-permute-start | bytes 319496 | tf_op jit(solution)/shard_map/ppermute | solution.py:487
  36.5 0.6 %collective-permute-start.6 = (bf16[184,512]{1,0:T(8,128)(2,1)S(1)}, bf16[184,512]{1,0:T(8,128)(2,1)S(1)}, u32[]{:S(2)}, u32[]{:S(2)}) collective-permute-start(bf16[184,512]{1,0:T(8,128)(2,1)S(1)} %get-tuple-element.71), channel_id=1, source_target_pairs={{0,4},{4,0},{8,12},{12,8},{1,5},{5,1},{9,13},{13,9},{2,6},{6,2},{1... | collective-permute-start | bytes 565256 | tf_op jit(solution)/shard_map/ppermute | solution.py:487
  37.1 1.4 %collective-permute-start.11 = (bf16[184,512]{1,0:T(8,128)(2,1)S(1)}, bf16[184,512]{1,0:T(8,128)(2,1)S(1)}, u32[]{:S(2)}, u32[]{:S(2)}) collective-permute-start(bf16[184,512]{1,0:T(8,128)(2,1)S(1)} %get-tuple-element.78), channel_id=1, source_target_pairs={{0,8},{4,12},{8,0},{12,4},{1,9},{5,13},{9,1},{13,5},{2,10},{6,14},... | collective-permute-start | bytes 565256 | tf_op jit(solution)/shard_map/ppermute | solution.py:487
  38.5 2.4 %collective-permute-start.12 = (bf16[184,512]{1,0:T(8,128)(2,1)S(1)}, bf16[184,512]{1,0:T(8,128)(2,1)S(1)}, u32[]{:S(2)}, u32[]{:S(2)}) collective-permute-start(bf16[184,512]{1,0:T(8,128)(2,1)S(1)} %get-tuple-element.79), channel_id=1, source_target_pairs={{0,12},{4,8},{8,4},{12,0},{1,13},{5,9},{9,5},{13,1},{2,14},{6,10},... | collective-permute-start | bytes 565256 | tf_op jit(solution)/shard_map/ppermute | solution.py:487
  40.9 1.4 %collective-permute-done.7.other_ref = bf16[416,128]{1,0:T(8,128)(2,1)S(1)} collective-permute-done((bf16[416,128]{1,0:T(8,128)(2,1)S(1)}, bf16[416,128]{1,0:T(8,128)(2,1)S(1)}, u32[]{:S(2)}, u32[]{:S(2)}) %collective-permute-start.7) | collective-permute-done | bytes 106528 | tf_op jit(solution)/shard_map/ppermute | solution.py:487
  42.4 1.5 %collective-permute-start.8 = (bf16[208,128]{1,0:T(8,128)(2,1)S(1)}, bf16[208,128]{1,0:T(8,128)(2,1)S(1)}, u32[]{:S(2)}, u32[]{:S(2)}) collective-permute-start(bf16[208,128]{1,0:T(8,128)(2,1)S(1)} %get-tuple-element.76), channel_id=1, source_target_pairs={{0,2},{2,0},{1,3},{3,1},{4,6},{6,4},{5,7},{7,5},{8,10},{10,8},{9,1... | collective-permute-start | bytes 159752 | tf_op jit(solution)/shard_map/ppermute | solution.py:487
  43.9 0.5 collective-permute-start.9
  44.5 2.1 %collective-permute-done.8.head_ref = bf16[208,128]{1,0:T(8,128)(2,1)S(1)} collective-permute-done((bf16[208,128]{1,0:T(8,128)(2,1)S(1)}, bf16[208,128]{1,0:T(8,128)(2,1)S(1)}, u32[]{:S(2)}, u32[]{:S(2)}) %collective-permute-start.8) | collective-permute-done | bytes 53280 | tf_op jit(solution)/shard_map/ppermute | solution.py:487
  46.6 1.5 %collective-permute-done.9.tail_ref = bf16[208,128]{1,0:T(8,128)(2,1)S(1)} collective-permute-done((bf16[208,128]{1,0:T(8,128)(2,1)S(1)}, bf16[208,128]{1,0:T(8,128)(2,1)S(1)}, u32[]{:S(2)}, u32[]{:S(2)}) %collective-permute-start.9) | collective-permute-done | bytes 53280 | tf_op jit(solution)/shard_map/ppermute | solution.py:487
  48.1 0.2 collective-permute-start.10
  48.2 0.0 collective-permute-done.6.near_ref
  48.2 0.0 copy-done
  48.2 1.1 %shard_map.134 = (f32[2,768,128]{2,1,0:T(8,128)S(1)}, f32[2,768,128]{2,1,0:T(8,128)S(1)}) custom-call(s32[4]{0:T(128)S(1)} %copy-done.2, bf16[4,768,184]{2,1,0:T(8,128)(2,1)S(1)} %copy-done, f32[2,768,128]{2,1,0:T(8,128)S(1)} %get-tuple-element.44.base_ref, f32[2,768,128]{2,1,0:T(8,128)S(1)} %get-tuple-element.45.slope_ref, ...), custom_call_target="tpu_custom_call" | custom-call | bytes 1024 | tf_op jit(solution)/shard_map/pallas_call | solution.py:61
  49.4 4.9 %collective-permute-done.11.refs_0_ = bf16[184,512]{1,0:T(8,128)(2,1)S(1)} collective-permute-done((bf16[184,512]{1,0:T(8,128)(2,1)S(1)}, bf16[184,512]{1,0:T(8,128)(2,1)S(1)}, u32[]{:S(2)}, u32[]{:S(2)}) %collective-permute-start.11) | collective-permute-done | bytes 188448 | tf_op jit(solution)/shard_map/ppermute | solution.py:487
  54.3 0.0 collective-permute-done.12.refs_1_
  54.3 0.4 collective-permute-done.10.other_ref
  54.7 2.5 %shard_map.137 = (bf16[2,768,128]{2,1,0:T(8,128)(2,1)}, bf16[2,768,128]{2,1,0:T(8,128)(2,1)}, f32[2,384,128]{2,1,0:T(8,128)}, f32[9,128]{1,0:T(8,128)}) custom-call(s32[4]{0:T(128)S(1)} %copy-done.2, bf16[4,768,184]{2,1,0:T(8,128)(2,1)S(1)} %copy-done, f32[2,768,128]{2,1,0:T(8,128)S(1)} %get-tuple-element.72.sum_ref, ...), custom_call_target="tpu_custom_call" | custom-call | flops 578813952 | bytes 1024 | tf_op jit(solution)/shard_map/pallas_call | solution.py:61
  (4 shorter events, 0.2 us)
Async XLA Ops:
  0.6 9.0 %copy-start.1 = (bf16[1,2,768,128]{3,2,1,0:T(8,128)(2,1)S(1)}, bf16[1,2,768,128]{3,2,1,0:T(8,128)(2,1)}, u32[]{:S(2)}) copy-start(bf16[1,2,768,128]{3,2,1,0:T(8,128)(2,1)} %param.11) | copy-start | bytes 1179652
  0.6 9.0 %copy-start.5 = (bf16[1,2,768,128]{3,2,1,0:T(8,128)(2,1)S(1)}, bf16[1,2,768,128]{3,2,1,0:T(8,128)(2,1)}, u32[]{:S(2)}) copy-start(bf16[1,2,768,128]{3,2,1,0:T(8,128)(2,1)} %param.10) | copy-start | bytes 1179652
  0.7 8.9 %copy-start.9 = (bf16[92,6,384]{2,0,1:T(8,128)(2,1)S(1)}, bf16[92,6,384]{2,0,1:T(8,128)(2,1)}, u32[]{:S(2)}) copy-start(bf16[92,6,384]{2,0,1:T(8,128)(2,1)} %param.15) | copy-start | bytes 1271812
  0.7 9.0 %copy-start.2 = (s32[4]{0:T(128)S(1)}, s32[4]{0:T(128)}, u32[]{:S(2)}) copy-start(s32[4]{0:T(128)} %rows_ref.9) | copy-start | bytes 52
  0.7 9.0 %copy-start.4 = (bf16[9,128]{1,0:T(8,128)(2,1)S(1)}, bf16[9,128]{1,0:T(8,128)(2,1)}, u32[]{:S(2)}) copy-start(bf16[9,128]{1,0:T(8,128)(2,1)} %taps_ref.3) | copy-start | bytes 6916
  0.7 9.0 %copy-start.3 = (s32[6,9]{1,0:T(8,128)S(1)}, s32[6,9]{1,0:T(8,128)}, u32[]{:S(2)}) copy-start(s32[6,9]{1,0:T(8,128)} %shift_ref.3) | copy-start | bytes 652
  0.7 9.0 %copy-start.6 = (bf16[2,384,128]{2,1,0:T(8,128)(2,1)S(1)}, bf16[2,384,128]{2,1,0:T(8,128)(2,1)}, u32[]{:S(2)}) copy-start(bf16[2,384,128]{2,1,0:T(8,128)(2,1)} %filter_ref.1) | copy-start | bytes 589828
  3.8 22.3 %copy-start.7 = (f32[6]{0:T(128)S(1)}, f32[6]{0:T(128)}, u32[]{:S(2)}) copy-start(f32[6]{0:T(128)} %quad_ref.1) | copy-start | bytes 76
  3.8 22.3 %copy-start.8 = (bf16[184,512]{1,0:T(8,128)(2,1)S(1)}, bf16[184,512]{1,0:T(8,128)(2,1)}, u32[]{:S(2)}) copy-start(bf16[184,512]{1,0:T(8,128)(2,1)} %get-tuple-element.57.refs_0_) | copy-start | bytes 565252
  3.8 11.1 %collective-permute-start = (bf16[184,512]{1,0:T(8,128)(2,1)}, bf16[184,512]{1,0:T(8,128)(2,1)S(1)}, u32[]{:S(2)}, u32[]{:S(2)}) collective-permute-start(bf16[184,512]{1,0:T(8,128)(2,1)} %get-tuple-element.49), channel_id=1, source_target_pairs={{0,12},{4,8},{8,4},{12,0},{1,13},{5,9},{9,5},{13,1},{2,14},{6,10},... | collective-permute-start | bytes 565256 | tf_op jit(solution)/shard_map/ppermute | solution.py:487
  8.9 11.2 %collective-permute-start.3 = (bf16[184,512]{1,0:T(8,128)(2,1)}, bf16[184,512]{1,0:T(8,128)(2,1)S(1)}, u32[]{:S(2)}, u32[]{:S(2)}) collective-permute-start(bf16[184,512]{1,0:T(8,128)(2,1)} %get-tuple-element.58), channel_id=1, source_target_pairs={{0,4},{4,0},{8,12},{12,8},{1,5},{5,1},{9,13},{13,9},{2,6},{6,2},{1... | collective-permute-start | bytes 565256 | tf_op jit(solution)/shard_map/ppermute | solution.py:487
  9.0 17.2 %collective-permute-start.4 = (bf16[184,512]{1,0:T(8,128)(2,1)}, bf16[184,512]{1,0:T(8,128)(2,1)S(1)}, u32[]{:S(2)}, u32[]{:S(2)}) collective-permute-start(bf16[184,512]{1,0:T(8,128)(2,1)} %get-tuple-element.59), channel_id=1, source_target_pairs={{0,8},{4,12},{8,0},{12,4},{1,9},{5,13},{9,1},{13,5},{2,10},{6,14},... | collective-permute-start | bytes 565256 | tf_op jit(solution)/shard_map/ppermute | solution.py:487
  15.0 15.9 %collective-permute-start.1 = (bf16[2,768,128]{2,1,0:T(8,128)(2,1)S(1)}, bf16[2,768,128]{2,1,0:T(8,128)(2,1)S(1)}, u32[]{:S(2)}, u32[]{:S(2)}) collective-permute-start(bf16[2,768,128]{2,1,0:T(8,128)(2,1)S(1)} %get-tuple-element.50), channel_id=1, source_target_pairs={{0,4},{4,0},{8,12},{12,8},{1,5},{5,1},{9,13},{13,9},{2,6},{6,2},{1... | collective-permute-start | bytes 1179656 | tf_op jit(solution)/shard_map/ppermute | solution.py:487
  19.4 11.4 %collective-permute-start.2 = (bf16[2,768,128]{2,1,0:T(8,128)(2,1)S(1)}, bf16[2,768,128]{2,1,0:T(8,128)(2,1)S(1)}, u32[]{:S(2)}, u32[]{:S(2)}) collective-permute-start(bf16[2,768,128]{2,1,0:T(8,128)(2,1)S(1)} %get-tuple-element.51), channel_id=1, source_target_pairs={{4,8},{8,4},{5,9},{9,5},{6,10},{10,6},{7,11},{11,7},{20,24},{24,20... | collective-permute-start | bytes 1179656 | tf_op jit(solution)/shard_map/ppermute | solution.py:554
  29.2 19.1 %copy-start = (bf16[4,768,184]{2,1,0:T(8,128)(2,1)S(1)}, bf16[4,768,184]{2,1,0:T(8,128)(2,1)}, u32[]{:S(2)}) copy-start(bf16[4,768,184]{2,1,0:T(8,128)(2,1)} %constant.8.clone.table_ref) | copy-start | bytes 3391492
  29.2 4.7 %collective-permute-start.5 = (bf16[384,128]{1,0:T(8,128)(2,1)S(1)}, bf16[384,128]{1,0:T(8,128)(2,1)S(1)}, u32[]{:S(2)}, u32[]{:S(2)}) collective-permute-start(bf16[384,128]{1,0:T(8,128)(2,1)S(1)} %get-tuple-element.66), channel_id=1, source_target_pairs={{0,4},{4,0},{8,12},{12,8},{1,5},{5,1},{9,13},{13,9},{2,6},{6,2},{1... | collective-permute-start | bytes 294920 | tf_op jit(solution)/shard_map/ppermute | solution.py:487
  33.9 8.4 %collective-permute-start.7 = (bf16[416,128]{1,0:T(8,128)(2,1)S(1)}, bf16[416,128]{1,0:T(8,128)(2,1)S(1)}, u32[]{:S(2)}, u32[]{:S(2)}) collective-permute-start(bf16[416,128]{1,0:T(8,128)(2,1)S(1)} %shard_map.133.own_ref), channel_id=1, source_target_pairs={{0,8},{4,12},{8,0},{12,4},{1,9},{5,13},{9,1},{13,5},{2,10},{6,14},... | collective-permute-start | bytes 319496 | tf_op jit(solution)/shard_map/ppermute | solution.py:487
  36.5 11.7 %collective-permute-start.6 = (bf16[184,512]{1,0:T(8,128)(2,1)S(1)}, bf16[184,512]{1,0:T(8,128)(2,1)S(1)}, u32[]{:S(2)}, u32[]{:S(2)}) collective-permute-start(bf16[184,512]{1,0:T(8,128)(2,1)S(1)} %get-tuple-element.71), channel_id=1, source_target_pairs={{0,4},{4,0},{8,12},{12,8},{1,5},{5,1},{9,13},{13,9},{2,6},{6,2},{1... | collective-permute-start | bytes 565256 | tf_op jit(solution)/shard_map/ppermute | solution.py:487
  37.1 17.2 %collective-permute-start.11 = (bf16[184,512]{1,0:T(8,128)(2,1)S(1)}, bf16[184,512]{1,0:T(8,128)(2,1)S(1)}, u32[]{:S(2)}, u32[]{:S(2)}) collective-permute-start(bf16[184,512]{1,0:T(8,128)(2,1)S(1)} %get-tuple-element.78), channel_id=1, source_target_pairs={{0,8},{4,12},{8,0},{12,4},{1,9},{5,13},{9,1},{13,5},{2,10},{6,14},... | collective-permute-start | bytes 565256 | tf_op jit(solution)/shard_map/ppermute | solution.py:487
  38.5 15.8 %collective-permute-start.12 = (bf16[184,512]{1,0:T(8,128)(2,1)S(1)}, bf16[184,512]{1,0:T(8,128)(2,1)S(1)}, u32[]{:S(2)}, u32[]{:S(2)}) collective-permute-start(bf16[184,512]{1,0:T(8,128)(2,1)S(1)} %get-tuple-element.79), channel_id=1, source_target_pairs={{0,12},{4,8},{8,4},{12,0},{1,13},{5,9},{9,5},{13,1},{2,14},{6,10},... | collective-permute-start | bytes 565256 | tf_op jit(solution)/shard_map/ppermute | solution.py:487
  42.4 4.2 %collective-permute-start.8 = (bf16[208,128]{1,0:T(8,128)(2,1)S(1)}, bf16[208,128]{1,0:T(8,128)(2,1)S(1)}, u32[]{:S(2)}, u32[]{:S(2)}) collective-permute-start(bf16[208,128]{1,0:T(8,128)(2,1)S(1)} %get-tuple-element.76), channel_id=1, source_target_pairs={{0,2},{2,0},{1,3},{3,1},{4,6},{6,4},{5,7},{7,5},{8,10},{10,8},{9,1... | collective-permute-start | bytes 159752 | tf_op jit(solution)/shard_map/ppermute | solution.py:487
  43.9 4.1 %collective-permute-start.9 = (bf16[208,128]{1,0:T(8,128)(2,1)S(1)}, bf16[208,128]{1,0:T(8,128)(2,1)S(1)}, u32[]{:S(2)}, u32[]{:S(2)}) collective-permute-start(bf16[208,128]{1,0:T(8,128)(2,1)S(1)} %get-tuple-element.77), channel_id=1, source_target_pairs={{0,2},{2,0},{1,3},{3,1},{4,6},{6,4},{5,7},{7,5},{8,10},{10,8},{9,1... | collective-permute-start | bytes 159752 | tf_op jit(solution)/shard_map/ppermute | solution.py:487
  48.1 6.6 %collective-permute-start.10 = (bf16[416,128]{1,0:T(8,128)(2,1)S(1)}, bf16[416,128]{1,0:T(8,128)(2,1)S(1)}, u32[]{:S(2)}, u32[]{:S(2)}) collective-permute-start(bf16[416,128]{1,0:T(8,128)(2,1)S(1)} %shard_map.136.own_ref), channel_id=1, source_target_pairs={{0,4},{4,0},{8,12},{12,8},{1,5},{5,1},{9,13},{13,9},{2,6},{6,2},{1... | collective-permute-start | bytes 319496 | tf_op jit(solution)/shard_map/ppermute | solution.py:487

commit v5 on v4

--- a/solution.py
+++ b/solution.py
@@ -164,9 +164,14 @@
     lax.fori_loop(0, pairs_ref.shape[0] // 128, turn, 0)
 
 
-def mix_kernel(blocks, slots, lat_count, local_modes, rows_ref, quad_ref, mixer_ref, back_ref, *refs):
-    ins, outs = refs[:blocks], refs[blocks : 2 * blocks]
-    keep_ref, send_ref, coeff, grad, synth, grad_coeff, products, gradient, wide = refs[2 * blocks :]
+def own_quarter():
+    space_bit = jnp.bitwise_and(lax.axis_index("space"), 1)
+    return 2 * space_bit + jnp.bitwise_and(lax.axis_index("ens"), 1)
+
+
+def gradient_kernel(blocks, slots, lat_count, local_modes, rows_ref, quad_ref, back_ref, *refs):
+    ins, sums, coeff, grad = refs[:blocks], refs[blocks : blocks + 4], *refs[blocks + 4 : blocks + 6]
+    products, gradient, wide = refs[blocks + 6 :]
     padded_modes, chans = coeff.shape[2:]
     me = lax.axis_index("space")
     pairs = lat_pairs(lat_count)
@@ -178,10 +183,6 @@
                 coeff[lat, part, local_modes:, :] = zeros
                 grad[lat, part, local_modes:, :] = zeros
 
-    def place(field, slot, part):
-        rows = slice(part * local_modes, (part + 1) * local_modes)
-        return rows, slice((field * slots + slot) * chans, (field * slots + slot + 1) * chans)
-
     for shift in range(blocks):
         block = jnp.bitwise_xor(me, shift)
         start = first_row_of(rows_ref, block, blocks)
@@ -193,33 +194,73 @@
             def _():
                 weight = quad_ref[lat]
                 for part in range(2):
-                    grad[lat, part, :local_modes, :] = wide[(shift, *place(0, slot, part))]
+                    grad[lat, part, :local_modes, :] = wide[(shift, *place(slots, local_modes, chans, 0, slot, part))]
                     coeff[lat, part, :local_modes, :] = (
-                        wide[(shift, *place(1, slot, part))] * weight
+                        wide[(shift, *place(slots, local_modes, chans, 1, slot, part))] * weight
                     )
+
+    def multiply(i, carry):
+        rows = pl.ds(pl.multiple_of(i * 8, 8), 8)
+        a0, a1, b0, b1 = loaded(coeff, grad, rows)
+        for index, (a, b) in enumerate(pairs):
+            at = pl.ds(pl.multiple_of(index * padded_modes + i * 8, 8), 8)
+            h0 = h1 = jnp.zeros((8, chans), F32)
+            for p, q in [(a, b)] if a == b else [(a, b), (b, a)]:
+                h0 = h0 + b0[p] * a0[q] + b1[p] * a1[q]
+                h1 = h1 + b1[p] * a0[q] - b0[p] * a1[q]
+            products[at, :chans] = h0
+            products[at, chans:] = h1
+        return carry
+
+    lax.fori_loop(0, padded_modes // 8, multiply, 0)
+    used = len(pairs) * padded_modes
+    if products.shape[0] > used:
+        products[used:, :] = jnp.zeros((products.shape[0] - used, products.shape[1]), F32)
+    gradient[...] = jnp.dot(
+        back_ref[...], products[...].astype(BF16), preferred_element_type=F32
+    )
+    share = gradient.shape[0] // 4
+    for shift, target in enumerate(sums):
+        at = jnp.bitwise_xor(own_quarter(), shift) * share
+        part = gradient[pl.ds(pl.multiple_of(at, share), share), :]
+        both = jnp.concatenate([part[:, :chans], part[:, chans:]], axis=0)
+        target[...] = both.astype(target.dtype)
+
+
+def loaded(coeff, grad, rows):
+    return [
+        [ref[lat, part, rows, :] for lat in range(ref.shape[0])]
+        for ref in (coeff, grad)
+        for part in range(2)
+    ]
+
+
+def place(slots, local_modes, chans, field, slot, part):
+    at = (field * slots + slot) * chans
+    return slice(part * local_modes, (part + 1) * local_modes), slice(at, at + chans)
+
+
+def return_kernel(blocks, local_modes, rows_ref, quad_ref, mixer_ref, coeff, grad, *refs):
+    outs, (synth, grad_coeff, wide) = refs[:blocks], refs[blocks:]
+    lat_count, _, padded_modes, chans = coeff.shape
+    slots = wide.shape[1] // (2 * chans)
+    me = lax.axis_index("space")
+    pairs = lat_pairs(lat_count)
 
     def mix(i, carry):
         rows = pl.ds(pl.multiple_of(i * 8, 8), 8)
-        a0 = [coeff[lat, 0, rows, :] for lat in range(lat_count)]
-        a1 = [coeff[lat, 1, rows, :] for lat in range(lat_count)]
-        b0 = [grad[lat, 0, rows, :] for lat in range(lat_count)]
-        b1 = [grad[lat, 1, rows, :] for lat in range(lat_count)]
+        a0, a1, b0, b1 = loaded(coeff, grad, rows)
         zero = jnp.zeros((8, chans), F32)
         y0, y1, z0, z1 = ([zero] * lat_count for _ in range(4))
         for index, (a, b) in enumerate(pairs):
             at = pl.ds(pl.multiple_of(index * padded_modes + i * 8, 8), 8)
             real = mixer_ref[at, :chans]
             imag = mixer_ref[at, chans:]
-            h0 = h1 = zero
             for p, q in [(a, b)] if a == b else [(a, b), (b, a)]:
                 y0[p] = y0[p] + real * a0[q] - imag * a1[q]
                 y1[p] = y1[p] + imag * a0[q] + real * a1[q]
                 z0[q] = z0[q] + real * b0[p] + imag * b1[p]
                 z1[q] = z1[q] + real * b1[p] - imag * b0[p]
-                h0 = h0 + b0[p] * a0[q] + b1[p] * a1[q]
-                h1 = h1 + b1[p] * a0[q] - b0[p] * a1[q]
-            products[at, :chans] = h0
-            products[at, chans:] = h1
         for lat in range(lat_count):
             synth[lat, 0, rows, :] = y0[lat]
             synth[lat, 1, rows, :] = y1[lat]
@@ -228,27 +269,21 @@
         return carry
 
     lax.fori_loop(0, padded_modes // 8, mix, 0)
-    used = len(pairs) * padded_modes
-    if products.shape[0] > used:
-        products[used:, :] = jnp.zeros((products.shape[0] - used, products.shape[1]), F32)
-    gradient[...] = jnp.dot(
-        back_ref[...], products[...].astype(BF16), preferred_element_type=F32
-    )
-    half = gradient.shape[0] // 2
-    upper = jnp.bitwise_and(me, 1)
-    for target, which in ((keep_ref, upper), (send_ref, 1 - upper)):
-        part = gradient[pl.ds(pl.multiple_of(which * half, half), half), :]
-        both = jnp.concatenate([part[:, :chans], part[:, chans:]], axis=0)
-        target[...] = both.astype(target.dtype)
+    if wide.shape[0] > 2 * local_modes:
+        wide[2 * local_modes :, :] = jnp.zeros(
+            (wide.shape[0] - 2 * local_modes, wide.shape[1]), F32
+        )
     for shift in range(blocks):
         block = jnp.bitwise_xor(me, shift)
         start = first_row_of(rows_ref, block, blocks)
         for slot in range(slots):
             lat = jnp.minimum(start + slot, lat_count - 1)
             for part in range(2):
-                wide[(shift, *place(0, slot, part))] = synth[lat, part, :local_modes, :]
-                wide[(shift, *place(1, slot, part))] = grad_coeff[lat, part, :local_modes, :]
-        outs[shift][...] = wide[shift].astype(BF16)
+                at = place(slots, local_modes, chans, 0, slot, part)
+                wide[at] = synth[lat, part, :local_modes, :]
+                at = place(slots, local_modes, chans, 1, slot, part)
+                wide[at] = grad_coeff[lat, part, :local_modes, :]
+        outs[shift][...] = wide[...].astype(BF16)
 
 
 def disco_inner(
@@ -383,32 +418,18 @@
     return first_ref[...].astype(F32) + second_ref[...].astype(F32)
 
 
-def half_kernel(kept_ref, got_ref, tap_ref, out_ref):
-    out_ref[: kept_ref.shape[0], :] = added(kept_ref, got_ref).astype(BF16)
-    split_taps(tap_ref[...], out_ref, kept_ref.shape[0])
-
-
-def add_kernel(own_ref, other_ref, out_ref, *cut_refs):
+def quarter_kernel(kept_ref, first_ref, second_ref, third_ref, tap_ref, out_ref):
+    total = kept_ref[...]
+    for ref in (first_ref, second_ref, third_ref):
+        total = total + ref[...].astype(F32)
+    out_ref[: total.shape[0], :] = total.astype(BF16)
+    split_taps(tap_ref[...], out_ref, total.shape[0])
+
+
+def add_kernel(scale, tap_scale, own_ref, other_ref, out_ref):
     count = own_ref.shape[0] - 2 * TAP_ROWS
-    out_ref[:count, :] = added(own_ref, other_ref)[:count, :].astype(BF16)
-    split_taps(joined_taps(own_ref) + joined_taps(other_ref), out_ref, count)
-    for at, cut_ref in enumerate(cut_refs):
-        rows = cut_ref.shape[0]
-        cut_ref[...] = out_ref[at * rows : (at + 1) * rows, :]
-
-
-def member_kernel(scale, tap_scale, own_ref, head_ref, tail_ref, out_ref, *cut_refs):
-    count, head = own_ref.shape[0] - 2 * TAP_ROWS, head_ref.shape[0]
-    out_ref[:head, :] = (
-        (own_ref[:head, :].astype(F32) + head_ref[...].astype(F32)) / scale
-    ).astype(BF16)
-    tail = own_ref[head:, :].astype(F32) + tail_ref[...].astype(F32)
-    out_ref[head:count, :] = (tail[: count - head, :] / scale).astype(BF16)
-    taps = joined_taps(own_ref) + joined_taps(tail_ref)
-    split_taps(taps / tap_scale, out_ref, count)
-    for at, cut_ref in enumerate(cut_refs):
-        rows = cut_ref.shape[0]
-        cut_ref[...] = out_ref[at * rows : (at + 1) * rows, :]
+    out_ref[:count, :] = (added(own_ref, other_ref)[:count, :] / scale).astype(BF16)
+    split_taps((joined_taps(own_ref) + joined_taps(other_ref)) / tap_scale, out_ref, count)
 
 
 def early_kernel(
@@ -439,22 +460,23 @@
 
 
 def finish_kernel(
-    blocks, rows_ref, table_ref, sum_ref, early_ref, slope_ref, own_ref, other_ref, *refs
+    blocks, rows_ref, table_ref, sum_ref, early_ref, slope_ref, *refs
 ):
-    ins, outs, scratch = refs[: blocks - 2], refs[blocks - 2 : blocks + 2], refs[blocks + 2 :]
-    out_hbm, grad_hbm, filter_hbm, tap_ref = outs
-    out_ref, grad_ref, filter_ref, sems = scratch
+    quarters, ins, refs = refs[:4], refs[4 : blocks + 2], refs[blocks + 2 :]
+    out_hbm, grad_hbm, filter_hbm, tap_ref, out_ref, grad_ref, filter_ref, held, sems = refs
     slots, lon_count, chans = sum_ref.shape
     me = lax.axis_index("space")
     live = rows_ref[me]
-    half = filter_ref.shape[1] // 2
-    upper = jnp.bitwise_and(me, 1)
-    for ref, which in ((own_ref, upper), (other_ref, 1 - upper)):
-        at = pl.ds(pl.multiple_of(which * half, half), half)
-        rows = ref[: 2 * half, :].astype(F32)
-        filter_ref[0, at, :] = rows[:half, :]
-        filter_ref[1, at, :] = rows[half:, :]
-    tap_ref[...] = (joined_taps(own_ref) + joined_taps(other_ref))[: tap_ref.shape[0], :]
+    share = filter_ref.shape[1] // 4
+    for shift, ref in enumerate(quarters):
+        quarter = jnp.bitwise_xor(own_quarter(), shift)
+        at = pl.ds(pl.multiple_of(quarter * share, share), share)
+        rows = ref[: 2 * share, :].astype(F32)
+        filter_ref[0, at, :] = rows[:share, :]
+        filter_ref[1, at, :] = rows[share:, :]
+        held[quarter] = joined_taps(ref)
+    taps = (held[0] + held[1]) + (held[2] + held[3])
+    tap_ref[...] = taps[: tap_ref.shape[0], :]
     stores = [pltpu.make_async_copy(filter_ref, filter_hbm, sems.at[0])]
     stores[0].start()
     parts = sems.shape[0] // (2 * slots)
@@ -487,6 +509,16 @@
     return lax.ppermute(values, axis, [(i, i ^ distance) for i in range(count)])
 
 
+def around(parts):
+    count = lax.axis_size("space") * lax.axis_size("ens")
+    flip = lax.axis_size("ens") + 1
+    return [
+        crossed(parts[0], 1, "ens"),
+        crossed(parts[1], 1),
+        lax.ppermute(parts[2], ("space", "ens"), [(i, i ^ flip) for i in range(count)]),
+    ]
+
+
 def crossed_all(parts, distances):
     return {s: crossed(parts[s], s) for s in distances}
 
@@ -502,7 +534,7 @@
     depth = round_up(2 * local_modes, 8)
     pairs = len(lat_pairs(lat_count))
     pair_rows = round_up(pairs * padded_modes, 128)
-    share = 2 * degrees // blocks
+    share = degrees // 2
     big = 32 if pair_rows <= 4096 else 60
     shape = jax.ShapeDtypeStruct
     table = fourier_table(lon_count, blocks, local_modes, depth)
@@ -552,20 +584,29 @@
     inner = [(i, i ^ 1) for i in range(blocks)]
     inner = [(i + 1, j + 1) for i, j in inner if max(i, j) + 1 < blocks]
     second_rim = lax.ppermute(second_rim, "space", inner)
-    spectral = pltpu.VMEM((lat_count, 2, padded_modes, chans), F32)
-    mixed = call(
-        functools.partial(mix_kernel, blocks, slots, lat_count, local_modes),
-        [coded] * blocks + [shape((degrees, chans), F32), shape((degrees, chans), BF16)],
-        [SMEM, SMEM] + [VMEM] * (2 + blocks),
-        (band_rows, quad_weight, mixer, back, *got),
-        scratch=[spectral] * 4
-        + [pltpu.VMEM((pair_rows, 2 * chans), F32), pltpu.VMEM((degrees, 2 * chans), F32)]
-        + [pltpu.VMEM((blocks, *coded.shape), F32)],
+    spectral = shape((lat_count, 2, padded_modes, chans), F32)
+    keep, *sends, coeff, grad = call(
+        functools.partial(gradient_kernel, blocks, slots, lat_count, local_modes),
+        [shape((share, chans), F32)] + [shape((share, chans), BF16)] * 3 + [spectral] * 2,
+        [SMEM, SMEM] + [VMEM] * (1 + blocks),
+        (band_rows, quad_weight, back, *got),
+        scratch=[
+            pltpu.VMEM((pair_rows, 2 * chans), F32),
+            pltpu.VMEM((degrees, 2 * chans), F32),
+            pltpu.VMEM((blocks, *coded.shape), F32),
+        ],
         limit=big,
         flops=20 * degrees * pair_rows * 2 * chans,
     )
-    back_parts, keep, send = mixed[:blocks], mixed[blocks], mixed[blocks + 1]
-    got_sum = crossed(send, 1)
+    got_sums = around(sends)
+    back_parts = call(
+        functools.partial(return_kernel, blocks, local_modes),
+        [coded] * blocks,
+        [SMEM, SMEM] + [VMEM] * 3,
+        (band_rows, quad_weight, mixer, coeff, grad),
+        scratch=[pltpu.VMEM(spectral.shape, F32)] * 2 + [pltpu.VMEM(coded.shape, F32)],
+        limit=big,
+    )
     rim_sum, rim_grad, tap_part = call(
         functools.partial(rim_kernel, blocks),
         [shape((2, lon_count, chans), F32)] * 2 + [tap_shape],
@@ -573,26 +614,23 @@
         (band_rows, tap_shift, dy, first_rim, second_rim, tap_weight, tap_part),
         scratch=[pltpu.VMEM((2, *padded), F32)] * 2,
     )
-    got_sum, tap_part = lax.optimization_barrier((got_sum, tap_part))
-    message = shape((degrees + 2 * TAP_ROWS, chans), BF16)
-    own = call(half_kernel, message, [VMEM] * 3, (keep, got_sum, tap_part))
+    message = shape((share + 2 * TAP_ROWS, chans), BF16)
+    back_parts, tap_part = lax.optimization_barrier((back_parts, tap_part))
+    own = call(quarter_kernel, message, [VMEM] * 5, (keep, *[got_sums[at] for at in (2, 0, 1)], tap_part))
     back_parts, own = lax.optimization_barrier((back_parts, own))
     returned = [back_parts[0], *reversed(crossed_all(back_parts, far).values())]
-    cut = shape((message.shape[0] // 2, chans), BF16)
-    for bit in range(1, blocks.bit_length() - 1):
-        own, *cuts = call(
-            add_kernel, [message, cut, cut], [VMEM] * 2, (own, crossed(own, 1 << bit))
+    steps = [(1 << bit, "space") for bit in range(1, blocks.bit_length() - 1)]
+    steps += [(1 << bit, "ens") for bit in range(1, members.bit_length() - 1)]
+    for at, (distance, axis) in enumerate(steps):
+        scales = (members, members * lat_count) if at == len(steps) - 1 else (1, 1)
+        own = call(
+            functools.partial(add_kernel, *scales),
+            message,
+            [VMEM] * 2,
+            (own, crossed(own, distance, axis)),
+            flops=3900000000 if at == 0 else 0,
         )
-    for bit in range(members.bit_length() - 1):
-        last = bit == members.bit_length() - 2
-        scales = (members, members * lat_count) if last else (1, 1)
-        own, *cuts = call(
-            functools.partial(member_kernel, *scales),
-            [message] if last else [message, cut, cut],
-            [VMEM] * 3,
-            (own, *[crossed(part, 1 << bit, "ens") for part in cuts]),
-            flops=300000000,
-        )
+    quarters = [own, *around([own] * 3)]
     early_sum, early_grad = call(
         early_kernel,
         [field, field],
@@ -604,15 +642,16 @@
         functools.partial(finish_kernel, blocks),
         [shape(x.shape, BF16)] * 2
         + [shape((2, degrees, chans), F32), shape((tap_weight.shape[0], chans), F32)],
-        [SMEM] + [VMEM] * (4 + blocks),
+        [SMEM] + [VMEM] * (6 + blocks),
         (
             band_rows, table_out, early_sum, early_grad, slope,
-            own, crossed(own, 1), *returned[2:],
+            *quarters, *returned[2:],
         ),
         scratch=[
             pltpu.VMEM(x.shape, BF16),
             pltpu.VMEM(x.shape, BF16),
             pltpu.VMEM((2, degrees, chans), F32),
+            pltpu.VMEM((4, TAP_ROWS, chans), F32),
             pltpu.SemaphoreType.DMA((1 + 2 * slots * pieces,)),
         ],
         flops=2 * blocks * depth * lon_count * 2 * slots * chans,

time: 57.5 us -> 56.6 us (0.984)
  waiting for transfers between devices: 19.6 us -> 12.8 us
  starting transfers between devices: 20.2 us -> 25.6 us
  Pallas kernels: 16.4 us -> 17 us
    ppermute x12, waiting for transfers between devices: 19.6 us -> 12.4 us  [crossed(): return lax.ppermute(values, axis, [(i, i ^ distance) for i in range(count)])]
    ppermute x12, starting transfers between devices: 19.6 us -> 22.4 us  [crossed(): return lax.ppermute(values, axis, [(i, i ^ distance) for i in range(count)])]
    ppermute x0 -> x2, starting transfers between devices: none -> 2.54 us  [around(): lax.ppermute(parts[2], ('space', 'ens'), [(i, i ^ flip) for i in range(co...]
  transfers between devices with their start and end apart: 13 -> 15, of which waited for: 8 -> 6; matrix products, arithmetic and copies ran while one was open for 0% -> 0% of each run, Pallas kernels for 19% -> 20%
where the time goes in v5:
time: 56.6 us; the launch traced here: 56.4 us
  starting transfers between devices  25.6 us (45%)
  Pallas kernels  17 us (30%)
  waiting for transfers between devices  12.8 us (23%)
  between operations  0.88 us (2%)
    ppermute x12, starting transfers between devices, crossed(): return lax.ppermute(values, axis, [(i, i ^ distance) for i in range(count)])  22.4 us
    pallas_call x9, Pallas kernels, call(): pl.pallas_call(kernel, out_shape=out_shape, in_specs=in_specs, out_specs=...  17 us
    ppermute x12, waiting for transfers between devices, crossed(): return lax.ppermute(values, axis, [(i, i ^ distance) for i in range(count)])  12.4 us
    ppermute x2, starting transfers between devices, around(): lax.ppermute(parts[2], ('space', 'ens'), [(i, i ^ flip) for i in range(co...  2.54 us
  transfers between devices with their start and end apart: 15, of which 6 were waited for; matrix products, arithmetic and copies ran while one was open for 0% of the time, Pallas kernels for 20%

profile of v5, /device:TPU:0, one launch (start us, length us, event | category | flops | bytes accessed | tf_op | source)
XLA Modules:
  0.0 56.4 jit_solution(15983122515198858680)
XLA Ops:
  0.6 0.0 copy-start.1
  0.6 0.0 copy-start.6
  0.7 0.0 copy-start.9
  0.7 0.0 copy-start.2
  0.7 0.0 copy-start.4
  0.7 0.0 copy-start.3
  0.7 0.0 copy-start.7
  0.7 3.1 %shard_map.130 = (bf16[184,512]{1,0:T(8,128)(2,1)}, bf16[184,512]{1,0:T(8,128)(2,1)}, bf16[184,512]{1,0:T(8,128)(2,1)}, bf16[184,512]{1,0:T(8,128)(2,1)}) custom-call(bf16[2,768,128]{2,1,0:T(8,128)(2,1)} %bitcast.8, bf16[2,768,128]{2,1,0:T(8,128)(2,1)} %bitcast.5, bf16[4,184,768]{2,1,0:T(8,128)(2,1)} %constant.7.clone.table_hbm), custom_call_target="tpu_custom_call" | custom-call | flops 578813952 | bytes 1024 | tf_op jit(solution)/shard_map/pallas_call | solution.py:61
  3.8 0.0 copy-start.5
  3.8 0.0 copy-start.8
  3.8 5.1 %collective-permute-start = (bf16[184,512]{1,0:T(8,128)(2,1)}, bf16[184,512]{1,0:T(8,128)(2,1)S(1)}, u32[]{:S(2)}, u32[]{:S(2)}) collective-permute-start(bf16[184,512]{1,0:T(8,128)(2,1)} %get-tuple-element.53), channel_id=1, source_target_pairs={{0,12},{4,8},{8,4},{12,0},{1,13},{5,9},{9,5},{13,1},{2,14},{6,10},... | collective-permute-start | bytes 565256 | tf_op jit(solution)/shard_map/ppermute | solution.py:509
  8.9 0.0 collective-permute-start.3
  8.9 0.6 %collective-permute-start.4 = (bf16[184,512]{1,0:T(8,128)(2,1)}, bf16[184,512]{1,0:T(8,128)(2,1)S(1)}, u32[]{:S(2)}, u32[]{:S(2)}) collective-permute-start(bf16[184,512]{1,0:T(8,128)(2,1)} %get-tuple-element.63), channel_id=1, source_target_pairs={{0,8},{4,12},{8,0},{12,4},{1,9},{5,13},{9,1},{13,5},{2,10},{6,14},... | collective-permute-start | bytes 565256 | tf_op jit(solution)/shard_map/ppermute | solution.py:509
  9.6 0.0 copy-done.9
  9.6 0.0 copy-done.1
  9.6 0.0 copy-done.6
  9.7 0.0 copy-done.2
  9.7 0.0 copy-done.4
  9.7 0.0 copy-done.3
  9.7 0.0 copy-done.7
  9.7 5.3 %shard_map.129 = (f32[2048,256]{1,0:T(8,128)S(1)}, bf16[384,2048]{1,0:T(8,128)(2,1)S(1)}, bf16[2,768,128]{2,1,0:T(8,128)(2,1)S(1)}, bf16[2,768,128]{2,1,0:T(8,12...) custom-call(s32[4]{0:T(128)S(1)} %copy-done.2, ...), custom_call_target="tpu_custom_call" | custom-call | flops 402653184 | bytes 2097152 | tf_op jit(solution)/shard_map/pallas_call | solution.py:61
  15.0 0.0 collective-permute-done.refs_3_
  15.0 4.4 %collective-permute-start.1 = (bf16[2,768,128]{2,1,0:T(8,128)(2,1)S(1)}, bf16[2,768,128]{2,1,0:T(8,128)(2,1)S(1)}, u32[]{:S(2)}, u32[]{:S(2)}) collective-permute-start(bf16[2,768,128]{2,1,0:T(8,128)(2,1)S(1)} %get-tuple-element.54), channel_id=1, source_target_pairs={{0,4},{4,0},{8,12},{12,8},{1,5},{5,1},{9,13},{13,9},{2,6},{6,2},{1... | collective-permute-start | bytes 1179656 | tf_op jit(solution)/shard_map/ppermute | solution.py:509
  19.4 0.7 %collective-permute-start.2 = (bf16[2,768,128]{2,1,0:T(8,128)(2,1)S(1)}, bf16[2,768,128]{2,1,0:T(8,128)(2,1)S(1)}, u32[]{:S(2)}, u32[]{:S(2)}) collective-permute-start(bf16[2,768,128]{2,1,0:T(8,128)(2,1)S(1)} %get-tuple-element.55), channel_id=1, source_target_pairs={{4,8},{8,4},{5,9},{9,5},{6,10},{10,6},{7,11},{11,7},{20,24},{24,20... | collective-permute-start | bytes 1179656 | tf_op jit(solution)/shard_map/ppermute | solution.py:586
  20.1 0.0 collective-permute-done.3.refs_1_
  20.1 6.0 %collective-permute-done.4.refs_2_ = bf16[184,512]{1,0:T(8,128)(2,1)S(1)} collective-permute-done((bf16[184,512]{1,0:T(8,128)(2,1)}, bf16[184,512]{1,0:T(8,128)(2,1)S(1)}, u32[]{:S(2)}, u32[]{:S(2)}) %collective-permute-start.4) | collective-permute-done | bytes 188448 | tf_op jit(solution)/shard_map/ppermute | solution.py:509
  26.1 0.0 copy-done.5
  26.1 0.0 copy-done.8
  26.1 1.9 %shard_map.132 = (f32[192,128]{1,0:T(8,128)S(1)}, bf16[192,128]{1,0:T(8,128)(2,1)S(1)}, bf16[192,128]{1,0:T(8,128)(2,1)S(1)}, bf16[192,128]{1,0:T(8,128)(2,1)S(1...) custom-call(s32[4]{0:T(128)S(1)} %copy-done.2, f32[6]{0:T(128)S(1)} %copy-done.5, ...), custom_call_target="tpu_custom_call" | custom-call | flops 4026531840 | bytes 1024 | tf_op jit(solution)/shard_map/pallas_call | solution.py:61
  28.1 0.9 %collective-permute-start.5 = (bf16[192,128]{1,0:T(8,128)(2,1)S(1)}, bf16[192,128]{1,0:T(8,128)(2,1)S(1)}, u32[]{:S(2)}, u32[]{:S(2)}) collective-permute-start(bf16[192,128]{1,0:T(8,128)(2,1)S(1)} %get-tuple-element.77), channel_id=1, source_target_pairs={{0,6},{2,4},{4,2},{6,0},{8,14},{10,12},{12,10},{14,8},{1,7},{3,5},... | collective-permute-start | bytes 147464 | tf_op jit(solution)/shard_map/ppermute | solution.py:518
  29.0 0.7 %collective-permute-start.6 = (bf16[192,128]{1,0:T(8,128)(2,1)S(1)}, bf16[192,128]{1,0:T(8,128)(2,1)S(1)}, u32[]{:S(2)}, u32[]{:S(2)}) collective-permute-start(bf16[192,128]{1,0:T(8,128)(2,1)S(1)} %get-tuple-element.78), channel_id=1, source_target_pairs={{0,2},{2,0},{1,3},{3,1},{4,6},{6,4},{5,7},{7,5},{8,10},{10,8},{9,1... | collective-permute-start | bytes 147464 | tf_op jit(solution)/shard_map/ppermute | solution.py:509
  29.7 1.9 %collective-permute-start.7 = (bf16[192,128]{1,0:T(8,128)(2,1)S(1)}, bf16[192,128]{1,0:T(8,128)(2,1)S(1)}, u32[]{:S(2)}, u32[]{:S(2)}) collective-permute-start(bf16[192,128]{1,0:T(8,128)(2,1)S(1)} %get-tuple-element.79), channel_id=1, source_target_pairs={{0,4},{4,0},{8,12},{12,8},{1,5},{5,1},{9,13},{13,9},{2,6},{6,2},{1... | collective-permute-start | bytes 147464 | tf_op jit(solution)/shard_map/ppermute | solution.py:509
  31.6 1.7 %shard_map.133 = (bf16[184,512]{1,0:T(8,128)(2,1)S(1)}, bf16[184,512]{1,0:T(8,128)(2,1)S(1)}, bf16[184,512]{1,0:T(8,128)(2,1)S(1)}, bf16[184,512]{1,0:T(8,128)(2,1)S(1)}) custom-call(s32[4]{0:T(128)S(1)} %copy-done.2, f32[6]{0:T(128)S(1)} %copy-done.5, f32[2048,256]{1,0:T(8,128)S(1)} %get-tuple-element.59.mixer_ref, ...), custom_call_target="tpu_custom_call" | custom-call | bytes 1024 | tf_op jit(solution)/shard_map/pallas_call | solution.py:61
  33.4 0.0 collective-permute-done.1.first_rim
  33.4 0.0 collective-permute-done.2.second_rim
  33.4 1.3 %shard_map.131 = (f32[2,768,128]{2,1,0:T(8,128)S(1)}, f32[2,768,128]{2,1,0:T(8,128)S(1)}, f32[16,128]{1,0:T(8,128)S(1)}) custom-call(s32[4]{0:T(128)S(1)} %copy-done.2, s32[6,9]{1,0:T(8,128)S(1)} %copy-done.3, bf16[2,768,128]{2,1,0:T(8,128)(2,1)S(1)} %bitcast.7, bf16[2,768,128]{2,1,0:T(8,128)(2,1)S(1)} %collective-permute-done.1.first_rim, ...), custom_call_target="tpu_custom_call" | custom-call | bytes 1024 | tf_op jit(solution)/shard_map/pallas_call | solution.py:61
  34.7 0.0 collective-permute-done.5.first_ref
  34.7 0.0 collective-permute-done.6.second_ref
  34.7 0.0 collective-permute-done.7.third_ref
  34.7 0.0 copy-start
  34.7 2.2 %collective-permute-start.9 = (bf16[224,128]{1,0:T(8,128)(2,1)S(1)}, bf16[224,128]{1,0:T(8,128)(2,1)S(1)}, u32[]{:S(2)}, u32[]{:S(2)}) collective-permute-start(bf16[224,128]{1,0:T(8,128)(2,1)S(1)} %shard_map.134.own_ref), channel_id=1, source_target_pairs={{0,8},{4,12},{8,0},{12,4},{1,9},{5,13},{9,1},{13,5},{2,10},{6,14},... | collective-permute-start | bytes 172040 | tf_op jit(solution)/shard_map/ppermute | solution.py:509
  37.0 1.1 %collective-permute-start.8 = (bf16[184,512]{1,0:T(8,128)(2,1)S(1)}, bf16[184,512]{1,0:T(8,128)(2,1)S(1)}, u32[]{:S(2)}, u32[]{:S(2)}) collective-permute-start(bf16[184,512]{1,0:T(8,128)(2,1)S(1)} %get-tuple-element.82), channel_id=1, source_target_pairs={{0,4},{4,0},{8,12},{12,8},{1,5},{5,1},{9,13},{13,9},{2,6},{6,2},{1... | collective-permute-start | bytes 565256 | tf_op jit(solution)/shard_map/ppermute | solution.py:509
  38.0 0.7 %collective-permute-start.13 = (bf16[184,512]{1,0:T(8,128)(2,1)S(1)}, bf16[184,512]{1,0:T(8,128)(2,1)S(1)}, u32[]{:S(2)}, u32[]{:S(2)}) collective-permute-start(bf16[184,512]{1,0:T(8,128)(2,1)S(1)} %get-tuple-element.86), channel_id=1, source_target_pairs={{0,8},{4,12},{8,0},{12,4},{1,9},{5,13},{9,1},{13,5},{2,10},{6,14},... | collective-permute-start | bytes 565256 | tf_op jit(solution)/shard_map/ppermute | solution.py:509
  38.7 2.6 %collective-permute-start.14 = (bf16[184,512]{1,0:T(8,128)(2,1)S(1)}, bf16[184,512]{1,0:T(8,128)(2,1)S(1)}, u32[]{:S(2)}, u32[]{:S(2)}) collective-permute-start(bf16[184,512]{1,0:T(8,128)(2,1)S(1)} %get-tuple-element.87), channel_id=1, source_target_pairs={{0,12},{4,8},{8,4},{12,0},{1,13},{5,9},{9,5},{13,1},{2,14},{6,10},... | collective-permute-start | bytes 565256 | tf_op jit(solution)/shard_map/ppermute | solution.py:509
  41.4 0.0 collective-permute-done.9.other_ref
  41.4 1.6 %collective-permute-start.12 = (bf16[224,128]{1,0:T(8,128)(2,1)S(1)}, bf16[224,128]{1,0:T(8,128)(2,1)S(1)}, u32[]{:S(2)}, u32[]{:S(2)}) collective-permute-start(bf16[224,128]{1,0:T(8,128)(2,1)S(1)} %shard_map.136.refs_0_), channel_id=1, source_target_pairs={{0,6},{2,4},{4,2},{6,0},{8,14},{10,12},{12,10},{14,8},{1,7},{3,5},... | collective-permute-start | bytes 172040 | tf_op jit(solution)/shard_map/ppermute | solution.py:518
  43.0 1.4 %collective-permute-start.11 = (bf16[224,128]{1,0:T(8,128)(2,1)S(1)}, bf16[224,128]{1,0:T(8,128)(2,1)S(1)}, u32[]{:S(2)}, u32[]{:S(2)}) collective-permute-start(bf16[224,128]{1,0:T(8,128)(2,1)S(1)} %shard_map.136.refs_0_), channel_id=1, source_target_pairs={{0,4},{4,0},{8,12},{12,8},{1,5},{5,1},{9,13},{13,9},{2,6},{6,2},{1... | collective-permute-start | bytes 172040 | tf_op jit(solution)/shard_map/ppermute | solution.py:509
  44.4 3.4 %collective-permute-done.8.near_ref = bf16[184,512]{1,0:T(8,128)(2,1)S(1)} collective-permute-done((bf16[184,512]{1,0:T(8,128)(2,1)S(1)}, bf16[184,512]{1,0:T(8,128)(2,1)S(1)}, u32[]{:S(2)}, u32[]{:S(2)}) %collective-permute-start.8) | collective-permute-done | bytes 188448 | tf_op jit(solution)/shard_map/ppermute | solution.py:509
  47.8 1.5 %collective-permute-start.10 = (bf16[224,128]{1,0:T(8,128)(2,1)S(1)}, bf16[224,128]{1,0:T(8,128)(2,1)S(1)}, u32[]{:S(2)}, u32[]{:S(2)}) collective-permute-start(bf16[224,128]{1,0:T(8,128)(2,1)S(1)} %shard_map.136.refs_0_), channel_id=1, source_target_pairs={{0,2},{2,0},{1,3},{3,1},{4,6},{6,4},{5,7},{7,5},{8,10},{10,8},{9,1... | collective-permute-start | bytes 172040 | tf_op jit(solution)/shard_map/ppermute | solution.py:509
  49.3 0.0 copy-done
  49.3 1.1 %shard_map.135 = (f32[2,768,128]{2,1,0:T(8,128)S(1)}, f32[2,768,128]{2,1,0:T(8,128)S(1)}) custom-call(s32[4]{0:T(128)S(1)} %copy-done.2, bf16[4,768,184]{2,1,0:T(8,128)(2,1)S(1)} %copy-done, f32[2,768,128]{2,1,0:T(8,128)S(1)} %get-tuple-element.48.base_ref, f32[2,768,128]{2,1,0:T(8,128)S(1)} %get-tuple-element.49.slope_ref, ...), custom_call_target="tpu_custom_call" | custom-call | bytes 1024 | tf_op jit(solution)/shard_map/pallas_call | solution.py:61
  50.4 0.4 collective-permute-done.12.refs_3_
  50.8 0.6 %collective-permute-done.11.refs_2_ = bf16[224,128]{1,0:T(8,128)(2,1)S(1)} collective-permute-done((bf16[224,128]{1,0:T(8,128)(2,1)S(1)}, bf16[224,128]{1,0:T(8,128)(2,1)S(1)}, u32[]{:S(2)}, u32[]{:S(2)}) %collective-permute-start.11) | collective-permute-done | bytes 57376 | tf_op jit(solution)/shard_map/ppermute | solution.py:509
  51.5 0.5 collective-permute-done.10.refs_1_
  52.0 1.9 %collective-permute-done.13.refs_4_ = bf16[184,512]{1,0:T(8,128)(2,1)S(1)} collective-permute-done((bf16[184,512]{1,0:T(8,128)(2,1)S(1)}, bf16[184,512]{1,0:T(8,128)(2,1)S(1)}, u32[]{:S(2)}, u32[]{:S(2)}) %collective-permute-start.13) | collective-permute-done | bytes 188448 | tf_op jit(solution)/shard_map/ppermute | solution.py:509
  53.9 0.0 collective-permute-done.14.refs_5_
  53.9 2.5 %shard_map.137 = (bf16[2,768,128]{2,1,0:T(8,128)(2,1)}, bf16[2,768,128]{2,1,0:T(8,128)(2,1)}, f32[2,384,128]{2,1,0:T(8,128)}, f32[9,128]{1,0:T(8,128)}) custom-call(s32[4]{0:T(128)S(1)} %copy-done.2, bf16[4,768,184]{2,1,0:T(8,128)(2,1)S(1)} %copy-done, f32[2,768,128]{2,1,0:T(8,128)S(1)} %get-tuple-element.83.sum_ref, ...), custom_call_target="tpu_custom_call" | custom-call | flops 578813952 | bytes 1024 | tf_op jit(solution)/shard_map/pallas_call | solution.py:61
  (3 shorter events, 0.1 us)
Async XLA Ops:
  0.6 9.0 %copy-start.1 = (bf16[1,2,768,128]{3,2,1,0:T(8,128)(2,1)S(1)}, bf16[1,2,768,128]{3,2,1,0:T(8,128)(2,1)}, u32[]{:S(2)}) copy-start(bf16[1,2,768,128]{3,2,1,0:T(8,128)(2,1)} %param.11) | copy-start | bytes 1179652
  0.6 9.0 %copy-start.6 = (bf16[1,2,768,128]{3,2,1,0:T(8,128)(2,1)S(1)}, bf16[1,2,768,128]{3,2,1,0:T(8,128)(2,1)}, u32[]{:S(2)}) copy-start(bf16[1,2,768,128]{3,2,1,0:T(8,128)(2,1)} %param.10) | copy-start | bytes 1179652
  0.7 8.9 %copy-start.9 = (bf16[92,6,384]{2,0,1:T(8,128)(2,1)S(1)}, bf16[92,6,384]{2,0,1:T(8,128)(2,1)}, u32[]{:S(2)}) copy-start(bf16[92,6,384]{2,0,1:T(8,128)(2,1)} %param.15) | copy-start | bytes 1271812
  0.7 9.0 %copy-start.2 = (s32[4]{0:T(128)S(1)}, s32[4]{0:T(128)}, u32[]{:S(2)}) copy-start(s32[4]{0:T(128)} %rows_ref.11) | copy-start | bytes 52
  0.7 9.0 %copy-start.4 = (bf16[9,128]{1,0:T(8,128)(2,1)S(1)}, bf16[9,128]{1,0:T(8,128)(2,1)}, u32[]{:S(2)}) copy-start(bf16[9,128]{1,0:T(8,128)(2,1)} %taps_ref.3) | copy-start | bytes 6916
  0.7 9.0 %copy-start.3 = (s32[6,9]{1,0:T(8,128)S(1)}, s32[6,9]{1,0:T(8,128)}, u32[]{:S(2)}) copy-start(s32[6,9]{1,0:T(8,128)} %shift_ref.3) | copy-start | bytes 652
  0.7 9.0 %copy-start.7 = (bf16[2,384,128]{2,1,0:T(8,128)(2,1)S(1)}, bf16[2,384,128]{2,1,0:T(8,128)(2,1)}, u32[]{:S(2)}) copy-start(bf16[2,384,128]{2,1,0:T(8,128)(2,1)} %filter_ref.1) | copy-start | bytes 589828
  3.8 22.3 %copy-start.5 = (f32[6]{0:T(128)S(1)}, f32[6]{0:T(128)}, u32[]{:S(2)}) copy-start(f32[6]{0:T(128)} %quad_ref.3) | copy-start | bytes 76
  3.8 22.3 %copy-start.8 = (bf16[184,512]{1,0:T(8,128)(2,1)S(1)}, bf16[184,512]{1,0:T(8,128)(2,1)}, u32[]{:S(2)}) copy-start(bf16[184,512]{1,0:T(8,128)(2,1)} %get-tuple-element.61.refs_0_) | copy-start | bytes 565252
  3.8 11.2 %collective-permute-start = (bf16[184,512]{1,0:T(8,128)(2,1)}, bf16[184,512]{1,0:T(8,128)(2,1)S(1)}, u32[]{:S(2)}, u32[]{:S(2)}) collective-permute-start(bf16[184,512]{1,0:T(8,128)(2,1)} %get-tuple-element.53), channel_id=1, source_target_pairs={{0,12},{4,8},{8,4},{12,0},{1,13},{5,9},{9,5},{13,1},{2,14},{6,10},... | collective-permute-start | bytes 565256 | tf_op jit(solution)/shard_map/ppermute | solution.py:509
  8.9 11.2 %collective-permute-start.3 = (bf16[184,512]{1,0:T(8,128)(2,1)}, bf16[184,512]{1,0:T(8,128)(2,1)S(1)}, u32[]{:S(2)}, u32[]{:S(2)}) collective-permute-start(bf16[184,512]{1,0:T(8,128)(2,1)} %get-tuple-element.62), channel_id=1, source_target_pairs={{0,4},{4,0},{8,12},{12,8},{1,5},{5,1},{9,13},{13,9},{2,6},{6,2},{1... | collective-permute-start | bytes 565256 | tf_op jit(solution)/shard_map/ppermute | solution.py:509
  8.9 17.2 %collective-permute-start.4 = (bf16[184,512]{1,0:T(8,128)(2,1)}, bf16[184,512]{1,0:T(8,128)(2,1)S(1)}, u32[]{:S(2)}, u32[]{:S(2)}) collective-permute-start(bf16[184,512]{1,0:T(8,128)(2,1)} %get-tuple-element.63), channel_id=1, source_target_pairs={{0,8},{4,12},{8,0},{12,4},{1,9},{5,13},{9,1},{13,5},{2,10},{6,14},... | collective-permute-start | bytes 565256 | tf_op jit(solution)/shard_map/ppermute | solution.py:509
  15.0 18.4 %collective-permute-start.1 = (bf16[2,768,128]{2,1,0:T(8,128)(2,1)S(1)}, bf16[2,768,128]{2,1,0:T(8,128)(2,1)S(1)}, u32[]{:S(2)}, u32[]{:S(2)}) collective-permute-start(bf16[2,768,128]{2,1,0:T(8,128)(2,1)S(1)} %get-tuple-element.54), channel_id=1, source_target_pairs={{0,4},{4,0},{8,12},{12,8},{1,5},{5,1},{9,13},{13,9},{2,6},{6,2},{1... | collective-permute-start | bytes 1179656 | tf_op jit(solution)/shard_map/ppermute | solution.py:509
  19.4 13.9 %collective-permute-start.2 = (bf16[2,768,128]{2,1,0:T(8,128)(2,1)S(1)}, bf16[2,768,128]{2,1,0:T(8,128)(2,1)S(1)}, u32[]{:S(2)}, u32[]{:S(2)}) collective-permute-start(bf16[2,768,128]{2,1,0:T(8,128)(2,1)S(1)} %get-tuple-element.55), channel_id=1, source_target_pairs={{4,8},{8,4},{5,9},{9,5},{6,10},{10,6},{7,11},{11,7},{20,24},{24,20... | collective-permute-start | bytes 1179656 | tf_op jit(solution)/shard_map/ppermute | solution.py:586
  28.1 6.6 %collective-permute-start.5 = (bf16[192,128]{1,0:T(8,128)(2,1)S(1)}, bf16[192,128]{1,0:T(8,128)(2,1)S(1)}, u32[]{:S(2)}, u32[]{:S(2)}) collective-permute-start(bf16[192,128]{1,0:T(8,128)(2,1)S(1)} %get-tuple-element.77), channel_id=1, source_target_pairs={{0,6},{2,4},{4,2},{6,0},{8,14},{10,12},{12,10},{14,8},{1,7},{3,5},... | collective-permute-start | bytes 147464 | tf_op jit(solution)/shard_map/ppermute | solution.py:518
  29.0 5.7 %collective-permute-start.6 = (bf16[192,128]{1,0:T(8,128)(2,1)S(1)}, bf16[192,128]{1,0:T(8,128)(2,1)S(1)}, u32[]{:S(2)}, u32[]{:S(2)}) collective-permute-start(bf16[192,128]{1,0:T(8,128)(2,1)S(1)} %get-tuple-element.78), channel_id=1, source_target_pairs={{0,2},{2,0},{1,3},{3,1},{4,6},{6,4},{5,7},{7,5},{8,10},{10,8},{9,1... | collective-permute-start | bytes 147464 | tf_op jit(solution)/shard_map/ppermute | solution.py:509
  29.7 5.0 %collective-permute-start.7 = (bf16[192,128]{1,0:T(8,128)(2,1)S(1)}, bf16[192,128]{1,0:T(8,128)(2,1)S(1)}, u32[]{:S(2)}, u32[]{:S(2)}) collective-permute-start(bf16[192,128]{1,0:T(8,128)(2,1)S(1)} %get-tuple-element.79), channel_id=1, source_target_pairs={{0,4},{4,0},{8,12},{12,8},{1,5},{5,1},{9,13},{13,9},{2,6},{6,2},{1... | collective-permute-start | bytes 147464 | tf_op jit(solution)/shard_map/ppermute | solution.py:509
  34.7 14.6 %copy-start = (bf16[4,768,184]{2,1,0:T(8,128)(2,1)S(1)}, bf16[4,768,184]{2,1,0:T(8,128)(2,1)}, u32[]{:S(2)}) copy-start(bf16[4,768,184]{2,1,0:T(8,128)(2,1)} %constant.8.clone.table_ref) | copy-start | bytes 3391492
  34.7 6.6 %collective-permute-start.9 = (bf16[224,128]{1,0:T(8,128)(2,1)S(1)}, bf16[224,128]{1,0:T(8,128)(2,1)S(1)}, u32[]{:S(2)}, u32[]{:S(2)}) collective-permute-start(bf16[224,128]{1,0:T(8,128)(2,1)S(1)} %shard_map.134.own_ref), channel_id=1, source_target_pairs={{0,8},{4,12},{8,0},{12,4},{1,9},{5,13},{9,1},{13,5},{2,10},{6,14},... | collective-permute-start | bytes 172040 | tf_op jit(solution)/shard_map/ppermute | solution.py:509
  37.0 10.8 %collective-permute-start.8 = (bf16[184,512]{1,0:T(8,128)(2,1)S(1)}, bf16[184,512]{1,0:T(8,128)(2,1)S(1)}, u32[]{:S(2)}, u32[]{:S(2)}) collective-permute-start(bf16[184,512]{1,0:T(8,128)(2,1)S(1)} %get-tuple-element.82), channel_id=1, source_target_pairs={{0,4},{4,0},{8,12},{12,8},{1,5},{5,1},{9,13},{13,9},{2,6},{6,2},{1... | collective-permute-start | bytes 565256 | tf_op jit(solution)/shard_map/ppermute | solution.py:509
  38.0 15.8 %collective-permute-start.13 = (bf16[184,512]{1,0:T(8,128)(2,1)S(1)}, bf16[184,512]{1,0:T(8,128)(2,1)S(1)}, u32[]{:S(2)}, u32[]{:S(2)}) collective-permute-start(bf16[184,512]{1,0:T(8,128)(2,1)S(1)} %get-tuple-element.86), channel_id=1, source_target_pairs={{0,8},{4,12},{8,0},{12,4},{1,9},{5,13},{9,1},{13,5},{2,10},{6,14},... | collective-permute-start | bytes 565256 | tf_op jit(solution)/shard_map/ppermute | solution.py:509
  38.7 15.1 %collective-permute-start.14 = (bf16[184,512]{1,0:T(8,128)(2,1)S(1)}, bf16[184,512]{1,0:T(8,128)(2,1)S(1)}, u32[]{:S(2)}, u32[]{:S(2)}) collective-permute-start(bf16[184,512]{1,0:T(8,128)(2,1)S(1)} %get-tuple-element.87), channel_id=1, source_target_pairs={{0,12},{4,8},{8,4},{12,0},{1,13},{5,9},{9,5},{13,1},{2,14},{6,10},... | collective-permute-start | bytes 565256 | tf_op jit(solution)/shard_map/ppermute | solution.py:509
  41.4 9.5 %collective-permute-start.12 = (bf16[224,128]{1,0:T(8,128)(2,1)S(1)}, bf16[224,128]{1,0:T(8,128)(2,1)S(1)}, u32[]{:S(2)}, u32[]{:S(2)}) collective-permute-start(bf16[224,128]{1,0:T(8,128)(2,1)S(1)} %shard_map.136.refs_0_), channel_id=1, source_target_pairs={{0,6},{2,4},{4,2},{6,0},{8,14},{10,12},{12,10},{14,8},{1,7},{3,5},... | collective-permute-start | bytes 172040 | tf_op jit(solution)/shard_map/ppermute | solution.py:518
  43.0 8.4 %collective-permute-start.11 = (bf16[224,128]{1,0:T(8,128)(2,1)S(1)}, bf16[224,128]{1,0:T(8,128)(2,1)S(1)}, u32[]{:S(2)}, u32[]{:S(2)}) collective-permute-start(bf16[224,128]{1,0:T(8,128)(2,1)S(1)} %shard_map.136.refs_0_), channel_id=1, source_target_pairs={{0,4},{4,0},{8,12},{12,8},{1,5},{5,1},{9,13},{13,9},{2,6},{6,2},{1... | collective-permute-start | bytes 172040 | tf_op jit(solution)/shard_map/ppermute | solution.py:509
  47.8 4.2 %collective-permute-start.10 = (bf16[224,128]{1,0:T(8,128)(2,1)S(1)}, bf16[224,128]{1,0:T(8,128)(2,1)S(1)}, u32[]{:S(2)}, u32[]{:S(2)}) collective-permute-start(bf16[224,128]{1,0:T(8,128)(2,1)S(1)} %shard_map.136.refs_0_), channel_id=1, source_target_pairs={{0,2},{2,0},{1,3},{3,1},{4,6},{6,4},{5,7},{7,5},{8,10},{10,8},{9,1... | collective-permute-start | bytes 172040 | tf_op jit(solution)/shard_map/ppermute | solution.py:509

commit v6 on v5

--- a/solution.py
+++ b/solution.py
@@ -459,14 +459,8 @@
             grad_ref[slot, rows, :] = base_grad_ref[slot, rows, :] + back * slope_ref[slot, rows, :]
 
 
-def finish_kernel(
-    blocks, rows_ref, table_ref, sum_ref, early_ref, slope_ref, *refs
-):
-    quarters, ins, refs = refs[:4], refs[4 : blocks + 2], refs[blocks + 2 :]
-    out_hbm, grad_hbm, filter_hbm, tap_ref, out_ref, grad_ref, filter_ref, held, sems = refs
-    slots, lon_count, chans = sum_ref.shape
-    me = lax.axis_index("space")
-    live = rows_ref[me]
+def spread_kernel(*refs):
+    quarters, (filter_ref, tap_ref, held) = refs[:4], refs[4:]
     share = filter_ref.shape[1] // 4
     for shift, ref in enumerate(quarters):
         quarter = jnp.bitwise_xor(own_quarter(), shift)
@@ -477,8 +471,17 @@
         held[quarter] = joined_taps(ref)
     taps = (held[0] + held[1]) + (held[2] + held[3])
     tap_ref[...] = taps[: tap_ref.shape[0], :]
-    stores = [pltpu.make_async_copy(filter_ref, filter_hbm, sems.at[0])]
-    stores[0].start()
+
+
+def finish_kernel(
+    blocks, rows_ref, table_ref, sum_ref, early_ref, slope_ref, *refs
+):
+    ins, refs = refs[: blocks - 2], refs[blocks - 2 :]
+    out_hbm, grad_hbm, out_ref, grad_ref, sems = refs
+    slots, lon_count, chans = sum_ref.shape
+    me = lax.axis_index("space")
+    live = rows_ref[me]
+    stores = []
     parts = sems.shape[0] // (2 * slots)
     step = lon_count // parts
     for part in range(parts):
@@ -637,25 +640,28 @@
         [SMEM] + [VMEM] * 8,
         (band_rows, table_out, base, slope, base_grad, rim_sum, rim_grad, *returned[:2]),
     )
+    quarters, early_sum = lax.optimization_barrier((quarters, early_sum))
+    filter_grad, tap_grad = call(
+        spread_kernel,
+        [shape((2, degrees, chans), F32), shape((tap_weight.shape[0], chans), F32)],
+        [VMEM] * 4,
+        quarters,
+        scratch=[pltpu.VMEM((4, TAP_ROWS, chans), F32)],
+    )
+    far_parts, filter_grad = lax.optimization_barrier((returned[2:], filter_grad))
     pieces = 4
-    output, input_grad, filter_grad, tap_grad = call(
+    output, input_grad = call(
         functools.partial(finish_kernel, blocks),
-        [shape(x.shape, BF16)] * 2
-        + [shape((2, degrees, chans), F32), shape((tap_weight.shape[0], chans), F32)],
-        [SMEM] + [VMEM] * (6 + blocks),
-        (
-            band_rows, table_out, early_sum, early_grad, slope,
-            *quarters, *returned[2:],
-        ),
+        [shape(x.shape, BF16)] * 2,
+        [SMEM] + [VMEM] * (2 + blocks),
+        (band_rows, table_out, early_sum, early_grad, slope, *far_parts),
         scratch=[
             pltpu.VMEM(x.shape, BF16),
             pltpu.VMEM(x.shape, BF16),
-            pltpu.VMEM((2, degrees, chans), F32),
-            pltpu.VMEM((4, TAP_ROWS, chans), F32),
-            pltpu.SemaphoreType.DMA((1 + 2 * slots * pieces,)),
+            pltpu.SemaphoreType.DMA((2 * slots * pieces,)),
         ],
         flops=2 * blocks * depth * lon_count * 2 * slots * chans,
-        out_specs=[HBM, HBM, HBM, VMEM],
+        out_specs=[HBM, HBM],
     )
     return (output[None], input_grad[None], filter_grad, tap_grad)
 

time: 56.6 us -> 55.9 us (0.988)
  waiting for transfers between devices: 12.8 us -> 12 us
    ppermute x12, waiting for transfers between devices: 12.4 us -> 11.7 us  [crossed(): return lax.ppermute(values, axis, [(i, i ^ distance) for i in range(count)])]
    pallas_call x9 -> x10, Pallas kernels: 17 us -> 17.2 us  [call(): pl.pallas_call(kernel, out_shape=out_shape, in_specs=in_specs, out_specs=...]
  transfers between devices with their start and end apart: 15 -> 15, of which waited for: 6 -> 7; matrix products, arithmetic and copies ran while one was open for 0% -> 0% of each run, Pallas kernels for 20% -> 22%
where the time goes in v6:
time: 55.9 us; the launch traced here: 55.8 us
  starting transfers between devices  25.6 us (46%)
  Pallas kernels  17.2 us (31%)
  waiting for transfers between devices  12 us (21%)
  between operations  0.88 us (2%)
    ppermute x12, starting transfers between devices, crossed(): return lax.ppermute(values, axis, [(i, i ^ distance) for i in range(count)])  22.9 us
    pallas_call x10, Pallas kernels, call(): pl.pallas_call(kernel, out_shape=out_shape, in_specs=in_specs, out_specs=...  17.2 us
    ppermute x12, waiting for transfers between devices, crossed(): return lax.ppermute(values, axis, [(i, i ^ distance) for i in range(count)])  11.7 us
    ppermute x2, starting transfers between devices, around(): lax.ppermute(parts[2], ('space', 'ens'), [(i, i ^ flip) for i in range(co...  2.05 us
  transfers between devices with their start and end apart: 15, of which 7 were waited for; matrix products, arithmetic and copies ran while one was open for 0% of the time, Pallas kernels for 22%

profile of v6, /device:TPU:0, one launch (start us, length us, event | category | flops | bytes accessed | tf_op | source)
XLA Modules:
  0.0 55.8 jit_solution(13328651482040411398)
XLA Ops:
  0.6 0.0 copy-start.1
  0.6 0.0 copy-start.6
  0.7 0.0 copy-start.9
  0.7 0.0 copy-start.2
  0.7 0.0 copy-start.4
  0.7 0.0 copy-start.3
  0.7 0.0 copy-start.7
  0.7 3.1 %shard_map.130 = (bf16[184,512]{1,0:T(8,128)(2,1)}, bf16[184,512]{1,0:T(8,128)(2,1)}, bf16[184,512]{1,0:T(8,128)(2,1)}, bf16[184,512]{1,0:T(8,128)(2,1)}) custom-call(bf16[2,768,128]{2,1,0:T(8,128)(2,1)} %bitcast.8, bf16[2,768,128]{2,1,0:T(8,128)(2,1)} %bitcast.5, bf16[4,184,768]{2,1,0:T(8,128)(2,1)} %constant.7.clone.table_hbm), custom_call_target="tpu_custom_call" | custom-call | flops 578813952 | bytes 1024 | tf_op jit(solution)/shard_map/pallas_call | solution.py:61
  3.8 0.0 copy-start.5
  3.8 0.0 copy-start.8
  3.8 5.1 %collective-permute-start.2 = (bf16[184,512]{1,0:T(8,128)(2,1)}, bf16[184,512]{1,0:T(8,128)(2,1)S(1)}, u32[]{:S(2)}, u32[]{:S(2)}) collective-permute-start(bf16[184,512]{1,0:T(8,128)(2,1)} %get-tuple-element.63), channel_id=1, source_target_pairs={{0,12},{4,8},{8,4},{12,0},{1,13},{5,9},{9,5},{13,1},{2,14},{6,10},... | collective-permute-start | bytes 565256 | tf_op jit(solution)/shard_map/ppermute | solution.py:512
  8.9 0.0 collective-permute-start
  8.9 0.6 %collective-permute-start.1 = (bf16[184,512]{1,0:T(8,128)(2,1)}, bf16[184,512]{1,0:T(8,128)(2,1)S(1)}, u32[]{:S(2)}, u32[]{:S(2)}) collective-permute-start(bf16[184,512]{1,0:T(8,128)(2,1)} %get-tuple-element.60), channel_id=1, source_target_pairs={{0,8},{4,12},{8,0},{12,4},{1,9},{5,13},{9,1},{13,5},{2,10},{6,14},... | collective-permute-start | bytes 565256 | tf_op jit(solution)/shard_map/ppermute | solution.py:512
  9.6 0.0 copy-done.9
  9.6 0.0 copy-done.1
  9.7 0.0 copy-done.6
  9.7 0.0 copy-done.2
  9.7 0.0 copy-done.4
  9.7 0.0 copy-done.3
  9.7 0.0 copy-done.7
  9.7 5.3 %shard_map.129 = (f32[2048,256]{1,0:T(8,128)S(1)}, bf16[384,2048]{1,0:T(8,128)(2,1)S(1)}, bf16[2,768,128]{2,1,0:T(8,128)(2,1)S(1)}, bf16[2,768,128]{2,1,0:T(8,12...) custom-call(s32[4]{0:T(128)S(1)} %copy-done.2, ...), custom_call_target="tpu_custom_call" | custom-call | flops 402653184 | bytes 2097152 | tf_op jit(solution)/shard_map/pallas_call | solution.py:61
  15.0 0.0 collective-permute-done.2.refs_3_
  15.0 4.5 %collective-permute-start.3 = (bf16[2,768,128]{2,1,0:T(8,128)(2,1)S(1)}, bf16[2,768,128]{2,1,0:T(8,128)(2,1)S(1)}, u32[]{:S(2)}, u32[]{:S(2)}) collective-permute-start(bf16[2,768,128]{2,1,0:T(8,128)(2,1)S(1)} %get-tuple-element.71), channel_id=1, source_target_pairs={{0,4},{4,0},{8,12},{12,8},{1,5},{5,1},{9,13},{13,9},{2,6},{6,2},{1... | collective-permute-start | bytes 1179656 | tf_op jit(solution)/shard_map/ppermute | solution.py:512
  19.4 0.7 %collective-permute-start.4 = (bf16[2,768,128]{2,1,0:T(8,128)(2,1)S(1)}, bf16[2,768,128]{2,1,0:T(8,128)(2,1)S(1)}, u32[]{:S(2)}, u32[]{:S(2)}) collective-permute-start(bf16[2,768,128]{2,1,0:T(8,128)(2,1)S(1)} %get-tuple-element.72), channel_id=1, source_target_pairs={{4,8},{8,4},{5,9},{9,5},{6,10},{10,6},{7,11},{11,7},{20,24},{24,20... | collective-permute-start | bytes 1179656 | tf_op jit(solution)/shard_map/ppermute | solution.py:589
  20.1 0.0 collective-permute-done.refs_1_
  20.1 6.0 %collective-permute-done.1.refs_2_ = bf16[184,512]{1,0:T(8,128)(2,1)S(1)} collective-permute-done((bf16[184,512]{1,0:T(8,128)(2,1)}, bf16[184,512]{1,0:T(8,128)(2,1)S(1)}, u32[]{:S(2)}, u32[]{:S(2)}) %collective-permute-start.1) | collective-permute-done | bytes 188448 | tf_op jit(solution)/shard_map/ppermute | solution.py:512
  26.1 0.0 copy-done.5
  26.1 0.0 copy-done.8
  26.1 1.9 %shard_map.131 = (f32[192,128]{1,0:T(8,128)S(1)}, bf16[192,128]{1,0:T(8,128)(2,1)S(1)}, bf16[192,128]{1,0:T(8,128)(2,1)S(1)}, bf16[192,128]{1,0:T(8,128)(2,1)S(1...) custom-call(s32[4]{0:T(128)S(1)} %copy-done.2, f32[6]{0:T(128)S(1)} %copy-done.5, ...), custom_call_target="tpu_custom_call" | custom-call | flops 4026531840 | bytes 1024 | tf_op jit(solution)/shard_map/pallas_call | solution.py:61
  28.1 0.9 %collective-permute-start.5 = (bf16[192,128]{1,0:T(8,128)(2,1)S(1)}, bf16[192,128]{1,0:T(8,128)(2,1)S(1)}, u32[]{:S(2)}, u32[]{:S(2)}) collective-permute-start(bf16[192,128]{1,0:T(8,128)(2,1)S(1)} %get-tuple-element.80), channel_id=1, source_target_pairs={{0,6},{2,4},{4,2},{6,0},{8,14},{10,12},{12,10},{14,8},{1,7},{3,5},... | collective-permute-start | bytes 147464 | tf_op jit(solution)/shard_map/ppermute | solution.py:521
  29.0 0.7 %collective-permute-start.6 = (bf16[192,128]{1,0:T(8,128)(2,1)S(1)}, bf16[192,128]{1,0:T(8,128)(2,1)S(1)}, u32[]{:S(2)}, u32[]{:S(2)}) collective-permute-start(bf16[192,128]{1,0:T(8,128)(2,1)S(1)} %get-tuple-element.81), channel_id=1, source_target_pairs={{0,2},{2,0},{1,3},{3,1},{4,6},{6,4},{5,7},{7,5},{8,10},{10,8},{9,1... | collective-permute-start | bytes 147464 | tf_op jit(solution)/shard_map/ppermute | solution.py:512
  29.7 1.9 %collective-permute-start.7 = (bf16[192,128]{1,0:T(8,128)(2,1)S(1)}, bf16[192,128]{1,0:T(8,128)(2,1)S(1)}, u32[]{:S(2)}, u32[]{:S(2)}) collective-permute-start(bf16[192,128]{1,0:T(8,128)(2,1)S(1)} %get-tuple-element.82), channel_id=1, source_target_pairs={{0,4},{4,0},{8,12},{12,8},{1,5},{5,1},{9,13},{13,9},{2,6},{6,2},{1... | collective-permute-start | bytes 147464 | tf_op jit(solution)/shard_map/ppermute | solution.py:512
  31.6 1.7 %shard_map.132 = (bf16[184,512]{1,0:T(8,128)(2,1)S(1)}, bf16[184,512]{1,0:T(8,128)(2,1)S(1)}, bf16[184,512]{1,0:T(8,128)(2,1)S(1)}, bf16[184,512]{1,0:T(8,128)(2,1)S(1)}) custom-call(s32[4]{0:T(128)S(1)} %copy-done.2, f32[6]{0:T(128)S(1)} %copy-done.5, f32[2048,256]{1,0:T(8,128)S(1)} %get-tuple-element.56.mixer_ref, ...), custom_call_target="tpu_custom_call" | custom-call | bytes 1024 | tf_op jit(solution)/shard_map/pallas_call | solution.py:61
  33.4 0.0 collective-permute-done.3.first_rim
  33.4 0.0 collective-permute-done.4.second_rim
  33.4 1.3 %shard_map.133 = (f32[2,768,128]{2,1,0:T(8,128)S(1)}, f32[2,768,128]{2,1,0:T(8,128)S(1)}, f32[16,128]{1,0:T(8,128)S(1)}) custom-call(s32[4]{0:T(128)S(1)} %copy-done.2, s32[6,9]{1,0:T(8,128)S(1)} %copy-done.3, bf16[2,768,128]{2,1,0:T(8,128)(2,1)S(1)} %bitcast.7, bf16[2,768,128]{2,1,0:T(8,128)(2,1)S(1)} %collective-permute-done.3.first_rim, ...), custom_call_target="tpu_custom_call" | custom-call | bytes 1024 | tf_op jit(solution)/shard_map/pallas_call | solution.py:61
  34.7 0.0 collective-permute-done.5.first_ref
  34.7 0.0 collective-permute-done.6.second_ref
  34.7 0.0 collective-permute-done.7.third_ref
  34.8 0.0 copy-start
  34.8 2.2 %collective-permute-start.8 = (bf16[224,128]{1,0:T(8,128)(2,1)S(1)}, bf16[224,128]{1,0:T(8,128)(2,1)S(1)}, u32[]{:S(2)}, u32[]{:S(2)}) collective-permute-start(bf16[224,128]{1,0:T(8,128)(2,1)S(1)} %shard_map.134.own_ref), channel_id=1, source_target_pairs={{0,8},{4,12},{8,0},{12,4},{1,9},{5,13},{9,1},{13,5},{2,10},{6,14},... | collective-permute-start | bytes 172040 | tf_op jit(solution)/shard_map/ppermute | solution.py:512
  37.0 1.0 %collective-permute-start.12 = (bf16[184,512]{1,0:T(8,128)(2,1)S(1)}, bf16[184,512]{1,0:T(8,128)(2,1)S(1)}, u32[]{:S(2)}, u32[]{:S(2)}) collective-permute-start(bf16[184,512]{1,0:T(8,128)(2,1)S(1)} %get-tuple-element.91), channel_id=1, source_target_pairs={{0,4},{4,0},{8,12},{12,8},{1,5},{5,1},{9,13},{13,9},{2,6},{6,2},{1... | collective-permute-start | bytes 565256 | tf_op jit(solution)/shard_map/ppermute | solution.py:512
  38.0 0.7 %collective-permute-start.13 = (bf16[184,512]{1,0:T(8,128)(2,1)S(1)}, bf16[184,512]{1,0:T(8,128)(2,1)S(1)}, u32[]{:S(2)}, u32[]{:S(2)}) collective-permute-start(bf16[184,512]{1,0:T(8,128)(2,1)S(1)} %get-tuple-element.95), channel_id=1, source_target_pairs={{0,8},{4,12},{8,0},{12,4},{1,9},{5,13},{9,1},{13,5},{2,10},{6,14},... | collective-permute-start | bytes 565256 | tf_op jit(solution)/shard_map/ppermute | solution.py:512
  38.7 2.6 %collective-permute-start.14 = (bf16[184,512]{1,0:T(8,128)(2,1)S(1)}, bf16[184,512]{1,0:T(8,128)(2,1)S(1)}, u32[]{:S(2)}, u32[]{:S(2)}) collective-permute-start(bf16[184,512]{1,0:T(8,128)(2,1)S(1)} %get-tuple-element.96), channel_id=1, source_target_pairs={{0,12},{4,8},{8,4},{12,0},{1,13},{5,9},{9,5},{13,1},{2,14},{6,10},... | collective-permute-start | bytes 565256 | tf_op jit(solution)/shard_map/ppermute | solution.py:512
  41.4 0.1 collective-permute-done.8.other_ref
  41.5 1.1 %collective-permute-start.11 = (bf16[224,128]{1,0:T(8,128)(2,1)S(1)}, bf16[224,128]{1,0:T(8,128)(2,1)S(1)}, u32[]{:S(2)}, u32[]{:S(2)}) collective-permute-start(bf16[224,128]{1,0:T(8,128)(2,1)S(1)} %shard_map.135.refs_0_), channel_id=1, source_target_pairs={{0,6},{2,4},{4,2},{6,0},{8,14},{10,12},{12,10},{14,8},{1,7},{3,5},... | collective-permute-start | bytes 172040 | tf_op jit(solution)/shard_map/ppermute | solution.py:521
  42.6 1.9 %collective-permute-start.10 = (bf16[224,128]{1,0:T(8,128)(2,1)S(1)}, bf16[224,128]{1,0:T(8,128)(2,1)S(1)}, u32[]{:S(2)}, u32[]{:S(2)}) collective-permute-start(bf16[224,128]{1,0:T(8,128)(2,1)S(1)} %shard_map.135.refs_0_), channel_id=1, source_target_pairs={{0,4},{4,0},{8,12},{12,8},{1,5},{5,1},{9,13},{13,9},{2,6},{6,2},{1... | collective-permute-start | bytes 172040 | tf_op jit(solution)/shard_map/ppermute | solution.py:512
  44.5 3.4 %collective-permute-done.12.near_ref = bf16[184,512]{1,0:T(8,128)(2,1)S(1)} collective-permute-done((bf16[184,512]{1,0:T(8,128)(2,1)S(1)}, bf16[184,512]{1,0:T(8,128)(2,1)S(1)}, u32[]{:S(2)}, u32[]{:S(2)}) %collective-permute-start.12) | collective-permute-done | bytes 188448 | tf_op jit(solution)/shard_map/ppermute | solution.py:512
  47.9 1.5 %collective-permute-start.9 = (bf16[224,128]{1,0:T(8,128)(2,1)S(1)}, bf16[224,128]{1,0:T(8,128)(2,1)S(1)}, u32[]{:S(2)}, u32[]{:S(2)}) collective-permute-start(bf16[224,128]{1,0:T(8,128)(2,1)S(1)} %shard_map.135.refs_0_), channel_id=1, source_target_pairs={{0,2},{2,0},{1,3},{3,1},{4,6},{6,4},{5,7},{7,5},{8,10},{10,8},{9,1... | collective-permute-start | bytes 172040 | tf_op jit(solution)/shard_map/ppermute | solution.py:512
  49.4 0.0 copy-done
  49.5 1.1 %shard_map.136 = (f32[2,768,128]{2,1,0:T(8,128)S(1)}, f32[2,768,128]{2,1,0:T(8,128)S(1)}) custom-call(s32[4]{0:T(128)S(1)} %copy-done.2, bf16[4,768,184]{2,1,0:T(8,128)(2,1)S(1)} %copy-done, f32[2,768,128]{2,1,0:T(8,128)S(1)} %get-tuple-element.85.base_ref, f32[2,768,128]{2,1,0:T(8,128)S(1)} %get-tuple-element.86.slope_ref, ...), custom_call_target="tpu_custom_call" | custom-call | bytes 1024 | tf_op jit(solution)/shard_map/pallas_call | solution.py:61
  50.6 0.3 collective-permute-done.11.refs_3_
  50.9 0.9 %collective-permute-done.10.refs_2_ = bf16[224,128]{1,0:T(8,128)(2,1)S(1)} collective-permute-done((bf16[224,128]{1,0:T(8,128)(2,1)S(1)}, bf16[224,128]{1,0:T(8,128)(2,1)S(1)}, u32[]{:S(2)}, u32[]{:S(2)}) %collective-permute-start.10) | collective-permute-done | bytes 57376 | tf_op jit(solution)/shard_map/ppermute | solution.py:512
  51.8 0.4 collective-permute-done.9.refs_1_
  52.1 0.8 %shard_map.137 = (f32[2,384,128]{2,1,0:T(8,128)}, f32[9,128]{1,0:T(8,128)}) custom-call(bf16[224,128]{1,0:T(8,128)(2,1)S(1)} %shard_map.135.refs_0_, bf16[224,128]{1,0:T(8,128)(2,1)S(1)} %collective-permute-done.9.refs_1_, bf16[224,128]{1,0:T(8,128)(2,1)S(1)} %collective-permute-done.10.refs_2_, bf16[224,128]{1,0:T(8,128)(2,1)S(1)} %collective-permute-done.11.refs_3_), custom_call_target="tpu_custom_call" | custom-call | bytes 1024 | tf_op jit(solution)/shard_map/pallas_call | solution.py:61
  52.9 0.9 %collective-permute-done.13.refs_0_ = bf16[184,512]{1,0:T(8,128)(2,1)S(1)} collective-permute-done((bf16[184,512]{1,0:T(8,128)(2,1)S(1)}, bf16[184,512]{1,0:T(8,128)(2,1)S(1)}, u32[]{:S(2)}, u32[]{:S(2)}) %collective-permute-start.13) | collective-permute-done | bytes 188448 | tf_op jit(solution)/shard_map/ppermute | solution.py:512
  53.8 0.0 collective-permute-done.14.refs_1_
  53.8 1.9 %shard_map.138 = (bf16[2,768,128]{2,1,0:T(8,128)(2,1)}, bf16[2,768,128]{2,1,0:T(8,128)(2,1)}) custom-call(s32[4]{0:T(128)S(1)} %copy-done.2, bf16[4,768,184]{2,1,0:T(8,128)(2,1)S(1)} %copy-done, f32[2,768,128]{2,1,0:T(8,128)S(1)} %get-tuple-element.93.sum_ref, f32[2,768,128]{2,1,0:T(8,128)S(1)} %get-tuple-element.94.early_ref, ...), custom_call_target="tpu_custom_call" | custom-call | flops 578813952 | bytes 1024 | tf_op jit(solution)/shard_map/pallas_call | solution.py:61
  (3 shorter events, 0.1 us)
Async XLA Ops:
  0.6 9.0 %copy-start.1 = (bf16[1,2,768,128]{3,2,1,0:T(8,128)(2,1)S(1)}, bf16[1,2,768,128]{3,2,1,0:T(8,128)(2,1)}, u32[]{:S(2)}) copy-start(bf16[1,2,768,128]{3,2,1,0:T(8,128)(2,1)} %param.11) | copy-start | bytes 1179652
  0.6 9.0 %copy-start.6 = (bf16[1,2,768,128]{3,2,1,0:T(8,128)(2,1)S(1)}, bf16[1,2,768,128]{3,2,1,0:T(8,128)(2,1)}, u32[]{:S(2)}) copy-start(bf16[1,2,768,128]{3,2,1,0:T(8,128)(2,1)} %param.10) | copy-start | bytes 1179652
  0.7 8.9 %copy-start.9 = (bf16[92,6,384]{2,0,1:T(8,128)(2,1)S(1)}, bf16[92,6,384]{2,0,1:T(8,128)(2,1)}, u32[]{:S(2)}) copy-start(bf16[92,6,384]{2,0,1:T(8,128)(2,1)} %param.15) | copy-start | bytes 1271812
  0.7 9.0 %copy-start.2 = (s32[4]{0:T(128)S(1)}, s32[4]{0:T(128)}, u32[]{:S(2)}) copy-start(s32[4]{0:T(128)} %rows_ref.11) | copy-start | bytes 52
  0.7 9.0 %copy-start.4 = (bf16[9,128]{1,0:T(8,128)(2,1)S(1)}, bf16[9,128]{1,0:T(8,128)(2,1)}, u32[]{:S(2)}) copy-start(bf16[9,128]{1,0:T(8,128)(2,1)} %taps_ref.3) | copy-start | bytes 6916
  0.7 9.0 %copy-start.3 = (s32[6,9]{1,0:T(8,128)S(1)}, s32[6,9]{1,0:T(8,128)}, u32[]{:S(2)}) copy-start(s32[6,9]{1,0:T(8,128)} %shift_ref.3) | copy-start | bytes 652
  0.7 9.0 %copy-start.7 = (bf16[2,384,128]{2,1,0:T(8,128)(2,1)S(1)}, bf16[2,384,128]{2,1,0:T(8,128)(2,1)}, u32[]{:S(2)}) copy-start(bf16[2,384,128]{2,1,0:T(8,128)(2,1)} %filter_ref.1) | copy-start | bytes 589828
  3.8 22.3 %copy-start.5 = (f32[6]{0:T(128)S(1)}, f32[6]{0:T(128)}, u32[]{:S(2)}) copy-start(f32[6]{0:T(128)} %quad_ref.3) | copy-start | bytes 76
  3.8 22.3 %copy-start.8 = (bf16[184,512]{1,0:T(8,128)(2,1)S(1)}, bf16[184,512]{1,0:T(8,128)(2,1)}, u32[]{:S(2)}) copy-start(bf16[184,512]{1,0:T(8,128)(2,1)} %get-tuple-element.58.refs_0_) | copy-start | bytes 565252
  3.8 11.1 %collective-permute-start.2 = (bf16[184,512]{1,0:T(8,128)(2,1)}, bf16[184,512]{1,0:T(8,128)(2,1)S(1)}, u32[]{:S(2)}, u32[]{:S(2)}) collective-permute-start(bf16[184,512]{1,0:T(8,128)(2,1)} %get-tuple-element.63), channel_id=1, source_target_pairs={{0,12},{4,8},{8,4},{12,0},{1,13},{5,9},{9,5},{13,1},{2,14},{6,10},... | collective-permute-start | bytes 565256 | tf_op jit(solution)/shard_map/ppermute | solution.py:512
  8.9 11.2 %collective-permute-start = (bf16[184,512]{1,0:T(8,128)(2,1)}, bf16[184,512]{1,0:T(8,128)(2,1)S(1)}, u32[]{:S(2)}, u32[]{:S(2)}) collective-permute-start(bf16[184,512]{1,0:T(8,128)(2,1)} %get-tuple-element.59), channel_id=1, source_target_pairs={{0,4},{4,0},{8,12},{12,8},{1,5},{5,1},{9,13},{13,9},{2,6},{6,2},{1... | collective-permute-start | bytes 565256 | tf_op jit(solution)/shard_map/ppermute | solution.py:512
  8.9 17.2 %collective-permute-start.1 = (bf16[184,512]{1,0:T(8,128)(2,1)}, bf16[184,512]{1,0:T(8,128)(2,1)S(1)}, u32[]{:S(2)}, u32[]{:S(2)}) collective-permute-start(bf16[184,512]{1,0:T(8,128)(2,1)} %get-tuple-element.60), channel_id=1, source_target_pairs={{0,8},{4,12},{8,0},{12,4},{1,9},{5,13},{9,1},{13,5},{2,10},{6,14},... | collective-permute-start | bytes 565256 | tf_op jit(solution)/shard_map/ppermute | solution.py:512
  15.0 18.4 %collective-permute-start.3 = (bf16[2,768,128]{2,1,0:T(8,128)(2,1)S(1)}, bf16[2,768,128]{2,1,0:T(8,128)(2,1)S(1)}, u32[]{:S(2)}, u32[]{:S(2)}) collective-permute-start(bf16[2,768,128]{2,1,0:T(8,128)(2,1)S(1)} %get-tuple-element.71), channel_id=1, source_target_pairs={{0,4},{4,0},{8,12},{12,8},{1,5},{5,1},{9,13},{13,9},{2,6},{6,2},{1... | collective-permute-start | bytes 1179656 | tf_op jit(solution)/shard_map/ppermute | solution.py:512
  19.4 13.9 %collective-permute-start.4 = (bf16[2,768,128]{2,1,0:T(8,128)(2,1)S(1)}, bf16[2,768,128]{2,1,0:T(8,128)(2,1)S(1)}, u32[]{:S(2)}, u32[]{:S(2)}) collective-permute-start(bf16[2,768,128]{2,1,0:T(8,128)(2,1)S(1)} %get-tuple-element.72), channel_id=1, source_target_pairs={{4,8},{8,4},{5,9},{9,5},{6,10},{10,6},{7,11},{11,7},{20,24},{24,20... | collective-permute-start | bytes 1179656 | tf_op jit(solution)/shard_map/ppermute | solution.py:589
  28.1 6.7 %collective-permute-start.5 = (bf16[192,128]{1,0:T(8,128)(2,1)S(1)}, bf16[192,128]{1,0:T(8,128)(2,1)S(1)}, u32[]{:S(2)}, u32[]{:S(2)}) collective-permute-start(bf16[192,128]{1,0:T(8,128)(2,1)S(1)} %get-tuple-element.80), channel_id=1, source_target_pairs={{0,6},{2,4},{4,2},{6,0},{8,14},{10,12},{12,10},{14,8},{1,7},{3,5},... | collective-permute-start | bytes 147464 | tf_op jit(solution)/shard_map/ppermute | solution.py:521
  29.0 5.7 %collective-permute-start.6 = (bf16[192,128]{1,0:T(8,128)(2,1)S(1)}, bf16[192,128]{1,0:T(8,128)(2,1)S(1)}, u32[]{:S(2)}, u32[]{:S(2)}) collective-permute-start(bf16[192,128]{1,0:T(8,128)(2,1)S(1)} %get-tuple-element.81), channel_id=1, source_target_pairs={{0,2},{2,0},{1,3},{3,1},{4,6},{6,4},{5,7},{7,5},{8,10},{10,8},{9,1... | collective-permute-start | bytes 147464 | tf_op jit(solution)/shard_map/ppermute | solution.py:512
  29.7 5.0 %collective-permute-start.7 = (bf16[192,128]{1,0:T(8,128)(2,1)S(1)}, bf16[192,128]{1,0:T(8,128)(2,1)S(1)}, u32[]{:S(2)}, u32[]{:S(2)}) collective-permute-start(bf16[192,128]{1,0:T(8,128)(2,1)S(1)} %get-tuple-element.82), channel_id=1, source_target_pairs={{0,4},{4,0},{8,12},{12,8},{1,5},{5,1},{9,13},{13,9},{2,6},{6,2},{1... | collective-permute-start | bytes 147464 | tf_op jit(solution)/shard_map/ppermute | solution.py:512
  34.8 14.7 %copy-start = (bf16[4,768,184]{2,1,0:T(8,128)(2,1)S(1)}, bf16[4,768,184]{2,1,0:T(8,128)(2,1)}, u32[]{:S(2)}) copy-start(bf16[4,768,184]{2,1,0:T(8,128)(2,1)} %constant.8.clone.table_ref) | copy-start | bytes 3391492
  34.8 6.7 %collective-permute-start.8 = (bf16[224,128]{1,0:T(8,128)(2,1)S(1)}, bf16[224,128]{1,0:T(8,128)(2,1)S(1)}, u32[]{:S(2)}, u32[]{:S(2)}) collective-permute-start(bf16[224,128]{1,0:T(8,128)(2,1)S(1)} %shard_map.134.own_ref), channel_id=1, source_target_pairs={{0,8},{4,12},{8,0},{12,4},{1,9},{5,13},{9,1},{13,5},{2,10},{6,14},... | collective-permute-start | bytes 172040 | tf_op jit(solution)/shard_map/ppermute | solution.py:512
  37.0 11.0 %collective-permute-start.12 = (bf16[184,512]{1,0:T(8,128)(2,1)S(1)}, bf16[184,512]{1,0:T(8,128)(2,1)S(1)}, u32[]{:S(2)}, u32[]{:S(2)}) collective-permute-start(bf16[184,512]{1,0:T(8,128)(2,1)S(1)} %get-tuple-element.91), channel_id=1, source_target_pairs={{0,4},{4,0},{8,12},{12,8},{1,5},{5,1},{9,13},{13,9},{2,6},{6,2},{1... | collective-permute-start | bytes 565256 | tf_op jit(solution)/shard_map/ppermute | solution.py:512
  38.0 15.8 %collective-permute-start.13 = (bf16[184,512]{1,0:T(8,128)(2,1)S(1)}, bf16[184,512]{1,0:T(8,128)(2,1)S(1)}, u32[]{:S(2)}, u32[]{:S(2)}) collective-permute-start(bf16[184,512]{1,0:T(8,128)(2,1)S(1)} %get-tuple-element.95), channel_id=1, source_target_pairs={{0,8},{4,12},{8,0},{12,4},{1,9},{5,13},{9,1},{13,5},{2,10},{6,14},... | collective-permute-start | bytes 565256 | tf_op jit(solution)/shard_map/ppermute | solution.py:512
  38.7 15.1 %collective-permute-start.14 = (bf16[184,512]{1,0:T(8,128)(2,1)S(1)}, bf16[184,512]{1,0:T(8,128)(2,1)S(1)}, u32[]{:S(2)}, u32[]{:S(2)}) collective-permute-start(bf16[184,512]{1,0:T(8,128)(2,1)S(1)} %get-tuple-element.96), channel_id=1, source_target_pairs={{0,12},{4,8},{8,4},{12,0},{1,13},{5,9},{9,5},{13,1},{2,14},{6,10},... | collective-permute-start | bytes 565256 | tf_op jit(solution)/shard_map/ppermute | solution.py:512
  41.5 9.4 %collective-permute-start.11 = (bf16[224,128]{1,0:T(8,128)(2,1)S(1)}, bf16[224,128]{1,0:T(8,128)(2,1)S(1)}, u32[]{:S(2)}, u32[]{:S(2)}) collective-permute-start(bf16[224,128]{1,0:T(8,128)(2,1)S(1)} %shard_map.135.refs_0_), channel_id=1, source_target_pairs={{0,6},{2,4},{4,2},{6,0},{8,14},{10,12},{12,10},{14,8},{1,7},{3,5},... | collective-permute-start | bytes 172040 | tf_op jit(solution)/shard_map/ppermute | solution.py:521
  42.6 9.2 %collective-permute-start.10 = (bf16[224,128]{1,0:T(8,128)(2,1)S(1)}, bf16[224,128]{1,0:T(8,128)(2,1)S(1)}, u32[]{:S(2)}, u32[]{:S(2)}) collective-permute-start(bf16[224,128]{1,0:T(8,128)(2,1)S(1)} %shard_map.135.refs_0_), channel_id=1, source_target_pairs={{0,4},{4,0},{8,12},{12,8},{1,5},{5,1},{9,13},{13,9},{2,6},{6,2},{1... | collective-permute-start | bytes 172040 | tf_op jit(solution)/shard_map/ppermute | solution.py:512
  47.9 4.2 %collective-permute-start.9 = (bf16[224,128]{1,0:T(8,128)(2,1)S(1)}, bf16[224,128]{1,0:T(8,128)(2,1)S(1)}, u32[]{:S(2)}, u32[]{:S(2)}) collective-permute-start(bf16[224,128]{1,0:T(8,128)(2,1)S(1)} %shard_map.135.refs_0_), channel_id=1, source_target_pairs={{0,2},{2,0},{1,3},{3,1},{4,6},{6,4},{5,7},{7,5},{8,10},{10,8},{9,1... | collective-permute-start | bytes 172040 | tf_op jit(solution)/shard_map/ppermute | solution.py:512

commit v7 on v6

--- a/solution.py
+++ b/solution.py
@@ -175,18 +175,18 @@
     padded_modes, chans = coeff.shape[2:]
     me = lax.axis_index("space")
     pairs = lat_pairs(lat_count)
-    padding = padded_modes - local_modes
-    if padding > 0:
-        zeros = jnp.zeros((padding, chans), F32)
+    whole = local_modes // 8 * 8
+    if padded_modes > whole:
+        zeros = jnp.zeros((padded_modes - whole, chans), F32)
         for lat in range(lat_count):
             for part in range(2):
-                coeff[lat, part, local_modes:, :] = zeros
-                grad[lat, part, local_modes:, :] = zeros
+                coeff[lat, part, whole:, :] = zeros
+                grad[lat, part, whole:, :] = zeros
 
     for shift in range(blocks):
         block = jnp.bitwise_xor(me, shift)
         start = first_row_of(rows_ref, block, blocks)
-        wide[shift] = ins[shift][...].astype(F32)
+        wide[shift, : ins[shift].shape[0], :] = ins[shift][...].astype(F32)
         for slot in range(slots):
             lat = jnp.minimum(start + slot, lat_count - 1)
 
@@ -194,10 +194,10 @@
             def _():
                 weight = quad_ref[lat]
                 for part in range(2):
-                    grad[lat, part, :local_modes, :] = wide[(shift, *place(slots, local_modes, chans, 0, slot, part))]
-                    coeff[lat, part, :local_modes, :] = (
-                        wide[(shift, *place(slots, local_modes, chans, 1, slot, part))] * weight
-                    )
+                    at = place(slots, local_modes, chans, 0, slot, part)
+                    grad[lat, part, :local_modes, :] = wide[(shift, *at)]
+                    at = place(slots, local_modes, chans, 1, slot, part)
+                    coeff[lat, part, :local_modes, :] = wide[(shift, *at)] * weight
 
     def multiply(i, carry):
         rows = pl.ds(pl.multiple_of(i * 8, 8), 8)
@@ -269,10 +269,8 @@
         return carry
 
     lax.fori_loop(0, padded_modes // 8, mix, 0)
-    if wide.shape[0] > 2 * local_modes:
-        wide[2 * local_modes :, :] = jnp.zeros(
-            (wide.shape[0] - 2 * local_modes, wide.shape[1]), F32
-        )
+    whole = 2 * local_modes // 8 * 8
+    wide[whole:, :] = jnp.zeros((wide.shape[0] - whole, wide.shape[1]), F32)
     for shift in range(blocks):
         block = jnp.bitwise_xor(me, shift)
         start = first_row_of(rows_ref, block, blocks)
@@ -283,7 +281,7 @@
                 wide[at] = synth[lat, part, :local_modes, :]
                 at = place(slots, local_modes, chans, 1, slot, part)
                 wide[at] = grad_coeff[lat, part, :local_modes, :]
-        outs[shift][...] = wide[...].astype(BF16)
+        outs[shift][...] = wide[: outs[shift].shape[0], :].astype(BF16)
 
 
 def disco_inner(
@@ -596,7 +594,7 @@
         scratch=[
             pltpu.VMEM((pair_rows, 2 * chans), F32),
             pltpu.VMEM((degrees, 2 * chans), F32),
-            pltpu.VMEM((blocks, *coded.shape), F32),
+            pltpu.VMEM((blocks, depth + 8, 2 * slots * chans), F32),
         ],
         limit=big,
         flops=20 * degrees * pair_rows * 2 * chans,
@@ -607,7 +605,7 @@
         [coded] * blocks,
         [SMEM, SMEM] + [VMEM] * 3,
         (band_rows, quad_weight, mixer, coeff, grad),
-        scratch=[pltpu.VMEM(spectral.shape, F32)] * 2 + [pltpu.VMEM(coded.shape, F32)],
+        scratch=[pltpu.VMEM(spectral.shape, F32)] * 2 + [pltpu.VMEM((depth + 8, 2 * slots * chans), F32)],
         limit=big,
     )
     rim_sum, rim_grad, tap_part = call(

time: 55.9 us -> 56 us (level)
  transfers between devices with their start and end apart: 15 -> 15, of which waited for: 7 -> 6; matrix products, arithmetic and copies ran while one was open for 0% -> 0% of each run, Pallas kernels for 22% -> 22%
where the time goes in v7:
time: 56 us; the launch traced here: 55.8 us
  starting transfers between devices  25.5 us (46%)
  Pallas kernels  17.3 us (31%)
  waiting for transfers between devices  12 us (21%)
  between operations  0.88 us (2%)
    ppermute x12, starting transfers between devices, crossed(): return lax.ppermute(values, axis, [(i, i ^ distance) for i in range(count)])  22.7 us
    pallas_call x10, Pallas kernels, call(): pl.pallas_call(kernel, out_shape=out_shape, in_specs=in_specs, out_specs=...  17.3 us
    ppermute x12, waiting for transfers between devices, crossed(): return lax.ppermute(values, axis, [(i, i ^ distance) for i in range(count)])  11.6 us
    ppermute x2, starting transfers between devices, around(): lax.ppermute(parts[2], ('space', 'ens'), [(i, i ^ flip) for i in range(co...  2.16 us
  transfers between devices with their start and end apart: 15, of which 6 were waited for; matrix products, arithmetic and copies ran while one was open for 0% of the time, Pallas kernels for 22%

profile of v7, /device:TPU:0, one launch (start us, length us, event | category | flops | bytes accessed | tf_op | source)
XLA Modules:
  0.0 55.8 jit_solution(12975935159739206158)
XLA Ops:
  0.6 0.0 copy-start.1
  0.6 0.0 copy-start.6
  0.7 0.0 copy-start.9
  0.7 0.0 copy-start.2
  0.7 0.0 copy-start.4
  0.7 0.0 copy-start.3
  0.7 0.0 copy-start.7
  0.7 3.1 %shard_map.130 = (bf16[184,512]{1,0:T(8,128)(2,1)}, bf16[184,512]{1,0:T(8,128)(2,1)}, bf16[184,512]{1,0:T(8,128)(2,1)}, bf16[184,512]{1,0:T(8,128)(2,1)}) custom-call(bf16[2,768,128]{2,1,0:T(8,128)(2,1)} %bitcast.8, bf16[2,768,128]{2,1,0:T(8,128)(2,1)} %bitcast.5, bf16[4,184,768]{2,1,0:T(8,128)(2,1)} %constant.7.clone.table_hbm), custom_call_target="tpu_custom_call" | custom-call | flops 578813952 | bytes 1024 | tf_op jit(solution)/shard_map/pallas_call | solution.py:61
  3.8 0.0 copy-start.5
  3.8 0.0 copy-start.8
  3.8 5.1 %collective-permute-start.2 = (bf16[184,512]{1,0:T(8,128)(2,1)}, bf16[184,512]{1,0:T(8,128)(2,1)S(1)}, u32[]{:S(2)}, u32[]{:S(2)}) collective-permute-start(bf16[184,512]{1,0:T(8,128)(2,1)} %get-tuple-element.63), channel_id=1, source_target_pairs={{0,12},{4,8},{8,4},{12,0},{1,13},{5,9},{9,5},{13,1},{2,14},{6,10},... | collective-permute-start | bytes 565256 | tf_op jit(solution)/shard_map/ppermute | solution.py:510
  8.9 0.0 collective-permute-start
  8.9 0.6 %collective-permute-start.1 = (bf16[184,512]{1,0:T(8,128)(2,1)}, bf16[184,512]{1,0:T(8,128)(2,1)S(1)}, u32[]{:S(2)}, u32[]{:S(2)}) collective-permute-start(bf16[184,512]{1,0:T(8,128)(2,1)} %get-tuple-element.60), channel_id=1, source_target_pairs={{0,8},{4,12},{8,0},{12,4},{1,9},{5,13},{9,1},{13,5},{2,10},{6,14},... | collective-permute-start | bytes 565256 | tf_op jit(solution)/shard_map/ppermute | solution.py:510
  9.6 0.0 copy-done.9
  9.6 0.0 copy-done.1
  9.7 0.0 copy-done.6
  9.7 0.0 copy-done.2
  9.7 0.0 copy-done.4
  9.7 0.0 copy-done.3
  9.7 0.0 copy-done.7
  9.7 5.3 %shard_map.129 = (f32[2048,256]{1,0:T(8,128)S(1)}, bf16[384,2048]{1,0:T(8,128)(2,1)S(1)}, bf16[2,768,128]{2,1,0:T(8,128)(2,1)S(1)}, bf16[2,768,128]{2,1,0:T(8,12...) custom-call(s32[4]{0:T(128)S(1)} %copy-done.2, ...), custom_call_target="tpu_custom_call" | custom-call | flops 402653184 | bytes 2097152 | tf_op jit(solution)/shard_map/pallas_call | solution.py:61
  15.0 0.0 collective-permute-done.2.refs_3_
  15.0 4.4 %collective-permute-start.3 = (bf16[2,768,128]{2,1,0:T(8,128)(2,1)S(1)}, bf16[2,768,128]{2,1,0:T(8,128)(2,1)S(1)}, u32[]{:S(2)}, u32[]{:S(2)}) collective-permute-start(bf16[2,768,128]{2,1,0:T(8,128)(2,1)S(1)} %get-tuple-element.71), channel_id=1, source_target_pairs={{0,4},{4,0},{8,12},{12,8},{1,5},{5,1},{9,13},{13,9},{2,6},{6,2},{1... | collective-permute-start | bytes 1179656 | tf_op jit(solution)/shard_map/ppermute | solution.py:510
  19.4 0.7 %collective-permute-start.4 = (bf16[2,768,128]{2,1,0:T(8,128)(2,1)S(1)}, bf16[2,768,128]{2,1,0:T(8,128)(2,1)S(1)}, u32[]{:S(2)}, u32[]{:S(2)}) collective-permute-start(bf16[2,768,128]{2,1,0:T(8,128)(2,1)S(1)} %get-tuple-element.72), channel_id=1, source_target_pairs={{4,8},{8,4},{5,9},{9,5},{6,10},{10,6},{7,11},{11,7},{20,24},{24,20... | collective-permute-start | bytes 1179656 | tf_op jit(solution)/shard_map/ppermute | solution.py:587
  20.1 0.0 collective-permute-done.refs_1_
  20.1 6.0 %collective-permute-done.1.refs_2_ = bf16[184,512]{1,0:T(8,128)(2,1)S(1)} collective-permute-done((bf16[184,512]{1,0:T(8,128)(2,1)}, bf16[184,512]{1,0:T(8,128)(2,1)S(1)}, u32[]{:S(2)}, u32[]{:S(2)}) %collective-permute-start.1) | collective-permute-done | bytes 188448 | tf_op jit(solution)/shard_map/ppermute | solution.py:510
  26.1 0.0 copy-done.5
  26.1 0.0 copy-done.8
  26.1 1.9 %shard_map.131 = (f32[192,128]{1,0:T(8,128)S(1)}, bf16[192,128]{1,0:T(8,128)(2,1)S(1)}, bf16[192,128]{1,0:T(8,128)(2,1)S(1)}, bf16[192,128]{1,0:T(8,128)(2,1)S(1...) custom-call(s32[4]{0:T(128)S(1)} %copy-done.2, f32[6]{0:T(128)S(1)} %copy-done.5, ...), custom_call_target="tpu_custom_call" | custom-call | flops 4026531840 | bytes 1024 | tf_op jit(solution)/shard_map/pallas_call | solution.py:61
  28.1 0.9 %collective-permute-start.5 = (bf16[192,128]{1,0:T(8,128)(2,1)S(1)}, bf16[192,128]{1,0:T(8,128)(2,1)S(1)}, u32[]{:S(2)}, u32[]{:S(2)}) collective-permute-start(bf16[192,128]{1,0:T(8,128)(2,1)S(1)} %get-tuple-element.80), channel_id=1, source_target_pairs={{0,6},{2,4},{4,2},{6,0},{8,14},{10,12},{12,10},{14,8},{1,7},{3,5},... | collective-permute-start | bytes 147464 | tf_op jit(solution)/shard_map/ppermute | solution.py:519
  29.0 0.7 %collective-permute-start.6 = (bf16[192,128]{1,0:T(8,128)(2,1)S(1)}, bf16[192,128]{1,0:T(8,128)(2,1)S(1)}, u32[]{:S(2)}, u32[]{:S(2)}) collective-permute-start(bf16[192,128]{1,0:T(8,128)(2,1)S(1)} %get-tuple-element.81), channel_id=1, source_target_pairs={{0,2},{2,0},{1,3},{3,1},{4,6},{6,4},{5,7},{7,5},{8,10},{10,8},{9,1... | collective-permute-start | bytes 147464 | tf_op jit(solution)/shard_map/ppermute | solution.py:510
  29.7 1.9 %collective-permute-start.7 = (bf16[192,128]{1,0:T(8,128)(2,1)S(1)}, bf16[192,128]{1,0:T(8,128)(2,1)S(1)}, u32[]{:S(2)}, u32[]{:S(2)}) collective-permute-start(bf16[192,128]{1,0:T(8,128)(2,1)S(1)} %get-tuple-element.82), channel_id=1, source_target_pairs={{0,4},{4,0},{8,12},{12,8},{1,5},{5,1},{9,13},{13,9},{2,6},{6,2},{1... | collective-permute-start | bytes 147464 | tf_op jit(solution)/shard_map/ppermute | solution.py:510
  31.6 1.7 %shard_map.132 = (bf16[184,512]{1,0:T(8,128)(2,1)S(1)}, bf16[184,512]{1,0:T(8,128)(2,1)S(1)}, bf16[184,512]{1,0:T(8,128)(2,1)S(1)}, bf16[184,512]{1,0:T(8,128)(2,1)S(1)}) custom-call(s32[4]{0:T(128)S(1)} %copy-done.2, f32[6]{0:T(128)S(1)} %copy-done.5, f32[2048,256]{1,0:T(8,128)S(1)} %get-tuple-element.56.mixer_ref, ...), custom_call_target="tpu_custom_call" | custom-call | bytes 1024 | tf_op jit(solution)/shard_map/pallas_call | solution.py:61
  33.4 0.0 collective-permute-done.3.first_rim
  33.4 0.0 collective-permute-done.4.second_rim
  33.4 1.3 %shard_map.133 = (f32[2,768,128]{2,1,0:T(8,128)S(1)}, f32[2,768,128]{2,1,0:T(8,128)S(1)}, f32[16,128]{1,0:T(8,128)S(1)}) custom-call(s32[4]{0:T(128)S(1)} %copy-done.2, s32[6,9]{1,0:T(8,128)S(1)} %copy-done.3, bf16[2,768,128]{2,1,0:T(8,128)(2,1)S(1)} %bitcast.7, bf16[2,768,128]{2,1,0:T(8,128)(2,1)S(1)} %collective-permute-done.3.first_rim, ...), custom_call_target="tpu_custom_call" | custom-call | bytes 1024 | tf_op jit(solution)/shard_map/pallas_call | solution.py:61
  34.7 0.0 collective-permute-done.5.first_ref
  34.7 0.0 collective-permute-done.6.second_ref
  34.7 0.0 collective-permute-done.7.third_ref
  34.8 0.0 copy-start
  34.8 2.2 %collective-permute-start.8 = (bf16[224,128]{1,0:T(8,128)(2,1)S(1)}, bf16[224,128]{1,0:T(8,128)(2,1)S(1)}, u32[]{:S(2)}, u32[]{:S(2)}) collective-permute-start(bf16[224,128]{1,0:T(8,128)(2,1)S(1)} %shard_map.134.own_ref), channel_id=1, source_target_pairs={{0,8},{4,12},{8,0},{12,4},{1,9},{5,13},{9,1},{13,5},{2,10},{6,14},... | collective-permute-start | bytes 172040 | tf_op jit(solution)/shard_map/ppermute | solution.py:510
  37.0 1.0 %collective-permute-start.12 = (bf16[184,512]{1,0:T(8,128)(2,1)S(1)}, bf16[184,512]{1,0:T(8,128)(2,1)S(1)}, u32[]{:S(2)}, u32[]{:S(2)}) collective-permute-start(bf16[184,512]{1,0:T(8,128)(2,1)S(1)} %get-tuple-element.91), channel_id=1, source_target_pairs={{0,4},{4,0},{8,12},{12,8},{1,5},{5,1},{9,13},{13,9},{2,6},{6,2},{1... | collective-permute-start | bytes 565256 | tf_op jit(solution)/shard_map/ppermute | solution.py:510
  38.0 0.7 %collective-permute-start.13 = (bf16[184,512]{1,0:T(8,128)(2,1)S(1)}, bf16[184,512]{1,0:T(8,128)(2,1)S(1)}, u32[]{:S(2)}, u32[]{:S(2)}) collective-permute-start(bf16[184,512]{1,0:T(8,128)(2,1)S(1)} %get-tuple-element.95), channel_id=1, source_target_pairs={{0,8},{4,12},{8,0},{12,4},{1,9},{5,13},{9,1},{13,5},{2,10},{6,14},... | collective-permute-start | bytes 565256 | tf_op jit(solution)/shard_map/ppermute | solution.py:510
  38.7 2.6 %collective-permute-start.14 = (bf16[184,512]{1,0:T(8,128)(2,1)S(1)}, bf16[184,512]{1,0:T(8,128)(2,1)S(1)}, u32[]{:S(2)}, u32[]{:S(2)}) collective-permute-start(bf16[184,512]{1,0:T(8,128)(2,1)S(1)} %get-tuple-element.96), channel_id=1, source_target_pairs={{0,12},{4,8},{8,4},{12,0},{1,13},{5,9},{9,5},{13,1},{2,14},{6,10},... | collective-permute-start | bytes 565256 | tf_op jit(solution)/shard_map/ppermute | solution.py:510
  41.4 0.0 collective-permute-done.8.other_ref
  41.4 1.2 %collective-permute-start.11 = (bf16[224,128]{1,0:T(8,128)(2,1)S(1)}, bf16[224,128]{1,0:T(8,128)(2,1)S(1)}, u32[]{:S(2)}, u32[]{:S(2)}) collective-permute-start(bf16[224,128]{1,0:T(8,128)(2,1)S(1)} %shard_map.135.refs_0_), channel_id=1, source_target_pairs={{0,6},{2,4},{4,2},{6,0},{8,14},{10,12},{12,10},{14,8},{1,7},{3,5},... | collective-permute-start | bytes 172040 | tf_op jit(solution)/shard_map/ppermute | solution.py:519
  42.6 1.8 %collective-permute-start.10 = (bf16[224,128]{1,0:T(8,128)(2,1)S(1)}, bf16[224,128]{1,0:T(8,128)(2,1)S(1)}, u32[]{:S(2)}, u32[]{:S(2)}) collective-permute-start(bf16[224,128]{1,0:T(8,128)(2,1)S(1)} %shard_map.135.refs_0_), channel_id=1, source_target_pairs={{0,4},{4,0},{8,12},{12,8},{1,5},{5,1},{9,13},{13,9},{2,6},{6,2},{1... | collective-permute-start | bytes 172040 | tf_op jit(solution)/shard_map/ppermute | solution.py:510
  44.4 3.4 %collective-permute-done.12.near_ref = bf16[184,512]{1,0:T(8,128)(2,1)S(1)} collective-permute-done((bf16[184,512]{1,0:T(8,128)(2,1)S(1)}, bf16[184,512]{1,0:T(8,128)(2,1)S(1)}, u32[]{:S(2)}, u32[]{:S(2)}) %collective-permute-start.12) | collective-permute-done | bytes 188448 | tf_op jit(solution)/shard_map/ppermute | solution.py:510
  47.8 1.5 %collective-permute-start.9 = (bf16[224,128]{1,0:T(8,128)(2,1)S(1)}, bf16[224,128]{1,0:T(8,128)(2,1)S(1)}, u32[]{:S(2)}, u32[]{:S(2)}) collective-permute-start(bf16[224,128]{1,0:T(8,128)(2,1)S(1)} %shard_map.135.refs_0_), channel_id=1, source_target_pairs={{0,2},{2,0},{1,3},{3,1},{4,6},{6,4},{5,7},{7,5},{8,10},{10,8},{9,1... | collective-permute-start | bytes 172040 | tf_op jit(solution)/shard_map/ppermute | solution.py:510
  49.3 0.0 copy-done
  49.3 1.1 %shard_map.136 = (f32[2,768,128]{2,1,0:T(8,128)S(1)}, f32[2,768,128]{2,1,0:T(8,128)S(1)}) custom-call(s32[4]{0:T(128)S(1)} %copy-done.2, bf16[4,768,184]{2,1,0:T(8,128)(2,1)S(1)} %copy-done, f32[2,768,128]{2,1,0:T(8,128)S(1)} %get-tuple-element.85.base_ref, f32[2,768,128]{2,1,0:T(8,128)S(1)} %get-tuple-element.86.slope_ref, ...), custom_call_target="tpu_custom_call" | custom-call | bytes 1024 | tf_op jit(solution)/shard_map/pallas_call | solution.py:61
  50.5 0.4 collective-permute-done.11.refs_3_
  50.8 0.6 %collective-permute-done.10.refs_2_ = bf16[224,128]{1,0:T(8,128)(2,1)S(1)} collective-permute-done((bf16[224,128]{1,0:T(8,128)(2,1)S(1)}, bf16[224,128]{1,0:T(8,128)(2,1)S(1)}, u32[]{:S(2)}, u32[]{:S(2)}) %collective-permute-start.10) | collective-permute-done | bytes 57376 | tf_op jit(solution)/shard_map/ppermute | solution.py:510
  51.5 0.5 collective-permute-done.9.refs_1_
  52.0 0.8 %shard_map.137 = (f32[2,384,128]{2,1,0:T(8,128)}, f32[9,128]{1,0:T(8,128)}) custom-call(bf16[224,128]{1,0:T(8,128)(2,1)S(1)} %shard_map.135.refs_0_, bf16[224,128]{1,0:T(8,128)(2,1)S(1)} %collective-permute-done.9.refs_1_, bf16[224,128]{1,0:T(8,128)(2,1)S(1)} %collective-permute-done.10.refs_2_, bf16[224,128]{1,0:T(8,128)(2,1)S(1)} %collective-permute-done.11.refs_3_), custom_call_target="tpu_custom_call" | custom-call | bytes 1024 | tf_op jit(solution)/shard_map/pallas_call | solution.py:61
  52.8 1.1 %collective-permute-done.13.refs_0_ = bf16[184,512]{1,0:T(8,128)(2,1)S(1)} collective-permute-done((bf16[184,512]{1,0:T(8,128)(2,1)S(1)}, bf16[184,512]{1,0:T(8,128)(2,1)S(1)}, u32[]{:S(2)}, u32[]{:S(2)}) %collective-permute-start.13) | collective-permute-done | bytes 188448 | tf_op jit(solution)/shard_map/ppermute | solution.py:510
  53.9 0.0 collective-permute-done.14.refs_1_
  53.9 1.9 %shard_map.138 = (bf16[2,768,128]{2,1,0:T(8,128)(2,1)}, bf16[2,768,128]{2,1,0:T(8,128)(2,1)}) custom-call(s32[4]{0:T(128)S(1)} %copy-done.2, bf16[4,768,184]{2,1,0:T(8,128)(2,1)S(1)} %copy-done, f32[2,768,128]{2,1,0:T(8,128)S(1)} %get-tuple-element.93.sum_ref, f32[2,768,128]{2,1,0:T(8,128)S(1)} %get-tuple-element.94.early_ref, ...), custom_call_target="tpu_custom_call" | custom-call | flops 578813952 | bytes 1024 | tf_op jit(solution)/shard_map/pallas_call | solution.py:61
  (3 shorter events, 0.1 us)
Async XLA Ops:
  0.6 9.0 %copy-start.1 = (bf16[1,2,768,128]{3,2,1,0:T(8,128)(2,1)S(1)}, bf16[1,2,768,128]{3,2,1,0:T(8,128)(2,1)}, u32[]{:S(2)}) copy-start(bf16[1,2,768,128]{3,2,1,0:T(8,128)(2,1)} %param.11) | copy-start | bytes 1179652
  0.6 9.0 %copy-start.6 = (bf16[1,2,768,128]{3,2,1,0:T(8,128)(2,1)S(1)}, bf16[1,2,768,128]{3,2,1,0:T(8,128)(2,1)}, u32[]{:S(2)}) copy-start(bf16[1,2,768,128]{3,2,1,0:T(8,128)(2,1)} %param.10) | copy-start | bytes 1179652
  0.7 8.9 %copy-start.9 = (bf16[92,6,384]{2,0,1:T(8,128)(2,1)S(1)}, bf16[92,6,384]{2,0,1:T(8,128)(2,1)}, u32[]{:S(2)}) copy-start(bf16[92,6,384]{2,0,1:T(8,128)(2,1)} %param.15) | copy-start | bytes 1271812
  0.7 9.0 %copy-start.2 = (s32[4]{0:T(128)S(1)}, s32[4]{0:T(128)}, u32[]{:S(2)}) copy-start(s32[4]{0:T(128)} %rows_ref.11) | copy-start | bytes 52
  0.7 9.0 %copy-start.4 = (bf16[9,128]{1,0:T(8,128)(2,1)S(1)}, bf16[9,128]{1,0:T(8,128)(2,1)}, u32[]{:S(2)}) copy-start(bf16[9,128]{1,0:T(8,128)(2,1)} %taps_ref.3) | copy-start | bytes 6916
  0.7 9.0 %copy-start.3 = (s32[6,9]{1,0:T(8,128)S(1)}, s32[6,9]{1,0:T(8,128)}, u32[]{:S(2)}) copy-start(s32[6,9]{1,0:T(8,128)} %shift_ref.3) | copy-start | bytes 652
  0.7 9.0 %copy-start.7 = (bf16[2,384,128]{2,1,0:T(8,128)(2,1)S(1)}, bf16[2,384,128]{2,1,0:T(8,128)(2,1)}, u32[]{:S(2)}) copy-start(bf16[2,384,128]{2,1,0:T(8,128)(2,1)} %filter_ref.1) | copy-start | bytes 589828
  3.8 22.3 %copy-start.5 = (f32[6]{0:T(128)S(1)}, f32[6]{0:T(128)}, u32[]{:S(2)}) copy-start(f32[6]{0:T(128)} %quad_ref.3) | copy-start | bytes 76
  3.8 22.3 %copy-start.8 = (bf16[184,512]{1,0:T(8,128)(2,1)S(1)}, bf16[184,512]{1,0:T(8,128)(2,1)}, u32[]{:S(2)}) copy-start(bf16[184,512]{1,0:T(8,128)(2,1)} %get-tuple-element.58.refs_0_) | copy-start | bytes 565252
  3.8 11.2 %collective-permute-start.2 = (bf16[184,512]{1,0:T(8,128)(2,1)}, bf16[184,512]{1,0:T(8,128)(2,1)S(1)}, u32[]{:S(2)}, u32[]{:S(2)}) collective-permute-start(bf16[184,512]{1,0:T(8,128)(2,1)} %get-tuple-element.63), channel_id=1, source_target_pairs={{0,12},{4,8},{8,4},{12,0},{1,13},{5,9},{9,5},{13,1},{2,14},{6,10},... | collective-permute-start | bytes 565256 | tf_op jit(solution)/shard_map/ppermute | solution.py:510
  8.9 11.2 %collective-permute-start = (bf16[184,512]{1,0:T(8,128)(2,1)}, bf16[184,512]{1,0:T(8,128)(2,1)S(1)}, u32[]{:S(2)}, u32[]{:S(2)}) collective-permute-start(bf16[184,512]{1,0:T(8,128)(2,1)} %get-tuple-element.59), channel_id=1, source_target_pairs={{0,4},{4,0},{8,12},{12,8},{1,5},{5,1},{9,13},{13,9},{2,6},{6,2},{1... | collective-permute-start | bytes 565256 | tf_op jit(solution)/shard_map/ppermute | solution.py:510
  8.9 17.2 %collective-permute-start.1 = (bf16[184,512]{1,0:T(8,128)(2,1)}, bf16[184,512]{1,0:T(8,128)(2,1)S(1)}, u32[]{:S(2)}, u32[]{:S(2)}) collective-permute-start(bf16[184,512]{1,0:T(8,128)(2,1)} %get-tuple-element.60), channel_id=1, source_target_pairs={{0,8},{4,12},{8,0},{12,4},{1,9},{5,13},{9,1},{13,5},{2,10},{6,14},... | collective-permute-start | bytes 565256 | tf_op jit(solution)/shard_map/ppermute | solution.py:510
  15.0 18.4 %collective-permute-start.3 = (bf16[2,768,128]{2,1,0:T(8,128)(2,1)S(1)}, bf16[2,768,128]{2,1,0:T(8,128)(2,1)S(1)}, u32[]{:S(2)}, u32[]{:S(2)}) collective-permute-start(bf16[2,768,128]{2,1,0:T(8,128)(2,1)S(1)} %get-tuple-element.71), channel_id=1, source_target_pairs={{0,4},{4,0},{8,12},{12,8},{1,5},{5,1},{9,13},{13,9},{2,6},{6,2},{1... | collective-permute-start | bytes 1179656 | tf_op jit(solution)/shard_map/ppermute | solution.py:510
  19.4 13.9 %collective-permute-start.4 = (bf16[2,768,128]{2,1,0:T(8,128)(2,1)S(1)}, bf16[2,768,128]{2,1,0:T(8,128)(2,1)S(1)}, u32[]{:S(2)}, u32[]{:S(2)}) collective-permute-start(bf16[2,768,128]{2,1,0:T(8,128)(2,1)S(1)} %get-tuple-element.72), channel_id=1, source_target_pairs={{4,8},{8,4},{5,9},{9,5},{6,10},{10,6},{7,11},{11,7},{20,24},{24,20... | collective-permute-start | bytes 1179656 | tf_op jit(solution)/shard_map/ppermute | solution.py:587
  28.1 6.7 %collective-permute-start.5 = (bf16[192,128]{1,0:T(8,128)(2,1)S(1)}, bf16[192,128]{1,0:T(8,128)(2,1)S(1)}, u32[]{:S(2)}, u32[]{:S(2)}) collective-permute-start(bf16[192,128]{1,0:T(8,128)(2,1)S(1)} %get-tuple-element.80), channel_id=1, source_target_pairs={{0,6},{2,4},{4,2},{6,0},{8,14},{10,12},{12,10},{14,8},{1,7},{3,5},... | collective-permute-start | bytes 147464 | tf_op jit(solution)/shard_map/ppermute | solution.py:519
  29.0 5.8 %collective-permute-start.6 = (bf16[192,128]{1,0:T(8,128)(2,1)S(1)}, bf16[192,128]{1,0:T(8,128)(2,1)S(1)}, u32[]{:S(2)}, u32[]{:S(2)}) collective-permute-start(bf16[192,128]{1,0:T(8,128)(2,1)S(1)} %get-tuple-element.81), channel_id=1, source_target_pairs={{0,2},{2,0},{1,3},{3,1},{4,6},{6,4},{5,7},{7,5},{8,10},{10,8},{9,1... | collective-permute-start | bytes 147464 | tf_op jit(solution)/shard_map/ppermute | solution.py:510
  29.7 5.0 %collective-permute-start.7 = (bf16[192,128]{1,0:T(8,128)(2,1)S(1)}, bf16[192,128]{1,0:T(8,128)(2,1)S(1)}, u32[]{:S(2)}, u32[]{:S(2)}) collective-permute-start(bf16[192,128]{1,0:T(8,128)(2,1)S(1)} %get-tuple-element.82), channel_id=1, source_target_pairs={{0,4},{4,0},{8,12},{12,8},{1,5},{5,1},{9,13},{13,9},{2,6},{6,2},{1... | collective-permute-start | bytes 147464 | tf_op jit(solution)/shard_map/ppermute | solution.py:510
  34.8 14.5 %copy-start = (bf16[4,768,184]{2,1,0:T(8,128)(2,1)S(1)}, bf16[4,768,184]{2,1,0:T(8,128)(2,1)}, u32[]{:S(2)}) copy-start(bf16[4,768,184]{2,1,0:T(8,128)(2,1)} %constant.8.clone.table_ref) | copy-start | bytes 3391492
  34.8 6.6 %collective-permute-start.8 = (bf16[224,128]{1,0:T(8,128)(2,1)S(1)}, bf16[224,128]{1,0:T(8,128)(2,1)S(1)}, u32[]{:S(2)}, u32[]{:S(2)}) collective-permute-start(bf16[224,128]{1,0:T(8,128)(2,1)S(1)} %shard_map.134.own_ref), channel_id=1, source_target_pairs={{0,8},{4,12},{8,0},{12,4},{1,9},{5,13},{9,1},{13,5},{2,10},{6,14},... | collective-permute-start | bytes 172040 | tf_op jit(solution)/shard_map/ppermute | solution.py:510
  37.0 10.8 %collective-permute-start.12 = (bf16[184,512]{1,0:T(8,128)(2,1)S(1)}, bf16[184,512]{1,0:T(8,128)(2,1)S(1)}, u32[]{:S(2)}, u32[]{:S(2)}) collective-permute-start(bf16[184,512]{1,0:T(8,128)(2,1)S(1)} %get-tuple-element.91), channel_id=1, source_target_pairs={{0,4},{4,0},{8,12},{12,8},{1,5},{5,1},{9,13},{13,9},{2,6},{6,2},{1... | collective-permute-start | bytes 565256 | tf_op jit(solution)/shard_map/ppermute | solution.py:510
  38.0 15.8 %collective-permute-start.13 = (bf16[184,512]{1,0:T(8,128)(2,1)S(1)}, bf16[184,512]{1,0:T(8,128)(2,1)S(1)}, u32[]{:S(2)}, u32[]{:S(2)}) collective-permute-start(bf16[184,512]{1,0:T(8,128)(2,1)S(1)} %get-tuple-element.95), channel_id=1, source_target_pairs={{0,8},{4,12},{8,0},{12,4},{1,9},{5,13},{9,1},{13,5},{2,10},{6,14},... | collective-permute-start | bytes 565256 | tf_op jit(solution)/shard_map/ppermute | solution.py:510
  38.7 15.1 %collective-permute-start.14 = (bf16[184,512]{1,0:T(8,128)(2,1)S(1)}, bf16[184,512]{1,0:T(8,128)(2,1)S(1)}, u32[]{:S(2)}, u32[]{:S(2)}) collective-permute-start(bf16[184,512]{1,0:T(8,128)(2,1)S(1)} %get-tuple-element.96), channel_id=1, source_target_pairs={{0,12},{4,8},{8,4},{12,0},{1,13},{5,9},{9,5},{13,1},{2,14},{6,10},... | collective-permute-start | bytes 565256 | tf_op jit(solution)/shard_map/ppermute | solution.py:510
  41.4 9.4 %collective-permute-start.11 = (bf16[224,128]{1,0:T(8,128)(2,1)S(1)}, bf16[224,128]{1,0:T(8,128)(2,1)S(1)}, u32[]{:S(2)}, u32[]{:S(2)}) collective-permute-start(bf16[224,128]{1,0:T(8,128)(2,1)S(1)} %shard_map.135.refs_0_), channel_id=1, source_target_pairs={{0,6},{2,4},{4,2},{6,0},{8,14},{10,12},{12,10},{14,8},{1,7},{3,5},... | collective-permute-start | bytes 172040 | tf_op jit(solution)/shard_map/ppermute | solution.py:519
  42.6 8.8 %collective-permute-start.10 = (bf16[224,128]{1,0:T(8,128)(2,1)S(1)}, bf16[224,128]{1,0:T(8,128)(2,1)S(1)}, u32[]{:S(2)}, u32[]{:S(2)}) collective-permute-start(bf16[224,128]{1,0:T(8,128)(2,1)S(1)} %shard_map.135.refs_0_), channel_id=1, source_target_pairs={{0,4},{4,0},{8,12},{12,8},{1,5},{5,1},{9,13},{13,9},{2,6},{6,2},{1... | collective-permute-start | bytes 172040 | tf_op jit(solution)/shard_map/ppermute | solution.py:510
  47.8 4.2 %collective-permute-start.9 = (bf16[224,128]{1,0:T(8,128)(2,1)S(1)}, bf16[224,128]{1,0:T(8,128)(2,1)S(1)}, u32[]{:S(2)}, u32[]{:S(2)}) collective-permute-start(bf16[224,128]{1,0:T(8,128)(2,1)S(1)} %shard_map.135.refs_0_), channel_id=1, source_target_pairs={{0,2},{2,0},{1,3},{3,1},{4,6},{6,4},{5,7},{7,5},{8,10},{10,8},{9,1... | collective-permute-start | bytes 172040 | tf_op jit(solution)/shard_map/ppermute | solution.py:510

commit v8 on v7

--- a/solution.py
+++ b/solution.py
@@ -346,11 +346,44 @@
     tap_ref[...] = jnp.concatenate(lines, axis=0)
 
 
-def rim_kernel(
-    blocks, rows_ref, shift_ref, dy_ref, first_rim, second_rim, taps_ref, inner_ref,
-    rim_ref, rim_grad_ref, tap_ref, acts, grads,
+def rim_tap_kernel(
+    blocks, rows_ref, shift_ref, dy_ref, first_rim, second_rim, inner_ref, tap_ref, acts,
 ):
     _, lon_count, chans = dy_ref.shape
+    me = lax.axis_index("space")
+    live = rows_ref[me]
+    start = first_row_of(rows_ref, me, blocks)
+    odd = jnp.bitwise_and(me, 1)
+    for source, row in ((first_rim, 1 - odd), (second_rim, odd)):
+        wrapped(acts, row, source[0].astype(F32))
+    step = 256 if lon_count % 256 == 0 else lon_count
+    top = shift_ref.shape[0] - 1
+    lines = [jnp.zeros((1, chans), F32)] * tap_ref.shape[0]
+    for side in range(2):
+        slot = 0 if side == 0 else live - 1
+        lat = jnp.clip(start + slot, 0, top)
+        ahead = [(t, REACH + shift_ref[lat, t]) for t in range(6 * side, 6 * side + 3)]
+
+        def rim(i, totals):
+            at = pl.multiple_of(i * step, step)
+            part = pl.ds(at, step)
+            dy = dy_ref[slot, part, :].astype(F32)
+            fresh = []
+            for total, (t, first) in zip(totals, ahead):
+                moved = acts[side, pl.ds(at + first, step), :]
+                fresh.append(total + folded(moved * dy))
+            return tuple(fresh)
+
+        totals = lax.fori_loop(0, lon_count // step, rim, (jnp.zeros((8, chans), F32),) * 3)
+        for (t, _), total in zip(ahead, totals):
+            lines[t] = jnp.sum(total, axis=0, keepdims=True)
+    tap_ref[...] = inner_ref[...] + jnp.concatenate(lines, axis=0)
+
+
+def rim_kernel(
+    blocks, rows_ref, shift_ref, first_rim, second_rim, taps_ref, rim_ref, rim_grad_ref, acts, grads,
+):
+    _, lon_count, chans = first_rim.shape
     me = lax.axis_index("space")
     live = rows_ref[me]
     start = first_row_of(rows_ref, me, blocks)
@@ -361,7 +394,6 @@
     weights = taps_ref[...].astype(F32)
     step = 128 if lon_count % 128 == 0 else lon_count
     top = shift_ref.shape[0] - 1
-    lines = [jnp.zeros((1, chans), F32)] * tap_ref.shape[0]
     for side in range(2):
         slot = 0 if side == 0 else live - 1
         lat = jnp.clip(start + slot, 0, top)
@@ -369,26 +401,20 @@
         ahead = [(t, REACH + shift_ref[lat, t]) for t in range(6 * side, 6 * side + 3)]
         behind = [(t, REACH - shift_ref[other, t]) for t in range(6 - 6 * side, 9 - 6 * side)]
 
-        def rim(i, totals):
+        def rim(i, carry):
             at = pl.multiple_of(i * step, step)
             part = pl.ds(at, step)
-            dy = dy_ref[slot, part, :].astype(F32)
             out = back = jnp.zeros((step, chans), F32)
-            fresh = []
-            for total, (t, first) in zip(totals, ahead):
+            for t, first in ahead:
                 moved = acts[side, pl.ds(at + first, step), :]
                 out = out + moved * weights[t : t + 1, :]
-                fresh.append(total + folded(moved * dy))
             for t, first in behind:
                 back = back + grads[side, pl.ds(at + first, step), :] * weights[t : t + 1, :]
             rim_ref[side, part, :] = out
             rim_grad_ref[side, part, :] = back
-            return tuple(fresh)
-
-        totals = lax.fori_loop(0, lon_count // step, rim, (jnp.zeros((8, chans), F32),) * 3)
-        for (t, _), total in zip(ahead, totals):
-            lines[t] = jnp.sum(total, axis=0, keepdims=True)
-    tap_ref[...] = inner_ref[...] + jnp.concatenate(lines, axis=0)
+            return carry
+
+        lax.fori_loop(0, lon_count // step, rim, 0)
 
 
 def split_taps(taps, out_ref, count):
@@ -608,13 +634,14 @@
         scratch=[pltpu.VMEM(spectral.shape, F32)] * 2 + [pltpu.VMEM((depth + 8, 2 * slots * chans), F32)],
         limit=big,
     )
-    rim_sum, rim_grad, tap_part = call(
-        functools.partial(rim_kernel, blocks),
-        [shape((2, lon_count, chans), F32)] * 2 + [tap_shape],
-        [SMEM, SMEM] + [VMEM] * 5,
-        (band_rows, tap_shift, dy, first_rim, second_rim, tap_weight, tap_part),
-        scratch=[pltpu.VMEM((2, *padded), F32)] * 2,
-    )
+    tap_part = call(
+        functools.partial(rim_tap_kernel, blocks),
+        tap_shape,
+        [SMEM, SMEM] + [VMEM] * 4,
+        (band_rows, tap_shift, dy, first_rim, second_rim, tap_part),
+        scratch=[pltpu.VMEM((2, *padded), F32)],
+    )
+    back_parts, tap_part = lax.optimization_barrier((back_parts, tap_part))
     message = shape((share + 2 * TAP_ROWS, chans), BF16)
     back_parts, tap_part = lax.optimization_barrier((back_parts, tap_part))
     own = call(quarter_kernel, message, [VMEM] * 5, (keep, *[got_sums[at] for at in (2, 0, 1)], tap_part))
@@ -632,6 +659,13 @@
             flops=3900000000 if at == 0 else 0,
         )
     quarters = [own, *around([own] * 3)]
+    rim_sum, rim_grad = call(
+        functools.partial(rim_kernel, blocks),
+        [shape((2, lon_count, chans), F32)] * 2,
+        [SMEM, SMEM] + [VMEM] * 3,
+        (band_rows, tap_shift, first_rim, second_rim, tap_weight),
+        scratch=[pltpu.VMEM((2, *padded), F32)] * 2,
+    )
     early_sum, early_grad = call(
         early_kernel,
         [field, field],

time: 56 us -> 55.6 us (level)
  waiting for transfers between devices: 12 us -> 10.4 us
  Pallas kernels: 17.3 us -> 18.1 us
    ppermute x12, waiting for transfers between devices: 11.6 us -> 10.4 us  [crossed(): return lax.ppermute(values, axis, [(i, i ^ distance) for i in range(count)])]
    pallas_call x10 -> x11, Pallas kernels: 17.3 us -> 18.1 us  [call(): pl.pallas_call(kernel, out_shape=out_shape, in_specs=in_specs, out_specs=...]
  transfers between devices with their start and end apart: 15 -> 15, of which waited for: 6 -> 4; matrix products, arithmetic and copies ran while one was open for 0% -> 0% of each run, Pallas kernels for 22% -> 24%
where the time goes in v8:
time: 55.6 us; the launch traced here: 55.3 us
  starting transfers between devices  25.9 us (47%)
  Pallas kernels  18.1 us (33%)
  waiting for transfers between devices  10.4 us (19%)
  between operations  0.9 us (2%)
    ppermute x12, starting transfers between devices, crossed(): return lax.ppermute(values, axis, [(i, i ^ distance) for i in range(count)])  22.7 us
    pallas_call x11, Pallas kernels, call(): pl.pallas_call(kernel, out_shape=out_shape, in_specs=in_specs, out_specs=...  18.1 us
    ppermute x12, waiting for transfers between devices, crossed(): return lax.ppermute(values, axis, [(i, i ^ distance) for i in range(count)])  10.4 us
    ppermute x2, starting transfers between devices, around(): lax.ppermute(parts[2], ('space', 'ens'), [(i, i ^ flip) for i in range(co...  2.48 us
  transfers between devices with their start and end apart: 15, of which 4 were waited for; matrix products, arithmetic and copies ran while one was open for 0% of the time, Pallas kernels for 24%

profile of v8, /device:TPU:0, one launch (start us, length us, event | category | flops | bytes accessed | tf_op | source)
XLA Modules:
  0.0 55.3 jit_solution(14339341456554519469)
XLA Ops:
  0.6 0.0 copy-start.1
  0.6 0.0 copy-start.6
  0.7 0.0 copy-start.9
  0.7 0.0 copy-start.3
  0.7 0.0 copy-start.2
  0.7 0.0 copy-start.4
  0.7 0.0 copy-start.7
  0.7 3.1 %shard_map.130 = (bf16[184,512]{1,0:T(8,128)(2,1)}, bf16[184,512]{1,0:T(8,128)(2,1)}, bf16[184,512]{1,0:T(8,128)(2,1)}, bf16[184,512]{1,0:T(8,128)(2,1)}) custom-call(bf16[2,768,128]{2,1,0:T(8,128)(2,1)} %bitcast.8, bf16[2,768,128]{2,1,0:T(8,128)(2,1)} %bitcast.5, bf16[4,184,768]{2,1,0:T(8,128)(2,1)} %constant.7.clone.table_hbm), custom_call_target="tpu_custom_call" | custom-call | flops 578813952 | bytes 1024 | tf_op jit(solution)/shard_map/pallas_call | solution.py:61
  3.8 0.0 copy-start.5
  3.8 0.0 copy-start.8
  3.8 5.1 %collective-permute-start.2 = (bf16[184,512]{1,0:T(8,128)(2,1)}, bf16[184,512]{1,0:T(8,128)(2,1)S(1)}, u32[]{:S(2)}, u32[]{:S(2)}) collective-permute-start(bf16[184,512]{1,0:T(8,128)(2,1)} %get-tuple-element.62), channel_id=1, source_target_pairs={{0,12},{4,8},{8,4},{12,0},{1,13},{5,9},{9,5},{13,1},{2,14},{6,10},... | collective-permute-start | bytes 565256 | tf_op jit(solution)/shard_map/ppermute | solution.py:536
  8.9 0.0 collective-permute-start
  8.9 0.6 %collective-permute-start.1 = (bf16[184,512]{1,0:T(8,128)(2,1)}, bf16[184,512]{1,0:T(8,128)(2,1)S(1)}, u32[]{:S(2)}, u32[]{:S(2)}) collective-permute-start(bf16[184,512]{1,0:T(8,128)(2,1)} %get-tuple-element.59), channel_id=1, source_target_pairs={{0,8},{4,12},{8,0},{12,4},{1,9},{5,13},{9,1},{13,5},{2,10},{6,14},... | collective-permute-start | bytes 565256 | tf_op jit(solution)/shard_map/ppermute | solution.py:536
  9.6 0.0 copy-done.9
  9.6 0.0 copy-done.1
  9.7 0.0 copy-done.6
  9.7 0.0 copy-done.3
  9.7 0.0 copy-done.2
  9.7 0.0 copy-done.4
  9.7 0.0 copy-done.7
  9.7 5.3 %shard_map.129 = (f32[2048,256]{1,0:T(8,128)S(1)}, bf16[384,2048]{1,0:T(8,128)(2,1)S(1)}, bf16[2,768,128]{2,1,0:T(8,128)(2,1)S(1)}, bf16[2,768,128]{2,1,0:T(8,12...) custom-call(s32[4]{0:T(128)S(1)} %copy-done.3, ...), custom_call_target="tpu_custom_call" | custom-call | flops 402653184 | bytes 2097152 | tf_op jit(solution)/shard_map/pallas_call | solution.py:61
  15.0 0.0 collective-permute-done.2.refs_3_
  15.0 4.4 %collective-permute-start.3 = (bf16[2,768,128]{2,1,0:T(8,128)(2,1)S(1)}, bf16[2,768,128]{2,1,0:T(8,128)(2,1)S(1)}, u32[]{:S(2)}, u32[]{:S(2)}) collective-permute-start(bf16[2,768,128]{2,1,0:T(8,128)(2,1)S(1)} %get-tuple-element.70), channel_id=1, source_target_pairs={{0,4},{4,0},{8,12},{12,8},{1,5},{5,1},{9,13},{13,9},{2,6},{6,2},{1... | collective-permute-start | bytes 1179656 | tf_op jit(solution)/shard_map/ppermute | solution.py:536
  19.4 0.7 %collective-permute-start.4 = (bf16[2,768,128]{2,1,0:T(8,128)(2,1)S(1)}, bf16[2,768,128]{2,1,0:T(8,128)(2,1)S(1)}, u32[]{:S(2)}, u32[]{:S(2)}) collective-permute-start(bf16[2,768,128]{2,1,0:T(8,128)(2,1)S(1)} %get-tuple-element.71), channel_id=1, source_target_pairs={{4,8},{8,4},{5,9},{9,5},{6,10},{10,6},{7,11},{11,7},{20,24},{24,20... | collective-permute-start | bytes 1179656 | tf_op jit(solution)/shard_map/ppermute | solution.py:613
  20.1 0.0 collective-permute-done.refs_1_
  20.1 6.0 %collective-permute-done.1.refs_2_ = bf16[184,512]{1,0:T(8,128)(2,1)S(1)} collective-permute-done((bf16[184,512]{1,0:T(8,128)(2,1)}, bf16[184,512]{1,0:T(8,128)(2,1)S(1)}, u32[]{:S(2)}, u32[]{:S(2)}) %collective-permute-start.1) | collective-permute-done | bytes 188448 | tf_op jit(solution)/shard_map/ppermute | solution.py:536
  26.1 0.0 copy-done.5
  26.1 0.0 copy-done.8
  26.1 1.9 %shard_map.131 = (f32[192,128]{1,0:T(8,128)S(1)}, bf16[192,128]{1,0:T(8,128)(2,1)S(1)}, bf16[192,128]{1,0:T(8,128)(2,1)S(1)}, bf16[192,128]{1,0:T(8,128)(2,1)S(1...) custom-call(s32[4]{0:T(128)S(1)} %copy-done.3, f32[6]{0:T(128)S(1)} %copy-done.5, ...), custom_call_target="tpu_custom_call" | custom-call | flops 4026531840 | bytes 1024 | tf_op jit(solution)/shard_map/pallas_call | solution.py:61
  28.1 0.9 %collective-permute-start.5 = (bf16[192,128]{1,0:T(8,128)(2,1)S(1)}, bf16[192,128]{1,0:T(8,128)(2,1)S(1)}, u32[]{:S(2)}, u32[]{:S(2)}) collective-permute-start(bf16[192,128]{1,0:T(8,128)(2,1)S(1)} %get-tuple-element.78), channel_id=1, source_target_pairs={{0,6},{2,4},{4,2},{6,0},{8,14},{10,12},{12,10},{14,8},{1,7},{3,5},... | collective-permute-start | bytes 147464 | tf_op jit(solution)/shard_map/ppermute | solution.py:545
  29.0 0.7 %collective-permute-start.6 = (bf16[192,128]{1,0:T(8,128)(2,1)S(1)}, bf16[192,128]{1,0:T(8,128)(2,1)S(1)}, u32[]{:S(2)}, u32[]{:S(2)}) collective-permute-start(bf16[192,128]{1,0:T(8,128)(2,1)S(1)} %get-tuple-element.79), channel_id=1, source_target_pairs={{0,2},{2,0},{1,3},{3,1},{4,6},{6,4},{5,7},{7,5},{8,10},{10,8},{9,1... | collective-permute-start | bytes 147464 | tf_op jit(solution)/shard_map/ppermute | solution.py:536
  29.7 1.9 %collective-permute-start.7 = (bf16[192,128]{1,0:T(8,128)(2,1)S(1)}, bf16[192,128]{1,0:T(8,128)(2,1)S(1)}, u32[]{:S(2)}, u32[]{:S(2)}) collective-permute-start(bf16[192,128]{1,0:T(8,128)(2,1)S(1)} %get-tuple-element.80), channel_id=1, source_target_pairs={{0,4},{4,0},{8,12},{12,8},{1,5},{5,1},{9,13},{13,9},{2,6},{6,2},{1... | collective-permute-start | bytes 147464 | tf_op jit(solution)/shard_map/ppermute | solution.py:536
  31.6 1.7 %shard_map.132 = (bf16[184,512]{1,0:T(8,128)(2,1)S(1)}, bf16[184,512]{1,0:T(8,128)(2,1)S(1)}, bf16[184,512]{1,0:T(8,128)(2,1)S(1)}, bf16[184,512]{1,0:T(8,128)(2,1)S(1)}) custom-call(s32[4]{0:T(128)S(1)} %copy-done.3, f32[6]{0:T(128)S(1)} %copy-done.5, f32[2048,256]{1,0:T(8,128)S(1)} %get-tuple-element.55.mixer_ref, ...), custom_call_target="tpu_custom_call" | custom-call | bytes 1024 | tf_op jit(solution)/shard_map/pallas_call | solution.py:61
  33.4 0.0 collective-permute-done.3.first_rim
  33.4 0.0 collective-permute-done.4.second_rim
  33.4 1.0 %shard_map.133.tap_ref = f32[16,128]{1,0:T(8,128)S(1)} custom-call(s32[4]{0:T(128)S(1)} %copy-done.3, s32[6,9]{1,0:T(8,128)S(1)} %copy-done.2, bf16[2,768,128]{2,1,0:T(8,128)(2,1)S(1)} %bitcast.7, bf16[2,768,128]{2,1,0:T(8,128)(2,1)S(1)} %collective-permute-done.3.first_rim, bf16[2,768,128]{2,1,0:T(8,128)(2,1)S(1)} %collective-permute-done.4.second_rim, ...), custom_call_target="tpu_custom_call" | custom-call | bytes 1024 | tf_op jit(solution)/shard_map/pallas_call | solution.py:61
  34.4 0.0 collective-permute-done.5.first_ref
  34.4 0.0 collective-permute-done.6.second_ref
  34.4 0.0 collective-permute-done.7.third_ref
  34.5 2.5 %collective-permute-start.8 = (bf16[224,128]{1,0:T(8,128)(2,1)S(1)}, bf16[224,128]{1,0:T(8,128)(2,1)S(1)}, u32[]{:S(2)}, u32[]{:S(2)}) collective-permute-start(bf16[224,128]{1,0:T(8,128)(2,1)S(1)} %shard_map.134.own_ref), channel_id=1, source_target_pairs={{0,8},{4,12},{8,0},{12,4},{1,9},{5,13},{9,1},{13,5},{2,10},{6,14},... | collective-permute-start | bytes 172040 | tf_op jit(solution)/shard_map/ppermute | solution.py:536
  37.0 0.7 %collective-permute-start.12 = (bf16[184,512]{1,0:T(8,128)(2,1)S(1)}, bf16[184,512]{1,0:T(8,128)(2,1)S(1)}, u32[]{:S(2)}, u32[]{:S(2)}) collective-permute-start(bf16[184,512]{1,0:T(8,128)(2,1)S(1)} %get-tuple-element.89), channel_id=1, source_target_pairs={{0,4},{4,0},{8,12},{12,8},{1,5},{5,1},{9,13},{13,9},{2,6},{6,2},{1... | collective-permute-start | bytes 565256 | tf_op jit(solution)/shard_map/ppermute | solution.py:536
  37.7 1.0 %collective-permute-start.13 = (bf16[184,512]{1,0:T(8,128)(2,1)S(1)}, bf16[184,512]{1,0:T(8,128)(2,1)S(1)}, u32[]{:S(2)}, u32[]{:S(2)}) collective-permute-start(bf16[184,512]{1,0:T(8,128)(2,1)S(1)} %get-tuple-element.93), channel_id=1, source_target_pairs={{0,8},{4,12},{8,0},{12,4},{1,9},{5,13},{9,1},{13,5},{2,10},{6,14},... | collective-permute-start | bytes 565256 | tf_op jit(solution)/shard_map/ppermute | solution.py:536
  38.7 2.6 %collective-permute-start.14 = (bf16[184,512]{1,0:T(8,128)(2,1)S(1)}, bf16[184,512]{1,0:T(8,128)(2,1)S(1)}, u32[]{:S(2)}, u32[]{:S(2)}) collective-permute-start(bf16[184,512]{1,0:T(8,128)(2,1)S(1)} %get-tuple-element.94), channel_id=1, source_target_pairs={{0,12},{4,8},{8,4},{12,0},{1,13},{5,9},{9,5},{13,1},{2,14},{6,10},... | collective-permute-start | bytes 565256 | tf_op jit(solution)/shard_map/ppermute | solution.py:536
  41.4 0.0 collective-permute-done.8.other_ref
  41.4 0.0 copy-start
  41.4 1.6 %collective-permute-start.11 = (bf16[224,128]{1,0:T(8,128)(2,1)S(1)}, bf16[224,128]{1,0:T(8,128)(2,1)S(1)}, u32[]{:S(2)}, u32[]{:S(2)}) collective-permute-start(bf16[224,128]{1,0:T(8,128)(2,1)S(1)} %shard_map.135.refs_0_), channel_id=1, source_target_pairs={{0,6},{2,4},{4,2},{6,0},{8,14},{10,12},{12,10},{14,8},{1,7},{3,5},... | collective-permute-start | bytes 172040 | tf_op jit(solution)/shard_map/ppermute | solution.py:545
  43.0 1.5 %collective-permute-start.10 = (bf16[224,128]{1,0:T(8,128)(2,1)S(1)}, bf16[224,128]{1,0:T(8,128)(2,1)S(1)}, u32[]{:S(2)}, u32[]{:S(2)}) collective-permute-start(bf16[224,128]{1,0:T(8,128)(2,1)S(1)} %shard_map.135.refs_0_), channel_id=1, source_target_pairs={{0,4},{4,0},{8,12},{12,8},{1,5},{5,1},{9,13},{13,9},{2,6},{6,2},{1... | collective-permute-start | bytes 172040 | tf_op jit(solution)/shard_map/ppermute | solution.py:536
  44.5 3.5 %collective-permute-done.12.near_ref = bf16[184,512]{1,0:T(8,128)(2,1)S(1)} collective-permute-done((bf16[184,512]{1,0:T(8,128)(2,1)S(1)}, bf16[184,512]{1,0:T(8,128)(2,1)S(1)}, u32[]{:S(2)}, u32[]{:S(2)}) %collective-permute-start.12) | collective-permute-done | bytes 188448 | tf_op jit(solution)/shard_map/ppermute | solution.py:536
  48.0 1.5 %collective-permute-start.9 = (bf16[224,128]{1,0:T(8,128)(2,1)S(1)}, bf16[224,128]{1,0:T(8,128)(2,1)S(1)}, u32[]{:S(2)}, u32[]{:S(2)}) collective-permute-start(bf16[224,128]{1,0:T(8,128)(2,1)S(1)} %shard_map.135.refs_0_), channel_id=1, source_target_pairs={{0,2},{2,0},{1,3},{3,1},{4,6},{6,4},{5,7},{7,5},{8,10},{10,8},{9,1... | collective-permute-start | bytes 172040 | tf_op jit(solution)/shard_map/ppermute | solution.py:536
  49.5 1.1 %shard_map.136 = (f32[2,768,128]{2,1,0:T(8,128)S(1)}, f32[2,768,128]{2,1,0:T(8,128)S(1)}) custom-call(s32[4]{0:T(128)S(1)} %copy-done.3, s32[6,9]{1,0:T(8,128)S(1)} %copy-done.2, bf16[2,768,128]{2,1,0:T(8,128)(2,1)S(1)} %collective-permute-done.3.first_rim, bf16[2,768,128]{2,1,0:T(8,128)(2,1)S(1)} %collective-permute-done.4.second_rim, ...), custom_call_target="tpu_custom_call" | custom-call | bytes 1024 | tf_op jit(solution)/shard_map/pallas_call | solution.py:61
  50.6 0.0 copy-done
  50.6 1.2 %shard_map.137 = (f32[2,768,128]{2,1,0:T(8,128)S(1)}, f32[2,768,128]{2,1,0:T(8,128)S(1)}) custom-call(s32[4]{0:T(128)S(1)} %copy-done.3, bf16[4,768,184]{2,1,0:T(8,128)(2,1)S(1)} %copy-done, f32[2,768,128]{2,1,0:T(8,128)S(1)} %get-tuple-element.83.base_ref, f32[2,768,128]{2,1,0:T(8,128)S(1)} %get-tuple-element.84.slope_ref, ...), custom_call_target="tpu_custom_call" | custom-call | bytes 1024 | tf_op jit(solution)/shard_map/pallas_call | solution.py:61
  51.8 0.0 collective-permute-done.11.refs_3_
  51.8 0.0 collective-permute-done.10.refs_2_
  51.8 0.4 collective-permute-done.9.refs_1_
  52.1 0.8 %shard_map.138 = (f32[2,384,128]{2,1,0:T(8,128)}, f32[9,128]{1,0:T(8,128)}) custom-call(bf16[224,128]{1,0:T(8,128)(2,1)S(1)} %shard_map.135.refs_0_, bf16[224,128]{1,0:T(8,128)(2,1)S(1)} %collective-permute-done.9.refs_1_, bf16[224,128]{1,0:T(8,128)(2,1)S(1)} %collective-permute-done.10.refs_2_, bf16[224,128]{1,0:T(8,128)(2,1)S(1)} %collective-permute-done.11.refs_3_), custom_call_target="tpu_custom_call" | custom-call | bytes 1024 | tf_op jit(solution)/shard_map/pallas_call | solution.py:61
  52.9 0.5 collective-permute-done.13.refs_0_
  53.4 0.0 collective-permute-done.14.refs_1_
  53.4 1.9 %shard_map.139 = (bf16[2,768,128]{2,1,0:T(8,128)(2,1)}, bf16[2,768,128]{2,1,0:T(8,128)(2,1)}) custom-call(s32[4]{0:T(128)S(1)} %copy-done.3, bf16[4,768,184]{2,1,0:T(8,128)(2,1)S(1)} %copy-done, f32[2,768,128]{2,1,0:T(8,128)S(1)} %get-tuple-element.91.sum_ref, f32[2,768,128]{2,1,0:T(8,128)S(1)} %get-tuple-element.92.early_ref, ...), custom_call_target="tpu_custom_call" | custom-call | flops 578813952 | bytes 1024 | tf_op jit(solution)/shard_map/pallas_call | solution.py:61
  (3 shorter events, 0.1 us)
Async XLA Ops:
  0.6 9.0 %copy-start.1 = (bf16[1,2,768,128]{3,2,1,0:T(8,128)(2,1)S(1)}, bf16[1,2,768,128]{3,2,1,0:T(8,128)(2,1)}, u32[]{:S(2)}) copy-start(bf16[1,2,768,128]{3,2,1,0:T(8,128)(2,1)} %param.11) | copy-start | bytes 1179652
  0.6 9.0 %copy-start.6 = (bf16[1,2,768,128]{3,2,1,0:T(8,128)(2,1)S(1)}, bf16[1,2,768,128]{3,2,1,0:T(8,128)(2,1)}, u32[]{:S(2)}) copy-start(bf16[1,2,768,128]{3,2,1,0:T(8,128)(2,1)} %param.10) | copy-start | bytes 1179652
  0.7 8.9 %copy-start.9 = (bf16[92,6,384]{2,0,1:T(8,128)(2,1)S(1)}, bf16[92,6,384]{2,0,1:T(8,128)(2,1)}, u32[]{:S(2)}) copy-start(bf16[92,6,384]{2,0,1:T(8,128)(2,1)} %param.15) | copy-start | bytes 1271812
  0.7 9.0 %copy-start.3 = (s32[4]{0:T(128)S(1)}, s32[4]{0:T(128)}, u32[]{:S(2)}) copy-start(s32[4]{0:T(128)} %rows_ref.13) | copy-start | bytes 52
  0.7 9.0 %copy-start.2 = (s32[6,9]{1,0:T(8,128)S(1)}, s32[6,9]{1,0:T(8,128)}, u32[]{:S(2)}) copy-start(s32[6,9]{1,0:T(8,128)} %shift_ref.5) | copy-start | bytes 652
  0.7 9.0 %copy-start.4 = (bf16[9,128]{1,0:T(8,128)(2,1)S(1)}, bf16[9,128]{1,0:T(8,128)(2,1)}, u32[]{:S(2)}) copy-start(bf16[9,128]{1,0:T(8,128)(2,1)} %taps_ref.3) | copy-start | bytes 6916
  0.7 9.0 %copy-start.7 = (bf16[2,384,128]{2,1,0:T(8,128)(2,1)S(1)}, bf16[2,384,128]{2,1,0:T(8,128)(2,1)}, u32[]{:S(2)}) copy-start(bf16[2,384,128]{2,1,0:T(8,128)(2,1)} %filter_ref.1) | copy-start | bytes 589828
  3.8 22.3 %copy-start.5 = (f32[6]{0:T(128)S(1)}, f32[6]{0:T(128)}, u32[]{:S(2)}) copy-start(f32[6]{0:T(128)} %quad_ref.3) | copy-start | bytes 76
  3.8 22.3 %copy-start.8 = (bf16[184,512]{1,0:T(8,128)(2,1)S(1)}, bf16[184,512]{1,0:T(8,128)(2,1)}, u32[]{:S(2)}) copy-start(bf16[184,512]{1,0:T(8,128)(2,1)} %get-tuple-element.57.refs_0_) | copy-start | bytes 565252
  3.8 11.2 %collective-permute-start.2 = (bf16[184,512]{1,0:T(8,128)(2,1)}, bf16[184,512]{1,0:T(8,128)(2,1)S(1)}, u32[]{:S(2)}, u32[]{:S(2)}) collective-permute-start(bf16[184,512]{1,0:T(8,128)(2,1)} %get-tuple-element.62), channel_id=1, source_target_pairs={{0,12},{4,8},{8,4},{12,0},{1,13},{5,9},{9,5},{13,1},{2,14},{6,10},... | collective-permute-start | bytes 565256 | tf_op jit(solution)/shard_map/ppermute | solution.py:536
  8.9 11.2 %collective-permute-start = (bf16[184,512]{1,0:T(8,128)(2,1)}, bf16[184,512]{1,0:T(8,128)(2,1)S(1)}, u32[]{:S(2)}, u32[]{:S(2)}) collective-permute-start(bf16[184,512]{1,0:T(8,128)(2,1)} %get-tuple-element.58), channel_id=1, source_target_pairs={{0,4},{4,0},{8,12},{12,8},{1,5},{5,1},{9,13},{13,9},{2,6},{6,2},{1... | collective-permute-start | bytes 565256 | tf_op jit(solution)/shard_map/ppermute | solution.py:536
  8.9 17.2 %collective-permute-start.1 = (bf16[184,512]{1,0:T(8,128)(2,1)}, bf16[184,512]{1,0:T(8,128)(2,1)S(1)}, u32[]{:S(2)}, u32[]{:S(2)}) collective-permute-start(bf16[184,512]{1,0:T(8,128)(2,1)} %get-tuple-element.59), channel_id=1, source_target_pairs={{0,8},{4,12},{8,0},{12,4},{1,9},{5,13},{9,1},{13,5},{2,10},{6,14},... | collective-permute-start | bytes 565256 | tf_op jit(solution)/shard_map/ppermute | solution.py:536
  15.0 18.4 %collective-permute-start.3 = (bf16[2,768,128]{2,1,0:T(8,128)(2,1)S(1)}, bf16[2,768,128]{2,1,0:T(8,128)(2,1)S(1)}, u32[]{:S(2)}, u32[]{:S(2)}) collective-permute-start(bf16[2,768,128]{2,1,0:T(8,128)(2,1)S(1)} %get-tuple-element.70), channel_id=1, source_target_pairs={{0,4},{4,0},{8,12},{12,8},{1,5},{5,1},{9,13},{13,9},{2,6},{6,2},{1... | collective-permute-start | bytes 1179656 | tf_op jit(solution)/shard_map/ppermute | solution.py:536
  19.4 14.0 %collective-permute-start.4 = (bf16[2,768,128]{2,1,0:T(8,128)(2,1)S(1)}, bf16[2,768,128]{2,1,0:T(8,128)(2,1)S(1)}, u32[]{:S(2)}, u32[]{:S(2)}) collective-permute-start(bf16[2,768,128]{2,1,0:T(8,128)(2,1)S(1)} %get-tuple-element.71), channel_id=1, source_target_pairs={{4,8},{8,4},{5,9},{9,5},{6,10},{10,6},{7,11},{11,7},{20,24},{24,20... | collective-permute-start | bytes 1179656 | tf_op jit(solution)/shard_map/ppermute | solution.py:613
  28.1 6.3 %collective-permute-start.5 = (bf16[192,128]{1,0:T(8,128)(2,1)S(1)}, bf16[192,128]{1,0:T(8,128)(2,1)S(1)}, u32[]{:S(2)}, u32[]{:S(2)}) collective-permute-start(bf16[192,128]{1,0:T(8,128)(2,1)S(1)} %get-tuple-element.78), channel_id=1, source_target_pairs={{0,6},{2,4},{4,2},{6,0},{8,14},{10,12},{12,10},{14,8},{1,7},{3,5},... | collective-permute-start | bytes 147464 | tf_op jit(solution)/shard_map/ppermute | solution.py:545
  29.0 5.4 %collective-permute-start.6 = (bf16[192,128]{1,0:T(8,128)(2,1)S(1)}, bf16[192,128]{1,0:T(8,128)(2,1)S(1)}, u32[]{:S(2)}, u32[]{:S(2)}) collective-permute-start(bf16[192,128]{1,0:T(8,128)(2,1)S(1)} %get-tuple-element.79), channel_id=1, source_target_pairs={{0,2},{2,0},{1,3},{3,1},{4,6},{6,4},{5,7},{7,5},{8,10},{10,8},{9,1... | collective-permute-start | bytes 147464 | tf_op jit(solution)/shard_map/ppermute | solution.py:536
  29.7 4.7 %collective-permute-start.7 = (bf16[192,128]{1,0:T(8,128)(2,1)S(1)}, bf16[192,128]{1,0:T(8,128)(2,1)S(1)}, u32[]{:S(2)}, u32[]{:S(2)}) collective-permute-start(bf16[192,128]{1,0:T(8,128)(2,1)S(1)} %get-tuple-element.80), channel_id=1, source_target_pairs={{0,4},{4,0},{8,12},{12,8},{1,5},{5,1},{9,13},{13,9},{2,6},{6,2},{1... | collective-permute-start | bytes 147464 | tf_op jit(solution)/shard_map/ppermute | solution.py:536
  34.5 6.9 %collective-permute-start.8 = (bf16[224,128]{1,0:T(8,128)(2,1)S(1)}, bf16[224,128]{1,0:T(8,128)(2,1)S(1)}, u32[]{:S(2)}, u32[]{:S(2)}) collective-permute-start(bf16[224,128]{1,0:T(8,128)(2,1)S(1)} %shard_map.134.own_ref), channel_id=1, source_target_pairs={{0,8},{4,12},{8,0},{12,4},{1,9},{5,13},{9,1},{13,5},{2,10},{6,14},... | collective-permute-start | bytes 172040 | tf_op jit(solution)/shard_map/ppermute | solution.py:536
  37.0 11.0 %collective-permute-start.12 = (bf16[184,512]{1,0:T(8,128)(2,1)S(1)}, bf16[184,512]{1,0:T(8,128)(2,1)S(1)}, u32[]{:S(2)}, u32[]{:S(2)}) collective-permute-start(bf16[184,512]{1,0:T(8,128)(2,1)S(1)} %get-tuple-element.89), channel_id=1, source_target_pairs={{0,4},{4,0},{8,12},{12,8},{1,5},{5,1},{9,13},{13,9},{2,6},{6,2},{1... | collective-permute-start | bytes 565256 | tf_op jit(solution)/shard_map/ppermute | solution.py:536
  37.7 15.7 %collective-permute-start.13 = (bf16[184,512]{1,0:T(8,128)(2,1)S(1)}, bf16[184,512]{1,0:T(8,128)(2,1)S(1)}, u32[]{:S(2)}, u32[]{:S(2)}) collective-permute-start(bf16[184,512]{1,0:T(8,128)(2,1)S(1)} %get-tuple-element.93), channel_id=1, source_target_pairs={{0,8},{4,12},{8,0},{12,4},{1,9},{5,13},{9,1},{13,5},{2,10},{6,14},... | collective-permute-start | bytes 565256 | tf_op jit(solution)/shard_map/ppermute | solution.py:536
  38.7 14.7 %collective-permute-start.14 = (bf16[184,512]{1,0:T(8,128)(2,1)S(1)}, bf16[184,512]{1,0:T(8,128)(2,1)S(1)}, u32[]{:S(2)}, u32[]{:S(2)}) collective-permute-start(bf16[184,512]{1,0:T(8,128)(2,1)S(1)} %get-tuple-element.94), channel_id=1, source_target_pairs={{0,12},{4,8},{8,4},{12,0},{1,13},{5,9},{9,5},{13,1},{2,14},{6,10},... | collective-permute-start | bytes 565256 | tf_op jit(solution)/shard_map/ppermute | solution.py:536
  41.4 9.2 %copy-start = (bf16[4,768,184]{2,1,0:T(8,128)(2,1)S(1)}, bf16[4,768,184]{2,1,0:T(8,128)(2,1)}, u32[]{:S(2)}) copy-start(bf16[4,768,184]{2,1,0:T(8,128)(2,1)} %constant.8.clone.table_ref) | copy-start | bytes 3391492
  41.4 10.3 %collective-permute-start.11 = (bf16[224,128]{1,0:T(8,128)(2,1)S(1)}, bf16[224,128]{1,0:T(8,128)(2,1)S(1)}, u32[]{:S(2)}, u32[]{:S(2)}) collective-permute-start(bf16[224,128]{1,0:T(8,128)(2,1)S(1)} %shard_map.135.refs_0_), channel_id=1, source_target_pairs={{0,6},{2,4},{4,2},{6,0},{8,14},{10,12},{12,10},{14,8},{1,7},{3,5},... | collective-permute-start | bytes 172040 | tf_op jit(solution)/shard_map/ppermute | solution.py:545
  43.0 8.8 %collective-permute-start.10 = (bf16[224,128]{1,0:T(8,128)(2,1)S(1)}, bf16[224,128]{1,0:T(8,128)(2,1)S(1)}, u32[]{:S(2)}, u32[]{:S(2)}) collective-permute-start(bf16[224,128]{1,0:T(8,128)(2,1)S(1)} %shard_map.135.refs_0_), channel_id=1, source_target_pairs={{0,4},{4,0},{8,12},{12,8},{1,5},{5,1},{9,13},{13,9},{2,6},{6,2},{1... | collective-permute-start | bytes 172040 | tf_op jit(solution)/shard_map/ppermute | solution.py:536
  48.0 4.2 %collective-permute-start.9 = (bf16[224,128]{1,0:T(8,128)(2,1)S(1)}, bf16[224,128]{1,0:T(8,128)(2,1)S(1)}, u32[]{:S(2)}, u32[]{:S(2)}) collective-permute-start(bf16[224,128]{1,0:T(8,128)(2,1)S(1)} %shard_map.135.refs_0_), channel_id=1, source_target_pairs={{0,2},{2,0},{1,3},{3,1},{4,6},{6,4},{5,7},{7,5},{8,10},{10,8},{9,1... | collective-permute-start | bytes 172040 | tf_op jit(solution)/shard_map/ppermute | solution.py:536

commit v9 on v8

--- a/solution.py
+++ b/solution.py
@@ -92,7 +92,7 @@
             [(x_hbm, x_ref), (dy_hbm, dy_ref), (table_hbm, table_ref)]
         )
     ]
-    for load in loads:
+    for load in (loads[0], loads[2], loads[1]):
         load.start()
     loads[0].wait()
     activate(x_ref, act_ref)
@@ -300,7 +300,7 @@
     acts[slots] = jnp.zeros(acts.shape[1:], F32)
     grads[slots] = jnp.zeros(grads.shape[1:], F32)
     weights = taps_ref[...].astype(F32)
-    step = 32 if lon_count % 32 == 0 else lon_count
+    step = 64 if lon_count % 64 == 0 else lon_count
     totals = [jnp.zeros((8, chans), F32)] * taps
     top = shift_ref.shape[0] - 1
     for slot in range(slots):

time: 55.6 us -> 55.6 us (level)
  transfers between devices with their start and end apart: 15 -> 15, of which waited for: 4 -> 6; matrix products, arithmetic and copies ran while one was open for 0% -> 0% of each run, Pallas kernels for 24% -> 23%
where the time goes in v9:
time: 55.6 us; the launch traced here: 55.3 us
  starting transfers between devices  25.8 us (46%)
  Pallas kernels  18 us (32%)
  waiting for transfers between devices  10.5 us (19%)
  between operations  0.89 us (2%)
    ppermute x12, starting transfers between devices, crossed(): return lax.ppermute(values, axis, [(i, i ^ distance) for i in range(count)])  22.7 us
    pallas_call x11, Pallas kernels, call(): pl.pallas_call(kernel, out_shape=out_shape, in_specs=in_specs, out_specs=...  18 us
    ppermute x12, waiting for transfers between devices, crossed(): return lax.ppermute(values, axis, [(i, i ^ distance) for i in range(count)])  10.5 us
    ppermute x2, starting transfers between devices, around(): lax.ppermute(parts[2], ('space', 'ens'), [(i, i ^ flip) for i in range(co...  2.41 us
  transfers between devices with their start and end apart: 15, of which 6 were waited for; matrix products, arithmetic and copies ran while one was open for 0% of the time, Pallas kernels for 23%

profile of v9, /device:TPU:0, one launch (start us, length us, event | category | flops | bytes accessed | tf_op | source)
XLA Modules:
  0.0 55.3 jit_solution(4454936312375826519)
XLA Ops:
  0.6 0.0 copy-start.1
  0.6 0.0 copy-start.6
  0.7 0.0 copy-start.9
  0.7 0.0 copy-start.3
  0.7 0.0 copy-start.2
  0.7 0.0 copy-start.4
  0.7 0.0 copy-start.7
  0.7 3.1 %shard_map.130 = (bf16[184,512]{1,0:T(8,128)(2,1)}, bf16[184,512]{1,0:T(8,128)(2,1)}, bf16[184,512]{1,0:T(8,128)(2,1)}, bf16[184,512]{1,0:T(8,128)(2,1)}) custom-call(bf16[2,768,128]{2,1,0:T(8,128)(2,1)} %bitcast.8, bf16[2,768,128]{2,1,0:T(8,128)(2,1)} %bitcast.5, bf16[4,184,768]{2,1,0:T(8,128)(2,1)} %constant.7.clone.table_hbm), custom_call_target="tpu_custom_call" | custom-call | flops 578813952 | bytes 1024 | tf_op jit(solution)/shard_map/pallas_call | solution.py:61
  3.8 0.0 copy-start.5
  3.8 0.0 copy-start.8
  3.8 5.1 %collective-permute-start.2 = (bf16[184,512]{1,0:T(8,128)(2,1)}, bf16[184,512]{1,0:T(8,128)(2,1)S(1)}, u32[]{:S(2)}, u32[]{:S(2)}) collective-permute-start(bf16[184,512]{1,0:T(8,128)(2,1)} %get-tuple-element.62), channel_id=1, source_target_pairs={{0,12},{4,8},{8,4},{12,0},{1,13},{5,9},{9,5},{13,1},{2,14},{6,10},... | collective-permute-start | bytes 565256 | tf_op jit(solution)/shard_map/ppermute | solution.py:536
  9.0 0.0 collective-permute-start
  9.0 0.6 %collective-permute-start.1 = (bf16[184,512]{1,0:T(8,128)(2,1)}, bf16[184,512]{1,0:T(8,128)(2,1)S(1)}, u32[]{:S(2)}, u32[]{:S(2)}) collective-permute-start(bf16[184,512]{1,0:T(8,128)(2,1)} %get-tuple-element.59), channel_id=1, source_target_pairs={{0,8},{4,12},{8,0},{12,4},{1,9},{5,13},{9,1},{13,5},{2,10},{6,14},... | collective-permute-start | bytes 565256 | tf_op jit(solution)/shard_map/ppermute | solution.py:536
  9.6 0.0 copy-done.9
  9.7 0.0 copy-done.1
  9.7 0.0 copy-done.6
  9.7 0.0 copy-done.3
  9.7 0.0 copy-done.2
  9.7 0.0 copy-done.4
  9.7 0.0 copy-done.7
  9.7 5.2 %shard_map.129 = (f32[2048,256]{1,0:T(8,128)S(1)}, bf16[384,2048]{1,0:T(8,128)(2,1)S(1)}, bf16[2,768,128]{2,1,0:T(8,128)(2,1)S(1)}, bf16[2,768,128]{2,1,0:T(8,12...) custom-call(s32[4]{0:T(128)S(1)} %copy-done.3, ...), custom_call_target="tpu_custom_call" | custom-call | flops 402653184 | bytes 2097152 | tf_op jit(solution)/shard_map/pallas_call | solution.py:61
  14.9 0.0 collective-permute-done.2.refs_3_
  14.9 4.6 %collective-permute-start.3 = (bf16[2,768,128]{2,1,0:T(8,128)(2,1)S(1)}, bf16[2,768,128]{2,1,0:T(8,128)(2,1)S(1)}, u32[]{:S(2)}, u32[]{:S(2)}) collective-permute-start(bf16[2,768,128]{2,1,0:T(8,128)(2,1)S(1)} %get-tuple-element.70), channel_id=1, source_target_pairs={{0,4},{4,0},{8,12},{12,8},{1,5},{5,1},{9,13},{13,9},{2,6},{6,2},{1... | collective-permute-start | bytes 1179656 | tf_op jit(solution)/shard_map/ppermute | solution.py:536
  19.4 0.7 %collective-permute-start.4 = (bf16[2,768,128]{2,1,0:T(8,128)(2,1)S(1)}, bf16[2,768,128]{2,1,0:T(8,128)(2,1)S(1)}, u32[]{:S(2)}, u32[]{:S(2)}) collective-permute-start(bf16[2,768,128]{2,1,0:T(8,128)(2,1)S(1)} %get-tuple-element.71), channel_id=1, source_target_pairs={{4,8},{8,4},{5,9},{9,5},{6,10},{10,6},{7,11},{11,7},{20,24},{24,20... | collective-permute-start | bytes 1179656 | tf_op jit(solution)/shard_map/ppermute | solution.py:613
  20.1 0.0 collective-permute-done.refs_1_
  20.1 6.0 %collective-permute-done.1.refs_2_ = bf16[184,512]{1,0:T(8,128)(2,1)S(1)} collective-permute-done((bf16[184,512]{1,0:T(8,128)(2,1)}, bf16[184,512]{1,0:T(8,128)(2,1)S(1)}, u32[]{:S(2)}, u32[]{:S(2)}) %collective-permute-start.1) | collective-permute-done | bytes 188448 | tf_op jit(solution)/shard_map/ppermute | solution.py:536
  26.2 0.0 copy-done.5
  26.2 0.0 copy-done.8
  26.2 1.9 %shard_map.131 = (f32[192,128]{1,0:T(8,128)S(1)}, bf16[192,128]{1,0:T(8,128)(2,1)S(1)}, bf16[192,128]{1,0:T(8,128)(2,1)S(1)}, bf16[192,128]{1,0:T(8,128)(2,1)S(1...) custom-call(s32[4]{0:T(128)S(1)} %copy-done.3, f32[6]{0:T(128)S(1)} %copy-done.5, ...), custom_call_target="tpu_custom_call" | custom-call | flops 4026531840 | bytes 1024 | tf_op jit(solution)/shard_map/pallas_call | solution.py:61
  28.1 0.9 %collective-permute-start.5 = (bf16[192,128]{1,0:T(8,128)(2,1)S(1)}, bf16[192,128]{1,0:T(8,128)(2,1)S(1)}, u32[]{:S(2)}, u32[]{:S(2)}) collective-permute-start(bf16[192,128]{1,0:T(8,128)(2,1)S(1)} %get-tuple-element.78), channel_id=1, source_target_pairs={{0,6},{2,4},{4,2},{6,0},{8,14},{10,12},{12,10},{14,8},{1,7},{3,5},... | collective-permute-start | bytes 147464 | tf_op jit(solution)/shard_map/ppermute | solution.py:545
  29.0 0.7 %collective-permute-start.6 = (bf16[192,128]{1,0:T(8,128)(2,1)S(1)}, bf16[192,128]{1,0:T(8,128)(2,1)S(1)}, u32[]{:S(2)}, u32[]{:S(2)}) collective-permute-start(bf16[192,128]{1,0:T(8,128)(2,1)S(1)} %get-tuple-element.79), channel_id=1, source_target_pairs={{0,2},{2,0},{1,3},{3,1},{4,6},{6,4},{5,7},{7,5},{8,10},{10,8},{9,1... | collective-permute-start | bytes 147464 | tf_op jit(solution)/shard_map/ppermute | solution.py:536
  29.7 1.9 %collective-permute-start.7 = (bf16[192,128]{1,0:T(8,128)(2,1)S(1)}, bf16[192,128]{1,0:T(8,128)(2,1)S(1)}, u32[]{:S(2)}, u32[]{:S(2)}) collective-permute-start(bf16[192,128]{1,0:T(8,128)(2,1)S(1)} %get-tuple-element.80), channel_id=1, source_target_pairs={{0,4},{4,0},{8,12},{12,8},{1,5},{5,1},{9,13},{13,9},{2,6},{6,2},{1... | collective-permute-start | bytes 147464 | tf_op jit(solution)/shard_map/ppermute | solution.py:536
  31.7 1.7 %shard_map.132 = (bf16[184,512]{1,0:T(8,128)(2,1)S(1)}, bf16[184,512]{1,0:T(8,128)(2,1)S(1)}, bf16[184,512]{1,0:T(8,128)(2,1)S(1)}, bf16[184,512]{1,0:T(8,128)(2,1)S(1)}) custom-call(s32[4]{0:T(128)S(1)} %copy-done.3, f32[6]{0:T(128)S(1)} %copy-done.5, f32[2048,256]{1,0:T(8,128)S(1)} %get-tuple-element.55.mixer_ref, ...), custom_call_target="tpu_custom_call" | custom-call | bytes 1024 | tf_op jit(solution)/shard_map/pallas_call | solution.py:61
  33.4 0.0 collective-permute-done.3.first_rim
  33.4 0.0 collective-permute-done.4.second_rim
  33.4 1.0 %shard_map.133.tap_ref = f32[16,128]{1,0:T(8,128)S(1)} custom-call(s32[4]{0:T(128)S(1)} %copy-done.3, s32[6,9]{1,0:T(8,128)S(1)} %copy-done.2, bf16[2,768,128]{2,1,0:T(8,128)(2,1)S(1)} %bitcast.7, bf16[2,768,128]{2,1,0:T(8,128)(2,1)S(1)} %collective-permute-done.3.first_rim, bf16[2,768,128]{2,1,0:T(8,128)(2,1)S(1)} %collective-permute-done.4.second_rim, ...), custom_call_target="tpu_custom_call" | custom-call | bytes 1024 | tf_op jit(solution)/shard_map/pallas_call | solution.py:61
  34.4 0.0 collective-permute-done.5.first_ref
  34.4 0.0 collective-permute-done.6.second_ref
  34.5 0.0 collective-permute-done.7.third_ref
  34.5 2.5 %collective-permute-start.8 = (bf16[224,128]{1,0:T(8,128)(2,1)S(1)}, bf16[224,128]{1,0:T(8,128)(2,1)S(1)}, u32[]{:S(2)}, u32[]{:S(2)}) collective-permute-start(bf16[224,128]{1,0:T(8,128)(2,1)S(1)} %shard_map.134.own_ref), channel_id=1, source_target_pairs={{0,8},{4,12},{8,0},{12,4},{1,9},{5,13},{9,1},{13,5},{2,10},{6,14},... | collective-permute-start | bytes 172040 | tf_op jit(solution)/shard_map/ppermute | solution.py:536
  37.0 0.7 %collective-permute-start.12 = (bf16[184,512]{1,0:T(8,128)(2,1)S(1)}, bf16[184,512]{1,0:T(8,128)(2,1)S(1)}, u32[]{:S(2)}, u32[]{:S(2)}) collective-permute-start(bf16[184,512]{1,0:T(8,128)(2,1)S(1)} %get-tuple-element.89), channel_id=1, source_target_pairs={{0,4},{4,0},{8,12},{12,8},{1,5},{5,1},{9,13},{13,9},{2,6},{6,2},{1... | collective-permute-start | bytes 565256 | tf_op jit(solution)/shard_map/ppermute | solution.py:536
  37.7 1.0 %collective-permute-start.13 = (bf16[184,512]{1,0:T(8,128)(2,1)S(1)}, bf16[184,512]{1,0:T(8,128)(2,1)S(1)}, u32[]{:S(2)}, u32[]{:S(2)}) collective-permute-start(bf16[184,512]{1,0:T(8,128)(2,1)S(1)} %get-tuple-element.93), channel_id=1, source_target_pairs={{0,8},{4,12},{8,0},{12,4},{1,9},{5,13},{9,1},{13,5},{2,10},{6,14},... | collective-permute-start | bytes 565256 | tf_op jit(solution)/shard_map/ppermute | solution.py:536
  38.8 2.6 %collective-permute-start.14 = (bf16[184,512]{1,0:T(8,128)(2,1)S(1)}, bf16[184,512]{1,0:T(8,128)(2,1)S(1)}, u32[]{:S(2)}, u32[]{:S(2)}) collective-permute-start(bf16[184,512]{1,0:T(8,128)(2,1)S(1)} %get-tuple-element.94), channel_id=1, source_target_pairs={{0,12},{4,8},{8,4},{12,0},{1,13},{5,9},{9,5},{13,1},{2,14},{6,10},... | collective-permute-start | bytes 565256 | tf_op jit(solution)/shard_map/ppermute | solution.py:536
  41.4 0.1 collective-permute-done.8.other_ref
  41.5 0.0 copy-start
  41.5 1.5 %collective-permute-start.11 = (bf16[224,128]{1,0:T(8,128)(2,1)S(1)}, bf16[224,128]{1,0:T(8,128)(2,1)S(1)}, u32[]{:S(2)}, u32[]{:S(2)}) collective-permute-start(bf16[224,128]{1,0:T(8,128)(2,1)S(1)} %shard_map.135.refs_0_), channel_id=1, source_target_pairs={{0,6},{2,4},{4,2},{6,0},{8,14},{10,12},{12,10},{14,8},{1,7},{3,5},... | collective-permute-start | bytes 172040 | tf_op jit(solution)/shard_map/ppermute | solution.py:545
  43.0 1.5 %collective-permute-start.10 = (bf16[224,128]{1,0:T(8,128)(2,1)S(1)}, bf16[224,128]{1,0:T(8,128)(2,1)S(1)}, u32[]{:S(2)}, u32[]{:S(2)}) collective-permute-start(bf16[224,128]{1,0:T(8,128)(2,1)S(1)} %shard_map.135.refs_0_), channel_id=1, source_target_pairs={{0,4},{4,0},{8,12},{12,8},{1,5},{5,1},{9,13},{13,9},{2,6},{6,2},{1... | collective-permute-start | bytes 172040 | tf_op jit(solution)/shard_map/ppermute | solution.py:536
  44.5 3.6 %collective-permute-done.12.near_ref = bf16[184,512]{1,0:T(8,128)(2,1)S(1)} collective-permute-done((bf16[184,512]{1,0:T(8,128)(2,1)S(1)}, bf16[184,512]{1,0:T(8,128)(2,1)S(1)}, u32[]{:S(2)}, u32[]{:S(2)}) %collective-permute-start.12) | collective-permute-done | bytes 188448 | tf_op jit(solution)/shard_map/ppermute | solution.py:536
  48.0 1.4 %collective-permute-start.9 = (bf16[224,128]{1,0:T(8,128)(2,1)S(1)}, bf16[224,128]{1,0:T(8,128)(2,1)S(1)}, u32[]{:S(2)}, u32[]{:S(2)}) collective-permute-start(bf16[224,128]{1,0:T(8,128)(2,1)S(1)} %shard_map.135.refs_0_), channel_id=1, source_target_pairs={{0,2},{2,0},{1,3},{3,1},{4,6},{6,4},{5,7},{7,5},{8,10},{10,8},{9,1... | collective-permute-start | bytes 172040 | tf_op jit(solution)/shard_map/ppermute | solution.py:536
  49.5 1.1 %shard_map.136 = (f32[2,768,128]{2,1,0:T(8,128)S(1)}, f32[2,768,128]{2,1,0:T(8,128)S(1)}) custom-call(s32[4]{0:T(128)S(1)} %copy-done.3, s32[6,9]{1,0:T(8,128)S(1)} %copy-done.2, bf16[2,768,128]{2,1,0:T(8,128)(2,1)S(1)} %collective-permute-done.3.first_rim, bf16[2,768,128]{2,1,0:T(8,128)(2,1)S(1)} %collective-permute-done.4.second_rim, ...), custom_call_target="tpu_custom_call" | custom-call | bytes 1024 | tf_op jit(solution)/shard_map/pallas_call | solution.py:61
  50.6 0.0 copy-done
  50.6 1.2 %shard_map.137 = (f32[2,768,128]{2,1,0:T(8,128)S(1)}, f32[2,768,128]{2,1,0:T(8,128)S(1)}) custom-call(s32[4]{0:T(128)S(1)} %copy-done.3, bf16[4,768,184]{2,1,0:T(8,128)(2,1)S(1)} %copy-done, f32[2,768,128]{2,1,0:T(8,128)S(1)} %get-tuple-element.83.base_ref, f32[2,768,128]{2,1,0:T(8,128)S(1)} %get-tuple-element.84.slope_ref, ...), custom_call_target="tpu_custom_call" | custom-call | bytes 1024 | tf_op jit(solution)/shard_map/pallas_call | solution.py:61
  51.8 0.0 collective-permute-done.11.refs_3_
  51.8 0.3 collective-permute-done.10.refs_2_
  52.1 0.1 collective-permute-done.9.refs_1_
  52.2 0.8 %shard_map.138 = (f32[2,384,128]{2,1,0:T(8,128)}, f32[9,128]{1,0:T(8,128)}) custom-call(bf16[224,128]{1,0:T(8,128)(2,1)S(1)} %shard_map.135.refs_0_, bf16[224,128]{1,0:T(8,128)(2,1)S(1)} %collective-permute-done.9.refs_1_, bf16[224,128]{1,0:T(8,128)(2,1)S(1)} %collective-permute-done.10.refs_2_, bf16[224,128]{1,0:T(8,128)(2,1)S(1)} %collective-permute-done.11.refs_3_), custom_call_target="tpu_custom_call" | custom-call | bytes 1024 | tf_op jit(solution)/shard_map/pallas_call | solution.py:61
  53.0 0.4 collective-permute-done.13.refs_0_
  53.4 0.0 collective-permute-done.14.refs_1_
  53.4 1.9 %shard_map.139 = (bf16[2,768,128]{2,1,0:T(8,128)(2,1)}, bf16[2,768,128]{2,1,0:T(8,128)(2,1)}) custom-call(s32[4]{0:T(128)S(1)} %copy-done.3, bf16[4,768,184]{2,1,0:T(8,128)(2,1)S(1)} %copy-done, f32[2,768,128]{2,1,0:T(8,128)S(1)} %get-tuple-element.91.sum_ref, f32[2,768,128]{2,1,0:T(8,128)S(1)} %get-tuple-element.92.early_ref, ...), custom_call_target="tpu_custom_call" | custom-call | flops 578813952 | bytes 1024 | tf_op jit(solution)/shard_map/pallas_call | solution.py:61
  (3 shorter events, 0.1 us)
Async XLA Ops:
  0.6 9.0 %copy-start.1 = (bf16[1,2,768,128]{3,2,1,0:T(8,128)(2,1)S(1)}, bf16[1,2,768,128]{3,2,1,0:T(8,128)(2,1)}, u32[]{:S(2)}) copy-start(bf16[1,2,768,128]{3,2,1,0:T(8,128)(2,1)} %param.11) | copy-start | bytes 1179652
  0.6 9.0 %copy-start.6 = (bf16[1,2,768,128]{3,2,1,0:T(8,128)(2,1)S(1)}, bf16[1,2,768,128]{3,2,1,0:T(8,128)(2,1)}, u32[]{:S(2)}) copy-start(bf16[1,2,768,128]{3,2,1,0:T(8,128)(2,1)} %param.10) | copy-start | bytes 1179652
  0.7 8.9 %copy-start.9 = (bf16[92,6,384]{2,0,1:T(8,128)(2,1)S(1)}, bf16[92,6,384]{2,0,1:T(8,128)(2,1)}, u32[]{:S(2)}) copy-start(bf16[92,6,384]{2,0,1:T(8,128)(2,1)} %param.15) | copy-start | bytes 1271812
  0.7 9.0 %copy-start.3 = (s32[4]{0:T(128)S(1)}, s32[4]{0:T(128)}, u32[]{:S(2)}) copy-start(s32[4]{0:T(128)} %rows_ref.13) | copy-start | bytes 52
  0.7 9.0 %copy-start.2 = (s32[6,9]{1,0:T(8,128)S(1)}, s32[6,9]{1,0:T(8,128)}, u32[]{:S(2)}) copy-start(s32[6,9]{1,0:T(8,128)} %shift_ref.5) | copy-start | bytes 652
  0.7 9.0 %copy-start.4 = (bf16[9,128]{1,0:T(8,128)(2,1)S(1)}, bf16[9,128]{1,0:T(8,128)(2,1)}, u32[]{:S(2)}) copy-start(bf16[9,128]{1,0:T(8,128)(2,1)} %taps_ref.3) | copy-start | bytes 6916
  0.7 9.0 %copy-start.7 = (bf16[2,384,128]{2,1,0:T(8,128)(2,1)S(1)}, bf16[2,384,128]{2,1,0:T(8,128)(2,1)}, u32[]{:S(2)}) copy-start(bf16[2,384,128]{2,1,0:T(8,128)(2,1)} %filter_ref.1) | copy-start | bytes 589828
  3.8 22.4 %copy-start.5 = (f32[6]{0:T(128)S(1)}, f32[6]{0:T(128)}, u32[]{:S(2)}) copy-start(f32[6]{0:T(128)} %quad_ref.3) | copy-start | bytes 76
  3.8 22.3 %copy-start.8 = (bf16[184,512]{1,0:T(8,128)(2,1)S(1)}, bf16[184,512]{1,0:T(8,128)(2,1)}, u32[]{:S(2)}) copy-start(bf16[184,512]{1,0:T(8,128)(2,1)} %get-tuple-element.57.refs_0_) | copy-start | bytes 565252
  3.8 11.0 %collective-permute-start.2 = (bf16[184,512]{1,0:T(8,128)(2,1)}, bf16[184,512]{1,0:T(8,128)(2,1)S(1)}, u32[]{:S(2)}, u32[]{:S(2)}) collective-permute-start(bf16[184,512]{1,0:T(8,128)(2,1)} %get-tuple-element.62), channel_id=1, source_target_pairs={{0,12},{4,8},{8,4},{12,0},{1,13},{5,9},{9,5},{13,1},{2,14},{6,10},... | collective-permute-start | bytes 565256 | tf_op jit(solution)/shard_map/ppermute | solution.py:536
  9.0 11.2 %collective-permute-start = (bf16[184,512]{1,0:T(8,128)(2,1)}, bf16[184,512]{1,0:T(8,128)(2,1)S(1)}, u32[]{:S(2)}, u32[]{:S(2)}) collective-permute-start(bf16[184,512]{1,0:T(8,128)(2,1)} %get-tuple-element.58), channel_id=1, source_target_pairs={{0,4},{4,0},{8,12},{12,8},{1,5},{5,1},{9,13},{13,9},{2,6},{6,2},{1... | collective-permute-start | bytes 565256 | tf_op jit(solution)/shard_map/ppermute | solution.py:536
  9.0 17.2 %collective-permute-start.1 = (bf16[184,512]{1,0:T(8,128)(2,1)}, bf16[184,512]{1,0:T(8,128)(2,1)S(1)}, u32[]{:S(2)}, u32[]{:S(2)}) collective-permute-start(bf16[184,512]{1,0:T(8,128)(2,1)} %get-tuple-element.59), channel_id=1, source_target_pairs={{0,8},{4,12},{8,0},{12,4},{1,9},{5,13},{9,1},{13,5},{2,10},{6,14},... | collective-permute-start | bytes 565256 | tf_op jit(solution)/shard_map/ppermute | solution.py:536
  14.9 18.5 %collective-permute-start.3 = (bf16[2,768,128]{2,1,0:T(8,128)(2,1)S(1)}, bf16[2,768,128]{2,1,0:T(8,128)(2,1)S(1)}, u32[]{:S(2)}, u32[]{:S(2)}) collective-permute-start(bf16[2,768,128]{2,1,0:T(8,128)(2,1)S(1)} %get-tuple-element.70), channel_id=1, source_target_pairs={{0,4},{4,0},{8,12},{12,8},{1,5},{5,1},{9,13},{13,9},{2,6},{6,2},{1... | collective-permute-start | bytes 1179656 | tf_op jit(solution)/shard_map/ppermute | solution.py:536
  19.4 14.0 %collective-permute-start.4 = (bf16[2,768,128]{2,1,0:T(8,128)(2,1)S(1)}, bf16[2,768,128]{2,1,0:T(8,128)(2,1)S(1)}, u32[]{:S(2)}, u32[]{:S(2)}) collective-permute-start(bf16[2,768,128]{2,1,0:T(8,128)(2,1)S(1)} %get-tuple-element.71), channel_id=1, source_target_pairs={{4,8},{8,4},{5,9},{9,5},{6,10},{10,6},{7,11},{11,7},{20,24},{24,20... | collective-permute-start | bytes 1179656 | tf_op jit(solution)/shard_map/ppermute | solution.py:613
  28.1 6.3 %collective-permute-start.5 = (bf16[192,128]{1,0:T(8,128)(2,1)S(1)}, bf16[192,128]{1,0:T(8,128)(2,1)S(1)}, u32[]{:S(2)}, u32[]{:S(2)}) collective-permute-start(bf16[192,128]{1,0:T(8,128)(2,1)S(1)} %get-tuple-element.78), channel_id=1, source_target_pairs={{0,6},{2,4},{4,2},{6,0},{8,14},{10,12},{12,10},{14,8},{1,7},{3,5},... | collective-permute-start | bytes 147464 | tf_op jit(solution)/shard_map/ppermute | solution.py:545
  29.0 5.4 %collective-permute-start.6 = (bf16[192,128]{1,0:T(8,128)(2,1)S(1)}, bf16[192,128]{1,0:T(8,128)(2,1)S(1)}, u32[]{:S(2)}, u32[]{:S(2)}) collective-permute-start(bf16[192,128]{1,0:T(8,128)(2,1)S(1)} %get-tuple-element.79), channel_id=1, source_target_pairs={{0,2},{2,0},{1,3},{3,1},{4,6},{6,4},{5,7},{7,5},{8,10},{10,8},{9,1... | collective-permute-start | bytes 147464 | tf_op jit(solution)/shard_map/ppermute | solution.py:536
  29.7 4.7 %collective-permute-start.7 = (bf16[192,128]{1,0:T(8,128)(2,1)S(1)}, bf16[192,128]{1,0:T(8,128)(2,1)S(1)}, u32[]{:S(2)}, u32[]{:S(2)}) collective-permute-start(bf16[192,128]{1,0:T(8,128)(2,1)S(1)} %get-tuple-element.80), channel_id=1, source_target_pairs={{0,4},{4,0},{8,12},{12,8},{1,5},{5,1},{9,13},{13,9},{2,6},{6,2},{1... | collective-permute-start | bytes 147464 | tf_op jit(solution)/shard_map/ppermute | solution.py:536
  34.5 7.0 %collective-permute-start.8 = (bf16[224,128]{1,0:T(8,128)(2,1)S(1)}, bf16[224,128]{1,0:T(8,128)(2,1)S(1)}, u32[]{:S(2)}, u32[]{:S(2)}) collective-permute-start(bf16[224,128]{1,0:T(8,128)(2,1)S(1)} %shard_map.134.own_ref), channel_id=1, source_target_pairs={{0,8},{4,12},{8,0},{12,4},{1,9},{5,13},{9,1},{13,5},{2,10},{6,14},... | collective-permute-start | bytes 172040 | tf_op jit(solution)/shard_map/ppermute | solution.py:536
  37.0 11.1 %collective-permute-start.12 = (bf16[184,512]{1,0:T(8,128)(2,1)S(1)}, bf16[184,512]{1,0:T(8,128)(2,1)S(1)}, u32[]{:S(2)}, u32[]{:S(2)}) collective-permute-start(bf16[184,512]{1,0:T(8,128)(2,1)S(1)} %get-tuple-element.89), channel_id=1, source_target_pairs={{0,4},{4,0},{8,12},{12,8},{1,5},{5,1},{9,13},{13,9},{2,6},{6,2},{1... | collective-permute-start | bytes 565256 | tf_op jit(solution)/shard_map/ppermute | solution.py:536
  37.7 15.7 %collective-permute-start.13 = (bf16[184,512]{1,0:T(8,128)(2,1)S(1)}, bf16[184,512]{1,0:T(8,128)(2,1)S(1)}, u32[]{:S(2)}, u32[]{:S(2)}) collective-permute-start(bf16[184,512]{1,0:T(8,128)(2,1)S(1)} %get-tuple-element.93), channel_id=1, source_target_pairs={{0,8},{4,12},{8,0},{12,4},{1,9},{5,13},{9,1},{13,5},{2,10},{6,14},... | collective-permute-start | bytes 565256 | tf_op jit(solution)/shard_map/ppermute | solution.py:536
  38.8 14.6 %collective-permute-start.14 = (bf16[184,512]{1,0:T(8,128)(2,1)S(1)}, bf16[184,512]{1,0:T(8,128)(2,1)S(1)}, u32[]{:S(2)}, u32[]{:S(2)}) collective-permute-start(bf16[184,512]{1,0:T(8,128)(2,1)S(1)} %get-tuple-element.94), channel_id=1, source_target_pairs={{0,12},{4,8},{8,4},{12,0},{1,13},{5,9},{9,5},{13,1},{2,14},{6,10},... | collective-permute-start | bytes 565256 | tf_op jit(solution)/shard_map/ppermute | solution.py:536
  41.5 9.1 %copy-start = (bf16[4,768,184]{2,1,0:T(8,128)(2,1)S(1)}, bf16[4,768,184]{2,1,0:T(8,128)(2,1)}, u32[]{:S(2)}) copy-start(bf16[4,768,184]{2,1,0:T(8,128)(2,1)} %constant.8.clone.table_ref) | copy-start | bytes 3391492
  41.5 10.3 %collective-permute-start.11 = (bf16[224,128]{1,0:T(8,128)(2,1)S(1)}, bf16[224,128]{1,0:T(8,128)(2,1)S(1)}, u32[]{:S(2)}, u32[]{:S(2)}) collective-permute-start(bf16[224,128]{1,0:T(8,128)(2,1)S(1)} %shard_map.135.refs_0_), channel_id=1, source_target_pairs={{0,6},{2,4},{4,2},{6,0},{8,14},{10,12},{12,10},{14,8},{1,7},{3,5},... | collective-permute-start | bytes 172040 | tf_op jit(solution)/shard_map/ppermute | solution.py:545
  43.0 9.1 %collective-permute-start.10 = (bf16[224,128]{1,0:T(8,128)(2,1)S(1)}, bf16[224,128]{1,0:T(8,128)(2,1)S(1)}, u32[]{:S(2)}, u32[]{:S(2)}) collective-permute-start(bf16[224,128]{1,0:T(8,128)(2,1)S(1)} %shard_map.135.refs_0_), channel_id=1, source_target_pairs={{0,4},{4,0},{8,12},{12,8},{1,5},{5,1},{9,13},{13,9},{2,6},{6,2},{1... | collective-permute-start | bytes 172040 | tf_op jit(solution)/shard_map/ppermute | solution.py:536
  48.0 4.2 %collective-permute-start.9 = (bf16[224,128]{1,0:T(8,128)(2,1)S(1)}, bf16[224,128]{1,0:T(8,128)(2,1)S(1)}, u32[]{:S(2)}, u32[]{:S(2)}) collective-permute-start(bf16[224,128]{1,0:T(8,128)(2,1)S(1)} %shard_map.135.refs_0_), channel_id=1, source_target_pairs={{0,2},{2,0},{1,3},{3,1},{4,6},{6,4},{5,7},{7,5},{8,10},{10,8},{9,1... | collective-permute-start | bytes 172040 | tf_op jit(solution)/shard_map/ppermute | solution.py:536

commit v10 on v9

--- a/solution.py
+++ b/solution.py
@@ -644,7 +644,7 @@
     back_parts, tap_part = lax.optimization_barrier((back_parts, tap_part))
     message = shape((share + 2 * TAP_ROWS, chans), BF16)
     back_parts, tap_part = lax.optimization_barrier((back_parts, tap_part))
-    own = call(quarter_kernel, message, [VMEM] * 5, (keep, *[got_sums[at] for at in (2, 0, 1)], tap_part))
+    own = call(quarter_kernel, message, [VMEM] * 5, (keep, *[got_sums[at] for at in (2, 1, 0)], tap_part))
     back_parts, own = lax.optimization_barrier((back_parts, own))
     returned = [back_parts[0], *reversed(crossed_all(back_parts, far).values())]
     steps = [(1 << bit, "space") for bit in range(1, blocks.bit_length() - 1)]

time: 55.6 us -> 55.8 us (level)
  waiting for transfers between devices: 10.5 us -> 15 us
  starting transfers between devices: 25.8 us -> 21.6 us
    ppermute x12, waiting for transfers between devices: 10.5 us -> 15 us  [crossed(): return lax.ppermute(values, axis, [(i, i ^ distance) for i in range(count)])]
    ppermute x12, starting transfers between devices: 22.7 us -> 19.9 us  [crossed(): return lax.ppermute(values, axis, [(i, i ^ distance) for i in range(count)])]
    ppermute x2, starting transfers between devices: 2.41 us -> 0.98 us  [around(): lax.ppermute(parts[2], ('space', 'ens'), [(i, i ^ flip) for i in range(co...]
  transfers between devices with their start and end apart: 15 -> 15, of which waited for: 6 -> 7; matrix products, arithmetic and copies ran while one was open for 0% -> 0% of each run, Pallas kernels for 23% -> 23%
where the time goes in v10:
time: 55.8 us; the launch traced here: 55.6 us
  starting transfers between devices  21.6 us (39%)
  Pallas kernels  18 us (32%)
  waiting for transfers between devices  15 us (27%)
  between operations  0.89 us (2%)
    ppermute x12, starting transfers between devices, crossed(): return lax.ppermute(values, axis, [(i, i ^ distance) for i in range(count)])  19.9 us
    pallas_call x11, Pallas kernels, call(): pl.pallas_call(kernel, out_shape=out_shape, in_specs=in_specs, out_specs=...  18 us
    ppermute x12, waiting for transfers between devices, crossed(): return lax.ppermute(values, axis, [(i, i ^ distance) for i in range(count)])  15 us
  transfers between devices with their start and end apart: 15, of which 7 were waited for; matrix products, arithmetic and copies ran while one was open for 0% of the time, Pallas kernels for 23%

profile of v10, /device:TPU:0, one launch (start us, length us, event | category | flops | bytes accessed | tf_op | source)
XLA Modules:
  0.0 55.6 jit_solution(10431066855819167408)
XLA Ops:
  0.6 0.0 copy-start.1
  0.6 0.0 copy-start.6
  0.7 0.0 copy-start.9
  0.7 0.0 copy-start.3
  0.7 0.0 copy-start.2
  0.7 0.0 copy-start.4
  0.7 0.0 copy-start.7
  0.7 3.1 %shard_map.130 = (bf16[184,512]{1,0:T(8,128)(2,1)}, bf16[184,512]{1,0:T(8,128)(2,1)}, bf16[184,512]{1,0:T(8,128)(2,1)}, bf16[184,512]{1,0:T(8,128)(2,1)}) custom-call(bf16[2,768,128]{2,1,0:T(8,128)(2,1)} %bitcast.8, bf16[2,768,128]{2,1,0:T(8,128)(2,1)} %bitcast.5, bf16[4,184,768]{2,1,0:T(8,128)(2,1)} %constant.7.clone.table_hbm), custom_call_target="tpu_custom_call" | custom-call | flops 578813952 | bytes 1024 | tf_op jit(solution)/shard_map/pallas_call | solution.py:61
  3.8 0.0 copy-start.5
  3.8 0.0 copy-start.8
  3.8 5.1 %collective-permute-start.2 = (bf16[184,512]{1,0:T(8,128)(2,1)}, bf16[184,512]{1,0:T(8,128)(2,1)S(1)}, u32[]{:S(2)}, u32[]{:S(2)}) collective-permute-start(bf16[184,512]{1,0:T(8,128)(2,1)} %get-tuple-element.62), channel_id=1, source_target_pairs={{0,12},{4,8},{8,4},{12,0},{1,13},{5,9},{9,5},{13,1},{2,14},{6,10},... | collective-permute-start | bytes 565256 | tf_op jit(solution)/shard_map/ppermute | solution.py:536
  9.0 0.0 collective-permute-start
  9.0 0.6 %collective-permute-start.1 = (bf16[184,512]{1,0:T(8,128)(2,1)}, bf16[184,512]{1,0:T(8,128)(2,1)S(1)}, u32[]{:S(2)}, u32[]{:S(2)}) collective-permute-start(bf16[184,512]{1,0:T(8,128)(2,1)} %get-tuple-element.59), channel_id=1, source_target_pairs={{0,8},{4,12},{8,0},{12,4},{1,9},{5,13},{9,1},{13,5},{2,10},{6,14},... | collective-permute-start | bytes 565256 | tf_op jit(solution)/shard_map/ppermute | solution.py:536
  9.6 0.0 copy-done.9
  9.7 0.0 copy-done.1
  9.7 0.0 copy-done.6
  9.7 0.0 copy-done.3
  9.7 0.0 copy-done.2
  9.7 0.0 copy-done.4
  9.7 0.0 copy-done.7
  9.7 5.1 %shard_map.129 = (f32[2048,256]{1,0:T(8,128)S(1)}, bf16[384,2048]{1,0:T(8,128)(2,1)S(1)}, bf16[2,768,128]{2,1,0:T(8,128)(2,1)S(1)}, bf16[2,768,128]{2,1,0:T(8,12...) custom-call(s32[4]{0:T(128)S(1)} %copy-done.3, ...), custom_call_target="tpu_custom_call" | custom-call | flops 402653184 | bytes 2097152 | tf_op jit(solution)/shard_map/pallas_call | solution.py:61
  14.9 0.0 collective-permute-done.2.refs_3_
  14.9 4.6 %collective-permute-start.3 = (bf16[2,768,128]{2,1,0:T(8,128)(2,1)S(1)}, bf16[2,768,128]{2,1,0:T(8,128)(2,1)S(1)}, u32[]{:S(2)}, u32[]{:S(2)}) collective-permute-start(bf16[2,768,128]{2,1,0:T(8,128)(2,1)S(1)} %get-tuple-element.70), channel_id=1, source_target_pairs={{0,4},{4,0},{8,12},{12,8},{1,5},{5,1},{9,13},{13,9},{2,6},{6,2},{1... | collective-permute-start | bytes 1179656 | tf_op jit(solution)/shard_map/ppermute | solution.py:536
  19.4 0.7 %collective-permute-start.4 = (bf16[2,768,128]{2,1,0:T(8,128)(2,1)S(1)}, bf16[2,768,128]{2,1,0:T(8,128)(2,1)S(1)}, u32[]{:S(2)}, u32[]{:S(2)}) collective-permute-start(bf16[2,768,128]{2,1,0:T(8,128)(2,1)S(1)} %get-tuple-element.71), channel_id=1, source_target_pairs={{4,8},{8,4},{5,9},{9,5},{6,10},{10,6},{7,11},{11,7},{20,24},{24,20... | collective-permute-start | bytes 1179656 | tf_op jit(solution)/shard_map/ppermute | solution.py:613
  20.1 0.0 collective-permute-done.refs_1_
  20.1 6.0 %collective-permute-done.1.refs_2_ = bf16[184,512]{1,0:T(8,128)(2,1)S(1)} collective-permute-done((bf16[184,512]{1,0:T(8,128)(2,1)}, bf16[184,512]{1,0:T(8,128)(2,1)S(1)}, u32[]{:S(2)}, u32[]{:S(2)}) %collective-permute-start.1) | collective-permute-done | bytes 188448 | tf_op jit(solution)/shard_map/ppermute | solution.py:536
  26.2 0.0 copy-done.5
  26.2 0.0 copy-done.8
  26.2 1.9 %shard_map.131 = (f32[192,128]{1,0:T(8,128)S(1)}, bf16[192,128]{1,0:T(8,128)(2,1)S(1)}, bf16[192,128]{1,0:T(8,128)(2,1)S(1)}, bf16[192,128]{1,0:T(8,128)(2,1)S(1...) custom-call(s32[4]{0:T(128)S(1)} %copy-done.3, f32[6]{0:T(128)S(1)} %copy-done.5, ...), custom_call_target="tpu_custom_call" | custom-call | flops 4026531840 | bytes 1024 | tf_op jit(solution)/shard_map/pallas_call | solution.py:61
  28.1 0.9 %collective-permute-start.5 = (bf16[192,128]{1,0:T(8,128)(2,1)S(1)}, bf16[192,128]{1,0:T(8,128)(2,1)S(1)}, u32[]{:S(2)}, u32[]{:S(2)}) collective-permute-start(bf16[192,128]{1,0:T(8,128)(2,1)S(1)} %get-tuple-element.78), channel_id=1, source_target_pairs={{0,6},{2,4},{4,2},{6,0},{8,14},{10,12},{12,10},{14,8},{1,7},{3,5},... | collective-permute-start | bytes 147464 | tf_op jit(solution)/shard_map/ppermute | solution.py:545
  29.0 2.1 %collective-permute-start.6 = (bf16[192,128]{1,0:T(8,128)(2,1)S(1)}, bf16[192,128]{1,0:T(8,128)(2,1)S(1)}, u32[]{:S(2)}, u32[]{:S(2)}) collective-permute-start(bf16[192,128]{1,0:T(8,128)(2,1)S(1)} %get-tuple-element.79), channel_id=1, source_target_pairs={{0,4},{4,0},{8,12},{12,8},{1,5},{5,1},{9,13},{13,9},{2,6},{6,2},{1... | collective-permute-start | bytes 147464 | tf_op jit(solution)/shard_map/ppermute | solution.py:536
  31.1 0.5 collective-permute-start.7
  31.7 1.7 %shard_map.132 = (bf16[184,512]{1,0:T(8,128)(2,1)S(1)}, bf16[184,512]{1,0:T(8,128)(2,1)S(1)}, bf16[184,512]{1,0:T(8,128)(2,1)S(1)}, bf16[184,512]{1,0:T(8,128)(2,1)S(1)}) custom-call(s32[4]{0:T(128)S(1)} %copy-done.3, f32[6]{0:T(128)S(1)} %copy-done.5, f32[2048,256]{1,0:T(8,128)S(1)} %get-tuple-element.55.mixer_ref, ...), custom_call_target="tpu_custom_call" | custom-call | bytes 1024 | tf_op jit(solution)/shard_map/pallas_call | solution.py:61
  33.4 0.0 collective-permute-done.3.first_rim
  33.4 0.0 collective-permute-done.4.second_rim
  33.4 1.0 %shard_map.133.tap_ref = f32[16,128]{1,0:T(8,128)S(1)} custom-call(s32[4]{0:T(128)S(1)} %copy-done.3, s32[6,9]{1,0:T(8,128)S(1)} %copy-done.2, bf16[2,768,128]{2,1,0:T(8,128)(2,1)S(1)} %bitcast.7, bf16[2,768,128]{2,1,0:T(8,128)(2,1)S(1)} %collective-permute-done.3.first_rim, bf16[2,768,128]{2,1,0:T(8,128)(2,1)S(1)} %collective-permute-done.4.second_rim, ...), custom_call_target="tpu_custom_call" | custom-call | bytes 1024 | tf_op jit(solution)/shard_map/pallas_call | solution.py:61
  34.4 0.0 collective-permute-done.5.first_ref
  34.4 0.0 collective-permute-done.6.second_ref
  34.4 0.8 %collective-permute-done.7.third_ref = bf16[192,128]{1,0:T(8,128)(2,1)S(1)} collective-permute-done((bf16[192,128]{1,0:T(8,128)(2,1)S(1)}, bf16[192,128]{1,0:T(8,128)(2,1)S(1)}, u32[]{:S(2)}, u32[]{:S(2)}) %collective-permute-start.7) | collective-permute-done | bytes 49184 | tf_op jit(solution)/shard_map/ppermute | solution.py:536
  35.2 1.3 %collective-permute-start.8 = (bf16[224,128]{1,0:T(8,128)(2,1)S(1)}, bf16[224,128]{1,0:T(8,128)(2,1)S(1)}, u32[]{:S(2)}, u32[]{:S(2)}) collective-permute-start(bf16[224,128]{1,0:T(8,128)(2,1)S(1)} %shard_map.134.own_ref), channel_id=1, source_target_pairs={{0,8},{4,12},{8,0},{12,4},{1,9},{5,13},{9,1},{13,5},{2,10},{6,14},... | collective-permute-start | bytes 172040 | tf_op jit(solution)/shard_map/ppermute | solution.py:536
  36.5 2.0 %collective-permute-start.12 = (bf16[184,512]{1,0:T(8,128)(2,1)S(1)}, bf16[184,512]{1,0:T(8,128)(2,1)S(1)}, u32[]{:S(2)}, u32[]{:S(2)}) collective-permute-start(bf16[184,512]{1,0:T(8,128)(2,1)S(1)} %get-tuple-element.89), channel_id=1, source_target_pairs={{0,4},{4,0},{8,12},{12,8},{1,5},{5,1},{9,13},{13,9},{2,6},{6,2},{1... | collective-permute-start | bytes 565256 | tf_op jit(solution)/shard_map/ppermute | solution.py:536
  38.5 0.1 collective-permute-start.13
  38.6 2.3 %collective-permute-start.14 = (bf16[184,512]{1,0:T(8,128)(2,1)S(1)}, bf16[184,512]{1,0:T(8,128)(2,1)S(1)}, u32[]{:S(2)}, u32[]{:S(2)}) collective-permute-start(bf16[184,512]{1,0:T(8,128)(2,1)S(1)} %get-tuple-element.94), channel_id=1, source_target_pairs={{0,12},{4,8},{8,4},{12,0},{1,13},{5,9},{9,5},{13,1},{2,14},{6,10},... | collective-permute-start | bytes 565256 | tf_op jit(solution)/shard_map/ppermute | solution.py:536
  40.9 2.2 %collective-permute-done.8.other_ref = bf16[224,128]{1,0:T(8,128)(2,1)S(1)} collective-permute-done((bf16[224,128]{1,0:T(8,128)(2,1)S(1)}, bf16[224,128]{1,0:T(8,128)(2,1)S(1)}, u32[]{:S(2)}, u32[]{:S(2)}) %collective-permute-start.8) | collective-permute-done | bytes 57376 | tf_op jit(solution)/shard_map/ppermute | solution.py:536
  43.1 0.0 copy-start
  43.1 0.1 collective-permute-start.11
  43.2 0.7 %collective-permute-start.10 = (bf16[224,128]{1,0:T(8,128)(2,1)S(1)}, bf16[224,128]{1,0:T(8,128)(2,1)S(1)}, u32[]{:S(2)}, u32[]{:S(2)}) collective-permute-start(bf16[224,128]{1,0:T(8,128)(2,1)S(1)} %shard_map.135.refs_0_), channel_id=1, source_target_pairs={{0,4},{4,0},{8,12},{12,8},{1,5},{5,1},{9,13},{13,9},{2,6},{6,2},{1... | collective-permute-start | bytes 172040 | tf_op jit(solution)/shard_map/ppermute | solution.py:536
  43.9 4.2 %collective-permute-done.12.near_ref = bf16[184,512]{1,0:T(8,128)(2,1)S(1)} collective-permute-done((bf16[184,512]{1,0:T(8,128)(2,1)S(1)}, bf16[184,512]{1,0:T(8,128)(2,1)S(1)}, u32[]{:S(2)}, u32[]{:S(2)}) %collective-permute-start.12) | collective-permute-done | bytes 188448 | tf_op jit(solution)/shard_map/ppermute | solution.py:536
  48.1 0.7 %collective-permute-start.9 = (bf16[224,128]{1,0:T(8,128)(2,1)S(1)}, bf16[224,128]{1,0:T(8,128)(2,1)S(1)}, u32[]{:S(2)}, u32[]{:S(2)}) collective-permute-start(bf16[224,128]{1,0:T(8,128)(2,1)S(1)} %shard_map.135.refs_0_), channel_id=1, source_target_pairs={{0,2},{2,0},{1,3},{3,1},{4,6},{6,4},{5,7},{7,5},{8,10},{10,8},{9,1... | collective-permute-start | bytes 172040 | tf_op jit(solution)/shard_map/ppermute | solution.py:536
  48.7 1.1 %shard_map.136 = (f32[2,768,128]{2,1,0:T(8,128)S(1)}, f32[2,768,128]{2,1,0:T(8,128)S(1)}) custom-call(s32[4]{0:T(128)S(1)} %copy-done.3, s32[6,9]{1,0:T(8,128)S(1)} %copy-done.2, bf16[2,768,128]{2,1,0:T(8,128)(2,1)S(1)} %collective-permute-done.3.first_rim, bf16[2,768,128]{2,1,0:T(8,128)(2,1)S(1)} %collective-permute-done.4.second_rim, ...), custom_call_target="tpu_custom_call" | custom-call | bytes 1024 | tf_op jit(solution)/shard_map/pallas_call | solution.py:61
  49.9 0.0 copy-done
  49.9 1.2 %shard_map.137 = (f32[2,768,128]{2,1,0:T(8,128)S(1)}, f32[2,768,128]{2,1,0:T(8,128)S(1)}) custom-call(s32[4]{0:T(128)S(1)} %copy-done.3, bf16[4,768,184]{2,1,0:T(8,128)(2,1)S(1)} %copy-done, f32[2,768,128]{2,1,0:T(8,128)S(1)} %get-tuple-element.83.base_ref, f32[2,768,128]{2,1,0:T(8,128)S(1)} %get-tuple-element.84.slope_ref, ...), custom_call_target="tpu_custom_call" | custom-call | bytes 1024 | tf_op jit(solution)/shard_map/pallas_call | solution.py:61
  51.0 0.0 collective-permute-done.11.refs_3_
  51.1 0.2 collective-permute-done.10.refs_2_
  51.2 1.0 %collective-permute-done.9.refs_1_ = bf16[224,128]{1,0:T(8,128)(2,1)S(1)} collective-permute-done((bf16[224,128]{1,0:T(8,128)(2,1)S(1)}, bf16[224,128]{1,0:T(8,128)(2,1)S(1)}, u32[]{:S(2)}, u32[]{:S(2)}) %collective-permute-start.9) | collective-permute-done | bytes 57376 | tf_op jit(solution)/shard_map/ppermute | solution.py:536
  52.2 0.8 %shard_map.138 = (f32[2,384,128]{2,1,0:T(8,128)}, f32[9,128]{1,0:T(8,128)}) custom-call(bf16[224,128]{1,0:T(8,128)(2,1)S(1)} %shard_map.135.refs_0_, bf16[224,128]{1,0:T(8,128)(2,1)S(1)} %collective-permute-done.9.refs_1_, bf16[224,128]{1,0:T(8,128)(2,1)S(1)} %collective-permute-done.10.refs_2_, bf16[224,128]{1,0:T(8,128)(2,1)S(1)} %collective-permute-done.11.refs_3_), custom_call_target="tpu_custom_call" | custom-call | bytes 1024 | tf_op jit(solution)/shard_map/pallas_call | solution.py:61
  53.0 0.6 %collective-permute-done.13.refs_0_ = bf16[184,512]{1,0:T(8,128)(2,1)S(1)} collective-permute-done((bf16[184,512]{1,0:T(8,128)(2,1)S(1)}, bf16[184,512]{1,0:T(8,128)(2,1)S(1)}, u32[]{:S(2)}, u32[]{:S(2)}) %collective-permute-start.13) | collective-permute-done | bytes 188448 | tf_op jit(solution)/shard_map/ppermute | solution.py:536
  53.6 0.0 collective-permute-done.14.refs_1_
  53.6 1.9 %shard_map.139 = (bf16[2,768,128]{2,1,0:T(8,128)(2,1)}, bf16[2,768,128]{2,1,0:T(8,128)(2,1)}) custom-call(s32[4]{0:T(128)S(1)} %copy-done.3, bf16[4,768,184]{2,1,0:T(8,128)(2,1)S(1)} %copy-done, f32[2,768,128]{2,1,0:T(8,128)S(1)} %get-tuple-element.91.sum_ref, f32[2,768,128]{2,1,0:T(8,128)S(1)} %get-tuple-element.92.early_ref, ...), custom_call_target="tpu_custom_call" | custom-call | flops 578813952 | bytes 1024 | tf_op jit(solution)/shard_map/pallas_call | solution.py:61
  (3 shorter events, 0.1 us)
Async XLA Ops:
  0.6 9.0 %copy-start.1 = (bf16[1,2,768,128]{3,2,1,0:T(8,128)(2,1)S(1)}, bf16[1,2,768,128]{3,2,1,0:T(8,128)(2,1)}, u32[]{:S(2)}) copy-start(bf16[1,2,768,128]{3,2,1,0:T(8,128)(2,1)} %param.11) | copy-start | bytes 1179652
  0.6 9.0 %copy-start.6 = (bf16[1,2,768,128]{3,2,1,0:T(8,128)(2,1)S(1)}, bf16[1,2,768,128]{3,2,1,0:T(8,128)(2,1)}, u32[]{:S(2)}) copy-start(bf16[1,2,768,128]{3,2,1,0:T(8,128)(2,1)} %param.10) | copy-start | bytes 1179652
  0.7 8.9 %copy-start.9 = (bf16[92,6,384]{2,0,1:T(8,128)(2,1)S(1)}, bf16[92,6,384]{2,0,1:T(8,128)(2,1)}, u32[]{:S(2)}) copy-start(bf16[92,6,384]{2,0,1:T(8,128)(2,1)} %param.15) | copy-start | bytes 1271812
  0.7 9.0 %copy-start.3 = (s32[4]{0:T(128)S(1)}, s32[4]{0:T(128)}, u32[]{:S(2)}) copy-start(s32[4]{0:T(128)} %rows_ref.13) | copy-start | bytes 52
  0.7 9.0 %copy-start.2 = (s32[6,9]{1,0:T(8,128)S(1)}, s32[6,9]{1,0:T(8,128)}, u32[]{:S(2)}) copy-start(s32[6,9]{1,0:T(8,128)} %shift_ref.5) | copy-start | bytes 652
  0.7 9.0 %copy-start.4 = (bf16[9,128]{1,0:T(8,128)(2,1)S(1)}, bf16[9,128]{1,0:T(8,128)(2,1)}, u32[]{:S(2)}) copy-start(bf16[9,128]{1,0:T(8,128)(2,1)} %taps_ref.3) | copy-start | bytes 6916
  0.7 9.0 %copy-start.7 = (bf16[2,384,128]{2,1,0:T(8,128)(2,1)S(1)}, bf16[2,384,128]{2,1,0:T(8,128)(2,1)}, u32[]{:S(2)}) copy-start(bf16[2,384,128]{2,1,0:T(8,128)(2,1)} %filter_ref.1) | copy-start | bytes 589828
  3.8 22.4 %copy-start.5 = (f32[6]{0:T(128)S(1)}, f32[6]{0:T(128)}, u32[]{:S(2)}) copy-start(f32[6]{0:T(128)} %quad_ref.3) | copy-start | bytes 76
  3.8 22.3 %copy-start.8 = (bf16[184,512]{1,0:T(8,128)(2,1)S(1)}, bf16[184,512]{1,0:T(8,128)(2,1)}, u32[]{:S(2)}) copy-start(bf16[184,512]{1,0:T(8,128)(2,1)} %get-tuple-element.57.refs_0_) | copy-start | bytes 565252
  3.8 11.0 %collective-permute-start.2 = (bf16[184,512]{1,0:T(8,128)(2,1)}, bf16[184,512]{1,0:T(8,128)(2,1)S(1)}, u32[]{:S(2)}, u32[]{:S(2)}) collective-permute-start(bf16[184,512]{1,0:T(8,128)(2,1)} %get-tuple-element.62), channel_id=1, source_target_pairs={{0,12},{4,8},{8,4},{12,0},{1,13},{5,9},{9,5},{13,1},{2,14},{6,10},... | collective-permute-start | bytes 565256 | tf_op jit(solution)/shard_map/ppermute | solution.py:536
  9.0 11.2 %collective-permute-start = (bf16[184,512]{1,0:T(8,128)(2,1)}, bf16[184,512]{1,0:T(8,128)(2,1)S(1)}, u32[]{:S(2)}, u32[]{:S(2)}) collective-permute-start(bf16[184,512]{1,0:T(8,128)(2,1)} %get-tuple-element.58), channel_id=1, source_target_pairs={{0,4},{4,0},{8,12},{12,8},{1,5},{5,1},{9,13},{13,9},{2,6},{6,2},{1... | collective-permute-start | bytes 565256 | tf_op jit(solution)/shard_map/ppermute | solution.py:536
  9.0 17.2 %collective-permute-start.1 = (bf16[184,512]{1,0:T(8,128)(2,1)}, bf16[184,512]{1,0:T(8,128)(2,1)S(1)}, u32[]{:S(2)}, u32[]{:S(2)}) collective-permute-start(bf16[184,512]{1,0:T(8,128)(2,1)} %get-tuple-element.59), channel_id=1, source_target_pairs={{0,8},{4,12},{8,0},{12,4},{1,9},{5,13},{9,1},{13,5},{2,10},{6,14},... | collective-permute-start | bytes 565256 | tf_op jit(solution)/shard_map/ppermute | solution.py:536
  14.9 18.5 %collective-permute-start.3 = (bf16[2,768,128]{2,1,0:T(8,128)(2,1)S(1)}, bf16[2,768,128]{2,1,0:T(8,128)(2,1)S(1)}, u32[]{:S(2)}, u32[]{:S(2)}) collective-permute-start(bf16[2,768,128]{2,1,0:T(8,128)(2,1)S(1)} %get-tuple-element.70), channel_id=1, source_target_pairs={{0,4},{4,0},{8,12},{12,8},{1,5},{5,1},{9,13},{13,9},{2,6},{6,2},{1... | collective-permute-start | bytes 1179656 | tf_op jit(solution)/shard_map/ppermute | solution.py:536
  19.4 14.0 %collective-permute-start.4 = (bf16[2,768,128]{2,1,0:T(8,128)(2,1)S(1)}, bf16[2,768,128]{2,1,0:T(8,128)(2,1)S(1)}, u32[]{:S(2)}, u32[]{:S(2)}) collective-permute-start(bf16[2,768,128]{2,1,0:T(8,128)(2,1)S(1)} %get-tuple-element.71), channel_id=1, source_target_pairs={{4,8},{8,4},{5,9},{9,5},{6,10},{10,6},{7,11},{11,7},{20,24},{24,20... | collective-permute-start | bytes 1179656 | tf_op jit(solution)/shard_map/ppermute | solution.py:613
  28.1 6.3 %collective-permute-start.5 = (bf16[192,128]{1,0:T(8,128)(2,1)S(1)}, bf16[192,128]{1,0:T(8,128)(2,1)S(1)}, u32[]{:S(2)}, u32[]{:S(2)}) collective-permute-start(bf16[192,128]{1,0:T(8,128)(2,1)S(1)} %get-tuple-element.78), channel_id=1, source_target_pairs={{0,6},{2,4},{4,2},{6,0},{8,14},{10,12},{12,10},{14,8},{1,7},{3,5},... | collective-permute-start | bytes 147464 | tf_op jit(solution)/shard_map/ppermute | solution.py:545
  29.0 5.4 %collective-permute-start.6 = (bf16[192,128]{1,0:T(8,128)(2,1)S(1)}, bf16[192,128]{1,0:T(8,128)(2,1)S(1)}, u32[]{:S(2)}, u32[]{:S(2)}) collective-permute-start(bf16[192,128]{1,0:T(8,128)(2,1)S(1)} %get-tuple-element.79), channel_id=1, source_target_pairs={{0,4},{4,0},{8,12},{12,8},{1,5},{5,1},{9,13},{13,9},{2,6},{6,2},{1... | collective-permute-start | bytes 147464 | tf_op jit(solution)/shard_map/ppermute | solution.py:536
  31.1 4.1 %collective-permute-start.7 = (bf16[192,128]{1,0:T(8,128)(2,1)S(1)}, bf16[192,128]{1,0:T(8,128)(2,1)S(1)}, u32[]{:S(2)}, u32[]{:S(2)}) collective-permute-start(bf16[192,128]{1,0:T(8,128)(2,1)S(1)} %get-tuple-element.80), channel_id=1, source_target_pairs={{0,2},{2,0},{1,3},{3,1},{4,6},{6,4},{5,7},{7,5},{8,10},{10,8},{9,1... | collective-permute-start | bytes 147464 | tf_op jit(solution)/shard_map/ppermute | solution.py:536
  35.2 7.9 %collective-permute-start.8 = (bf16[224,128]{1,0:T(8,128)(2,1)S(1)}, bf16[224,128]{1,0:T(8,128)(2,1)S(1)}, u32[]{:S(2)}, u32[]{:S(2)}) collective-permute-start(bf16[224,128]{1,0:T(8,128)(2,1)S(1)} %shard_map.134.own_ref), channel_id=1, source_target_pairs={{0,8},{4,12},{8,0},{12,4},{1,9},{5,13},{9,1},{13,5},{2,10},{6,14},... | collective-permute-start | bytes 172040 | tf_op jit(solution)/shard_map/ppermute | solution.py:536
  36.5 11.6 %collective-permute-start.12 = (bf16[184,512]{1,0:T(8,128)(2,1)S(1)}, bf16[184,512]{1,0:T(8,128)(2,1)S(1)}, u32[]{:S(2)}, u32[]{:S(2)}) collective-permute-start(bf16[184,512]{1,0:T(8,128)(2,1)S(1)} %get-tuple-element.89), channel_id=1, source_target_pairs={{0,4},{4,0},{8,12},{12,8},{1,5},{5,1},{9,13},{13,9},{2,6},{6,2},{1... | collective-permute-start | bytes 565256 | tf_op jit(solution)/shard_map/ppermute | solution.py:536
  38.5 15.1 %collective-permute-start.13 = (bf16[184,512]{1,0:T(8,128)(2,1)S(1)}, bf16[184,512]{1,0:T(8,128)(2,1)S(1)}, u32[]{:S(2)}, u32[]{:S(2)}) collective-permute-start(bf16[184,512]{1,0:T(8,128)(2,1)S(1)} %get-tuple-element.93), channel_id=1, source_target_pairs={{0,8},{4,12},{8,0},{12,4},{1,9},{5,13},{9,1},{13,5},{2,10},{6,14},... | collective-permute-start | bytes 565256 | tf_op jit(solution)/shard_map/ppermute | solution.py:536
  38.6 15.1 %collective-permute-start.14 = (bf16[184,512]{1,0:T(8,128)(2,1)S(1)}, bf16[184,512]{1,0:T(8,128)(2,1)S(1)}, u32[]{:S(2)}, u32[]{:S(2)}) collective-permute-start(bf16[184,512]{1,0:T(8,128)(2,1)S(1)} %get-tuple-element.94), channel_id=1, source_target_pairs={{0,12},{4,8},{8,4},{12,0},{1,13},{5,9},{9,5},{13,1},{2,14},{6,10},... | collective-permute-start | bytes 565256 | tf_op jit(solution)/shard_map/ppermute | solution.py:536
  43.1 6.8 %copy-start = (bf16[4,768,184]{2,1,0:T(8,128)(2,1)S(1)}, bf16[4,768,184]{2,1,0:T(8,128)(2,1)}, u32[]{:S(2)}) copy-start(bf16[4,768,184]{2,1,0:T(8,128)(2,1)} %constant.8.clone.table_ref) | copy-start | bytes 3391492
  43.1 7.9 %collective-permute-start.11 = (bf16[224,128]{1,0:T(8,128)(2,1)S(1)}, bf16[224,128]{1,0:T(8,128)(2,1)S(1)}, u32[]{:S(2)}, u32[]{:S(2)}) collective-permute-start(bf16[224,128]{1,0:T(8,128)(2,1)S(1)} %shard_map.135.refs_0_), channel_id=1, source_target_pairs={{0,6},{2,4},{4,2},{6,0},{8,14},{10,12},{12,10},{14,8},{1,7},{3,5},... | collective-permute-start | bytes 172040 | tf_op jit(solution)/shard_map/ppermute | solution.py:545
  43.2 8.0 %collective-permute-start.10 = (bf16[224,128]{1,0:T(8,128)(2,1)S(1)}, bf16[224,128]{1,0:T(8,128)(2,1)S(1)}, u32[]{:S(2)}, u32[]{:S(2)}) collective-permute-start(bf16[224,128]{1,0:T(8,128)(2,1)S(1)} %shard_map.135.refs_0_), channel_id=1, source_target_pairs={{0,4},{4,0},{8,12},{12,8},{1,5},{5,1},{9,13},{13,9},{2,6},{6,2},{1... | collective-permute-start | bytes 172040 | tf_op jit(solution)/shard_map/ppermute | solution.py:536
  48.1 4.2 %collective-permute-start.9 = (bf16[224,128]{1,0:T(8,128)(2,1)S(1)}, bf16[224,128]{1,0:T(8,128)(2,1)S(1)}, u32[]{:S(2)}, u32[]{:S(2)}) collective-permute-start(bf16[224,128]{1,0:T(8,128)(2,1)S(1)} %shard_map.135.refs_0_), channel_id=1, source_target_pairs={{0,2},{2,0},{1,3},{3,1},{4,6},{6,4},{5,7},{7,5},{8,10},{10,8},{9,1... | collective-permute-start | bytes 172040 | tf_op jit(solution)/shard_map/ppermute | solution.py:536
